TPU v7x, 32 devices: a whole 2x2x4 slice. The times are simulated.
32 devices in a mesh: section: 4 (over y, core), table: 8 (over z, x).
Axes of the slice: x: 2, y: 2, z: 4, core: 2. Of those that a mesh axis runs over, the one named last changes fastest.
Arguments:
- emb_table: bfloat16 [131072, 128], P(('section', 'table')), may hold values from -6 to 6
- lcb_weight: bfloat16 [8, 512], replicated, may hold values from -0.25 to 0.25
- fm_proj: bfloat16 [4, 8, 128], P('section'), may hold values from -2 to 2
- norm_gain: bfloat16 [4, 1024], P('section'), may hold values from 0.25 to 1.75
- w_up: bfloat16 [4, 1024, 4096], P('section'), may hold values from -0.1875 to 0.1875
- w_down: bfloat16 [4, 4096, 1024], P('section'), may hold values from -0.09375 to 0.09375
- top_grad: bfloat16 [8, 4, 64, 1024], P('table'), may hold values from -12 to 12
- lookup_slot: int32 [8, 256, 512], P('table', 'section'), may hold values from 0 to 4095, as said below
- wanted_rows: int32 [32, 32, 128], P(('section', 'table')), may hold values from 0 to 4095, as said below
- row_counts: int32 [32, 32], P(('section', 'table')), may hold values from 32 to 128, as said below
Outputs:
- table_grad: float32 [131072, 128], P(('section', 'table'))
Inputs may be any that keep to these rules, and one draw needn't show every extreme that they name: The first row_counts[o, q] entries of wanted_rows[o, q] are distinct rows; the others are also rows of the owner. `row_counts`: some owners have 128 live slots for every asking device. `lookup_slot`: A lookup of asking device q names slot o * 128 + c with c below row_counts[o, q].
All inputs are finite; a program needn't handle non-finite values.
Results may differ from a plain program's by a relative error of at most 0.025.
Values may be sent and summed in bfloat16 or wider, within the bound.
No kernel may reach another device: no remote copies, remote signals or barrier semaphores. Data moves between devices by JAX's collectives and lax.ppermute only.
A program may use at most 128 MiB of HBM per device.

v0:
```python
import jax
import jax.numpy as jnp
from jax import lax
from jax.sharding import PartitionSpec as P

EPSILON = 1e-05
DECAY_WEIGHT = 0.5


def shifted(value, axis, steps):
    count = lax.axis_size(axis)
    first, last = (max(0, -steps), min(count, count - steps))
    return lax.ppermute(value, axis, [(source, source + steps) for source in range(first, last)])


def fm_forward(inputs, proj, gain, w_up, w_down):
    batch_rows = inputs.shape[0]
    embed_count = proj.shape[0]
    features = inputs.reshape(batch_rows, embed_count, -1)
    mixed_cols = jnp.einsum(
        "bke,kr->bre", features, proj, preferred_element_type=jnp.float32
    ).astype(jnp.bfloat16)
    interact = jnp.einsum(
        "bke,bre->bkr", features, mixed_cols, preferred_element_type=jnp.float32
    ).reshape(batch_rows, -1)
    inv_scale = lax.rsqrt(jnp.mean(interact * interact, axis=1, keepdims=True) + EPSILON)
    normed = (interact * inv_scale * gain.astype(jnp.float32)).astype(jnp.bfloat16)
    before = jnp.dot(normed, w_up, preferred_element_type=jnp.float32)
    hidden = jnp.maximum(before, 0.0).astype(jnp.bfloat16)
    output = inputs.astype(jnp.float32) + jnp.dot(
        hidden, w_down, preferred_element_type=jnp.float32
    )
    return (output.astype(jnp.bfloat16), (features, mixed_cols, interact, inv_scale, before))


def fm_backward(inputs, grad_out, proj, gain, w_up, w_down):
    batch_rows = inputs.shape[0]
    embed_count = proj.shape[0]
    unused, saved = fm_forward(inputs, proj, gain, w_up, w_down)
    features, mixed_cols, interact, inv_scale, before = saved
    last_dims = (((1,), (1,)), ((), ()))
    g_hidden = lax.dot_general(grad_out, w_down, last_dims, preferred_element_type=jnp.float32)
    g_before = jnp.where(before > 0.0, g_hidden, 0.0).astype(jnp.bfloat16)
    g_normed = lax.dot_general(g_before, w_up, last_dims, preferred_element_type=jnp.float32)
    weighted = g_normed * gain.astype(jnp.float32)
    g_interact = inv_scale * (
        weighted
        - interact * inv_scale * inv_scale * jnp.mean(weighted * interact, axis=1, keepdims=True)
    )
    g_interact = g_interact.astype(jnp.bfloat16).reshape(batch_rows, embed_count, -1)
    g_features = jnp.einsum(
        "bkr,bre->bke", g_interact, mixed_cols, preferred_element_type=jnp.float32
    )
    g_mixed = jnp.einsum(
        "bkr,bke->bre", g_interact, features, preferred_element_type=jnp.float32
    ).astype(jnp.bfloat16)
    g_features = g_features + jnp.einsum(
        "bre,kr->bke", g_mixed, proj, preferred_element_type=jnp.float32
    )
    return (grad_out.astype(jnp.float32) + g_features.reshape(batch_rows, -1)).astype(jnp.bfloat16)


def pass_on(payload, offset):
    return shifted(payload, "section", offset)


def per_device(
    emb_table,
    lcb_weight,
    fm_proj,
    norm_gain,
    w_up,
    w_down,
    top_grad,
    lookup_slot,
    wanted_rows,
    row_counts,
):
    section_count = lax.axis_size("section")
    shard_count = lax.axis_size("table")
    my_section = lax.axis_index("section")
    owners = section_count * shard_count
    cap = wanted_rows.shape[2]
    embed_width = emb_table.shape[1]
    picked_rows = wanted_rows[0]
    outgoing = jnp.take(emb_table, picked_rows.reshape(-1), axis=0).reshape(
        owners, cap, embed_width
    )
    fetched = lax.all_to_all(
        outgoing, ("section", "table"), split_axis=0, concat_axis=0, tiled=True
    )
    fetched = fetched.reshape(owners * cap, embed_width)
    lookup_slots = lookup_slot[0]
    look_dev = lookup_slots.shape[0]
    feature_count = lookup_slots.shape[1]
    embedded = jnp.take(fetched, lookup_slots.reshape(-1), axis=0).reshape(
        look_dev, feature_count, embed_width
    )
    compressed = jnp.einsum(
        "kf,bfe->bke", lcb_weight, embedded, preferred_element_type=jnp.float32
    ).astype(jnp.bfloat16)
    compressed = compressed.reshape(look_dev, -1)
    leading = lax.all_gather(compressed, "section", axis=0, tiled=True)
    micro_count = top_grad.shape[1]
    batch_rows = top_grad.shape[2]
    model_width = top_grad.shape[3]
    leading = leading.reshape(micro_count, batch_rows, model_width)
    weights = (fm_proj[0], norm_gain[0], w_up[0], w_down[0])
    tick_count = micro_count + section_count - 1

    def forward_tick(tick, state):
        incoming, stash = state
        micro_idx = tick - my_section
        is_valid = (micro_idx >= 0) & (micro_idx < micro_count)
        clipped = jnp.clip(micro_idx, 0, micro_count - 1)
        inputs = jnp.where(
            my_section == 0, lax.dynamic_index_in_dim(leading, clipped, 0, keepdims=False), incoming
        )
        outputs = lax.cond(
            is_valid,
            lambda value: fm_forward(value, *weights)[0],
            lambda value: jnp.zeros_like(value),
            inputs,
        )
        kept_rows = jnp.where(
            is_valid, inputs, lax.dynamic_index_in_dim(stash, clipped, 0, keepdims=False)
        )
        stash = lax.dynamic_update_index_in_dim(stash, kept_rows, clipped, 0)
        return (pass_on(outputs, 1), stash)

    empty_rows = jnp.zeros((batch_rows, model_width), jnp.bfloat16)
    empty_stash = jnp.zeros((micro_count, batch_rows, model_width), jnp.bfloat16)
    unused, stash = lax.fori_loop(0, tick_count, forward_tick, (empty_rows, empty_stash))
    grads_top = top_grad[0]

    def backward_tick(tick, state):
        incoming, lead_grad = state
        micro_idx = tick - (section_count - 1 - my_section)
        is_valid = (micro_idx >= 0) & (micro_idx < micro_count)
        clipped = jnp.clip(micro_idx, 0, micro_count - 1)
        given = jnp.where(
            my_section == section_count - 1,
            lax.dynamic_index_in_dim(grads_top, clipped, 0, keepdims=False),
            incoming,
        )
        saved_rows = lax.dynamic_index_in_dim(stash, clipped, 0, keepdims=False)
        result = lax.cond(
            is_valid,
            lambda pair: fm_backward(pair[0], pair[1], *weights),
            lambda pair: jnp.zeros_like(pair[0]),
            (saved_rows, given),
        )
        record = jnp.where(
            is_valid & (my_section == 0),
            result,
            lax.dynamic_index_in_dim(lead_grad, clipped, 0, keepdims=False),
        )
        lead_grad = lax.dynamic_update_index_in_dim(lead_grad, record, clipped, 0)
        return (pass_on(result, -1), lead_grad)

    unused, lead_grad = lax.fori_loop(0, tick_count, backward_tick, (empty_rows, empty_stash))
    terms = jnp.where(my_section == 0, lead_grad.astype(jnp.float32), 0.0).reshape(
        micro_count * batch_rows, model_width
    )
    lead_share = lax.psum_scatter(
        terms.astype(jnp.bfloat16), "section", scatter_dimension=0, tiled=True
    )
    embed_count = lcb_weight.shape[0]
    feature_grad = jnp.einsum(
        "kf,bke->bfe",
        lcb_weight,
        lead_share.reshape(look_dev, embed_count, embed_width),
        preferred_element_type=jnp.float32,
    )
    slot_grad = jax.ops.segment_sum(
        feature_grad.reshape(-1, embed_width), lookup_slots.reshape(-1), num_segments=owners * cap
    )
    slot_grad = slot_grad.reshape(owners, cap, embed_width)
    returned = lax.all_to_all(
        slot_grad.astype(jnp.bfloat16),
        ("section", "table"),
        split_axis=0,
        concat_axis=0,
        tiled=True,
    ).astype(slot_grad.dtype)
    live_slots = jnp.arange(cap)[None, :] < row_counts[0][:, None]
    decay_term = jnp.where(live_slots[..., None], DECAY_WEIGHT * outgoing.astype(jnp.float32), 0.0)
    table_grad = (
        jnp.zeros(emb_table.shape, jnp.float32)
        .at[picked_rows.reshape(-1)]
        .add((returned + decay_term).reshape(-1, embed_width))
    )
    return table_grad


def solution(mesh):
    in_specs = (
        P(("section", "table"), None),
        P(),
        P("section", None, None),
        P("section", None),
        P("section", None, None),
        P("section", None, None),
        P("table", None, None, None),
        P("table", "section", None),
        P(("section", "table"), None, None),
        P(("section", "table"), None),
    )
    out_specs = P(("section", "table"), None)
    return jax.shard_map(
        per_device, mesh=mesh, in_specs=in_specs, out_specs=out_specs, check_vma=False
    )
```

profile of v0, /device:TPU:0, one launch (start us, length us, event | category | flops | bytes accessed | tf_op | source)
XLA Modules:
  0.0 789.9 jit_solution(16605242310247008547)
XLA Ops:
  8.1 12.1 %gather_fusion = bf16[4096,128]{1,0:T(8,128)(2,1)S(1)} fusion(bf16[4096,128]{1,0:T(8,128)(2,1)S(1)} %copy-done, s32[4096]{0:T(1024)S(1)} %broadcast_clamp_fusion.1), kind=kCustom, calls=%fused_computation | custom fusion | bytes 2113536 | tf_op jit(solution)/shard_map/jit(_take)/gather | solution.py:86
  29.6 27.1 %all-to-all-done = bf16[32,128,128]{2,1,0:T(8,128)(2,1)S(1)} async-done(((bf16[32,128,128]{2,1,0:T(8,128)(2,1)}), bf16[32,128,128]{2,1,0:T(8,128)(2,1)S(1)}, u32[]{:S(2)}, u32[]{:S(2)}) %all-to-all-start) | async-done | bytes 1048608 | tf_op jit(solution)/shard_map/all_to_all | solution.py:89
  56.7 114.1 %gather_fusion.1 = bf16[32768,128]{1,0:T(8,128)(2,1)} fusion(bf16[4096,128]{1,0:T(8,128)(2,1)S(1)} %bitcast.147, s32[32768]{0:T(1024)S(1)} %broadcast_clamp_fusion), kind=kCustom, calls=%fused_computation.1 | custom fusion | bytes 16908288 | tf_op jit(solution)/shard_map/jit(_take)/gather | solution.py:96
  170.8 8.8 %fusion.43 = bf16[64,128,8]{1,2,0:T(8,128)(2,1)S(1)} fusion(bf16[64,512,128]{2,1,0:T(8,128)(2,1)} %bitcast.163, pred[64,512]{1,0:T(8,128)(4,1)S(1)} %compare_and_fusion, bf16[8,512]{1,0:T(8,128)(2,1)S(1)} %copy-done.6), kind=kOutput, calls=%fused_computation.66 | convolution fusion | flops 71368704 | bytes 8560640 | tf_op jit(solution)/shard_map/kf,bfe->bke/dot_general | solution.py:99
  187.1 111.2 %while.33 = (s32[]{:T(128)}, bf16[64,1024]{1,0:T(8,128)(2,1)S(1)}, bf16[4,64,1024]{2,1,0:T(8,128)(2,1)}, s32[]{:T(128)}, pred[]{:T(512)}, /*index=5*/bf16[4,64,1...) while((s32[]{:T(128)}, bf16[64,1024]{1,0:T(8,128)(2,1)S(1)}, ...), condition=%wide.region_4.5_spmd, body=%wide.region_0.4_spmd.sunk | while | flops 1109525504 | bytes 19412772 | solution.py:133
  188.8 10.9 %conditional.4 = (bf16[64,1024]{1,0:T(8,128)(2,1)S(1)}) conditional(s32[]{:T(128)} %convert_element_type.154, () %tuple.88, (bf16[64,1024]{1,0:T(8,128)(2,1)S(1)}, bf16[8,128]{1,0:T(8,128)(2,1)S(1)}, bf16[1024]{0:T(1024)(128)(2,1)S(1)}, bf16[1024,4096]{1,0:T(8,128)(2,1)}, bf16[4096,1024]{1,0:T(8,128)(2,1)}) %tuple.89), branch_computations={%region_1.1_spmd, %region_2.3_spmd} | conditional | flops 1109394432 | bytes 17970184 | solution.py:119
  190.7 8.9 %fusion.6 = bf16[64,1024]{1,0:T(8,128)(2,1)S(1)} fusion(bf16[4096,1024]{1,0:T(8,128)(2,1)} %get-tuple-element.515, bf16[1024,4096]{1,0:T(8,128)(2,1)} %get-tuple-element.514, bf16[64,1024]{1,0:T(8,128)(2,1)S(1)} %get-tuple-element.511, f32[8,8,8,128]{3,2,1,0:T(8,128)S(1)} %bitcast.164, f32[1024]{0:T(1024)S(1)} %convert_element_type.84, f32[64]{0:T(128)S(1)} %add_rsqrt_fusion), kind=kOutput, calls=%fused_computation.11 | convolution fusion | flops 1074659328 | bytes 17305856 | tf_op jit(solution)/shard_map/while/body/eval_jaxpr/cond/branch_1_fun/dot_general | solution.py:30
  203.6 10.9 %conditional.4 = (bf16[64,1024]{1,0:T(8,128)(2,1)S(1)}) conditional(s32[]{:T(128)} %convert_element_type.154, () %tuple.88, (bf16[64,1024]{1,0:T(8,128)(2,1)S(1)}, bf16[8,128]{1,0:T(8,128)(2,1)S(1)}, bf16[1024]{0:T(1024)(128)(2,1)S(1)}, bf16[1024,4096]{1,0:T(8,128)(2,1)}, bf16[4096,1024]{1,0:T(8,128)(2,1)}) %tuple.89), branch_computations={%region_1.1_spmd, %region_2.3_spmd} | conditional | flops 1109394432 | bytes 17970184 | solution.py:119
  205.5 8.9 %fusion.6 = bf16[64,1024]{1,0:T(8,128)(2,1)S(1)} fusion(bf16[4096,1024]{1,0:T(8,128)(2,1)} %get-tuple-element.515, bf16[1024,4096]{1,0:T(8,128)(2,1)} %get-tuple-element.514, bf16[64,1024]{1,0:T(8,128)(2,1)S(1)} %get-tuple-element.511, f32[8,8,8,128]{3,2,1,0:T(8,128)S(1)} %bitcast.164, f32[1024]{0:T(1024)S(1)} %convert_element_type.84, f32[64]{0:T(128)S(1)} %add_rsqrt_fusion), kind=kOutput, calls=%fused_computation.11 | convolution fusion | flops 1074659328 | bytes 17305856 | tf_op jit(solution)/shard_map/while/body/eval_jaxpr/cond/branch_1_fun/dot_general | solution.py:30
  219.3 10.9 %conditional.4 = (bf16[64,1024]{1,0:T(8,128)(2,1)S(1)}) conditional(s32[]{:T(128)} %convert_element_type.154, () %tuple.88, (bf16[64,1024]{1,0:T(8,128)(2,1)S(1)}, bf16[8,128]{1,0:T(8,128)(2,1)S(1)}, bf16[1024]{0:T(1024)(128)(2,1)S(1)}, bf16[1024,4096]{1,0:T(8,128)(2,1)}, bf16[4096,1024]{1,0:T(8,128)(2,1)}) %tuple.89), branch_computations={%region_1.1_spmd, %region_2.3_spmd} | conditional | flops 1109394432 | bytes 17970184 | solution.py:119
  221.3 8.9 %fusion.6 = bf16[64,1024]{1,0:T(8,128)(2,1)S(1)} fusion(bf16[4096,1024]{1,0:T(8,128)(2,1)} %get-tuple-element.515, bf16[1024,4096]{1,0:T(8,128)(2,1)} %get-tuple-element.514, bf16[64,1024]{1,0:T(8,128)(2,1)S(1)} %get-tuple-element.511, f32[8,8,8,128]{3,2,1,0:T(8,128)S(1)} %bitcast.164, f32[1024]{0:T(1024)S(1)} %convert_element_type.84, f32[64]{0:T(128)S(1)} %add_rsqrt_fusion), kind=kOutput, calls=%fused_computation.11 | convolution fusion | flops 1074659328 | bytes 17305856 | tf_op jit(solution)/shard_map/while/body/eval_jaxpr/cond/branch_1_fun/dot_general | solution.py:30
  235.7 10.9 %conditional.4 = (bf16[64,1024]{1,0:T(8,128)(2,1)S(1)}) conditional(s32[]{:T(128)} %convert_element_type.154, () %tuple.88, (bf16[64,1024]{1,0:T(8,128)(2,1)S(1)}, bf16[8,128]{1,0:T(8,128)(2,1)S(1)}, bf16[1024]{0:T(1024)(128)(2,1)S(1)}, bf16[1024,4096]{1,0:T(8,128)(2,1)}, bf16[4096,1024]{1,0:T(8,128)(2,1)}) %tuple.89), branch_computations={%region_1.1_spmd, %region_2.3_spmd} | conditional | flops 1109394432 | bytes 17970184 | solution.py:119
  237.6 8.9 %fusion.6 = bf16[64,1024]{1,0:T(8,128)(2,1)S(1)} fusion(bf16[4096,1024]{1,0:T(8,128)(2,1)} %get-tuple-element.515, bf16[1024,4096]{1,0:T(8,128)(2,1)} %get-tuple-element.514, bf16[64,1024]{1,0:T(8,128)(2,1)S(1)} %get-tuple-element.511, f32[8,8,8,128]{3,2,1,0:T(8,128)S(1)} %bitcast.164, f32[1024]{0:T(1024)S(1)} %convert_element_type.84, f32[64]{0:T(128)S(1)} %add_rsqrt_fusion), kind=kOutput, calls=%fused_computation.11 | convolution fusion | flops 1074659328 | bytes 17305856 | tf_op jit(solution)/shard_map/while/body/eval_jaxpr/cond/branch_1_fun/dot_general | solution.py:30
  254.5 16.2 %collective-permute-start = (bf16[64,1024]{1,0:T(8,128)(2,1)S(1)}, bf16[64,1024]{1,0:T(8,128)(2,1)S(1)}, u32[]{:S(2)}, u32[]{:S(2)}) collective-permute-start(bf16[64,1024]{1,0:T(8,128)(2,1)S(1)} %get-tuple-element.833), channel_id=1, source_target_pairs={{0,8},{8,16},{16,24},{1,9},{9,17},{17,25},{2,10},{10,18},{18,26},{... | collective-permute-start | bytes 393224 | tf_op jit(solution)/shard_map/while/body/eval_jaxpr/ppermute | solution.py:13
  281.2 16.2 %collective-permute-start = (bf16[64,1024]{1,0:T(8,128)(2,1)S(1)}, bf16[64,1024]{1,0:T(8,128)(2,1)S(1)}, u32[]{:S(2)}, u32[]{:S(2)}) collective-permute-start(bf16[64,1024]{1,0:T(8,128)(2,1)S(1)} %get-tuple-element.833), channel_id=1, source_target_pairs={{0,8},{8,16},{16,24},{1,9},{9,17},{17,25},{2,10},{10,18},{18,26},{... | collective-permute-start | bytes 393224 | tf_op jit(solution)/shard_map/while/body/eval_jaxpr/ppermute | solution.py:13
  299.2 198.4 %while.34 = (s32[]{:T(128)}, bf16[64,1024]{1,0:T(8,128)(2,1)S(1)}, bf16[4,64,1024]{2,1,0:T(8,128)(2,1)}, s32[]{:T(128)}, pred[]{:T(512)}, /*index=5*/bf16[4,64,1...) while((s32[]{:T(128)}, bf16[64,1024]{1,0:T(8,128)(2,1)S(1)}, ...), condition=%wide.region_10.11_spmd, body=%wide.region_5.10_spmd.sunk | while | flops 1698759680 | bytes 38033496 | solution.py:161
  308.5 8.5 %collective-permute-done.1 = bf16[64,1024]{1,0:T(8,128)(2,1)S(1)} collective-permute-done((bf16[64,1024]{1,0:T(8,128)(2,1)S(1)}, bf16[64,1024]{1,0:T(8,128)(2,1)S(1)}, u32[]{:S(2)}, u32[]{:S(2)}) %collective-permute-start.1) | collective-permute-done | bytes 131104 | tf_op jit(solution)/shard_map/while/body/eval_jaxpr/ppermute | solution.py:13
  320.0 66.4 %collective-permute-done.1 = bf16[64,1024]{1,0:T(8,128)(2,1)S(1)} collective-permute-done((bf16[64,1024]{1,0:T(8,128)(2,1)S(1)}, bf16[64,1024]{1,0:T(8,128)(2,1)S(1)}, u32[]{:S(2)}, u32[]{:S(2)}) %collective-permute-start.1) | collective-permute-done | bytes 131104 | tf_op jit(solution)/shard_map/while/body/eval_jaxpr/ppermute | solution.py:13
  386.3 22.3 %conditional.5 = (bf16[64,1024]{1,0:T(8,128)(2,1)S(1)}) conditional(s32[]{:T(128)} %convert_element_type.155, () %tuple.91, (pred[]{:T(512)}, bf16[4,64,1024]{2,1,0:T(8,128)(2,1)}, s32[]{:T(128)}, bf16[64,1024]{1,0:T(8,128)(2,1)S(1)}, bf16[4,64,1024]{2,1,0:T(8,128)(2,1)}, /*index=5*/bf16[8,128]{1,0:T(8,128)(2,1)S(1)}, bf16[1024]{0:T(1024)(128)(2,1)S(1)}, ...), branch_computations={%region_6.6_spmd, %region_7.9_spmd} | conditional | flops 1698694144 | bytes 36853008 | solution.py:147
  394.1 11.1 %fusion.30 = (f32[64]{0:T(128)S(1)}, f32[64,1024]{1,0:T(8,128)S(1)}) fusion(f32[8,8,8,128]{3,2,1,0:T(8,128)S(1)} %bitcast.151, f32[1024]{0:T(1024)S(1)} %convert_element_type.91, bf16[1024,4096]{1,0:T(8,128)(2,1)} %get-tuple-element.534, pred[64,4096]{1,0:T(32,128)(4,1)S(1)} %convolution_compare_fusion, bf16[4096,1024]{1,0:T(8,128)(2,1)} %get-tuple-element.535, ...), kind=kOutput, calls=%fused_computation.42 | convolution fusion | flops 1074528256 | bytes 17831168 | tf_op jit(solution)/shard_map/while/body/eval_jaxpr/cond/branch_1_fun/dot_general | solution.py:44
  414.9 22.3 %conditional.5 = (bf16[64,1024]{1,0:T(8,128)(2,1)S(1)}) conditional(s32[]{:T(128)} %convert_element_type.155, () %tuple.91, (pred[]{:T(512)}, bf16[4,64,1024]{2,1,0:T(8,128)(2,1)}, s32[]{:T(128)}, bf16[64,1024]{1,0:T(8,128)(2,1)S(1)}, bf16[4,64,1024]{2,1,0:T(8,128)(2,1)}, /*index=5*/bf16[8,128]{1,0:T(8,128)(2,1)S(1)}, bf16[1024]{0:T(1024)(128)(2,1)S(1)}, ...), branch_computations={%region_6.6_spmd, %region_7.9_spmd} | conditional | flops 1698694144 | bytes 36853008 | solution.py:147
  422.7 11.1 %fusion.30 = (f32[64]{0:T(128)S(1)}, f32[64,1024]{1,0:T(8,128)S(1)}) fusion(f32[8,8,8,128]{3,2,1,0:T(8,128)S(1)} %bitcast.151, f32[1024]{0:T(1024)S(1)} %convert_element_type.91, bf16[1024,4096]{1,0:T(8,128)(2,1)} %get-tuple-element.534, pred[64,4096]{1,0:T(32,128)(4,1)S(1)} %convolution_compare_fusion, bf16[4096,1024]{1,0:T(8,128)(2,1)} %get-tuple-element.535, ...), kind=kOutput, calls=%fused_computation.42 | convolution fusion | flops 1074528256 | bytes 17831168 | tf_op jit(solution)/shard_map/while/body/eval_jaxpr/cond/branch_1_fun/dot_general | solution.py:44
  443.5 22.3 %conditional.5 = (bf16[64,1024]{1,0:T(8,128)(2,1)S(1)}) conditional(s32[]{:T(128)} %convert_element_type.155, () %tuple.91, (pred[]{:T(512)}, bf16[4,64,1024]{2,1,0:T(8,128)(2,1)}, s32[]{:T(128)}, bf16[64,1024]{1,0:T(8,128)(2,1)S(1)}, bf16[4,64,1024]{2,1,0:T(8,128)(2,1)}, /*index=5*/bf16[8,128]{1,0:T(8,128)(2,1)S(1)}, bf16[1024]{0:T(1024)(128)(2,1)S(1)}, ...), branch_computations={%region_6.6_spmd, %region_7.9_spmd} | conditional | flops 1698694144 | bytes 36853008 | solution.py:147
  451.3 11.1 %fusion.30 = (f32[64]{0:T(128)S(1)}, f32[64,1024]{1,0:T(8,128)S(1)}) fusion(f32[8,8,8,128]{3,2,1,0:T(8,128)S(1)} %bitcast.151, f32[1024]{0:T(1024)S(1)} %convert_element_type.91, bf16[1024,4096]{1,0:T(8,128)(2,1)} %get-tuple-element.534, pred[64,4096]{1,0:T(32,128)(4,1)S(1)} %convolution_compare_fusion, bf16[4096,1024]{1,0:T(8,128)(2,1)} %get-tuple-element.535, ...), kind=kOutput, calls=%fused_computation.42 | convolution fusion | flops 1074528256 | bytes 17831168 | tf_op jit(solution)/shard_map/while/body/eval_jaxpr/cond/branch_1_fun/dot_general | solution.py:44
  472.1 22.3 %conditional.5 = (bf16[64,1024]{1,0:T(8,128)(2,1)S(1)}) conditional(s32[]{:T(128)} %convert_element_type.155, () %tuple.91, (pred[]{:T(512)}, bf16[4,64,1024]{2,1,0:T(8,128)(2,1)}, s32[]{:T(128)}, bf16[64,1024]{1,0:T(8,128)(2,1)S(1)}, bf16[4,64,1024]{2,1,0:T(8,128)(2,1)}, /*index=5*/bf16[8,128]{1,0:T(8,128)(2,1)S(1)}, bf16[1024]{0:T(1024)(128)(2,1)S(1)}, ...), branch_computations={%region_6.6_spmd, %region_7.9_spmd} | conditional | flops 1698694144 | bytes 36853008 | solution.py:147
  479.8 11.1 %fusion.30 = (f32[64]{0:T(128)S(1)}, f32[64,1024]{1,0:T(8,128)S(1)}) fusion(f32[8,8,8,128]{3,2,1,0:T(8,128)S(1)} %bitcast.151, f32[1024]{0:T(1024)S(1)} %convert_element_type.91, bf16[1024,4096]{1,0:T(8,128)(2,1)} %get-tuple-element.534, pred[64,4096]{1,0:T(32,128)(4,1)S(1)} %convolution_compare_fusion, bf16[4096,1024]{1,0:T(8,128)(2,1)} %get-tuple-element.535, ...), kind=kOutput, calls=%fused_computation.42 | convolution fusion | flops 1074528256 | bytes 17831168 | tf_op jit(solution)/shard_map/while/body/eval_jaxpr/cond/branch_1_fun/dot_general | solution.py:44
  499.6 19.6 %reduce-scatter.2.cloned.1.call-done = bf16[64,1024]{1,0:T(8,128)(2,1)} async-done(((bf16[256,1024]{1,0:T(8,128)(2,1)}), bf16[64,1024]{1,0:T(8,128)(2,1)}) %reduce-scatter.2.cloned.1.call-update) | async-done | bytes 131088 | tf_op jit(solution)/shard_map/reduce_scatter | solution.py:165
  520.1 8.1 %convolution_bitcast_fusion = f32[64,512,128]{1,2,0:T(8,128)} fusion(bf16[64,8,128]{2,1,0:T(8,128)(2,1)S(1)} %bitcast.172, bf16[8,512]{1,0:T(8,128)(2,1)S(1)} %copy-done.6), kind=kOutput, calls=%fused_computation.60 | convolution fusion | flops 67108864 | bytes 16916480 | tf_op jit(solution)/shard_map/kf,bke->bfe/dot_general | solution.py:169
  528.3 17.4 %copy.11 = f32[64,512,128]{2,1,0:T(8,128)} copy(f32[64,512,128]{1,2,0:T(8,128)} %convolution_bitcast_fusion) | data formatting | bytes 33554432 | tf_op jit(solution)/shard_map/kf,bke->bfe/transpose | solution.py:169
  545.6 175.9 %scatter_custom_fusion = f32[4096,128]{1,0:T(8,128)} fusion(s32[32768]{0:T(1024)S(1)} %bitcast.176, f32[32768,128]{1,0:T(8,128)} %bitcast.158, f32[]{:T(128)} %constant.165.clone.1), kind=kCustom, calls=%fused_computation.70 | custom fusion | flops 4194304 | bytes 2097664 | tf_op jit(solution)/shard_map/scatter-add | solution.py:175
  728.9 27.5 %all-to-all-done.1 = bf16[32,128,128]{2,1,0:T(8,128)(2,1)S(1)} async-done(((bf16[32,128,128]{2,1,0:T(8,128)(2,1)}), bf16[32,128,128]{2,1,0:T(8,128)(2,1)S(1)}, u32[]{:S(2)}, u32[]{:S(2)}) %all-to-all-start.1) | async-done | bytes 1048608 | tf_op jit(solution)/shard_map/all_to_all | solution.py:179
  759.0 24.1 %scatter_custom_fusion.1 = f32[4096,128]{1,0:T(8,128)} fusion(s32[4096]{0:T(1024)S(1)} %bitcast.181, f32[4096,128]{1,0:T(8,128)} %bitcast.168, f32[]{:T(128)} %constant.165.clone.1), kind=kCustom, calls=%fused_computation.68 | custom fusion | flops 524288 | bytes 2097664 | tf_op jit(solution)/shard_map/scatter-add | solution.py:191
  (175 shorter events, 153.7 us)
Async XLA Ops:
  6.5 1.6 copy-start
  20.3 150.5 %copy-start.2 = (bf16[4096,128]{1,0:T(8,128)(2,1)}, bf16[4096,128]{1,0:T(8,128)(2,1)S(1)}, u32[]{:S(2)}) copy-start(bf16[4096,128]{1,0:T(8,128)(2,1)S(1)} %gather_fusion) | copy-start | bytes 3145732
  20.3 8.9 %copy-start.4 = (s32[1,64,512]{2,1,0:T(8,128)S(1)}, s32[1,64,512]{2,1,0:T(8,128)}, u32[]{:S(2)}) copy-start(s32[1,64,512]{2,1,0:T(8,128)} %param.25) | copy-start | bytes 393220
  20.3 9.2 %copy-start.7 = (bf16[1,1024]{1,0:T(2,128)(2,1)S(1)}, bf16[1,1024]{1,0:T(2,128)(2,1)}, u32[]{:S(2)}) copy-start(bf16[1,1024]{1,0:T(2,128)(2,1)} %param.21) | copy-start | bytes 6148
  21.8 34.9 %all-to-all-start = ((bf16[32,128,128]{2,1,0:T(8,128)(2,1)}), bf16[32,128,128]{2,1,0:T(8,128)(2,1)S(1)}, u32[]{:S(2)}, u32[]{:S(2)}) async-start(bf16[32,128,128]{2,1,0:T(8,128)(2,1)} %broadcast_select_fusion), calls=%async_computation | async-start | bytes 2097152 | tf_op jit(solution)/shard_map/all_to_all | solution.py:89
  29.1 490.1 %reduce-scatter.2.cloned.1.call-start = ((), (), s32[]{:S(2)}) async-start(), calls=%async_computation.3 | async-start | bytes 655360 | tf_op jit(solution)/shard_map/reduce_scatter | solution.py:165
  56.7 114.1 %copy-start.6 = (bf16[8,512]{1,0:T(8,128)(2,1)S(1)}, bf16[8,512]{1,0:T(8,128)(2,1)}, u32[]{:S(2)}) copy-start(bf16[8,512]{1,0:T(8,128)(2,1)} %param.19) | copy-start | bytes 24580
  170.8 16.3 %copy-start.5 = (bf16[1,8,128]{2,1,0:T(8,128)(2,1)S(1)}, bf16[1,8,128]{2,1,0:T(8,128)(2,1)}, u32[]{:S(2)}) copy-start(bf16[1,8,128]{2,1,0:T(8,128)(2,1)} %param.20) | copy-start | bytes 6148
  199.6 2.3 collective-permute-start
  214.4 3.2 collective-permute-start
  230.2 3.9 collective-permute-start
  246.5 6.3 collective-permute-start
  254.5 17.1 %collective-permute-start = (bf16[64,1024]{1,0:T(8,128)(2,1)S(1)}, bf16[64,1024]{1,0:T(8,128)(2,1)S(1)}, u32[]{:S(2)}, u32[]{:S(2)}) collective-permute-start(bf16[64,1024]{1,0:T(8,128)(2,1)S(1)} %get-tuple-element.833), channel_id=1, source_target_pairs={{0,8},{8,16},{16,24},{1,9},{9,17},{17,25},{2,10},{10,18},{18,26},{... | collective-permute-start | bytes 393224 | tf_op jit(solution)/shard_map/while/body/eval_jaxpr/ppermute | solution.py:13
  273.3 6.3 collective-permute-start
  281.2 17.1 %collective-permute-start = (bf16[64,1024]{1,0:T(8,128)(2,1)S(1)}, bf16[64,1024]{1,0:T(8,128)(2,1)S(1)}, u32[]{:S(2)}, u32[]{:S(2)}) collective-permute-start(bf16[64,1024]{1,0:T(8,128)(2,1)S(1)} %get-tuple-element.833), channel_id=1, source_target_pairs={{0,8},{8,16},{16,24},{1,9},{9,17},{17,25},{2,10},{10,18},{18,26},{... | collective-permute-start | bytes 393224 | tf_op jit(solution)/shard_map/while/body/eval_jaxpr/ppermute | solution.py:13
  299.4 6.2 collective-permute-start.1
  305.6 11.4 %collective-permute-start.1 = (bf16[64,1024]{1,0:T(8,128)(2,1)S(1)}, bf16[64,1024]{1,0:T(8,128)(2,1)S(1)}, u32[]{:S(2)}, u32[]{:S(2)}) collective-permute-start(bf16[64,1024]{1,0:T(8,128)(2,1)S(1)} %get-tuple-element.834), channel_id=1, source_target_pairs={{8,0},{16,8},{24,16},{9,1},{17,9},{25,17},{10,2},{18,10},{26,18},{... | collective-permute-start | bytes 393224 | tf_op jit(solution)/shard_map/while/body/eval_jaxpr/ppermute | solution.py:13
  317.0 69.3 %collective-permute-start.1 = (bf16[64,1024]{1,0:T(8,128)(2,1)S(1)}, bf16[64,1024]{1,0:T(8,128)(2,1)S(1)}, u32[]{:S(2)}, u32[]{:S(2)}) collective-permute-start(bf16[64,1024]{1,0:T(8,128)(2,1)S(1)} %get-tuple-element.834), channel_id=1, source_target_pairs={{8,0},{16,8},{24,16},{9,1},{17,9},{25,17},{10,2},{18,10},{26,18},{... | collective-permute-start | bytes 393224 | tf_op jit(solution)/shard_map/while/body/eval_jaxpr/ppermute | solution.py:13
  408.6 6.3 collective-permute-start.1
  437.2 6.3 collective-permute-start.1
  465.8 6.3 collective-permute-start.1
  494.3 3.2 collective-permute-start.1
  545.6 183.1 %copy-start.8 = (s32[1,32]{1,0:T(1,128)S(1)}, s32[1,32]{1,0:T(1,128)}, u32[]{:S(2)}) copy-start(s32[1,32]{1,0:T(1,128)} %param.27) | copy-start | bytes 388
  545.6 210.7 %copy-start.3 = (bf16[4096,128]{1,0:T(8,128)(2,1)S(1)}, bf16[4096,128]{1,0:T(8,128)(2,1)}, u32[]{:S(2)}) copy-start(bf16[4096,128]{1,0:T(8,128)(2,1)} %copy-done.2) | copy-start | bytes 3145732
  724.2 58.9 %copy-start.1 = (bf16[4096,128]{1,0:T(8,128)(2,1)S(1)}, bf16[4096,128]{1,0:T(8,128)(2,1)}, u32[]{:S(2)}) copy-start(bf16[4096,128]{1,0:T(8,128)(2,1)} %param.18) | copy-start | bytes 3145732
  724.2 32.2 %all-to-all-start.1 = ((bf16[32,128,128]{2,1,0:T(8,128)(2,1)}), bf16[32,128,128]{2,1,0:T(8,128)(2,1)S(1)}, u32[]{:S(2)}, u32[]{:S(2)}) async-start(bf16[32,128,128]{2,1,0:T(8,128)(2,1)} %bitcast.29), calls=%async_computation.2 | async-start | bytes 2097152 | tf_op jit(solution)/shard_map/all_to_all | solution.py:179
Sparse Core Ops, SparseCore 0:
  499.7 19.5 reduce-scatter.1
where the time goes:
time: 792 us; the launch traced here: 790 us
  other arithmetic  225 us (28%)
  waiting for transfers between devices  169 us (21%)
  local copies, waits for them, and re-layouts  163 us (21%)
  matrix products  141 us (18%)
  starting transfers between devices  70.4 us (9%)
  between operations  13.6 us (2%)
    scatter-add x1, other arithmetic, per_device(): jax.ops.segment_sum(feature_grad.reshape(-1, embed_width), lookup_slots.r...  176 us
    gather x1, local copies, waits for them, and re-layouts, per_device(): jnp.take(fetched, lookup_slots.reshape(-1), axis=0)  114 us
    ppermute x14, waiting for transfers between devices, shifted(): lax.ppermute(value, axis, [(source, source + steps) for source in range(f...  95.2 us
    ppermute x14, starting transfers between devices, shifted(): lax.ppermute(value, axis, [(source, source + steps) for source in range(f...  58.4 us
    dot_general x4, matrix products, fm_backward(): lax.dot_general(g_before, w_up, last_dims, preferred_element_type=jnp.flo...  44.4 us
    dot_general x4, matrix products, fm_forward(): jnp.dot(hidden, w_down, preferred_element_type=jnp.float32)  35.6 us
    all_to_all x1, waiting for transfers between devices, per_device(): lax.all_to_all(slot_grad.astype(jnp.bfloat16), ('section', 'table'), spli...  27.5 us
    all_to_all x1, waiting for transfers between devices, per_device(): lax.all_to_all(outgoing, ('section', 'table'), split_axis=0, concat_axis=...  27.1 us
  transfers between devices with their start and end apart: 17, of which 17 were waited for; matrix products, arithmetic and copies ran while one was open for 1% of the time, Pallas kernels for 0%

commit v1 on v0

--- a/solution.py
+++ b/solution.py
@@ -1,10 +1,244 @@
 import jax
 import jax.numpy as jnp
 from jax import lax
+from jax.experimental import pallas as pl
+from jax.experimental.pallas import tpu as pltpu
 from jax.sharding import PartitionSpec as P
 
 EPSILON = 1e-05
 DECAY_WEIGHT = 0.5
+VMEM_LIMIT = 40 * 1024 * 1024
+UNROLL = 16
+
+
+def whole(memory_space=pltpu.VMEM):
+    return pl.BlockSpec(memory_space=memory_space)
+
+
+def params():
+    return pltpu.CompilerParams(vmem_limit_bytes=VMEM_LIMIT)
+
+
+def tiles_of(count, most):
+    return max(step for step in range(1, most + 1) if count % step == 0)
+
+
+def pick_rows(emb_table, picked):
+    rows, width = emb_table.shape
+    count = picked.shape[0]
+    chunk = min(count, 1024)
+
+    def kernel(picked_ref, table_ref, out_ref, wide, lines):
+        step = pl.program_id(0)
+
+        @pl.when(step == 0)
+        def _():
+            wide[...] = table_ref[...].astype(jnp.float32)
+
+        def body(group, carry):
+            first = pl.multiple_of(group * UNROLL, UNROLL)
+            for lane in range(UNROLL):
+                row = picked_ref[step * chunk + first + lane]
+                lines[pl.ds(first + lane, 1), :] = wide[pl.ds(row, 1), :]
+            return carry
+
+        lax.fori_loop(0, chunk // UNROLL, body, 0)
+        out_ref[...] = lines[...].astype(out_ref.dtype)
+
+    return pl.pallas_call(
+        kernel,
+        out_shape=jax.ShapeDtypeStruct((count, width), emb_table.dtype),
+        grid_spec=pltpu.PrefetchScalarGridSpec(
+            num_scalar_prefetch=1,
+            grid=(count // chunk,),
+            in_specs=[pl.BlockSpec((rows, width), lambda i, ids: (0, 0))],
+            out_specs=pl.BlockSpec((chunk, width), lambda i, ids: (i, 0)),
+            scratch_shapes=[
+                pltpu.VMEM((rows, width), jnp.float32),
+                pltpu.VMEM((chunk, width), jnp.float32),
+            ],
+        ),
+        compiler_params=params(),
+        name="pick_rows",
+    )(picked, emb_table)
+
+
+def spread_weights(lookup_slots, lcb_weight, owners, cap):
+    samples, feature_count = lookup_slots.shape
+    embed_count = lcb_weight.shape[0]
+    group = tiles_of(samples, 8)
+
+    def kernel(slots_ref, lcb_ref, out_ref):
+        lcb = lcb_ref[...].astype(jnp.float32)
+        owner_of = lax.broadcasted_iota(jnp.int32, (owners, embed_count, feature_count), 0)
+        column_of = lax.broadcasted_iota(jnp.int32, (cap, feature_count), 0)
+        for pair in range(0, group, 2):
+            made = []
+            for sample in (pair, pair + 1):
+                slots = slots_ref[sample : sample + 1, :]
+                owner = lax.div(slots, cap)
+                column = slots - owner * cap
+                left = jnp.where(owner_of == owner[None], lcb[None], 0.0)
+                left = left.reshape(owners * embed_count, feature_count).astype(jnp.bfloat16)
+                right = jnp.where(column_of == column, 1.0, 0.0).astype(jnp.bfloat16)
+                both = lax.dot_general(
+                    left, right, (((1,), (1,)), ((), ())), preferred_element_type=jnp.float32
+                )
+                made.append(both.reshape(owners, embed_count, cap))
+            rows = pl.ds(pair * embed_count, 2 * embed_count)
+            out_ref[:, rows, :] = jnp.concatenate(made, axis=1).astype(out_ref.dtype)
+
+    return pl.pallas_call(
+        kernel,
+        out_shape=jax.ShapeDtypeStruct((owners, samples * embed_count, cap), jnp.bfloat16),
+        grid=(samples // group,),
+        in_specs=[
+            pl.BlockSpec((group, feature_count), lambda i: (i, 0)),
+            pl.BlockSpec((embed_count, feature_count), lambda i: (0, 0)),
+        ],
+        out_specs=pl.BlockSpec((owners, group * embed_count, cap), lambda i: (0, i, 0)),
+        compiler_params=params(),
+        cost_estimate=pl.CostEstimate(
+            flops=2 * samples * owners * embed_count * feature_count * cap,
+            bytes_accessed=2 * owners * samples * embed_count * cap,
+            transcendentals=0,
+        ),
+        name="spread_weights",
+    )(lookup_slots, lcb_weight)
+
+
+def compress(spread, fetched, embed_count):
+    owners, lines, cap = spread.shape
+    width = fetched.shape[2]
+    samples = lines // embed_count
+    part = tiles_of(owners, 4)
+
+    def kernel(spread_ref, rows_ref, out_ref, total):
+        step = pl.program_id(0)
+        left = jnp.concatenate([spread_ref[o] for o in range(part)], axis=1)
+        right = rows_ref[...].reshape(part * cap, width)
+        term = jnp.dot(left, right, preferred_element_type=jnp.float32)
+
+        @pl.when(step == 0)
+        def _():
+            total[...] = term
+
+        @pl.when(step > 0)
+        def _():
+            total[...] += term
+
+        @pl.when(step == owners // part - 1)
+        def _():
+            for k in range(embed_count):
+                piece = total[pl.ds(k, samples, stride=embed_count), :]
+                out_ref[:, k * width : (k + 1) * width] = piece.astype(out_ref.dtype)
+
+    return pl.pallas_call(
+        kernel,
+        out_shape=jax.ShapeDtypeStruct((samples, embed_count * width), jnp.bfloat16),
+        grid=(owners // part,),
+        in_specs=[
+            pl.BlockSpec((part, lines, cap), lambda i: (i, 0, 0)),
+            pl.BlockSpec((part, cap, width), lambda i: (i, 0, 0)),
+        ],
+        out_specs=pl.BlockSpec((samples, embed_count * width), lambda i: (0, 0)),
+        scratch_shapes=[pltpu.VMEM((lines, width), jnp.float32)],
+        compiler_params=params(),
+        name="compress",
+    )(spread, fetched)
+
+
+def expand(spread, lead_share, embed_count):
+    owners, lines, cap = spread.shape
+    samples = lines // embed_count
+    width = lead_share.shape[1] // embed_count
+    part = tiles_of(owners, 4)
+
+    def kernel(spread_ref, grad_ref, out_ref, tall, turned):
+        @pl.when(pl.program_id(0) == 0)
+        def _():
+            for k in range(embed_count):
+                piece = grad_ref[:, k * width : (k + 1) * width].astype(jnp.float32)
+                tall[pl.ds(k, samples, stride=embed_count), :] = piece
+            turned[...] = tall[...].T.astype(jnp.bfloat16)
+
+        right = jnp.concatenate([spread_ref[o] for o in range(part)], axis=1)
+        term = jnp.dot(turned[...], right, preferred_element_type=jnp.float32)
+        out_ref[...] = term.T.astype(out_ref.dtype).reshape(part, cap, width)
+
+    return pl.pallas_call(
+        kernel,
+        out_shape=jax.ShapeDtypeStruct((owners, cap, width), jnp.bfloat16),
+        grid=(owners // part,),
+        in_specs=[
+            pl.BlockSpec((part, lines, cap), lambda i: (i, 0, 0)),
+            pl.BlockSpec(lead_share.shape, lambda i: (0, 0)),
+        ],
+        out_specs=pl.BlockSpec((part, cap, width), lambda i: (i, 0, 0)),
+        scratch_shapes=[
+            pltpu.VMEM((lines, width), jnp.float32),
+            pltpu.VMEM((width, lines), jnp.bfloat16),
+        ],
+        compiler_params=params(),
+        name="expand",
+    )(spread, lead_share)
+
+
+def add_rows(targets, returned, outgoing, rows):
+    count, width = returned.shape
+    chunk = min(count, 1024)
+    steps = count // chunk
+
+    def kernel(targets_ref, back_ref, sent_ref, out_ref, total, terms, done):
+        step = pl.program_id(0)
+
+        @pl.when(step == 0)
+        def _():
+            total[...] = jnp.zeros_like(total)
+
+        terms[...] = back_ref[...].astype(jnp.float32) + DECAY_WEIGHT * sent_ref[...].astype(
+            jnp.float32
+        )
+
+        def body(group, carry):
+            first = pl.multiple_of(group * UNROLL, UNROLL)
+            places = [targets_ref[step * chunk + first + lane] for lane in range(UNROLL)]
+            sums = [
+                total[pl.ds(places[lane], 1), :] + terms[pl.ds(first + lane, 1), :]
+                for lane in range(UNROLL)
+            ]
+            for lane in range(UNROLL):
+                total[pl.ds(places[lane], 1), :] = sums[lane]
+            return carry
+
+        lax.fori_loop(0, chunk // UNROLL, body, 0)
+
+        @pl.when(step == steps - 1)
+        def _():
+            copy = pltpu.make_async_copy(total.at[pl.ds(0, rows), :], out_ref, done)
+            copy.start()
+            copy.wait()
+
+    return pl.pallas_call(
+        kernel,
+        out_shape=jax.ShapeDtypeStruct((rows, width), jnp.float32),
+        grid_spec=pltpu.PrefetchScalarGridSpec(
+            num_scalar_prefetch=1,
+            grid=(steps,),
+            in_specs=[
+                pl.BlockSpec((chunk, width), lambda i, ids: (i, 0)),
+                pl.BlockSpec((chunk, width), lambda i, ids: (i, 0)),
+            ],
+            out_specs=pl.BlockSpec(memory_space=pl.ANY),
+            scratch_shapes=[
+                pltpu.VMEM((rows + 8, width), jnp.float32),
+                pltpu.VMEM((chunk, width), jnp.float32),
+                pltpu.SemaphoreType.DMA,
+            ],
+        ),
+        compiler_params=params(),
+        name="add_rows",
+    )(targets, returned, outgoing)
 
 
 def shifted(value, axis, steps):
@@ -83,23 +317,18 @@
     cap = wanted_rows.shape[2]
     embed_width = emb_table.shape[1]
     picked_rows = wanted_rows[0]
-    outgoing = jnp.take(emb_table, picked_rows.reshape(-1), axis=0).reshape(
-        owners, cap, embed_width
-    )
+    look_dev = lookup_slot.shape[1]
+    embed_count = lcb_weight.shape[0]
+    outgoing = pick_rows(emb_table, picked_rows.reshape(-1))
     fetched = lax.all_to_all(
-        outgoing, ("section", "table"), split_axis=0, concat_axis=0, tiled=True
-    )
-    fetched = fetched.reshape(owners * cap, embed_width)
-    lookup_slots = lookup_slot[0]
-    look_dev = lookup_slots.shape[0]
-    feature_count = lookup_slots.shape[1]
-    embedded = jnp.take(fetched, lookup_slots.reshape(-1), axis=0).reshape(
-        look_dev, feature_count, embed_width
-    )
-    compressed = jnp.einsum(
-        "kf,bfe->bke", lcb_weight, embedded, preferred_element_type=jnp.float32
-    ).astype(jnp.bfloat16)
-    compressed = compressed.reshape(look_dev, -1)
+        outgoing.reshape(owners, cap, embed_width),
+        ("section", "table"),
+        split_axis=0,
+        concat_axis=0,
+        tiled=True,
+    )
+    spread = spread_weights(lookup_slot[0], lcb_weight, owners, cap)
+    compressed = compress(spread, fetched, embed_count)
     leading = lax.all_gather(compressed, "section", axis=0, tiled=True)
     micro_count = top_grad.shape[1]
     batch_rows = top_grad.shape[2]
@@ -165,32 +394,13 @@
     lead_share = lax.psum_scatter(
         terms.astype(jnp.bfloat16), "section", scatter_dimension=0, tiled=True
     )
-    embed_count = lcb_weight.shape[0]
-    feature_grad = jnp.einsum(
-        "kf,bke->bfe",
-        lcb_weight,
-        lead_share.reshape(look_dev, embed_count, embed_width),
-        preferred_element_type=jnp.float32,
-    )
-    slot_grad = jax.ops.segment_sum(
-        feature_grad.reshape(-1, embed_width), lookup_slots.reshape(-1), num_segments=owners * cap
-    )
-    slot_grad = slot_grad.reshape(owners, cap, embed_width)
+    slot_grad = expand(spread, lead_share, embed_count)
     returned = lax.all_to_all(
-        slot_grad.astype(jnp.bfloat16),
-        ("section", "table"),
-        split_axis=0,
-        concat_axis=0,
-        tiled=True,
-    ).astype(slot_grad.dtype)
+        slot_grad, ("section", "table"), split_axis=0, concat_axis=0, tiled=True
+    )
     live_slots = jnp.arange(cap)[None, :] < row_counts[0][:, None]
-    decay_term = jnp.where(live_slots[..., None], DECAY_WEIGHT * outgoing.astype(jnp.float32), 0.0)
-    table_grad = (
-        jnp.zeros(emb_table.shape, jnp.float32)
-        .at[picked_rows.reshape(-1)]
-        .add((returned + decay_term).reshape(-1, embed_width))
-    )
-    return table_grad
+    targets = jnp.where(live_slots, picked_rows, emb_table.shape[0]).reshape(-1)
+    return add_rows(targets, returned.reshape(-1, embed_width), outgoing, emb_table.shape[0])
 
 
 def solution(mesh):

time: 792 us -> 453 us (0.57)
  other arithmetic: 225 us -> 17.3 us
  local copies, waits for them, and re-layouts: 163 us -> 29.3 us
  Pallas kernels: 0 us -> 29.8 us
  matrix products: 141 us -> 124 us
  waiting for transfers between devices: 169 us -> 160 us
    scatter-add x2 -> x0, other arithmetic: 200 us -> none  [the longest x1 176 us: per_device(): jax.ops.segment_sum(feature_grad.reshape(-1, embed_width), lookup_slots.r...]
    gather x2 -> x0, local copies, waits for them, and re-layouts: 126 us -> none  [the longest x1 114 us: per_device(): jnp.take(fetched, lookup_slots.reshape(-1), axis=0)]
    pallas_call x0 -> x5, Pallas kernels: none -> 29.8 us  [the longest x1 10.4 us: add_rows(): pl.pallas_call(kernel, out_shape=jax.ShapeDtypeStruct((rows, width), jnp....]
    transpose x1 -> x0, local copies, waits for them, and re-layouts: 17.4 us -> none  [per_device(): jnp.einsum('kf,bke->bfe', lcb_weight, lead_share.reshape(look_dev, embed_...]
    dot_general x2 -> x0, matrix products: 16.9 us -> none  [the longest x1 8.76 us: per_device(): jnp.einsum('kf,bfe->bke', lcb_weight, embedded, preferred_element_type=jn...]
    all_to_all x2, waiting for transfers between devices: 54.6 us -> 44.8 us  [the longest x1 27.5 us: per_device(): lax.all_to_all(slot_grad, ('section', 'table'), split_axis=0, concat_axis...]
    unnamed x22, local copies, waits for them, and re-layouts: 1.16 us -> 10.8 us
  transfers between devices with their start and end apart: 17 -> 17, of which waited for: 17 -> 17; matrix products, arithmetic and copies ran while one was open for 1% -> 3% of each run, Pallas kernels for 0% -> 1%
where the time goes in v1:
time: 453 us; the launch traced here: 451 us
  waiting for transfers between devices  160 us (35%)
  matrix products  124 us (27%)
  starting transfers between devices  70.4 us (16%)
  Pallas kernels  29.8 us (7%)
  local copies, waits for them, and re-layouts  29.3 us (6%)
  other arithmetic  17.3 us (4%)
  between operations  13.5 us (3%)
  blocking collectives  6.61 us (1%)
    ppermute x14, waiting for transfers between devices, shifted(): lax.ppermute(value, axis, [(source, source + steps) for source in range(f...  95.2 us
    ppermute x14, starting transfers between devices, shifted(): lax.ppermute(value, axis, [(source, source + steps) for source in range(f...  58.5 us
    dot_general x4, matrix products, fm_backward(): lax.dot_general(g_before, w_up, last_dims, preferred_element_type=jnp.flo...  44.4 us
    dot_general x4, matrix products, fm_forward(): jnp.dot(hidden, w_down, preferred_element_type=jnp.float32)  35.6 us
    all_to_all x1, waiting for transfers between devices, per_device(): lax.all_to_all(slot_grad, ('section', 'table'), split_axis=0, concat_axis...  27.5 us
    dot_general x4, matrix products, fm_forward(): before = jnp.dot(normed, w_up, preferred_element_type=jnp.float32)  20.3 us
    reduce_scatter x1, waiting for transfers between devices, per_device(): lax.psum_scatter(terms.astype(jnp.bfloat16), 'section', scatter_dimension...  19.6 us
    all_to_all x1, waiting for transfers between devices, per_device(): lax.all_to_all(outgoing.reshape(owners, cap, embed_width), ('section', 't...  17.3 us
  transfers between devices with their start and end apart: 17, of which 17 were waited for; matrix products, arithmetic and copies ran while one was open for 3% of the time, Pallas kernels for 1%

profile of v1, /device:TPU:0, one launch (start us, length us, event | category | flops | bytes accessed | tf_op | source)
XLA Modules:
  0.0 451.3 jit_solution(18394611410549856521)
XLA Ops:
  8.5 6.4 %pick_rows.1.sent_ref = bf16[4096,128]{1,0:T(8,128)(2,1)} custom-call(s32[4096]{0:T(1024)S(1)} %bitcast.120, bf16[4096,128]{1,0:T(8,128)(2,1)S(1)} %copy-done.3), custom_call_target="tpu_custom_call" | custom-call | tf_op jit(solution)/shard_map/pick_rows/pallas_call | solution.py:48
  14.9 7.3 %all-to-all-start = ((bf16[32,128,128]{2,1,0:T(8,128)(2,1)}), bf16[32,128,128]{2,1,0:T(8,128)(2,1)S(1)}, u32[]{:S(2)}, u32[]{:S(2)}) async-start(bf16[32,128,128]{2,1,0:T(8,128)(2,1)} %bitcast.16), calls=%async_computation | async-start | bytes 2097152 | tf_op jit(solution)/shard_map/all_to_all | solution.py:323
  24.6 6.0 %spread_weights.1.spread_ref = bf16[32,512,128]{2,1,0:T(8,128)(2,1)S(1)} custom-call(s32[64,512]{1,0:T(8,128)S(1)} %bitcast.121, bf16[8,512]{1,0:T(8,128)(2,1)S(1)} %copy-done.8), custom_call_target="tpu_custom_call" | custom-call | flops 2147483648 | bytes 4194304 | tf_op jit(solution)/shard_map/spread_weights/pallas_call | solution.py:91
  32.5 17.3 %all-to-all-done.rows_ref = bf16[32,128,128]{2,1,0:T(8,128)(2,1)S(1)} async-done(((bf16[32,128,128]{2,1,0:T(8,128)(2,1)}), bf16[32,128,128]{2,1,0:T(8,128)(2,1)S(1)}, u32[]{:S(2)}, u32[]{:S(2)}) %all-to-all-start) | async-done | bytes 1048608 | tf_op jit(solution)/shard_map/all_to_all | solution.py:323
  54.6 6.6 %all_gather.3 = bf16[256,1024]{1,0:T(8,128)(2,1)S(1)} all-gather(bf16[64,1024]{1,0:T(8,128)(2,1)S(1)} %compress.1), channel_id=1, replica_groups=mesh['section'=4,'table'=8] {'section'}, dimensions={0}, use_global_device_ids=true | all-gather | bytes 655360 | tf_op jit(solution)/shard_map/all_gather | solution.py:332
  62.2 111.3 %while.33 = (s32[]{:T(128)}, bf16[64,1024]{1,0:T(8,128)(2,1)S(1)}, bf16[4,64,1024]{2,1,0:T(8,128)(2,1)}, s32[]{:T(128)}, pred[]{:T(512)}, /*index=5*/bf16[4,64,1...) while((s32[]{:T(128)}, bf16[64,1024]{1,0:T(8,128)(2,1)S(1)}, ...), condition=%wide.region_4.5_spmd, body=%wide.region_0.4_spmd.sunk | while | flops 1109525504 | bytes 19412772 | solution.py:362
  63.9 10.9 %conditional.4 = (bf16[64,1024]{1,0:T(8,128)(2,1)S(1)}) conditional(s32[]{:T(128)} %convert_element_type.127, () %tuple.88, (bf16[64,1024]{1,0:T(8,128)(2,1)S(1)}, bf16[8,128]{1,0:T(8,128)(2,1)S(1)}, bf16[1024]{0:T(1024)(128)(2,1)S(1)}, bf16[1024,4096]{1,0:T(8,128)(2,1)}, bf16[4096,1024]{1,0:T(8,128)(2,1)}) %tuple.89), branch_computations={%region_1.1_spmd, %region_2.3_spmd} | conditional | flops 1109394432 | bytes 17970184 | solution.py:348
  65.8 8.9 %fusion.6 = bf16[64,1024]{1,0:T(8,128)(2,1)S(1)} fusion(bf16[4096,1024]{1,0:T(8,128)(2,1)} %get-tuple-element.515, bf16[1024,4096]{1,0:T(8,128)(2,1)} %get-tuple-element.514, bf16[64,1024]{1,0:T(8,128)(2,1)S(1)} %get-tuple-element.511, f32[8,8,8,128]{3,2,1,0:T(8,128)S(1)} %bitcast.134, f32[1024]{0:T(1024)S(1)} %convert_element_type.72, f32[64]{0:T(128)S(1)} %add_rsqrt_fusion), kind=kOutput, calls=%fused_computation.7 | convolution fusion | flops 1074659328 | bytes 17305856 | tf_op jit(solution)/shard_map/while/body/eval_jaxpr/cond/branch_1_fun/dot_general | solution.py:264
  78.6 10.9 %conditional.4 = (bf16[64,1024]{1,0:T(8,128)(2,1)S(1)}) conditional(s32[]{:T(128)} %convert_element_type.127, () %tuple.88, (bf16[64,1024]{1,0:T(8,128)(2,1)S(1)}, bf16[8,128]{1,0:T(8,128)(2,1)S(1)}, bf16[1024]{0:T(1024)(128)(2,1)S(1)}, bf16[1024,4096]{1,0:T(8,128)(2,1)}, bf16[4096,1024]{1,0:T(8,128)(2,1)}) %tuple.89), branch_computations={%region_1.1_spmd, %region_2.3_spmd} | conditional | flops 1109394432 | bytes 17970184 | solution.py:348
  80.6 8.9 %fusion.6 = bf16[64,1024]{1,0:T(8,128)(2,1)S(1)} fusion(bf16[4096,1024]{1,0:T(8,128)(2,1)} %get-tuple-element.515, bf16[1024,4096]{1,0:T(8,128)(2,1)} %get-tuple-element.514, bf16[64,1024]{1,0:T(8,128)(2,1)S(1)} %get-tuple-element.511, f32[8,8,8,128]{3,2,1,0:T(8,128)S(1)} %bitcast.134, f32[1024]{0:T(1024)S(1)} %convert_element_type.72, f32[64]{0:T(128)S(1)} %add_rsqrt_fusion), kind=kOutput, calls=%fused_computation.7 | convolution fusion | flops 1074659328 | bytes 17305856 | tf_op jit(solution)/shard_map/while/body/eval_jaxpr/cond/branch_1_fun/dot_general | solution.py:264
  94.4 10.9 %conditional.4 = (bf16[64,1024]{1,0:T(8,128)(2,1)S(1)}) conditional(s32[]{:T(128)} %convert_element_type.127, () %tuple.88, (bf16[64,1024]{1,0:T(8,128)(2,1)S(1)}, bf16[8,128]{1,0:T(8,128)(2,1)S(1)}, bf16[1024]{0:T(1024)(128)(2,1)S(1)}, bf16[1024,4096]{1,0:T(8,128)(2,1)}, bf16[4096,1024]{1,0:T(8,128)(2,1)}) %tuple.89), branch_computations={%region_1.1_spmd, %region_2.3_spmd} | conditional | flops 1109394432 | bytes 17970184 | solution.py:348
  96.4 8.9 %fusion.6 = bf16[64,1024]{1,0:T(8,128)(2,1)S(1)} fusion(bf16[4096,1024]{1,0:T(8,128)(2,1)} %get-tuple-element.515, bf16[1024,4096]{1,0:T(8,128)(2,1)} %get-tuple-element.514, bf16[64,1024]{1,0:T(8,128)(2,1)S(1)} %get-tuple-element.511, f32[8,8,8,128]{3,2,1,0:T(8,128)S(1)} %bitcast.134, f32[1024]{0:T(1024)S(1)} %convert_element_type.72, f32[64]{0:T(128)S(1)} %add_rsqrt_fusion), kind=kOutput, calls=%fused_computation.7 | convolution fusion | flops 1074659328 | bytes 17305856 | tf_op jit(solution)/shard_map/while/body/eval_jaxpr/cond/branch_1_fun/dot_general | solution.py:264
  110.8 10.9 %conditional.4 = (bf16[64,1024]{1,0:T(8,128)(2,1)S(1)}) conditional(s32[]{:T(128)} %convert_element_type.127, () %tuple.88, (bf16[64,1024]{1,0:T(8,128)(2,1)S(1)}, bf16[8,128]{1,0:T(8,128)(2,1)S(1)}, bf16[1024]{0:T(1024)(128)(2,1)S(1)}, bf16[1024,4096]{1,0:T(8,128)(2,1)}, bf16[4096,1024]{1,0:T(8,128)(2,1)}) %tuple.89), branch_computations={%region_1.1_spmd, %region_2.3_spmd} | conditional | flops 1109394432 | bytes 17970184 | solution.py:348
  112.7 8.9 %fusion.6 = bf16[64,1024]{1,0:T(8,128)(2,1)S(1)} fusion(bf16[4096,1024]{1,0:T(8,128)(2,1)} %get-tuple-element.515, bf16[1024,4096]{1,0:T(8,128)(2,1)} %get-tuple-element.514, bf16[64,1024]{1,0:T(8,128)(2,1)S(1)} %get-tuple-element.511, f32[8,8,8,128]{3,2,1,0:T(8,128)S(1)} %bitcast.134, f32[1024]{0:T(1024)S(1)} %convert_element_type.72, f32[64]{0:T(128)S(1)} %add_rsqrt_fusion), kind=kOutput, calls=%fused_computation.7 | convolution fusion | flops 1074659328 | bytes 17305856 | tf_op jit(solution)/shard_map/while/body/eval_jaxpr/cond/branch_1_fun/dot_general | solution.py:264
  121.6 5.3 %collective-permute-start = (bf16[64,1024]{1,0:T(8,128)(2,1)S(1)}, bf16[64,1024]{1,0:T(8,128)(2,1)S(1)}, u32[]{:S(2)}, u32[]{:S(2)}) collective-permute-start(bf16[64,1024]{1,0:T(8,128)(2,1)S(1)} %get-tuple-element.833), channel_id=1, source_target_pairs={{0,8},{8,16},{16,24},{1,9},{9,17},{17,25},{2,10},{10,18},{18,26},{... | collective-permute-start | bytes 393224 | tf_op jit(solution)/shard_map/while/body/eval_jaxpr/ppermute | solution.py:247
  129.6 16.2 %collective-permute-start = (bf16[64,1024]{1,0:T(8,128)(2,1)S(1)}, bf16[64,1024]{1,0:T(8,128)(2,1)S(1)}, u32[]{:S(2)}, u32[]{:S(2)}) collective-permute-start(bf16[64,1024]{1,0:T(8,128)(2,1)S(1)} %get-tuple-element.833), channel_id=1, source_target_pairs={{0,8},{8,16},{16,24},{1,9},{9,17},{17,25},{2,10},{10,18},{18,26},{... | collective-permute-start | bytes 393224 | tf_op jit(solution)/shard_map/while/body/eval_jaxpr/ppermute | solution.py:247
  148.4 5.3 %collective-permute-start = (bf16[64,1024]{1,0:T(8,128)(2,1)S(1)}, bf16[64,1024]{1,0:T(8,128)(2,1)S(1)}, u32[]{:S(2)}, u32[]{:S(2)}) collective-permute-start(bf16[64,1024]{1,0:T(8,128)(2,1)S(1)} %get-tuple-element.833), channel_id=1, source_target_pairs={{0,8},{8,16},{16,24},{1,9},{9,17},{17,25},{2,10},{10,18},{18,26},{... | collective-permute-start | bytes 393224 | tf_op jit(solution)/shard_map/while/body/eval_jaxpr/ppermute | solution.py:247
  156.3 16.2 %collective-permute-start = (bf16[64,1024]{1,0:T(8,128)(2,1)S(1)}, bf16[64,1024]{1,0:T(8,128)(2,1)S(1)}, u32[]{:S(2)}, u32[]{:S(2)}) collective-permute-start(bf16[64,1024]{1,0:T(8,128)(2,1)S(1)} %get-tuple-element.833), channel_id=1, source_target_pairs={{0,8},{8,16},{16,24},{1,9},{9,17},{17,25},{2,10},{10,18},{18,26},{... | collective-permute-start | bytes 393224 | tf_op jit(solution)/shard_map/while/body/eval_jaxpr/ppermute | solution.py:247
  174.3 198.4 %while.34 = (s32[]{:T(128)}, bf16[64,1024]{1,0:T(8,128)(2,1)S(1)}, bf16[4,64,1024]{2,1,0:T(8,128)(2,1)}, s32[]{:T(128)}, pred[]{:T(512)}, /*index=5*/bf16[4,64,1...) while((s32[]{:T(128)}, bf16[64,1024]{1,0:T(8,128)(2,1)S(1)}, ...), condition=%wide.region_10.11_spmd, body=%wide.region_5.10_spmd.sunk | while | flops 1698759680 | bytes 38033496 | solution.py:390
  183.7 8.5 %collective-permute-done.1 = bf16[64,1024]{1,0:T(8,128)(2,1)S(1)} collective-permute-done((bf16[64,1024]{1,0:T(8,128)(2,1)S(1)}, bf16[64,1024]{1,0:T(8,128)(2,1)S(1)}, u32[]{:S(2)}, u32[]{:S(2)}) %collective-permute-start.1) | collective-permute-done | bytes 131104 | tf_op jit(solution)/shard_map/while/body/eval_jaxpr/ppermute | solution.py:247
  195.1 66.4 %collective-permute-done.1 = bf16[64,1024]{1,0:T(8,128)(2,1)S(1)} collective-permute-done((bf16[64,1024]{1,0:T(8,128)(2,1)S(1)}, bf16[64,1024]{1,0:T(8,128)(2,1)S(1)}, u32[]{:S(2)}, u32[]{:S(2)}) %collective-permute-start.1) | collective-permute-done | bytes 131104 | tf_op jit(solution)/shard_map/while/body/eval_jaxpr/ppermute | solution.py:247
  261.5 22.3 %conditional.5 = (bf16[64,1024]{1,0:T(8,128)(2,1)S(1)}) conditional(s32[]{:T(128)} %convert_element_type.128, () %tuple.91, (pred[]{:T(512)}, bf16[4,64,1024]{2,1,0:T(8,128)(2,1)}, s32[]{:T(128)}, bf16[64,1024]{1,0:T(8,128)(2,1)S(1)}, bf16[4,64,1024]{2,1,0:T(8,128)(2,1)}, /*index=5*/bf16[8,128]{1,0:T(8,128)(2,1)S(1)}, bf16[1024]{0:T(1024)(128)(2,1)S(1)}, ...), branch_computations={%region_6.6_spmd, %region_7.9_spmd} | conditional | flops 1698694144 | bytes 36853008 | solution.py:376
  269.3 11.1 %fusion.30 = (f32[64]{0:T(128)S(1)}, f32[64,1024]{1,0:T(8,128)S(1)}) fusion(f32[8,8,8,128]{3,2,1,0:T(8,128)S(1)} %bitcast.125, f32[1024]{0:T(1024)S(1)} %convert_element_type.79, bf16[1024,4096]{1,0:T(8,128)(2,1)} %get-tuple-element.534, pred[64,4096]{1,0:T(32,128)(4,1)S(1)} %convolution_compare_fusion, bf16[4096,1024]{1,0:T(8,128)(2,1)} %get-tuple-element.535, ...), kind=kOutput, calls=%fused_computation.38 | convolution fusion | flops 1074528256 | bytes 17831168 | tf_op jit(solution)/shard_map/while/body/eval_jaxpr/cond/branch_1_fun/dot_general | solution.py:278
  290.1 22.3 %conditional.5 = (bf16[64,1024]{1,0:T(8,128)(2,1)S(1)}) conditional(s32[]{:T(128)} %convert_element_type.128, () %tuple.91, (pred[]{:T(512)}, bf16[4,64,1024]{2,1,0:T(8,128)(2,1)}, s32[]{:T(128)}, bf16[64,1024]{1,0:T(8,128)(2,1)S(1)}, bf16[4,64,1024]{2,1,0:T(8,128)(2,1)}, /*index=5*/bf16[8,128]{1,0:T(8,128)(2,1)S(1)}, bf16[1024]{0:T(1024)(128)(2,1)S(1)}, ...), branch_computations={%region_6.6_spmd, %region_7.9_spmd} | conditional | flops 1698694144 | bytes 36853008 | solution.py:376
  297.9 11.1 %fusion.30 = (f32[64]{0:T(128)S(1)}, f32[64,1024]{1,0:T(8,128)S(1)}) fusion(f32[8,8,8,128]{3,2,1,0:T(8,128)S(1)} %bitcast.125, f32[1024]{0:T(1024)S(1)} %convert_element_type.79, bf16[1024,4096]{1,0:T(8,128)(2,1)} %get-tuple-element.534, pred[64,4096]{1,0:T(32,128)(4,1)S(1)} %convolution_compare_fusion, bf16[4096,1024]{1,0:T(8,128)(2,1)} %get-tuple-element.535, ...), kind=kOutput, calls=%fused_computation.38 | convolution fusion | flops 1074528256 | bytes 17831168 | tf_op jit(solution)/shard_map/while/body/eval_jaxpr/cond/branch_1_fun/dot_general | solution.py:278
  318.7 22.3 %conditional.5 = (bf16[64,1024]{1,0:T(8,128)(2,1)S(1)}) conditional(s32[]{:T(128)} %convert_element_type.128, () %tuple.91, (pred[]{:T(512)}, bf16[4,64,1024]{2,1,0:T(8,128)(2,1)}, s32[]{:T(128)}, bf16[64,1024]{1,0:T(8,128)(2,1)S(1)}, bf16[4,64,1024]{2,1,0:T(8,128)(2,1)}, /*index=5*/bf16[8,128]{1,0:T(8,128)(2,1)S(1)}, bf16[1024]{0:T(1024)(128)(2,1)S(1)}, ...), branch_computations={%region_6.6_spmd, %region_7.9_spmd} | conditional | flops 1698694144 | bytes 36853008 | solution.py:376
  326.4 11.1 %fusion.30 = (f32[64]{0:T(128)S(1)}, f32[64,1024]{1,0:T(8,128)S(1)}) fusion(f32[8,8,8,128]{3,2,1,0:T(8,128)S(1)} %bitcast.125, f32[1024]{0:T(1024)S(1)} %convert_element_type.79, bf16[1024,4096]{1,0:T(8,128)(2,1)} %get-tuple-element.534, pred[64,4096]{1,0:T(32,128)(4,1)S(1)} %convolution_compare_fusion, bf16[4096,1024]{1,0:T(8,128)(2,1)} %get-tuple-element.535, ...), kind=kOutput, calls=%fused_computation.38 | convolution fusion | flops 1074528256 | bytes 17831168 | tf_op jit(solution)/shard_map/while/body/eval_jaxpr/cond/branch_1_fun/dot_general | solution.py:278
  347.2 22.3 %conditional.5 = (bf16[64,1024]{1,0:T(8,128)(2,1)S(1)}) conditional(s32[]{:T(128)} %convert_element_type.128, () %tuple.91, (pred[]{:T(512)}, bf16[4,64,1024]{2,1,0:T(8,128)(2,1)}, s32[]{:T(128)}, bf16[64,1024]{1,0:T(8,128)(2,1)S(1)}, bf16[4,64,1024]{2,1,0:T(8,128)(2,1)}, /*index=5*/bf16[8,128]{1,0:T(8,128)(2,1)S(1)}, bf16[1024]{0:T(1024)(128)(2,1)S(1)}, ...), branch_computations={%region_6.6_spmd, %region_7.9_spmd} | conditional | flops 1698694144 | bytes 36853008 | solution.py:376
  355.0 11.1 %fusion.30 = (f32[64]{0:T(128)S(1)}, f32[64,1024]{1,0:T(8,128)S(1)}) fusion(f32[8,8,8,128]{3,2,1,0:T(8,128)S(1)} %bitcast.125, f32[1024]{0:T(1024)S(1)} %convert_element_type.79, bf16[1024,4096]{1,0:T(8,128)(2,1)} %get-tuple-element.534, pred[64,4096]{1,0:T(32,128)(4,1)S(1)} %convolution_compare_fusion, bf16[4096,1024]{1,0:T(8,128)(2,1)} %get-tuple-element.535, ...), kind=kOutput, calls=%fused_computation.38 | convolution fusion | flops 1074528256 | bytes 17831168 | tf_op jit(solution)/shard_map/while/body/eval_jaxpr/cond/branch_1_fun/dot_general | solution.py:278
  374.8 19.6 %reduce-scatter.2.cloned.1.call-done.grad_ref = bf16[64,1024]{1,0:T(8,128)(2,1)} async-done(((bf16[256,1024]{1,0:T(8,128)(2,1)}), bf16[64,1024]{1,0:T(8,128)(2,1)}) %reduce-scatter.2.cloned.1.call-update) | async-done | bytes 131088 | tf_op jit(solution)/shard_map/reduce_scatter | solution.py:394
  406.5 27.5 %all-to-all-done.1 = bf16[32,128,128]{2,1,0:T(8,128)(2,1)S(1)} async-done(((bf16[32,128,128]{2,1,0:T(8,128)(2,1)}), bf16[32,128,128]{2,1,0:T(8,128)(2,1)S(1)}, u32[]{:S(2)}, u32[]{:S(2)}) %all-to-all-start.1) | async-done | bytes 1048608 | tf_op jit(solution)/shard_map/all_to_all | solution.py:398
  434.0 10.4 %add_rows.1 = f32[4096,128]{1,0:T(8,128)} custom-call(s32[4096]{0:T(1024)S(1)} %fusion.40.targets_ref, bf16[4096,128]{1,0:T(8,128)(2,1)S(1)} %bitcast.119, bf16[4096,128]{1,0:T(8,128)(2,1)} %pick_rows.1.sent_ref), custom_call_target="tpu_custom_call" | custom-call | tf_op jit(solution)/shard_map/add_rows/pallas_call | solution.py:222
  (164 shorter events, 138.0 us)
Async XLA Ops:
  6.5 1.2 copy-start.3
  7.8 0.7 copy-start.5
  14.9 47.3 %copy-start.9 = (bf16[1,8,128]{2,1,0:T(8,128)(2,1)S(1)}, bf16[1,8,128]{2,1,0:T(8,128)(2,1)}, u32[]{:S(2)}) copy-start(bf16[1,8,128]{2,1,0:T(8,128)(2,1)} %param.20) | copy-start | bytes 6148
  14.9 34.9 %all-to-all-start = ((bf16[32,128,128]{2,1,0:T(8,128)(2,1)}), bf16[32,128,128]{2,1,0:T(8,128)(2,1)S(1)}, u32[]{:S(2)}, u32[]{:S(2)}) async-start(bf16[32,128,128]{2,1,0:T(8,128)(2,1)} %bitcast.16), calls=%async_computation | async-start | bytes 2097152 | tf_op jit(solution)/shard_map/all_to_all | solution.py:323
  22.2 372.2 %reduce-scatter.2.cloned.1.call-start = ((), (), s32[]{:S(2)}) async-start(), calls=%async_computation.3 | async-start | bytes 655360 | tf_op jit(solution)/shard_map/reduce_scatter | solution.py:394
  23.0 0.9 copy-start.7
  23.9 0.7 copy-start.8
  30.6 2.0 copy-start
  49.8 2.2 copy-start.1
  74.7 2.3 collective-permute-start
  89.5 3.3 collective-permute-start
  105.3 3.9 collective-permute-start
  121.6 6.3 %collective-permute-start = (bf16[64,1024]{1,0:T(8,128)(2,1)S(1)}, bf16[64,1024]{1,0:T(8,128)(2,1)S(1)}, u32[]{:S(2)}, u32[]{:S(2)}) collective-permute-start(bf16[64,1024]{1,0:T(8,128)(2,1)S(1)} %get-tuple-element.833), channel_id=1, source_target_pairs={{0,8},{8,16},{16,24},{1,9},{9,17},{17,25},{2,10},{10,18},{18,26},{... | collective-permute-start | bytes 393224 | tf_op jit(solution)/shard_map/while/body/eval_jaxpr/ppermute | solution.py:247
  129.6 17.1 %collective-permute-start = (bf16[64,1024]{1,0:T(8,128)(2,1)S(1)}, bf16[64,1024]{1,0:T(8,128)(2,1)S(1)}, u32[]{:S(2)}, u32[]{:S(2)}) collective-permute-start(bf16[64,1024]{1,0:T(8,128)(2,1)S(1)} %get-tuple-element.833), channel_id=1, source_target_pairs={{0,8},{8,16},{16,24},{1,9},{9,17},{17,25},{2,10},{10,18},{18,26},{... | collective-permute-start | bytes 393224 | tf_op jit(solution)/shard_map/while/body/eval_jaxpr/ppermute | solution.py:247
  148.4 6.3 %collective-permute-start = (bf16[64,1024]{1,0:T(8,128)(2,1)S(1)}, bf16[64,1024]{1,0:T(8,128)(2,1)S(1)}, u32[]{:S(2)}, u32[]{:S(2)}) collective-permute-start(bf16[64,1024]{1,0:T(8,128)(2,1)S(1)} %get-tuple-element.833), channel_id=1, source_target_pairs={{0,8},{8,16},{16,24},{1,9},{9,17},{17,25},{2,10},{10,18},{18,26},{... | collective-permute-start | bytes 393224 | tf_op jit(solution)/shard_map/while/body/eval_jaxpr/ppermute | solution.py:247
  156.3 17.1 %collective-permute-start = (bf16[64,1024]{1,0:T(8,128)(2,1)S(1)}, bf16[64,1024]{1,0:T(8,128)(2,1)S(1)}, u32[]{:S(2)}, u32[]{:S(2)}) collective-permute-start(bf16[64,1024]{1,0:T(8,128)(2,1)S(1)} %get-tuple-element.833), channel_id=1, source_target_pairs={{0,8},{8,16},{16,24},{1,9},{9,17},{17,25},{2,10},{10,18},{18,26},{... | collective-permute-start | bytes 393224 | tf_op jit(solution)/shard_map/while/body/eval_jaxpr/ppermute | solution.py:247
  174.6 6.2 %collective-permute-start.1 = (bf16[64,1024]{1,0:T(8,128)(2,1)S(1)}, bf16[64,1024]{1,0:T(8,128)(2,1)S(1)}, u32[]{:S(2)}, u32[]{:S(2)}) collective-permute-start(bf16[64,1024]{1,0:T(8,128)(2,1)S(1)} %get-tuple-element.834), channel_id=1, source_target_pairs={{8,0},{16,8},{24,16},{9,1},{17,9},{25,17},{10,2},{18,10},{26,18},{... | collective-permute-start | bytes 393224 | tf_op jit(solution)/shard_map/while/body/eval_jaxpr/ppermute | solution.py:247
  180.8 11.4 %collective-permute-start.1 = (bf16[64,1024]{1,0:T(8,128)(2,1)S(1)}, bf16[64,1024]{1,0:T(8,128)(2,1)S(1)}, u32[]{:S(2)}, u32[]{:S(2)}) collective-permute-start(bf16[64,1024]{1,0:T(8,128)(2,1)S(1)} %get-tuple-element.834), channel_id=1, source_target_pairs={{8,0},{16,8},{24,16},{9,1},{17,9},{25,17},{10,2},{18,10},{26,18},{... | collective-permute-start | bytes 393224 | tf_op jit(solution)/shard_map/while/body/eval_jaxpr/ppermute | solution.py:247
  192.2 69.3 %collective-permute-start.1 = (bf16[64,1024]{1,0:T(8,128)(2,1)S(1)}, bf16[64,1024]{1,0:T(8,128)(2,1)S(1)}, u32[]{:S(2)}, u32[]{:S(2)}) collective-permute-start(bf16[64,1024]{1,0:T(8,128)(2,1)S(1)} %get-tuple-element.834), channel_id=1, source_target_pairs={{8,0},{16,8},{24,16},{9,1},{17,9},{25,17},{10,2},{18,10},{26,18},{... | collective-permute-start | bytes 393224 | tf_op jit(solution)/shard_map/while/body/eval_jaxpr/ppermute | solution.py:247
  283.8 6.3 %collective-permute-start.1 = (bf16[64,1024]{1,0:T(8,128)(2,1)S(1)}, bf16[64,1024]{1,0:T(8,128)(2,1)S(1)}, u32[]{:S(2)}, u32[]{:S(2)}) collective-permute-start(bf16[64,1024]{1,0:T(8,128)(2,1)S(1)} %get-tuple-element.834), channel_id=1, source_target_pairs={{8,0},{16,8},{24,16},{9,1},{17,9},{25,17},{10,2},{18,10},{26,18},{... | collective-permute-start | bytes 393224 | tf_op jit(solution)/shard_map/while/body/eval_jaxpr/ppermute | solution.py:247
  312.4 6.3 %collective-permute-start.1 = (bf16[64,1024]{1,0:T(8,128)(2,1)S(1)}, bf16[64,1024]{1,0:T(8,128)(2,1)S(1)}, u32[]{:S(2)}, u32[]{:S(2)}) collective-permute-start(bf16[64,1024]{1,0:T(8,128)(2,1)S(1)} %get-tuple-element.834), channel_id=1, source_target_pairs={{8,0},{16,8},{24,16},{9,1},{17,9},{25,17},{10,2},{18,10},{26,18},{... | collective-permute-start | bytes 393224 | tf_op jit(solution)/shard_map/while/body/eval_jaxpr/ppermute | solution.py:247
  340.9 6.3 %collective-permute-start.1 = (bf16[64,1024]{1,0:T(8,128)(2,1)S(1)}, bf16[64,1024]{1,0:T(8,128)(2,1)S(1)}, u32[]{:S(2)}, u32[]{:S(2)}) collective-permute-start(bf16[64,1024]{1,0:T(8,128)(2,1)S(1)} %get-tuple-element.834), channel_id=1, source_target_pairs={{8,0},{16,8},{24,16},{9,1},{17,9},{25,17},{10,2},{18,10},{26,18},{... | collective-permute-start | bytes 393224 | tf_op jit(solution)/shard_map/while/body/eval_jaxpr/ppermute | solution.py:247
  369.5 3.2 collective-permute-start.1
  372.8 33.6 %copy-start.6 = (s32[1,32,128]{2,1,0:T(8,128)S(1)}, s32[1,32,128]{2,1,0:T(8,128)}, u32[]{:S(2)}) copy-start(s32[1,32,128]{2,1,0:T(8,128)} %param.26) | copy-start | bytes 49156
  372.8 33.6 %copy-start.10 = (s32[1,32]{1,0:T(1,128)S(1)}, s32[1,32]{1,0:T(1,128)}, u32[]{:S(2)}) copy-start(s32[1,32]{1,0:T(1,128)} %param.27) | copy-start | bytes 388
  394.4 2.2 copy-start.2
  396.6 0.9 copy-start.4
  401.8 32.2 %all-to-all-start.1 = ((bf16[32,128,128]{2,1,0:T(8,128)(2,1)}), bf16[32,128,128]{2,1,0:T(8,128)(2,1)S(1)}, u32[]{:S(2)}, u32[]{:S(2)}) async-start(bf16[32,128,128]{2,1,0:T(8,128)(2,1)} %expand.1), calls=%async_computation.2 | async-start | bytes 2097152 | tf_op jit(solution)/shard_map/all_to_all | solution.py:398
Sparse Core Ops, SparseCore 0:
  374.9 19.4 reduce-scatter.1

commit v2 on v1

--- a/solution.py
+++ b/solution.py
@@ -7,7 +7,7 @@
 
 EPSILON = 1e-05
 DECAY_WEIGHT = 0.5
-VMEM_LIMIT = 40 * 1024 * 1024
+VMEM_LIMIT = 20 * 1024 * 1024
 UNROLL = 16
 
 
@@ -241,61 +241,285 @@
     )(targets, returned, outgoing)
 
 
-def shifted(value, axis, steps):
-    count = lax.axis_size(axis)
-    first, last = (max(0, -steps), min(count, count - steps))
-    return lax.ppermute(value, axis, [(source, source + steps) for source in range(first, last)])
-
-
-def fm_forward(inputs, proj, gain, w_up, w_down):
-    batch_rows = inputs.shape[0]
-    embed_count = proj.shape[0]
-    features = inputs.reshape(batch_rows, embed_count, -1)
-    mixed_cols = jnp.einsum(
-        "bke,kr->bre", features, proj, preferred_element_type=jnp.float32
-    ).astype(jnp.bfloat16)
-    interact = jnp.einsum(
-        "bke,bre->bkr", features, mixed_cols, preferred_element_type=jnp.float32
-    ).reshape(batch_rows, -1)
-    inv_scale = lax.rsqrt(jnp.mean(interact * interact, axis=1, keepdims=True) + EPSILON)
-    normed = (interact * inv_scale * gain.astype(jnp.float32)).astype(jnp.bfloat16)
-    before = jnp.dot(normed, w_up, preferred_element_type=jnp.float32)
-    hidden = jnp.maximum(before, 0.0).astype(jnp.bfloat16)
-    output = inputs.astype(jnp.float32) + jnp.dot(
-        hidden, w_down, preferred_element_type=jnp.float32
+GROUP = 32
+SMALL_LIMIT = 20 * 1024 * 1024
+NT = (((1,), (1,)), ((), ()))
+
+
+def dot_nt(left, right):
+    return lax.dot_general(left, right, NT, preferred_element_type=jnp.float32)
+
+
+def dot(left, right):
+    return jnp.dot(left, right, preferred_element_type=jnp.float32)
+
+
+def split_dot(left, right):
+    high = left.astype(jnp.bfloat16)
+    low = (left - high.astype(jnp.float32)).astype(jnp.bfloat16)
+    return dot(high, right) + dot(low, right)
+
+
+def same_sample(count):
+    first = lax.broadcasted_iota(jnp.int32, (count * GROUP, count * GROUP), 0)
+    second = lax.broadcasted_iota(jnp.int32, (count * GROUP, count * GROUP), 1)
+    return (first & (GROUP - 1)) == (second & (GROUP - 1))
+
+
+def stacked(ref, rows, count, width):
+    return jnp.concatenate([ref[rows, k * width : (k + 1) * width] for k in range(count)], axis=0)
+
+
+def repeated(proj):
+    count, width = proj.shape
+    lines = [jnp.broadcast_to(proj[k : k + 1, :], (GROUP, width)) for k in range(count)]
+    return jnp.concatenate(lines, axis=0).astype(jnp.bfloat16)
+
+
+def mix_forward(small, layer, acts, inter, scale, normed, count):
+    batch, model_width = acts.shape
+    width = model_width // count
+    both = small[layer].astype(jnp.float32)
+    proj = repeated(both[:count])
+    keep = same_sample(count)
+    for start in range(0, batch, GROUP):
+        rows = pl.ds(start, GROUP)
+        block = stacked(acts, rows, count, width)
+        gram = jnp.where(keep, dot_nt(block, block), 0.0)
+        mixed = split_dot(gram, proj)
+        parts = [mixed[k * GROUP : (k + 1) * GROUP] for k in range(count)]
+        squares = sum(part * part for part in parts)
+        mean = jnp.sum(squares, axis=1, keepdims=True) * (1.0 / model_width)
+        inv = lax.rsqrt(mean + EPSILON)
+        scale[rows, :] = jnp.broadcast_to(inv, (GROUP, width))
+        for k in range(count):
+            columns = slice(k * width, (k + 1) * width)
+            inter[rows, columns] = parts[k]
+            gain = both[count + k : count + k + 1]
+            normed[rows, columns] = (parts[k] * inv * gain).astype(jnp.bfloat16)
+
+
+def up_product(normed, w_up, layer, hidden, tile=512):
+    def body(step, carry):
+        columns = pl.ds(pl.multiple_of(step * tile, tile), tile)
+        before = dot(normed[...], w_up[layer, :, columns])
+        hidden[:, columns] = jnp.maximum(before, 0.0).astype(jnp.bfloat16)
+        return carry
+
+    lax.fori_loop(0, hidden.shape[1] // tile, body, 0)
+
+
+def down_product(hidden, w_down, layer, acts, out, tile=256):
+    def body(step, carry):
+        columns = pl.ds(pl.multiple_of(step * tile, tile), tile)
+        term = dot(hidden[...], w_down[layer, :, columns])
+        out[:, columns] = (acts[:, columns].astype(jnp.float32) + term).astype(jnp.bfloat16)
+        return carry
+
+    lax.fori_loop(0, out.shape[1] // tile, body, 0)
+
+
+def layer_backward(small, layer, grad, acts, inter, scale, hidden, w_up, w_down, out, g_before, weighted, count):
+    batch, model_width = acts.shape
+    width = model_width // count
+    tile = 512
+
+    def masked(step, carry):
+        columns = pl.ds(pl.multiple_of(step * tile, tile), tile)
+        g_hidden = dot_nt(grad[...], w_down[layer, columns, :])
+        is_open = hidden[:, columns].astype(jnp.float32) > 0.0
+        g_before[:, columns] = jnp.where(is_open, g_hidden, 0.0).astype(jnp.bfloat16)
+        return carry
+
+    lax.fori_loop(0, hidden.shape[1] // tile, masked, 0)
+
+    def to_normed(step, carry):
+        columns = pl.ds(pl.multiple_of(step * 256, 256), 256)
+        weighted[:, columns] = dot_nt(g_before[...], w_up[layer, columns, :])
+        return carry
+
+    lax.fori_loop(0, model_width // 256, to_normed, 0)
+    both = small[layer].astype(jnp.float32)
+    proj = repeated(both[:count])
+    keep = same_sample(count)
+    for start in range(0, batch, GROUP):
+        rows = pl.ds(start, GROUP)
+        columns = [slice(k * width, (k + 1) * width) for k in range(count)]
+        gained = [weighted[rows, columns[k]] * both[count + k : count + k + 1] for k in range(count)]
+        shared = sum(gained[k] * inter[rows, columns[k]] for k in range(count))
+        mean = jnp.sum(shared, axis=1, keepdims=True) * (1.0 / model_width)
+        inv = scale[rows, 0:1]
+        pull = inv * inv * mean
+        parts = [
+            (inv * (gained[k] - inter[rows, columns[k]] * pull)).astype(jnp.bfloat16)
+            for k in range(count)
+        ]
+        block = stacked(acts, rows, count, width)
+        g_inter = jnp.concatenate(parts, axis=0)
+        left = jnp.concatenate([g_inter, proj], axis=1)
+        right = jnp.concatenate([proj, g_inter], axis=1)
+        links = jnp.where(keep, dot_nt(left, right), 0.0)
+        g_acts = split_dot(links, block)
+        for k in range(count):
+            piece = g_acts[k * GROUP : (k + 1) * GROUP] + grad[rows, columns[k]].astype(jnp.float32)
+            out[rows, columns[k]] = piece.astype(jnp.bfloat16)
+
+
+def in_vmem(shape, dtype):
+    return pltpu.VMEM(shape, dtype)
+
+
+def hold_weights(core, pairs):
+    def kernel(core_ref, *refs):
+        own, other = refs[0 : len(pairs)], refs[len(pairs) : 2 * len(pairs)]
+        outs, sems = refs[2 * len(pairs) : 3 * len(pairs)], refs[3 * len(pairs)]
+        here = core_ref[0]
+        copies = []
+        for i in range(len(pairs)):
+            copies.append(pltpu.make_async_copy(own[i], outs[i].at[here], sems.at[2 * i]))
+            copies.append(pltpu.make_async_copy(other[i], outs[i].at[1 - here], sems.at[2 * i + 1]))
+        for copy in copies:
+            copy.start()
+        for copy in copies:
+            copy.wait()
+
+    return pl.pallas_call(
+        kernel,
+        out_shape=[in_vmem((2,) + own.shape, own.dtype) for own, other in pairs],
+        in_specs=[pl.BlockSpec(memory_space=pltpu.SMEM)]
+        + [pl.BlockSpec(memory_space=pl.ANY)] * (2 * len(pairs)),
+        out_specs=[whole() for pair in pairs],
+        scratch_shapes=[pltpu.SemaphoreType.DMA((2 * len(pairs),))],
+        compiler_params=pltpu.CompilerParams(vmem_limit_bytes=SMALL_LIMIT),
+        name="hold_weights",
+    )(core, *[own for own, other in pairs], *[other for own, other in pairs])
+
+
+def saved_shapes(batch, model_width, hidden_width, width):
+    return [
+        in_vmem((2, batch, hidden_width), jnp.bfloat16),
+        in_vmem((2, batch, model_width), jnp.float32),
+        in_vmem((2, batch, width), jnp.float32),
+        in_vmem((2, batch, model_width), jnp.bfloat16),
+    ]
+
+
+def forward_stage(active, acts, weights, count):
+    small, w_up, w_down = weights
+    batch, model_width = acts.shape
+    hidden_width = w_up.shape[2]
+    width = model_width // count
+
+    def kernel(active_ref, acts_ref, small_ref, up_ref, down_ref, out_ref, hid, inter, scale, kept, normed):
+        @pl.when(active_ref[0] == 1)
+        def _():
+            kept[0] = acts_ref[...]
+            for layer in (0, 1):
+                mix_forward(
+                    small_ref, layer, kept.at[layer], inter.at[layer], scale.at[layer], normed, count
+                )
+                up_product(normed, up_ref, layer, hid.at[layer])
+                to = kept.at[1] if layer == 0 else out_ref
+                down_product(hid.at[layer], down_ref, layer, kept.at[layer], to)
+
+    out = pl.pallas_call(
+        kernel,
+        out_shape=[jax.ShapeDtypeStruct(acts.shape, jnp.bfloat16)]
+        + saved_shapes(batch, model_width, hidden_width, width),
+        in_specs=[pl.BlockSpec(memory_space=pltpu.SMEM)] + [whole()] * 4,
+        out_specs=[whole()] * 5,
+        scratch_shapes=[pltpu.VMEM((batch, model_width), jnp.bfloat16)],
+        compiler_params=pltpu.CompilerParams(vmem_limit_bytes=SMALL_LIMIT),
+        cost_estimate=stage_cost(4, batch, model_width, hidden_width),
+        name="forward_stage",
+    )(active, acts, small, w_up, w_down)
+    return out[0], out[1:]
+
+
+def stage_cost(products, batch, model_width, hidden_width):
+    return pl.CostEstimate(
+        flops=2 * products * batch * model_width * hidden_width, bytes_accessed=1 << 20, transcendentals=0
     )
-    return (output.astype(jnp.bfloat16), (features, mixed_cols, interact, inv_scale, before))
-
-
-def fm_backward(inputs, grad_out, proj, gain, w_up, w_down):
-    batch_rows = inputs.shape[0]
-    embed_count = proj.shape[0]
-    unused, saved = fm_forward(inputs, proj, gain, w_up, w_down)
-    features, mixed_cols, interact, inv_scale, before = saved
-    last_dims = (((1,), (1,)), ((), ()))
-    g_hidden = lax.dot_general(grad_out, w_down, last_dims, preferred_element_type=jnp.float32)
-    g_before = jnp.where(before > 0.0, g_hidden, 0.0).astype(jnp.bfloat16)
-    g_normed = lax.dot_general(g_before, w_up, last_dims, preferred_element_type=jnp.float32)
-    weighted = g_normed * gain.astype(jnp.float32)
-    g_interact = inv_scale * (
-        weighted
-        - interact * inv_scale * inv_scale * jnp.mean(weighted * interact, axis=1, keepdims=True)
-    )
-    g_interact = g_interact.astype(jnp.bfloat16).reshape(batch_rows, embed_count, -1)
-    g_features = jnp.einsum(
-        "bkr,bre->bke", g_interact, mixed_cols, preferred_element_type=jnp.float32
-    )
-    g_mixed = jnp.einsum(
-        "bkr,bke->bre", g_interact, features, preferred_element_type=jnp.float32
-    ).astype(jnp.bfloat16)
-    g_features = g_features + jnp.einsum(
-        "bre,kr->bke", g_mixed, proj, preferred_element_type=jnp.float32
-    )
-    return (grad_out.astype(jnp.float32) + g_features.reshape(batch_rows, -1)).astype(jnp.bfloat16)
-
-
-def pass_on(payload, offset):
-    return shifted(payload, "section", offset)
+
+
+def turn_stage(active, acts, top, weights, count):
+    small, w_up, w_down = weights
+    batch, model_width = acts.shape
+    hidden_width = w_up.shape[2]
+    width = model_width // count
+
+    def kernel(active_ref, acts_ref, top_ref, small_ref, up_ref, down_ref, out_ref, hid, inter, scale, upper, grad, normed, weighted, g_before):
+        @pl.when(active_ref[0] == 1)
+        def _():
+            mix_forward(small_ref, 0, acts_ref, inter.at[0], scale.at[0], normed, count)
+            up_product(normed, up_ref, 0, hid.at[0])
+            down_product(hid.at[0], down_ref, 0, acts_ref, upper)
+            mix_forward(small_ref, 1, upper, inter.at[1], scale.at[1], normed, count)
+            up_product(normed, up_ref, 1, hid.at[1])
+            for layer, given, source, to in ((1, top_ref, upper, grad), (0, grad, acts_ref, out_ref)):
+                layer_backward(
+                    small_ref, layer, given, source, inter.at[layer], scale.at[layer], hid.at[layer],
+                    up_ref, down_ref, to, g_before, weighted, count,
+                )
+
+    return pl.pallas_call(
+        kernel,
+        out_shape=jax.ShapeDtypeStruct(acts.shape, jnp.bfloat16),
+        in_specs=[pl.BlockSpec(memory_space=pltpu.SMEM)] + [whole()] * 5,
+        out_specs=whole(),
+        scratch_shapes=[
+            pltpu.VMEM((2, batch, hidden_width), jnp.bfloat16),
+            pltpu.VMEM((2, batch, model_width), jnp.float32),
+            pltpu.VMEM((2, batch, width), jnp.float32),
+            pltpu.VMEM((batch, model_width), jnp.bfloat16),
+            pltpu.VMEM((batch, model_width), jnp.bfloat16),
+            pltpu.VMEM((batch, model_width), jnp.bfloat16),
+            pltpu.VMEM((batch, model_width), jnp.float32),
+            pltpu.VMEM((batch, hidden_width), jnp.bfloat16),
+        ],
+        compiler_params=pltpu.CompilerParams(vmem_limit_bytes=SMALL_LIMIT),
+        cost_estimate=stage_cost(7, batch, model_width, hidden_width),
+        name="turn_stage",
+    )(active, acts, top, small, w_up, w_down)
+
+
+def backward_stage(active, grad, saved, weights, count):
+    small, w_up, w_down = weights
+    batch, model_width = grad.shape
+    hidden_width = w_up.shape[2]
+
+    def kernel(active_ref, grad_ref, hid, inter, scale, kept, small_ref, up_ref, down_ref, out_ref, middle, weighted, g_before):
+        @pl.when(active_ref[0] == 1)
+        def _():
+            for layer, given, to in ((1, grad_ref, middle), (0, middle, out_ref)):
+                layer_backward(
+                    small_ref, layer, given, kept.at[layer], inter.at[layer], scale.at[layer],
+                    hid.at[layer], up_ref, down_ref, to, g_before, weighted, count,
+                )
+
+    return pl.pallas_call(
+        kernel,
+        out_shape=jax.ShapeDtypeStruct(grad.shape, jnp.bfloat16),
+        in_specs=[pl.BlockSpec(memory_space=pltpu.SMEM)] + [whole()] * 8,
+        out_specs=whole(),
+        scratch_shapes=[
+            pltpu.VMEM((batch, model_width), jnp.bfloat16),
+            pltpu.VMEM((batch, model_width), jnp.float32),
+            pltpu.VMEM((batch, hidden_width), jnp.bfloat16),
+        ],
+        compiler_params=pltpu.CompilerParams(vmem_limit_bytes=SMALL_LIMIT),
+        cost_estimate=stage_cost(4, batch, model_width, hidden_width),
+        name="backward_stage",
+    )(active, grad, *saved, small, w_up, w_down)
+
+
+def swapped(value, section_count):
+    return lax.ppermute(value, "section", [(s, s ^ 1) for s in range(section_count)])
+
+
+def moved(value, from_stage, to_stage):
+    pairs = [(2 * from_stage + core, 2 * to_stage + core) for core in (0, 1)]
+    return lax.ppermute(value, "section", pairs)
 
 
 def per_device(
@@ -311,96 +535,67 @@
     row_counts,
 ):
     section_count = lax.axis_size("section")
-    shard_count = lax.axis_size("table")
-    my_section = lax.axis_index("section")
-    owners = section_count * shard_count
+    owners = section_count * lax.axis_size("table")
+    stages = section_count // 2
+    stage = lax.axis_index("section") // 2
+    core = lax.axis_index("section") % 2
     cap = wanted_rows.shape[2]
-    embed_width = emb_table.shape[1]
-    picked_rows = wanted_rows[0]
+    rows, embed_width = emb_table.shape
+    embed_count = lcb_weight.shape[0]
     look_dev = lookup_slot.shape[1]
-    embed_count = lcb_weight.shape[0]
-    outgoing = pick_rows(emb_table, picked_rows.reshape(-1))
+    model_width = top_grad.shape[3]
+    table_axes = ("section", "table")
+
+    small = jnp.concatenate([fm_proj[0], norm_gain[0].reshape(embed_count, -1)], axis=0)
+    other_up = swapped(w_up[0], section_count)
+    other_down = swapped(w_down[0], section_count)
+    other_small = swapped(small, section_count)
+
+    picked = wanted_rows[0]
+    outgoing = pick_rows(emb_table, picked.reshape(-1))
     fetched = lax.all_to_all(
-        outgoing.reshape(owners, cap, embed_width),
-        ("section", "table"),
-        split_axis=0,
-        concat_axis=0,
-        tiled=True,
+        outgoing.reshape(owners, cap, embed_width), table_axes, split_axis=0, concat_axis=0, tiled=True
     )
     spread = spread_weights(lookup_slot[0], lcb_weight, owners, cap)
-    compressed = compress(spread, fetched, embed_count)
-    leading = lax.all_gather(compressed, "section", axis=0, tiled=True)
-    micro_count = top_grad.shape[1]
-    batch_rows = top_grad.shape[2]
-    model_width = top_grad.shape[3]
-    leading = leading.reshape(micro_count, batch_rows, model_width)
-    weights = (fm_proj[0], norm_gain[0], w_up[0], w_down[0])
-    tick_count = micro_count + section_count - 1
-
-    def forward_tick(tick, state):
-        incoming, stash = state
-        micro_idx = tick - my_section
-        is_valid = (micro_idx >= 0) & (micro_idx < micro_count)
-        clipped = jnp.clip(micro_idx, 0, micro_count - 1)
-        inputs = jnp.where(
-            my_section == 0, lax.dynamic_index_in_dim(leading, clipped, 0, keepdims=False), incoming
-        )
-        outputs = lax.cond(
-            is_valid,
-            lambda value: fm_forward(value, *weights)[0],
-            lambda value: jnp.zeros_like(value),
-            inputs,
-        )
-        kept_rows = jnp.where(
-            is_valid, inputs, lax.dynamic_index_in_dim(stash, clipped, 0, keepdims=False)
-        )
-        stash = lax.dynamic_update_index_in_dim(stash, kept_rows, clipped, 0)
-        return (pass_on(outputs, 1), stash)
-
-    empty_rows = jnp.zeros((batch_rows, model_width), jnp.bfloat16)
-    empty_stash = jnp.zeros((micro_count, batch_rows, model_width), jnp.bfloat16)
-    unused, stash = lax.fori_loop(0, tick_count, forward_tick, (empty_rows, empty_stash))
-    grads_top = top_grad[0]
-
-    def backward_tick(tick, state):
-        incoming, lead_grad = state
-        micro_idx = tick - (section_count - 1 - my_section)
-        is_valid = (micro_idx >= 0) & (micro_idx < micro_count)
-        clipped = jnp.clip(micro_idx, 0, micro_count - 1)
-        given = jnp.where(
-            my_section == section_count - 1,
-            lax.dynamic_index_in_dim(grads_top, clipped, 0, keepdims=False),
-            incoming,
-        )
-        saved_rows = lax.dynamic_index_in_dim(stash, clipped, 0, keepdims=False)
-        result = lax.cond(
-            is_valid,
-            lambda pair: fm_backward(pair[0], pair[1], *weights),
-            lambda pair: jnp.zeros_like(pair[0]),
-            (saved_rows, given),
-        )
-        record = jnp.where(
-            is_valid & (my_section == 0),
-            result,
-            lax.dynamic_index_in_dim(lead_grad, clipped, 0, keepdims=False),
-        )
-        lead_grad = lax.dynamic_update_index_in_dim(lead_grad, record, clipped, 0)
-        return (pass_on(result, -1), lead_grad)
-
-    unused, lead_grad = lax.fori_loop(0, tick_count, backward_tick, (empty_rows, empty_stash))
-    terms = jnp.where(my_section == 0, lead_grad.astype(jnp.float32), 0.0).reshape(
-        micro_count * batch_rows, model_width
+    smalls = jnp.stack(
+        [jnp.where(core == 0, small, other_small), jnp.where(core == 0, other_small, small)]
     )
-    lead_share = lax.psum_scatter(
-        terms.astype(jnp.bfloat16), "section", scatter_dimension=0, tiled=True
+    core_id = core.astype(jnp.int32).reshape(1)
+    weights = [smalls] + list(
+        hold_weights(core_id, [(w_up[0], other_up), (w_down[0], other_down)])
     )
+    lead = compress(spread, fetched, embed_count)
+
+    acts = jnp.concatenate([lead] + [moved(lead, s, 0) for s in range(1, stages)], axis=0)
+    top = top_grad.reshape(stages, 2, look_dev, model_width)
+    top = lax.dynamic_index_in_dim(top, core, 1, keepdims=False).reshape(-1, model_width)
+
+    def at(tick):
+        return (stage == tick).astype(jnp.int32).reshape(1)
+
+    saved = None
+    for tick in range(stages - 1):
+        out, fresh = forward_stage(at(tick), acts, weights, embed_count)
+        if saved is None:
+            saved = fresh
+        else:
+            saved = [jnp.where(stage == tick, new, old) for new, old in zip(fresh, saved)]
+        acts = moved(out, tick, tick + 1)
+    grad = turn_stage(at(stages - 1), acts, top, weights, embed_count)
+    for tick in reversed(range(stages - 1)):
+        grad = moved(grad, tick + 1, tick)
+        grad = backward_stage(at(tick), grad, saved, weights, embed_count)
+
+    lead_share = grad[:look_dev]
+    for s in range(1, stages):
+        arrived = moved(grad[s * look_dev : (s + 1) * look_dev], 0, s)
+        lead_share = jnp.where(stage == s, arrived, lead_share)
+
     slot_grad = expand(spread, lead_share, embed_count)
-    returned = lax.all_to_all(
-        slot_grad, ("section", "table"), split_axis=0, concat_axis=0, tiled=True
-    )
+    returned = lax.all_to_all(slot_grad, table_axes, split_axis=0, concat_axis=0, tiled=True)
     live_slots = jnp.arange(cap)[None, :] < row_counts[0][:, None]
-    targets = jnp.where(live_slots, picked_rows, emb_table.shape[0]).reshape(-1)
-    return add_rows(targets, returned.reshape(-1, embed_width), outgoing, emb_table.shape[0])
+    targets = jnp.where(live_slots, picked, rows).reshape(-1)
+    return add_rows(targets, returned.reshape(-1, embed_width), outgoing, rows)
 
 
 def solution(mesh):

time: 453 us -> 229 us (0.51)
  matrix products: 124 us -> 0 us
  waiting for transfers between devices: 160 us -> 89.9 us
  starting transfers between devices: 70.4 us -> 18.3 us
  Pallas kernels: 29.8 us -> 81 us
  other arithmetic: 17.3 us -> 1.52 us
  between operations: 13.5 us -> 0.4 us
  local copies, waits for them, and re-layouts: 29.3 us -> 37.6 us
  blocking collectives: 6.61 us -> 0 us
    dot_general x32 -> x0, matrix products: 124 us -> none  [the longest x4 44.4 us: fm_backward(): lax.dot_general(g_before, w_up, last_dims, preferred_element_type=jnp.flo...]
    ppermute x14 -> x7, starting transfers between devices: 58.5 us -> 6.07 us  [the longest x4 5.29 us: moved(): return lax.ppermute(value, 'section', pairs)]
    pallas_call x0 -> x4, Pallas kernels: none -> 51.1 us  [the longest x1 22.8 us: backward_stage(): pl.pallas_call(kernel, out_shape=jax.ShapeDtypeStruct(grad.shape, jnp.bfl...]
    ppermute x14 -> x7, waiting for transfers between devices: 95.2 us -> 46.1 us  [the longest x4 46.1 us: moved(): return lax.ppermute(value, 'section', pairs)]
    unnamed x22 -> x38, local copies, waits for them, and re-layouts: 10.8 us -> 37.5 us
    reduce_scatter x1 -> x0, waiting for transfers between devices: 19.6 us -> none  [per_device(): lax.psum_scatter(terms.astype(jnp.bfloat16), 'section', scatter_dimension...]
    dynamic_slice x14 -> x1, local copies, waits for them, and re-layouts: 12.8 us -> 0.02 us  [per_device(): lax.dynamic_index_in_dim(top, core, 1, keepdims=False)]
    dynamic_update_slice x14 -> x0, other arithmetic: 9.94 us -> none  [the longest x7 5.08 us: forward_tick(): stash = lax.dynamic_update_index_in_dim(stash, kept_rows, clipped, 0)]
  transfers between devices with their start and end apart: 17 -> 9, of which waited for: 17 -> 6; matrix products, arithmetic and copies ran while one was open for 3% -> 1% of each run, Pallas kernels for 1% -> 7%
where the time goes in v2:
time: 229 us
  waiting for transfers between devices  89.9 us (39%)
  Pallas kernels  81 us (35%)
  local copies, waits for them, and re-layouts  37.6 us (16%)
  starting transfers between devices  18.3 us (8%)
    ppermute x4, waiting for transfers between devices, moved(): return lax.ppermute(value, 'section', pairs)  46.1 us
    unnamed x38, local copies, waits for them, and re-layouts  37.5 us
    all_to_all x1, waiting for transfers between devices, per_device(): lax.all_to_all(slot_grad, table_axes, split_axis=0, concat_axis=0, tiled=...  27.5 us
    pallas_call x1, Pallas kernels, backward_stage(): pl.pallas_call(kernel, out_shape=jax.ShapeDtypeStruct(grad.shape, jnp.bfl...  22.8 us
    pallas_call x1, Pallas kernels, forward_stage(): pl.pallas_call(kernel, out_shape=[jax.ShapeDtypeStruct(acts.shape, jnp.bf...  17.7 us
    all_to_all x1, waiting for transfers between devices, per_device(): lax.all_to_all(outgoing.reshape(owners, cap, embed_width), table_axes, sp...  16.3 us
    pallas_call x1, Pallas kernels, hold_weights(): pl.pallas_call(kernel, out_shape=[in_vmem((2,) + own.shape, own.dtype) fo...  10.6 us
    pallas_call x1, Pallas kernels, add_rows(): pl.pallas_call(kernel, out_shape=jax.ShapeDtypeStruct((rows, width), jnp....  10.4 us
  transfers between devices with their start and end apart: 9, of which 6 were waited for; matrix products, arithmetic and copies ran while one was open for 1% of the time, Pallas kernels for 7%

profile of v2, /device:TPU:0, one launch (start us, length us, event | category | flops | bytes accessed | tf_op | source)
XLA Modules:
  0.0 228.6 jit_solution(17746163407211983907)
XLA Ops:
  0.5 1.2 copy-done.12
  1.8 0.7 copy-done.13
  2.5 6.4 %pick_rows.1.sent_ref = bf16[4096,128]{1,0:T(8,128)(2,1)} custom-call(s32[4096]{0:T(1024)S(1)} %bitcast.28, bf16[4096,128]{1,0:T(8,128)(2,1)S(1)} %copy-done.12), custom_call_target="tpu_custom_call" | custom-call | tf_op jit(solution)/shard_map/pick_rows/pallas_call | solution.py:48
  8.9 7.3 %all-to-all-start = ((bf16[32,128,128]{2,1,0:T(8,128)(2,1)}), bf16[32,128,128]{2,1,0:T(8,128)(2,1)S(1)}, u32[]{:S(2)}, u32[]{:S(2)}) async-start(bf16[32,128,128]{2,1,0:T(8,128)(2,1)} %bitcast.6), calls=%async_computation | async-start | bytes 2097152 | tf_op jit(solution)/shard_map/all_to_all | solution.py:556
  16.2 0.7 reduce
  17.8 0.9 copy-done.15
  19.4 6.0 %spread_weights.1.spread_ref = bf16[32,512,128]{2,1,0:T(8,128)(2,1)S(1)} custom-call(s32[64,512]{1,0:T(8,128)S(1)} %bitcast.29, bf16[8,512]{1,0:T(8,128)(2,1)S(1)} %copy-done.16), custom_call_target="tpu_custom_call" | custom-call | flops 2147483648 | bytes 4194304 | tf_op jit(solution)/shard_map/spread_weights/pallas_call | solution.py:91
  25.4 2.0 copy-done.7
  27.5 16.3 %all-to-all-done.rows_ref = bf16[32,128,128]{2,1,0:T(8,128)(2,1)S(1)} async-done(((bf16[32,128,128]{2,1,0:T(8,128)(2,1)}), bf16[32,128,128]{2,1,0:T(8,128)(2,1)S(1)}, u32[]{:S(2)}, u32[]{:S(2)}) %all-to-all-start) | async-done | bytes 1048608 | tf_op jit(solution)/shard_map/all_to_all | solution.py:556
  43.8 2.2 copy-done.8
  45.9 2.7 %compress.1 = bf16[64,1024]{1,0:T(8,128)(2,1)S(1)} custom-call(bf16[32,512,128]{2,1,0:T(8,128)(2,1)S(1)} %copy-done.8, bf16[32,128,128]{2,1,0:T(8,128)(2,1)S(1)} %all-to-all-done.rows_ref), custom_call_target="tpu_custom_call" | custom-call | tf_op jit(solution)/shard_map/compress/pallas_call | solution.py:136
  48.6 1.3 collective-permute-start
  50.0 5.6 %collective-permute-done = bf16[64,1024]{1,0:T(8,128)(2,1)S(1)} collective-permute-done((bf16[64,1024]{1,0:T(8,128)(2,1)S(1)}, bf16[64,1024]{1,0:T(8,128)(2,1)S(1)}, u32[]{:S(2)}, u32[]{:S(2)}) %collective-permute-start) | collective-permute-done | bytes 131104 | tf_op jit(solution)/shard_map/ppermute | solution.py:522
  55.6 10.6 %hold_weights.1 = (bf16[2,1024,4096]{2,1,0:T(8,128)(2,1)S(1)}, bf16[2,4096,1024]{2,1,0:T(8,128)(2,1)S(1)}) custom-call(s32[1]{0:T(128)} %bitcast.10.core_ref, bf16[1024,4096]{1,0:T(8,128)(2,1)} %bitcast.31, bf16[4096,1024]{1,0:T(8,128)(2,1)} %bitcast.33, bf16[1024,4096]{1,0:T(8,128)(2,1)} %collective-permute-done.2.refs_2_, ...), custom_call_target="tpu_custom_call" | custom-call | tf_op jit(solution)/shard_map/hold_weights/pallas_call | solution.py:386
  66.2 5.7 %copy-done.2 = bf16[2,1024,4096]{2,1,0:T(8,128)(2,1)} copy-done((bf16[2,1024,4096]{2,1,0:T(8,128)(2,1)}, bf16[2,1024,4096]{2,1,0:T(8,128)(2,1)S(1)}, u32[]{:S(2)}) %copy-start.2) | copy-done | bytes 16777240
  72.0 5.7 %copy-done.5 = bf16[2,4096,1024]{2,1,0:T(8,128)(2,1)} copy-done((bf16[2,4096,1024]{2,1,0:T(8,128)(2,1)}, bf16[2,4096,1024]{2,1,0:T(8,128)(2,1)S(1)}, u32[]{:S(2)}) %copy-start.5) | copy-done | bytes 16777240
  77.7 5.8 %copy-done.3 = bf16[2,1024,4096]{2,1,0:T(8,128)(2,1)S(1)} copy-done((bf16[2,1024,4096]{2,1,0:T(8,128)(2,1)S(1)}, bf16[2,1024,4096]{2,1,0:T(8,128)(2,1)}, u32[]{:S(2)}) %copy-start.3) | copy-done | bytes 16777240
  83.4 17.7 %forward_stage.1 = (bf16[128,1024]{1,0:T(8,128)(2,1)}, bf16[2,128,4096]{2,1,0:T(8,128)(2,1)S(1)}, f32[2,128,1024]{2,1,0:T(8,128)S(1)}, f32[2,128,128]{2,1,0:T(8,128)S(1)}, bf16[2,128,1024]{2,1,0:T(8,128)(2,1)S(1)}) custom-call(s32[1]{0:T(128)} %bitcast.4.active_ref, bf16[128,1024]{1,0:T(8,128)(2,1)S(1)} %pad_maximum_fusion.acts_ref, ...), custom_call_target="tpu_custom_call" | custom-call | flops 4294967296 | bytes 1048576 | tf_op jit(solution)/shard_map/forward_stage/pallas_call | solution.py:425
  101.2 1.0 copy-done.10
  102.1 1.3 collective-permute-start.4
  103.5 5.0 %collective-permute-done.4.acts_ref = bf16[128,1024]{1,0:T(8,128)(2,1)S(1)} collective-permute-done((bf16[128,1024]{1,0:T(8,128)(2,1)}, bf16[128,1024]{1,0:T(8,128)(2,1)S(1)}, u32[]{:S(2)}, u32[]{:S(2)}) %collective-permute-start.4) | collective-permute-done | bytes 262176 | tf_op jit(solution)/shard_map/ppermute | solution.py:522
  108.5 5.8 %copy-done.4 = bf16[2,1024,4096]{2,1,0:T(8,128)(2,1)S(1)} copy-done((bf16[2,1024,4096]{2,1,0:T(8,128)(2,1)S(1)}, bf16[2,1024,4096]{2,1,0:T(8,128)(2,1)}, u32[]{:S(2)}) %copy-start.4) | copy-done | bytes 16777240
  114.3 5.8 %copy-done.6 = bf16[2,4096,1024]{2,1,0:T(8,128)(2,1)S(1)} copy-done((bf16[2,4096,1024]{2,1,0:T(8,128)(2,1)S(1)}, bf16[2,4096,1024]{2,1,0:T(8,128)(2,1)}, u32[]{:S(2)}) %copy-start.6) | copy-done | bytes 16777240
  120.1 1.4 collective-permute-start.5
  121.5 32.9 %collective-permute-done.5.grad_ref = bf16[128,1024]{1,0:T(8,128)(2,1)S(1)} collective-permute-done((bf16[128,1024]{1,0:T(8,128)(2,1)S(1)}, bf16[128,1024]{1,0:T(8,128)(2,1)S(1)}, u32[]{:S(2)}, u32[]{:S(2)}) %collective-permute-start.5) | collective-permute-done | bytes 262176 | tf_op jit(solution)/shard_map/ppermute | solution.py:522
  154.5 22.8 %backward_stage.1 = bf16[128,1024]{1,0:T(8,128)(2,1)S(1)} custom-call(s32[1]{0:T(128)} %bitcast.4.active_ref, bf16[128,1024]{1,0:T(8,128)(2,1)S(1)} %collective-permute-done.5.grad_ref, bf16[2,128,4096]{2,1,0:T(8,128)(2,1)S(1)} %get-tuple-element.15.hid, f32[2,128,1024]{2,1,0:T(8,128)S(1)} %copy-done.11, f32[2,128,128]{2,1,0:T(8,128)S(1)} %get-tuple-element.17.scale, ...), custom_call_target="tpu_custom_call" | custom-call | flops 4294967296 | bytes 1048576 | tf_op jit(solution)/shard_map/backward_stage/pallas_call | solution.py:500
  177.3 1.3 collective-permute-start.6
  178.6 2.5 %collective-permute-done.6 = bf16[64,1024]{1,0:T(8,128)(2,1)S(1)} collective-permute-done((bf16[64,1024]{1,0:T(8,128)(2,1)S(1)}, bf16[64,1024]{1,0:T(8,128)(2,1)S(1)}, u32[]{:S(2)}, u32[]{:S(2)}) %collective-permute-start.6) | collective-permute-done | bytes 131104 | tf_op jit(solution)/shard_map/ppermute | solution.py:522
  181.1 4.3 %expand.1 = bf16[32,128,128]{2,1,0:T(8,128)(2,1)} custom-call(bf16[32,512,128]{2,1,0:T(8,128)(2,1)S(1)} %copy-done.9, bf16[64,1024]{1,0:T(8,128)(2,1)S(1)} %slice_select_fusion.grad_ref), custom_call_target="tpu_custom_call" | custom-call | tf_op jit(solution)/shard_map/expand/pallas_call | solution.py:169
  185.5 4.9 %all-to-all-start.1 = ((bf16[32,128,128]{2,1,0:T(8,128)(2,1)}), bf16[32,128,128]{2,1,0:T(8,128)(2,1)S(1)}, u32[]{:S(2)}, u32[]{:S(2)}) async-start(bf16[32,128,128]{2,1,0:T(8,128)(2,1)} %expand.1), calls=%async_computation.1 | async-start | bytes 2097152 | tf_op jit(solution)/shard_map/all_to_all | solution.py:595
  190.5 27.5 %all-to-all-done.1 = bf16[32,128,128]{2,1,0:T(8,128)(2,1)S(1)} async-done(((bf16[32,128,128]{2,1,0:T(8,128)(2,1)}), bf16[32,128,128]{2,1,0:T(8,128)(2,1)S(1)}, u32[]{:S(2)}, u32[]{:S(2)}) %all-to-all-start.1) | async-done | bytes 1048608 | tf_op jit(solution)/shard_map/all_to_all | solution.py:595
  218.0 10.4 %add_rows.1 = f32[4096,128]{1,0:T(8,128)} custom-call(s32[4096]{0:T(1024)S(1)} %fusion.1.targets_ref, bf16[4096,128]{1,0:T(8,128)(2,1)S(1)} %bitcast.26, bf16[4096,128]{1,0:T(8,128)(2,1)} %pick_rows.1.sent_ref), custom_call_target="tpu_custom_call" | custom-call | tf_op jit(solution)/shard_map/add_rows/pallas_call | solution.py:222
  (42 shorter events, 2.4 us)
Async XLA Ops:
  0.0 103.5 %copy-start = (bf16[1,4,64,1024]{3,2,1,0:T(8,128)(2,1)S(1)}, bf16[1,4,64,1024]{3,2,1,0:T(8,128)(2,1)}, u32[]{:S(2)}) copy-start(bf16[1,4,64,1024]{3,2,1,0:T(8,128)(2,1)} %param.16) | copy-start | bytes 1572868
  0.0 55.6 %collective-permute-start.2 = (bf16[1024,4096]{1,0:T(8,128)(2,1)}, bf16[1024,4096]{1,0:T(8,128)(2,1)}, u32[]{:S(2)}, u32[]{:S(2)}) collective-permute-start(bf16[1024,4096]{1,0:T(8,128)(2,1)} %bitcast.30), channel_id=1, source_target_pairs={{0,8},{8,0},{16,24},{24,16},{1,9},{9,1},{17,25},{25,17},{2,10},{10... | collective-permute-start | bytes 25165832 | tf_op jit(solution)/shard_map/ppermute | solution.py:517
  0.5 55.2 %collective-permute-start.3 = (bf16[4096,1024]{1,0:T(8,128)(2,1)}, bf16[4096,1024]{1,0:T(8,128)(2,1)}, u32[]{:S(2)}, u32[]{:S(2)}) collective-permute-start(bf16[4096,1024]{1,0:T(8,128)(2,1)} %bitcast.32), channel_id=1, source_target_pairs={{0,8},{8,0},{16,24},{24,16},{1,9},{9,1},{17,25},{25,17},{2,10},{10... | collective-permute-start | bytes 25165832 | tf_op jit(solution)/shard_map/ppermute | solution.py:517
  0.5 1.2 copy-start.12
  1.8 0.7 copy-start.13
  2.5 47.5 %copy-start.17 = (bf16[1,8,128]{2,1,0:T(8,128)(2,1)S(1)}, bf16[1,8,128]{2,1,0:T(8,128)(2,1)}, u32[]{:S(2)}) copy-start(bf16[1,8,128]{2,1,0:T(8,128)(2,1)} %param.12) | copy-start | bytes 6148
  8.9 34.9 %all-to-all-start = ((bf16[32,128,128]{2,1,0:T(8,128)(2,1)}), bf16[32,128,128]{2,1,0:T(8,128)(2,1)S(1)}, u32[]{:S(2)}, u32[]{:S(2)}) async-start(bf16[32,128,128]{2,1,0:T(8,128)(2,1)} %bitcast.6), calls=%async_computation | async-start | bytes 2097152 | tf_op jit(solution)/shard_map/all_to_all | solution.py:556
  17.6 32.4 %collective-permute-start.1 = (bf16[16,128]{1,0:T(8,128)(2,1)S(1)}, bf16[16,128]{1,0:T(8,128)(2,1)S(1)}, u32[]{:S(2)}, u32[]{:S(2)}) collective-permute-start(bf16[16,128]{1,0:T(8,128)(2,1)S(1)} %pad_maximum_fusion.2), channel_id=1, source_target_pairs={{0,8},{8,0},{16,24},{24,16},{1,9},{9,1},{17,25},{25,17},{2,10},{10... | collective-permute-start | bytes 12296 | tf_op jit(solution)/shard_map/ppermute | solution.py:517
  17.8 0.9 copy-start.15
  18.7 0.7 copy-start.16
  25.4 2.1 copy-start.7
  43.8 2.2 copy-start.8
  48.6 7.0 %collective-permute-start = (bf16[64,1024]{1,0:T(8,128)(2,1)S(1)}, bf16[64,1024]{1,0:T(8,128)(2,1)S(1)}, u32[]{:S(2)}, u32[]{:S(2)}) collective-permute-start(bf16[64,1024]{1,0:T(8,128)(2,1)S(1)} %compress.1), channel_id=1, source_target_pairs={{16,0},{24,8},{17,1},{25,9},{18,2},{26,10},{19,3},{27,11},{20,4},{... | collective-permute-start | bytes 393224 | tf_op jit(solution)/shard_map/ppermute | solution.py:522
  66.2 5.7 %copy-start.2 = (bf16[2,1024,4096]{2,1,0:T(8,128)(2,1)}, bf16[2,1024,4096]{2,1,0:T(8,128)(2,1)S(1)}, u32[]{:S(2)}) copy-start(bf16[2,1024,4096]{2,1,0:T(8,128)(2,1)S(1)} %get-tuple-element.12.up_ref) | copy-start | bytes 50331652
  72.0 5.7 %copy-start.5 = (bf16[2,4096,1024]{2,1,0:T(8,128)(2,1)}, bf16[2,4096,1024]{2,1,0:T(8,128)(2,1)S(1)}, u32[]{:S(2)}) copy-start(bf16[2,4096,1024]{2,1,0:T(8,128)(2,1)S(1)} %get-tuple-element.13.down_ref) | copy-start | bytes 50331652
  77.7 5.8 %copy-start.3 = (bf16[2,1024,4096]{2,1,0:T(8,128)(2,1)S(1)}, bf16[2,1024,4096]{2,1,0:T(8,128)(2,1)}, u32[]{:S(2)}) copy-start(bf16[2,1024,4096]{2,1,0:T(8,128)(2,1)} %copy-done.2) | copy-start | bytes 50331652
  101.2 1.0 copy-start.10
  102.1 6.4 %collective-permute-start.4 = (bf16[128,1024]{1,0:T(8,128)(2,1)}, bf16[128,1024]{1,0:T(8,128)(2,1)S(1)}, u32[]{:S(2)}, u32[]{:S(2)}) collective-permute-start(bf16[128,1024]{1,0:T(8,128)(2,1)} %get-tuple-element.14), channel_id=1, source_target_pairs={{0,16},{8,24},{1,17},{9,25},{2,18},{10,26},{3,19},{11,27},{4,20},{... | collective-permute-start | bytes 786440 | tf_op jit(solution)/shard_map/ppermute | solution.py:522
  108.5 5.8 %copy-start.4 = (bf16[2,1024,4096]{2,1,0:T(8,128)(2,1)S(1)}, bf16[2,1024,4096]{2,1,0:T(8,128)(2,1)}, u32[]{:S(2)}) copy-start(bf16[2,1024,4096]{2,1,0:T(8,128)(2,1)} %copy-done.2) | copy-start | bytes 50331652
  114.3 5.8 %copy-start.6 = (bf16[2,4096,1024]{2,1,0:T(8,128)(2,1)S(1)}, bf16[2,4096,1024]{2,1,0:T(8,128)(2,1)}, u32[]{:S(2)}) copy-start(bf16[2,4096,1024]{2,1,0:T(8,128)(2,1)} %copy-done.5) | copy-start | bytes 50331652
  120.1 34.4 %copy-start.11 = (f32[2,128,1024]{2,1,0:T(8,128)S(1)}, f32[2,128,1024]{2,1,0:T(8,128)}, u32[]{:S(2)}) copy-start(f32[2,128,1024]{2,1,0:T(8,128)} %copy-done.10) | copy-start | bytes 3145732
  120.1 34.4 %collective-permute-start.5 = (bf16[128,1024]{1,0:T(8,128)(2,1)S(1)}, bf16[128,1024]{1,0:T(8,128)(2,1)S(1)}, u32[]{:S(2)}, u32[]{:S(2)}) collective-permute-start(bf16[128,1024]{1,0:T(8,128)(2,1)S(1)} %turn_stage.1), channel_id=1, source_target_pairs={{16,0},{24,8},{17,1},{25,9},{18,2},{26,10},{19,3},{27,11},{20,4},{... | collective-permute-start | bytes 786440 | tf_op jit(solution)/shard_map/ppermute | solution.py:522
  154.4 26.7 %copy-start.9 = (bf16[32,512,128]{2,1,0:T(8,128)(2,1)S(1)}, bf16[32,512,128]{2,1,0:T(8,128)(2,1)}, u32[]{:S(2)}) copy-start(bf16[32,512,128]{2,1,0:T(8,128)(2,1)} %copy-done.7) | copy-start | bytes 12582916
  154.4 36.0 %copy-start.14 = (s32[1,32,128]{2,1,0:T(8,128)S(1)}, s32[1,32,128]{2,1,0:T(8,128)}, u32[]{:S(2)}) copy-start(s32[1,32,128]{2,1,0:T(8,128)} %param.18) | copy-start | bytes 49156
  154.4 36.0 %copy-start.18 = (s32[1,32]{1,0:T(1,128)S(1)}, s32[1,32]{1,0:T(1,128)}, u32[]{:S(2)}) copy-start(s32[1,32]{1,0:T(1,128)} %param.19) | copy-start | bytes 388
  154.4 74.0 %copy-start.1 = (bf16[1,4,64,1024]{3,2,1,0:T(8,128)(2,1)S(1)}, bf16[1,4,64,1024]{3,2,1,0:T(8,128)(2,1)}, u32[]{:S(2)}) copy-start(bf16[1,4,64,1024]{3,2,1,0:T(8,128)(2,1)} %param.16) | copy-start | bytes 1572868
  177.3 3.8 %collective-permute-start.6 = (bf16[64,1024]{1,0:T(8,128)(2,1)S(1)}, bf16[64,1024]{1,0:T(8,128)(2,1)S(1)}, u32[]{:S(2)}, u32[]{:S(2)}) collective-permute-start(bf16[64,1024]{1,0:T(8,128)(2,1)S(1)} %slice.8), channel_id=1, source_target_pairs={{0,16},{8,24},{1,17},{9,25},{2,18},{10,26},{3,19},{11,27},{4,20},{... | collective-permute-start | bytes 393224 | tf_op jit(solution)/shard_map/ppermute | solution.py:522
  185.5 32.5 %all-to-all-start.1 = ((bf16[32,128,128]{2,1,0:T(8,128)(2,1)}), bf16[32,128,128]{2,1,0:T(8,128)(2,1)S(1)}, u32[]{:S(2)}, u32[]{:S(2)}) async-start(bf16[32,128,128]{2,1,0:T(8,128)(2,1)} %expand.1), calls=%async_computation.1 | async-start | bytes 2097152 | tf_op jit(solution)/shard_map/all_to_all | solution.py:595

commit v3 on v2

--- a/solution.py
+++ b/solution.py
@@ -90,7 +90,7 @@
 
     return pl.pallas_call(
         kernel,
-        out_shape=jax.ShapeDtypeStruct((owners, samples * embed_count, cap), jnp.bfloat16),
+        out_shape=pltpu.HBM((owners, samples * embed_count, cap), jnp.bfloat16),
         grid=(samples // group,),
         in_specs=[
             pl.BlockSpec((group, feature_count), lambda i: (i, 0)),
@@ -242,7 +242,7 @@
 
 
 GROUP = 32
-SMALL_LIMIT = 20 * 1024 * 1024
+STAGE_LIMIT = 44 * 1024 * 1024
 NT = (((1,), (1,)), ((), ()))
 
 
@@ -299,46 +299,105 @@
             normed[rows, columns] = (parts[k] * inv * gain).astype(jnp.bfloat16)
 
 
-def up_product(normed, w_up, layer, hidden, tile=512):
+def hidden_tile(hidden_width):
+    return min(hidden_width, 512)
+
+
+def model_tile(model_width):
+    return min(model_width, 256)
+
+
+def tile_at(step, size):
+    return pl.ds(pl.multiple_of(step * size, size), size)
+
+
+class Stream:
+    def __init__(self, mine, own, other, held, sems, axis, size):
+        self.mine, self.own, self.other, self.held, self.sems = mine, own, other, held, sems
+        self.axis, self.size = axis, size
+        self.tiles = own.shape[axis] // size
+
+    def copy(self, source, step):
+        cut = tile_at(step, self.size)
+        index = (slice(None), cut) if self.axis == 1 else (cut, slice(None))
+        return pltpu.make_async_copy(source.at[index], self.held.at[index], self.sems.at[step])
+
+    def start(self):
+        @pl.when(self.mine)
+        def _():
+            for step in range(self.tiles):
+                self.copy(self.own, step).start()
+
+        @pl.when(jnp.logical_not(self.mine))
+        def _():
+            for step in range(self.tiles):
+                self.copy(self.other, step).start()
+
+    def wait(self, step):
+        self.copy(self.own, step).wait()
+
+
+def no_wait(step):
+    return None
+
+
+def up_product(normed, w_up, hidden, wait):
+    tile = hidden_tile(hidden.shape[1])
+
     def body(step, carry):
-        columns = pl.ds(pl.multiple_of(step * tile, tile), tile)
-        before = dot(normed[...], w_up[layer, :, columns])
+        wait(step)
+        columns = tile_at(step, tile)
+        before = dot(normed[...], w_up[:, columns])
         hidden[:, columns] = jnp.maximum(before, 0.0).astype(jnp.bfloat16)
         return carry
 
     lax.fori_loop(0, hidden.shape[1] // tile, body, 0)
 
 
-def down_product(hidden, w_down, layer, acts, out, tile=256):
+def down_product(hidden, w_down, acts, out, wait):
+    tile = model_tile(out.shape[1])
+
     def body(step, carry):
-        columns = pl.ds(pl.multiple_of(step * tile, tile), tile)
-        term = dot(hidden[...], w_down[layer, :, columns])
+        wait(step)
+        columns = tile_at(step, tile)
+        term = dot(hidden[...], w_down[:, columns])
         out[:, columns] = (acts[:, columns].astype(jnp.float32) + term).astype(jnp.bfloat16)
         return carry
 
     lax.fori_loop(0, out.shape[1] // tile, body, 0)
 
 
-def layer_backward(small, layer, grad, acts, inter, scale, hidden, w_up, w_down, out, g_before, weighted, count):
+def down_back(grad, w_down, hidden, out, wait):
+    tile = hidden_tile(out.shape[1])
+
+    def body(step, carry):
+        wait(step)
+        columns = tile_at(step, tile)
+        g_hidden = dot_nt(grad[...], w_down[columns, :])
+        if hidden is not None:
+            is_open = hidden[:, columns].astype(jnp.float32) > 0.0
+            g_hidden = jnp.where(is_open, g_hidden, 0.0)
+        out[:, columns] = g_hidden.astype(jnp.bfloat16)
+        return carry
+
+    lax.fori_loop(0, out.shape[1] // tile, body, 0)
+
+
+def up_back(g_before, w_up, weighted, wait):
+    tile = model_tile(weighted.shape[1])
+
+    def body(step, carry):
+        wait(step)
+        columns = tile_at(step, tile)
+        weighted[:, columns] = dot_nt(g_before[...], w_up[columns, :])
+        return carry
+
+    lax.fori_loop(0, weighted.shape[1] // tile, body, 0)
+
+
+def mix_backward(small, layer, grad, acts, inter, scale, weighted, out, count):
     batch, model_width = acts.shape
     width = model_width // count
-    tile = 512
-
-    def masked(step, carry):
-        columns = pl.ds(pl.multiple_of(step * tile, tile), tile)
-        g_hidden = dot_nt(grad[...], w_down[layer, columns, :])
-        is_open = hidden[:, columns].astype(jnp.float32) > 0.0
-        g_before[:, columns] = jnp.where(is_open, g_hidden, 0.0).astype(jnp.bfloat16)
-        return carry
-
-    lax.fori_loop(0, hidden.shape[1] // tile, masked, 0)
-
-    def to_normed(step, carry):
-        columns = pl.ds(pl.multiple_of(step * 256, 256), 256)
-        weighted[:, columns] = dot_nt(g_before[...], w_up[layer, columns, :])
-        return carry
-
-    lax.fori_loop(0, model_width // 256, to_normed, 0)
     both = small[layer].astype(jnp.float32)
     proj = repeated(both[:count])
     keep = same_sample(count)
@@ -365,75 +424,46 @@
             out[rows, columns[k]] = piece.astype(jnp.bfloat16)
 
 
-def in_vmem(shape, dtype):
-    return pltpu.VMEM(shape, dtype)
-
-
-def hold_weights(core, pairs):
-    def kernel(core_ref, *refs):
-        own, other = refs[0 : len(pairs)], refs[len(pairs) : 2 * len(pairs)]
-        outs, sems = refs[2 * len(pairs) : 3 * len(pairs)], refs[3 * len(pairs)]
-        here = core_ref[0]
-        copies = []
-        for i in range(len(pairs)):
-            copies.append(pltpu.make_async_copy(own[i], outs[i].at[here], sems.at[2 * i]))
-            copies.append(pltpu.make_async_copy(other[i], outs[i].at[1 - here], sems.at[2 * i + 1]))
-        for copy in copies:
-            copy.start()
-        for copy in copies:
-            copy.wait()
-
-    return pl.pallas_call(
-        kernel,
-        out_shape=[in_vmem((2,) + own.shape, own.dtype) for own, other in pairs],
-        in_specs=[pl.BlockSpec(memory_space=pltpu.SMEM)]
-        + [pl.BlockSpec(memory_space=pl.ANY)] * (2 * len(pairs)),
-        out_specs=[whole() for pair in pairs],
-        scratch_shapes=[pltpu.SemaphoreType.DMA((2 * len(pairs),))],
-        compiler_params=pltpu.CompilerParams(vmem_limit_bytes=SMALL_LIMIT),
-        name="hold_weights",
-    )(core, *[own for own, other in pairs], *[other for own, other in pairs])
-
-
 def saved_shapes(batch, model_width, hidden_width, width):
     return [
-        in_vmem((2, batch, hidden_width), jnp.bfloat16),
-        in_vmem((2, batch, model_width), jnp.float32),
-        in_vmem((2, batch, width), jnp.float32),
-        in_vmem((2, batch, model_width), jnp.bfloat16),
+        jax.ShapeDtypeStruct((2, batch, hidden_width), jnp.bfloat16),
+        jax.ShapeDtypeStruct((2, batch, model_width), jnp.float32),
+        jax.ShapeDtypeStruct((2, batch, width), jnp.float32),
+        jax.ShapeDtypeStruct((2, batch, model_width), jnp.bfloat16),
     ]
 
 
-def forward_stage(active, acts, weights, count):
-    small, w_up, w_down = weights
-    batch, model_width = acts.shape
-    hidden_width = w_up.shape[2]
-    width = model_width // count
-
-    def kernel(active_ref, acts_ref, small_ref, up_ref, down_ref, out_ref, hid, inter, scale, kept, normed):
-        @pl.when(active_ref[0] == 1)
-        def _():
-            kept[0] = acts_ref[...]
-            for layer in (0, 1):
-                mix_forward(
-                    small_ref, layer, kept.at[layer], inter.at[layer], scale.at[layer], normed, count
-                )
-                up_product(normed, up_ref, layer, hid.at[layer])
-                to = kept.at[1] if layer == 0 else out_ref
-                down_product(hid.at[layer], down_ref, layer, kept.at[layer], to)
-
-    out = pl.pallas_call(
-        kernel,
-        out_shape=[jax.ShapeDtypeStruct(acts.shape, jnp.bfloat16)]
-        + saved_shapes(batch, model_width, hidden_width, width),
-        in_specs=[pl.BlockSpec(memory_space=pltpu.SMEM)] + [whole()] * 4,
-        out_specs=[whole()] * 5,
-        scratch_shapes=[pltpu.VMEM((batch, model_width), jnp.bfloat16)],
-        compiler_params=pltpu.CompilerParams(vmem_limit_bytes=SMALL_LIMIT),
-        cost_estimate=stage_cost(4, batch, model_width, hidden_width),
-        name="forward_stage",
-    )(active, acts, small, w_up, w_down)
-    return out[0], out[1:]
+def weight_specs():
+    return [whole()] + [whole(pl.ANY)] * 4
+
+
+def weight_scratch(model_width, hidden_width):
+    tiles = max(hidden_width // hidden_tile(hidden_width), model_width // model_tile(model_width))
+    return [
+        pltpu.VMEM((2, model_width, hidden_width), jnp.bfloat16),
+        pltpu.VMEM((2, hidden_width, model_width), jnp.bfloat16),
+        pltpu.SemaphoreType.DMA((4, tiles)),
+    ]
+
+
+def streams_of(core, weights, held, forward):
+    own_up, other_up, own_down, other_down = weights
+    held_up, held_down, sems = held
+    model_width, hidden_width = own_up.shape
+    wide, narrow = hidden_tile(hidden_width), model_tile(model_width)
+    made = []
+    for layer in (0, 1):
+        mine = core == layer
+        up_forward, down_forward = forward[layer]
+        up_cut = (1, wide) if up_forward else (0, narrow)
+        down_cut = (1, narrow) if down_forward else (0, wide)
+        made.append(
+            (
+                Stream(mine, own_up, other_up, held_up.at[layer], sems.at[2 * layer], *up_cut),
+                Stream(mine, own_down, other_down, held_down.at[layer], sems.at[2 * layer + 1], *down_cut),
+            )
+        )
+    return made
 
 
 def stage_cost(products, batch, model_width, hidden_width):
@@ -442,33 +472,104 @@
     )
 
 
-def turn_stage(active, acts, top, weights, count):
-    small, w_up, w_down = weights
+def stage_params():
+    return pltpu.CompilerParams(vmem_limit_bytes=STAGE_LIMIT)
+
+
+def forward_stage(place, acts, top, weights, count):
     batch, model_width = acts.shape
-    hidden_width = w_up.shape[2]
+    hidden_width = weights[1].shape[1]
     width = model_width // count
 
-    def kernel(active_ref, acts_ref, top_ref, small_ref, up_ref, down_ref, out_ref, hid, inter, scale, upper, grad, normed, weighted, g_before):
-        @pl.when(active_ref[0] == 1)
-        def _():
+    def kernel(place_ref, acts_ref, top_ref, small_ref, *refs):
+        matrices, refs = refs[:4], refs[4:]
+        out_ref, hid, inter, scale, kept, g_hidden = refs[:6]
+        held, normed = refs[6:9], refs[9]
+        core = place_ref[0]
+
+        @pl.when(place_ref[1] == 1)
+        def _():
+            layers = streams_of(core, matrices, held, [(True, True), (True, True)])
+            for up, down in layers:
+                up.start()
+                down.start()
+            kept[0] = acts_ref[...]
+            for layer, (up, down) in enumerate(layers):
+                mix_forward(
+                    small_ref, layer, kept.at[layer], inter.at[layer], scale.at[layer], normed, count
+                )
+                up_product(normed, up.held, hid.at[layer], up.wait)
+                to = kept.at[1] if layer == 0 else out_ref
+                down_product(hid.at[layer], down.held, kept.at[layer], to, down.wait)
+
+        @pl.when(place_ref[2] == 1)
+        def _():
+            layers = streams_of(core, matrices, held, [(True, True), (True, False)])
+            down = layers[1][1]
+            down.start()
+            down_back(top_ref, down.held, None, g_hidden, down.wait)
+
+    out = pl.pallas_call(
+        kernel,
+        out_shape=[jax.ShapeDtypeStruct(acts.shape, jnp.bfloat16)]
+        + saved_shapes(batch, model_width, hidden_width, width)
+        + [jax.ShapeDtypeStruct((batch, hidden_width), jnp.bfloat16)],
+        in_specs=[whole(pltpu.SMEM), whole(), whole()] + weight_specs(),
+        out_specs=[whole()] * 6,
+        scratch_shapes=weight_scratch(model_width, hidden_width)
+        + [pltpu.VMEM((batch, model_width), jnp.bfloat16)],
+        compiler_params=stage_params(),
+        cost_estimate=stage_cost(4, batch, model_width, hidden_width),
+        name="forward_stage",
+    )(place, acts, top, *weights)
+    return out[0], out[1:5], out[5]
+
+
+def turn_stage(place, acts, top, g_hidden, weights, count):
+    batch, model_width = acts.shape
+    hidden_width = weights[1].shape[1]
+    width = model_width // count
+
+    def kernel(place_ref, acts_ref, top_ref, ghid_ref, small_ref, *refs):
+        matrices, refs = refs[:4], refs[4:]
+        out_ref, held = refs[0], refs[1:4]
+        hid, inter, scale, upper, grad, normed, weighted, g_before = refs[4:]
+
+        @pl.when(place_ref[1] == 1)
+        def _():
+            layers = streams_of(place_ref[0], matrices, held, [(True, True), (True, True)])
+            (up0, down0), (up1, down1) = layers
+            for stream in (up0, down0, up1):
+                stream.start()
             mix_forward(small_ref, 0, acts_ref, inter.at[0], scale.at[0], normed, count)
-            up_product(normed, up_ref, 0, hid.at[0])
-            down_product(hid.at[0], down_ref, 0, acts_ref, upper)
+            up_product(normed, up0.held, hid, up0.wait)
+            down_product(hid, down0.held, acts_ref, upper, down0.wait)
             mix_forward(small_ref, 1, upper, inter.at[1], scale.at[1], normed, count)
-            up_product(normed, up_ref, 1, hid.at[1])
-            for layer, given, source, to in ((1, top_ref, upper, grad), (0, grad, acts_ref, out_ref)):
-                layer_backward(
-                    small_ref, layer, given, source, inter.at[layer], scale.at[layer], hid.at[layer],
-                    up_ref, down_ref, to, g_before, weighted, count,
-                )
+            tile = hidden_tile(hidden_width)
+
+            def masked(step, carry):
+                up1.wait(step)
+                columns = tile_at(step, tile)
+                before = dot(normed[...], up1.held[:, columns])
+                g_open = jnp.where(before > 0.0, ghid_ref[:, columns].astype(jnp.float32), 0.0)
+                g_before[:, columns] = g_open.astype(jnp.bfloat16)
+                return carry
+
+            lax.fori_loop(0, hidden_width // tile, masked, 0)
+            up_back(g_before, up1.held, weighted, no_wait)
+            mix_backward(small_ref, 1, top_ref, upper, inter.at[1], scale.at[1], weighted, grad, count)
+            down_back(grad, down0.held, hid, g_before, no_wait)
+            up_back(g_before, up0.held, weighted, no_wait)
+            mix_backward(small_ref, 0, grad, acts_ref, inter.at[0], scale.at[0], weighted, out_ref, count)
 
     return pl.pallas_call(
         kernel,
         out_shape=jax.ShapeDtypeStruct(acts.shape, jnp.bfloat16),
-        in_specs=[pl.BlockSpec(memory_space=pltpu.SMEM)] + [whole()] * 5,
+        in_specs=[whole(pltpu.SMEM)] + [whole()] * 3 + weight_specs(),
         out_specs=whole(),
-        scratch_shapes=[
-            pltpu.VMEM((2, batch, hidden_width), jnp.bfloat16),
+        scratch_shapes=weight_scratch(model_width, hidden_width)
+        + [
+            pltpu.VMEM((batch, hidden_width), jnp.bfloat16),
             pltpu.VMEM((2, batch, model_width), jnp.float32),
             pltpu.VMEM((2, batch, width), jnp.float32),
             pltpu.VMEM((batch, model_width), jnp.bfloat16),
@@ -477,40 +578,51 @@
             pltpu.VMEM((batch, model_width), jnp.float32),
             pltpu.VMEM((batch, hidden_width), jnp.bfloat16),
         ],
-        compiler_params=pltpu.CompilerParams(vmem_limit_bytes=SMALL_LIMIT),
-        cost_estimate=stage_cost(7, batch, model_width, hidden_width),
+        compiler_params=stage_params(),
+        cost_estimate=stage_cost(6, batch, model_width, hidden_width),
         name="turn_stage",
-    )(active, acts, top, small, w_up, w_down)
-
-
-def backward_stage(active, grad, saved, weights, count):
-    small, w_up, w_down = weights
+    )(place, acts, top, g_hidden, *weights)
+
+
+def backward_stage(place, grad, saved, weights, count):
     batch, model_width = grad.shape
-    hidden_width = w_up.shape[2]
-
-    def kernel(active_ref, grad_ref, hid, inter, scale, kept, small_ref, up_ref, down_ref, out_ref, middle, weighted, g_before):
-        @pl.when(active_ref[0] == 1)
-        def _():
+    hidden_width = weights[1].shape[1]
+
+    def kernel(place_ref, grad_ref, hid, inter, scale, kept, small_ref, *refs):
+        matrices, refs = refs[:4], refs[4:]
+        out_ref, held = refs[0], refs[1:4]
+        middle, weighted, g_before = refs[4:]
+
+        @pl.when(place_ref[1] == 1)
+        def _():
+            layers = streams_of(place_ref[0], matrices, held, [(False, False), (False, False)])
+            for up, down in reversed(layers):
+                down.start()
+                up.start()
             for layer, given, to in ((1, grad_ref, middle), (0, middle, out_ref)):
-                layer_backward(
+                up, down = layers[layer]
+                down_back(given, down.held, hid.at[layer], g_before, down.wait)
+                up_back(g_before, up.held, weighted, up.wait)
+                mix_backward(
                     small_ref, layer, given, kept.at[layer], inter.at[layer], scale.at[layer],
-                    hid.at[layer], up_ref, down_ref, to, g_before, weighted, count,
+                    weighted, to, count,
                 )
 
     return pl.pallas_call(
         kernel,
         out_shape=jax.ShapeDtypeStruct(grad.shape, jnp.bfloat16),
-        in_specs=[pl.BlockSpec(memory_space=pltpu.SMEM)] + [whole()] * 8,
+        in_specs=[whole(pltpu.SMEM)] + [whole()] * 5 + weight_specs(),
         out_specs=whole(),
-        scratch_shapes=[
+        scratch_shapes=weight_scratch(model_width, hidden_width)
+        + [
             pltpu.VMEM((batch, model_width), jnp.bfloat16),
             pltpu.VMEM((batch, model_width), jnp.float32),
             pltpu.VMEM((batch, hidden_width), jnp.bfloat16),
         ],
-        compiler_params=pltpu.CompilerParams(vmem_limit_bytes=SMALL_LIMIT),
+        compiler_params=stage_params(),
         cost_estimate=stage_cost(4, batch, model_width, hidden_width),
         name="backward_stage",
-    )(active, grad, *saved, small, w_up, w_down)
+    )(place, grad, *saved, *weights)
 
 
 def swapped(value, section_count):
@@ -560,10 +672,7 @@
     smalls = jnp.stack(
         [jnp.where(core == 0, small, other_small), jnp.where(core == 0, other_small, small)]
     )
-    core_id = core.astype(jnp.int32).reshape(1)
-    weights = [smalls] + list(
-        hold_weights(core_id, [(w_up[0], other_up), (w_down[0], other_down)])
-    )
+    weights = [smalls, w_up[0], other_up, w_down[0], other_down]
     lead = compress(spread, fetched, embed_count)
 
     acts = jnp.concatenate([lead] + [moved(lead, s, 0) for s in range(1, stages)], axis=0)
@@ -571,17 +680,18 @@
     top = lax.dynamic_index_in_dim(top, core, 1, keepdims=False).reshape(-1, model_width)
 
     def at(tick):
-        return (stage == tick).astype(jnp.int32).reshape(1)
+        is_last = (stage == stages - 1) & (tick == 0)
+        return jnp.stack([core, stage == tick, is_last]).astype(jnp.int32)
 
     saved = None
     for tick in range(stages - 1):
-        out, fresh = forward_stage(at(tick), acts, weights, embed_count)
+        out, fresh, product = forward_stage(at(tick), acts, top, weights, embed_count)
         if saved is None:
-            saved = fresh
+            saved, g_hidden = fresh, product
         else:
             saved = [jnp.where(stage == tick, new, old) for new, old in zip(fresh, saved)]
         acts = moved(out, tick, tick + 1)
-    grad = turn_stage(at(stages - 1), acts, top, weights, embed_count)
+    grad = turn_stage(at(stages - 1), acts, top, g_hidden, weights, embed_count)
     for tick in reversed(range(stages - 1)):
         grad = moved(grad, tick + 1, tick)
         grad = backward_stage(at(tick), grad, saved, weights, embed_count)

time: 229 us -> 183 us (0.80)
  local copies, waits for them, and re-layouts: 37.6 us -> 9.15 us
  Pallas kernels: 81 us -> 64.3 us
    unnamed x38 -> x22, local copies, waits for them, and re-layouts: 37.5 us -> 9.12 us
    pallas_call x2 -> x1, Pallas kernels: 16.6 us -> 7.03 us  [spread_weights(): pl.pallas_call(kernel, out_shape=pltpu.HBM((owners, samples * embed_count...]
    pallas_call x1, Pallas kernels: 17.7 us -> 13.1 us  [forward_stage(): pl.pallas_call(kernel, out_shape=[jax.ShapeDtypeStruct(acts.shape, jnp.bf...]
    pallas_call x1, Pallas kernels: 22.8 us -> 19.5 us  [backward_stage(): pl.pallas_call(kernel, out_shape=jax.ShapeDtypeStruct(grad.shape, jnp.bfl...]
  transfers between devices with their start and end apart: 9 -> 9, of which waited for: 6 -> 6; matrix products, arithmetic and copies ran while one was open for 1% -> 1% of each run, Pallas kernels for 7% -> 9%
where the time goes in v3:
time: 183 us; the launch traced here: 182 us
  waiting for transfers between devices  88.5 us (48%)
  Pallas kernels  64.3 us (35%)
  starting transfers between devices  18.2 us (10%)
  local copies, waits for them, and re-layouts  9.15 us (5%)
    ppermute x4, waiting for transfers between devices, moved(): return lax.ppermute(value, 'section', pairs)  43.8 us
    all_to_all x1, waiting for transfers between devices, per_device(): lax.all_to_all(slot_grad, table_axes, split_axis=0, concat_axis=0, tiled=...  27.5 us
    pallas_call x1, Pallas kernels, backward_stage(): pl.pallas_call(kernel, out_shape=jax.ShapeDtypeStruct(grad.shape, jnp.bfl...  19.5 us
    all_to_all x1, waiting for transfers between devices, per_device(): lax.all_to_all(outgoing.reshape(owners, cap, embed_width), table_axes, sp...  17.2 us
    pallas_call x1, Pallas kernels, forward_stage(): pl.pallas_call(kernel, out_shape=[jax.ShapeDtypeStruct(acts.shape, jnp.bf...  13.1 us
    pallas_call x1, Pallas kernels, add_rows(): pl.pallas_call(kernel, out_shape=jax.ShapeDtypeStruct((rows, width), jnp....  10.4 us
    unnamed x22, local copies, waits for them, and re-layouts  9.12 us
    all_to_all x1, starting transfers between devices, per_device(): lax.all_to_all(outgoing.reshape(owners, cap, embed_width), table_axes, sp...  7.28 us
  transfers between devices with their start and end apart: 9, of which 6 were waited for; matrix products, arithmetic and copies ran while one was open for 1% of the time, Pallas kernels for 9%

profile of v3, /device:TPU:0, one launch (start us, length us, event | category | flops | bytes accessed | tf_op | source)
XLA Modules:
  0.0 182.2 jit_solution(8714076448856837005)
XLA Ops:
  0.0 0.5 collective-permute-start.2
  0.5 1.2 copy-done.4
  1.8 0.7 copy-done.5
  2.5 6.4 %pick_rows.1.sent_ref = bf16[4096,128]{1,0:T(8,128)(2,1)} custom-call(s32[4096]{0:T(1024)S(1)} %bitcast.33, bf16[4096,128]{1,0:T(8,128)(2,1)S(1)} %copy-done.4), custom_call_target="tpu_custom_call" | custom-call | tf_op jit(solution)/shard_map/pick_rows/pallas_call | solution.py:48
  8.9 7.3 %all-to-all-start = ((bf16[32,128,128]{2,1,0:T(8,128)(2,1)}), bf16[32,128,128]{2,1,0:T(8,128)(2,1)S(1)}, u32[]{:S(2)}, u32[]{:S(2)}) async-start(bf16[32,128,128]{2,1,0:T(8,128)(2,1)} %bitcast.7), calls=%async_computation | async-start | bytes 2097152 | tf_op jit(solution)/shard_map/all_to_all | solution.py:668
  16.2 0.7 reduce
  16.9 0.7 pad_maximum_fusion.2
  17.6 0.3 collective-permute-start.1
  17.8 0.9 copy-done.7
  18.7 0.7 copy-done.8
  19.4 7.0 %spread_weights.1.spread_ref = bf16[32,512,128]{2,1,0:T(8,128)(2,1)} custom-call(s32[64,512]{1,0:T(8,128)S(1)} %bitcast.34, bf16[8,512]{1,0:T(8,128)(2,1)S(1)} %copy-done.8), custom_call_target="tpu_custom_call" | custom-call | flops 2147483648 | bytes 4194304 | tf_op jit(solution)/shard_map/spread_weights/pallas_call | solution.py:91
  26.5 0.1 pad_add_fusion.place_ref
  26.6 17.2 %all-to-all-done.rows_ref = bf16[32,128,128]{2,1,0:T(8,128)(2,1)S(1)} async-done(((bf16[32,128,128]{2,1,0:T(8,128)(2,1)}), bf16[32,128,128]{2,1,0:T(8,128)(2,1)S(1)}, u32[]{:S(2)}, u32[]{:S(2)}) %all-to-all-start) | async-done | bytes 1048608 | tf_op jit(solution)/shard_map/all_to_all | solution.py:668
  43.8 2.2 %copy-done.2 = bf16[32,512,128]{2,1,0:T(8,128)(2,1)S(1)} copy-done((bf16[32,512,128]{2,1,0:T(8,128)(2,1)S(1)}, bf16[32,512,128]{2,1,0:T(8,128)(2,1)}, u32[]{:S(2)}) %copy-start.2) | copy-done | bytes 4194328
  45.9 2.7 %compress.1 = bf16[64,1024]{1,0:T(8,128)(2,1)S(1)} custom-call(bf16[32,512,128]{2,1,0:T(8,128)(2,1)S(1)} %copy-done.2, bf16[32,128,128]{2,1,0:T(8,128)(2,1)S(1)} %all-to-all-done.rows_ref), custom_call_target="tpu_custom_call" | custom-call | tf_op jit(solution)/shard_map/compress/pallas_call | solution.py:136
  48.6 1.3 collective-permute-start
  50.0 5.6 %collective-permute-done = bf16[64,1024]{1,0:T(8,128)(2,1)S(1)} collective-permute-done((bf16[64,1024]{1,0:T(8,128)(2,1)S(1)}, bf16[64,1024]{1,0:T(8,128)(2,1)S(1)}, u32[]{:S(2)}, u32[]{:S(2)}) %collective-permute-start) | collective-permute-done | bytes 131104 | tf_op jit(solution)/shard_map/ppermute | solution.py:634
  55.6 13.1 %forward_stage.1 = (bf16[128,1024]{1,0:T(8,128)(2,1)S(1)}, bf16[2,128,4096]{2,1,0:T(8,128)(2,1)S(1)}, f32[2,128,1024]{2,1,0:T(8,128)S(1)}, f32[2,128,128]{2,1,0:...) custom-call(s32[3]{0:T(128)S(1)} %pad_add_fusion.place_ref, ...), custom_call_target="tpu_custom_call" | custom-call | flops 4294967296 | bytes 1048576 | tf_op jit(solution)/shard_map/forward_stage/pallas_call | solution.py:512
  68.7 1.3 collective-permute-start.4
  70.0 0.1 pad_add_fusion.1.place_ref
  70.1 5.0 %collective-permute-done.4.acts_ref = bf16[128,1024]{1,0:T(8,128)(2,1)S(1)} collective-permute-done((bf16[128,1024]{1,0:T(8,128)(2,1)S(1)}, bf16[128,1024]{1,0:T(8,128)(2,1)S(1)}, u32[]{:S(2)}, u32[]{:S(2)}) %collective-permute-start.4) | collective-permute-done | bytes 262176 | tf_op jit(solution)/shard_map/ppermute | solution.py:634
  75.1 3.4 %copy-done.1 = bf16[1,1024,4096]{2,1,0:T(8,128)(2,1)S(1)} copy-done((bf16[1,1024,4096]{2,1,0:T(8,128)(2,1)S(1)}, bf16[1,1024,4096]{2,1,0:T(8,128)(2,1)}, u32[]{:S(2)}) %copy-start.1) | copy-done | bytes 8388632
  78.5 0.8 turn_stage.1
  79.3 1.3 collective-permute-start.5
  80.6 30.7 %collective-permute-done.5.grad_ref = bf16[128,1024]{1,0:T(8,128)(2,1)S(1)} collective-permute-done((bf16[128,1024]{1,0:T(8,128)(2,1)S(1)}, bf16[128,1024]{1,0:T(8,128)(2,1)S(1)}, u32[]{:S(2)}, u32[]{:S(2)}) %collective-permute-start.5) | collective-permute-done | bytes 262176 | tf_op jit(solution)/shard_map/ppermute | solution.py:634
  111.4 19.5 %backward_stage.1 = bf16[128,1024]{1,0:T(8,128)(2,1)S(1)} custom-call(s32[3]{0:T(128)S(1)} %pad_add_fusion.place_ref, bf16[128,1024]{1,0:T(8,128)(2,1)S(1)} %collective-permute-done.5.grad_ref, bf16[2,128,4096]{2,1,0:T(8,128)(2,1)S(1)} %get-tuple-element.13.hid, f32[2,128,1024]{2,1,0:T(8,128)S(1)} %get-tuple-element.14.inter, ...), custom_call_target="tpu_custom_call" | custom-call | flops 4294967296 | bytes 1048576 | tf_op jit(solution)/shard_map/backward_stage/pallas_call | solution.py:611
  130.8 1.3 collective-permute-start.6
  132.2 2.5 %collective-permute-done.6 = bf16[64,1024]{1,0:T(8,128)(2,1)S(1)} collective-permute-done((bf16[64,1024]{1,0:T(8,128)(2,1)S(1)}, bf16[64,1024]{1,0:T(8,128)(2,1)S(1)}, u32[]{:S(2)}, u32[]{:S(2)}) %collective-permute-start.6) | collective-permute-done | bytes 131104 | tf_op jit(solution)/shard_map/ppermute | solution.py:634
  134.7 4.3 %expand.1 = bf16[32,128,128]{2,1,0:T(8,128)(2,1)} custom-call(bf16[32,512,128]{2,1,0:T(8,128)(2,1)S(1)} %copy-done.3, bf16[64,1024]{1,0:T(8,128)(2,1)S(1)} %slice_select_fusion.grad_ref), custom_call_target="tpu_custom_call" | custom-call | tf_op jit(solution)/shard_map/expand/pallas_call | solution.py:169
  139.0 5.0 %all-to-all-start.1 = ((bf16[32,128,128]{2,1,0:T(8,128)(2,1)}), bf16[32,128,128]{2,1,0:T(8,128)(2,1)S(1)}, u32[]{:S(2)}, u32[]{:S(2)}) async-start(bf16[32,128,128]{2,1,0:T(8,128)(2,1)} %expand.1), calls=%async_computation.1 | async-start | bytes 2097152 | tf_op jit(solution)/shard_map/all_to_all | solution.py:705
  144.1 27.5 %all-to-all-done.1 = bf16[32,128,128]{2,1,0:T(8,128)(2,1)S(1)} async-done(((bf16[32,128,128]{2,1,0:T(8,128)(2,1)}), bf16[32,128,128]{2,1,0:T(8,128)(2,1)S(1)}, u32[]{:S(2)}, u32[]{:S(2)}) %all-to-all-start.1) | async-done | bytes 1048608 | tf_op jit(solution)/shard_map/all_to_all | solution.py:705
  171.6 10.4 %add_rows.1 = f32[4096,128]{1,0:T(8,128)} custom-call(s32[4096]{0:T(1024)S(1)} %fusion.1.targets_ref, bf16[4096,128]{1,0:T(8,128)(2,1)S(1)} %bitcast.30, bf16[4096,128]{1,0:T(8,128)(2,1)} %pick_rows.1.sent_ref), custom_call_target="tpu_custom_call" | custom-call | tf_op jit(solution)/shard_map/add_rows/pallas_call | solution.py:222
  (27 shorter events, 0.3 us)
Async XLA Ops:
  0.0 17.8 %copy-start = (bf16[1,4,64,1024]{3,2,1,0:T(8,128)(2,1)S(1)}, bf16[1,4,64,1024]{3,2,1,0:T(8,128)(2,1)}, u32[]{:S(2)}) copy-start(bf16[1,4,64,1024]{3,2,1,0:T(8,128)(2,1)} %param.16) | copy-start | bytes 1572868
  0.0 55.6 %collective-permute-start.2 = (bf16[1024,4096]{1,0:T(8,128)(2,1)}, bf16[1024,4096]{1,0:T(8,128)(2,1)}, u32[]{:S(2)}, u32[]{:S(2)}) collective-permute-start(bf16[1024,4096]{1,0:T(8,128)(2,1)} %bitcast.26), channel_id=1, source_target_pairs={{0,8},{8,0},{16,24},{24,16},{1,9},{9,1},{17,25},{25,17},{2,10},{10... | collective-permute-start | bytes 25165832 | tf_op jit(solution)/shard_map/ppermute | solution.py:629
  0.5 55.2 %collective-permute-start.3 = (bf16[4096,1024]{1,0:T(8,128)(2,1)}, bf16[4096,1024]{1,0:T(8,128)(2,1)}, u32[]{:S(2)}, u32[]{:S(2)}) collective-permute-start(bf16[4096,1024]{1,0:T(8,128)(2,1)} %bitcast.35), channel_id=1, source_target_pairs={{0,8},{8,0},{16,24},{24,16},{1,9},{9,1},{17,25},{25,17},{2,10},{10... | collective-permute-start | bytes 25165832 | tf_op jit(solution)/shard_map/ppermute | solution.py:629
  0.5 1.2 copy-start.4
  1.8 0.7 copy-start.5
  8.9 41.1 %copy-start.9 = (bf16[1,8,128]{2,1,0:T(8,128)(2,1)S(1)}, bf16[1,8,128]{2,1,0:T(8,128)(2,1)}, u32[]{:S(2)}) copy-start(bf16[1,8,128]{2,1,0:T(8,128)(2,1)} %param.12) | copy-start | bytes 6148
  8.9 34.9 %all-to-all-start = ((bf16[32,128,128]{2,1,0:T(8,128)(2,1)}), bf16[32,128,128]{2,1,0:T(8,128)(2,1)S(1)}, u32[]{:S(2)}, u32[]{:S(2)}) async-start(bf16[32,128,128]{2,1,0:T(8,128)(2,1)} %bitcast.7), calls=%async_computation | async-start | bytes 2097152 | tf_op jit(solution)/shard_map/all_to_all | solution.py:668
  17.6 32.4 %collective-permute-start.1 = (bf16[16,128]{1,0:T(8,128)(2,1)S(1)}, bf16[16,128]{1,0:T(8,128)(2,1)S(1)}, u32[]{:S(2)}, u32[]{:S(2)}) collective-permute-start(bf16[16,128]{1,0:T(8,128)(2,1)S(1)} %pad_maximum_fusion.2), channel_id=1, source_target_pairs={{0,8},{8,0},{16,24},{24,16},{1,9},{9,1},{17,25},{25,17},{2,10},{10... | collective-permute-start | bytes 12296 | tf_op jit(solution)/shard_map/ppermute | solution.py:629
  17.8 0.9 copy-start.7
  18.7 0.7 copy-start.8
  43.8 2.2 %copy-start.2 = (bf16[32,512,128]{2,1,0:T(8,128)(2,1)S(1)}, bf16[32,512,128]{2,1,0:T(8,128)(2,1)}, u32[]{:S(2)}) copy-start(bf16[32,512,128]{2,1,0:T(8,128)(2,1)} %spread_weights.1.spread_ref) | copy-start | bytes 12582916
  48.6 7.0 %collective-permute-start = (bf16[64,1024]{1,0:T(8,128)(2,1)S(1)}, bf16[64,1024]{1,0:T(8,128)(2,1)S(1)}, u32[]{:S(2)}, u32[]{:S(2)}) collective-permute-start(bf16[64,1024]{1,0:T(8,128)(2,1)S(1)} %compress.1), channel_id=1, source_target_pairs={{16,0},{24,8},{17,1},{25,9},{18,2},{26,10},{19,3},{27,11},{20,4},{... | collective-permute-start | bytes 393224 | tf_op jit(solution)/shard_map/ppermute | solution.py:634
  68.7 6.4 %collective-permute-start.4 = (bf16[128,1024]{1,0:T(8,128)(2,1)S(1)}, bf16[128,1024]{1,0:T(8,128)(2,1)S(1)}, u32[]{:S(2)}, u32[]{:S(2)}) collective-permute-start(bf16[128,1024]{1,0:T(8,128)(2,1)S(1)} %get-tuple-element.11), channel_id=1, source_target_pairs={{0,16},{8,24},{1,17},{9,25},{2,18},{10,26},{3,19},{11,27},{4,20},{... | collective-permute-start | bytes 786440 | tf_op jit(solution)/shard_map/ppermute | solution.py:634
  75.1 3.4 %copy-start.1 = (bf16[1,1024,4096]{2,1,0:T(8,128)(2,1)S(1)}, bf16[1,1024,4096]{2,1,0:T(8,128)(2,1)}, u32[]{:S(2)}) copy-start(bf16[1,1024,4096]{2,1,0:T(8,128)(2,1)} %param.14) | copy-start | bytes 25165828
  79.3 32.0 %collective-permute-start.5 = (bf16[128,1024]{1,0:T(8,128)(2,1)S(1)}, bf16[128,1024]{1,0:T(8,128)(2,1)S(1)}, u32[]{:S(2)}, u32[]{:S(2)}) collective-permute-start(bf16[128,1024]{1,0:T(8,128)(2,1)S(1)} %turn_stage.1), channel_id=1, source_target_pairs={{16,0},{24,8},{17,1},{25,9},{18,2},{26,10},{19,3},{27,11},{20,4},{... | collective-permute-start | bytes 786440 | tf_op jit(solution)/shard_map/ppermute | solution.py:634
  111.4 23.3 %copy-start.3 = (bf16[32,512,128]{2,1,0:T(8,128)(2,1)S(1)}, bf16[32,512,128]{2,1,0:T(8,128)(2,1)}, u32[]{:S(2)}) copy-start(bf16[32,512,128]{2,1,0:T(8,128)(2,1)} %spread_weights.1.spread_ref) | copy-start | bytes 12582916
  111.4 32.6 %copy-start.6 = (s32[1,32,128]{2,1,0:T(8,128)S(1)}, s32[1,32,128]{2,1,0:T(8,128)}, u32[]{:S(2)}) copy-start(s32[1,32,128]{2,1,0:T(8,128)} %param.18) | copy-start | bytes 49156
  111.4 32.7 %copy-start.10 = (s32[1,32]{1,0:T(1,128)S(1)}, s32[1,32]{1,0:T(1,128)}, u32[]{:S(2)}) copy-start(s32[1,32]{1,0:T(1,128)} %param.19) | copy-start | bytes 388
  130.8 3.8 %collective-permute-start.6 = (bf16[64,1024]{1,0:T(8,128)(2,1)S(1)}, bf16[64,1024]{1,0:T(8,128)(2,1)S(1)}, u32[]{:S(2)}, u32[]{:S(2)}) collective-permute-start(bf16[64,1024]{1,0:T(8,128)(2,1)S(1)} %slice.8), channel_id=1, source_target_pairs={{0,16},{8,24},{1,17},{9,25},{2,18},{10,26},{3,19},{11,27},{4,20},{... | collective-permute-start | bytes 393224 | tf_op jit(solution)/shard_map/ppermute | solution.py:634
  139.0 32.6 %all-to-all-start.1 = ((bf16[32,128,128]{2,1,0:T(8,128)(2,1)}), bf16[32,128,128]{2,1,0:T(8,128)(2,1)S(1)}, u32[]{:S(2)}, u32[]{:S(2)}) async-start(bf16[32,128,128]{2,1,0:T(8,128)(2,1)} %expand.1), calls=%async_computation.1 | async-start | bytes 2097152 | tf_op jit(solution)/shard_map/all_to_all | solution.py:705

commit v4 on v3

--- a/solution.py
+++ b/solution.py
@@ -7,8 +7,8 @@
 
 EPSILON = 1e-05
 DECAY_WEIGHT = 0.5
-VMEM_LIMIT = 20 * 1024 * 1024
-UNROLL = 16
+VMEM_LIMIT = 28 * 1024 * 1024
+UNROLL = 32
 
 
 def whole(memory_space=pltpu.VMEM):
@@ -29,35 +29,33 @@
     chunk = min(count, 1024)
 
     def kernel(picked_ref, table_ref, out_ref, wide, lines):
-        step = pl.program_id(0)
-
-        @pl.when(step == 0)
-        def _():
-            wide[...] = table_ref[...].astype(jnp.float32)
-
-        def body(group, carry):
-            first = pl.multiple_of(group * UNROLL, UNROLL)
-            for lane in range(UNROLL):
-                row = picked_ref[step * chunk + first + lane]
-                lines[pl.ds(first + lane, 1), :] = wide[pl.ds(row, 1), :]
+        wide[...] = table_ref[...].astype(jnp.float32)
+
+        def fill(part, carry):
+            base = pl.multiple_of(part * chunk, chunk)
+
+            def body(group, inner):
+                first = pl.multiple_of(group * UNROLL, UNROLL)
+                for lane in range(UNROLL):
+                    row = picked_ref[base + first + lane]
+                    lines[pl.ds(first + lane, 1), :] = wide[pl.ds(row, 1), :]
+                return inner
+
+            lax.fori_loop(0, chunk // UNROLL, body, 0)
+            out_ref[pl.ds(base, chunk), :] = lines[...].astype(out_ref.dtype)
             return carry
 
-        lax.fori_loop(0, chunk // UNROLL, body, 0)
-        out_ref[...] = lines[...].astype(out_ref.dtype)
+        lax.fori_loop(0, count // chunk, fill, 0)
 
     return pl.pallas_call(
         kernel,
         out_shape=jax.ShapeDtypeStruct((count, width), emb_table.dtype),
-        grid_spec=pltpu.PrefetchScalarGridSpec(
-            num_scalar_prefetch=1,
-            grid=(count // chunk,),
-            in_specs=[pl.BlockSpec((rows, width), lambda i, ids: (0, 0))],
-            out_specs=pl.BlockSpec((chunk, width), lambda i, ids: (i, 0)),
-            scratch_shapes=[
-                pltpu.VMEM((rows, width), jnp.float32),
-                pltpu.VMEM((chunk, width), jnp.float32),
-            ],
-        ),
+        in_specs=[whole(pltpu.SMEM), whole()],
+        out_specs=whole(),
+        scratch_shapes=[
+            pltpu.VMEM((rows, width), jnp.float32),
+            pltpu.VMEM((chunk, width), jnp.float32),
+        ],
         compiler_params=params(),
         name="pick_rows",
     )(picked, emb_table)
@@ -112,37 +110,40 @@
     width = fetched.shape[2]
     samples = lines // embed_count
     part = tiles_of(owners, 4)
-
-    def kernel(spread_ref, rows_ref, out_ref, total):
-        step = pl.program_id(0)
-        left = jnp.concatenate([spread_ref[o] for o in range(part)], axis=1)
-        right = rows_ref[...].reshape(part * cap, width)
-        term = jnp.dot(left, right, preferred_element_type=jnp.float32)
-
-        @pl.when(step == 0)
-        def _():
-            total[...] = term
-
-        @pl.when(step > 0)
-        def _():
-            total[...] += term
-
-        @pl.when(step == owners // part - 1)
-        def _():
-            for k in range(embed_count):
-                piece = total[pl.ds(k, samples, stride=embed_count), :]
-                out_ref[:, k * width : (k + 1) * width] = piece.astype(out_ref.dtype)
+    steps = owners // part
+
+    def kernel(spread_ref, rows_ref, out_ref, held, total, sems):
+        def copy(step):
+            piece = tile_at(step, part)
+            return pltpu.make_async_copy(spread_ref.at[piece], held.at[piece], sems.at[step])
+
+        for step in range(steps):
+            copy(step).start()
+        total[...] = jnp.zeros_like(total)
+
+        def body(step, carry):
+            copy(step).wait()
+            first = step * part
+            left = jnp.concatenate([held[first + o] for o in range(part)], axis=1)
+            right = rows_ref[tile_at(step, part)].reshape(part * cap, width)
+            total[...] += jnp.dot(left, right, preferred_element_type=jnp.float32)
+            return carry
+
+        lax.fori_loop(0, steps, body, 0)
+        for k in range(embed_count):
+            piece = total[pl.ds(k, samples, stride=embed_count), :]
+            out_ref[:, k * width : (k + 1) * width] = piece.astype(out_ref.dtype)
 
     return pl.pallas_call(
         kernel,
         out_shape=jax.ShapeDtypeStruct((samples, embed_count * width), jnp.bfloat16),
-        grid=(owners // part,),
-        in_specs=[
-            pl.BlockSpec((part, lines, cap), lambda i: (i, 0, 0)),
-            pl.BlockSpec((part, cap, width), lambda i: (i, 0, 0)),
+        in_specs=[whole(pltpu.HBM), whole()],
+        out_specs=whole(),
+        scratch_shapes=[
+            pltpu.VMEM(spread.shape, jnp.bfloat16),
+            pltpu.VMEM((lines, width), jnp.float32),
+            pltpu.SemaphoreType.DMA((steps,)),
         ],
-        out_specs=pl.BlockSpec((samples, embed_count * width), lambda i: (0, 0)),
-        scratch_shapes=[pltpu.VMEM((lines, width), jnp.float32)],
         compiler_params=params(),
         name="compress",
     )(spread, fetched)
@@ -155,26 +156,26 @@
     part = tiles_of(owners, 4)
 
     def kernel(spread_ref, grad_ref, out_ref, tall, turned):
-        @pl.when(pl.program_id(0) == 0)
-        def _():
-            for k in range(embed_count):
-                piece = grad_ref[:, k * width : (k + 1) * width].astype(jnp.float32)
-                tall[pl.ds(k, samples, stride=embed_count), :] = piece
-            turned[...] = tall[...].T.astype(jnp.bfloat16)
-
-        right = jnp.concatenate([spread_ref[o] for o in range(part)], axis=1)
-        term = jnp.dot(turned[...], right, preferred_element_type=jnp.float32)
-        out_ref[...] = term.T.astype(out_ref.dtype).reshape(part, cap, width)
+        for k in range(embed_count):
+            piece = grad_ref[:, k * width : (k + 1) * width].astype(jnp.float32)
+            tall[pl.ds(k, samples, stride=embed_count), :] = piece
+        turned[...] = tall[...].T.astype(jnp.bfloat16)
+
+        def body(step, carry):
+            first = step * part
+            right = jnp.concatenate([spread_ref[first + o] for o in range(part)], axis=1)
+            term = jnp.dot(turned[...], right, preferred_element_type=jnp.float32)
+            piece = term.T.astype(out_ref.dtype).reshape(part, cap, width)
+            out_ref[tile_at(step, part)] = piece
+            return carry
+
+        lax.fori_loop(0, owners // part, body, 0)
 
     return pl.pallas_call(
         kernel,
         out_shape=jax.ShapeDtypeStruct((owners, cap, width), jnp.bfloat16),
-        grid=(owners // part,),
-        in_specs=[
-            pl.BlockSpec((part, lines, cap), lambda i: (i, 0, 0)),
-            pl.BlockSpec(lead_share.shape, lambda i: (0, 0)),
-        ],
-        out_specs=pl.BlockSpec((part, cap, width), lambda i: (i, 0, 0)),
+        in_specs=[whole(), whole()],
+        out_specs=whole(),
         scratch_shapes=[
             pltpu.VMEM((lines, width), jnp.float32),
             pltpu.VMEM((width, lines), jnp.bfloat16),
@@ -187,55 +188,46 @@
 def add_rows(targets, returned, outgoing, rows):
     count, width = returned.shape
     chunk = min(count, 1024)
-    steps = count // chunk
 
     def kernel(targets_ref, back_ref, sent_ref, out_ref, total, terms, done):
-        step = pl.program_id(0)
-
-        @pl.when(step == 0)
-        def _():
-            total[...] = jnp.zeros_like(total)
-
-        terms[...] = back_ref[...].astype(jnp.float32) + DECAY_WEIGHT * sent_ref[...].astype(
-            jnp.float32
-        )
-
-        def body(group, carry):
-            first = pl.multiple_of(group * UNROLL, UNROLL)
-            places = [targets_ref[step * chunk + first + lane] for lane in range(UNROLL)]
-            sums = [
-                total[pl.ds(places[lane], 1), :] + terms[pl.ds(first + lane, 1), :]
-                for lane in range(UNROLL)
-            ]
-            for lane in range(UNROLL):
-                total[pl.ds(places[lane], 1), :] = sums[lane]
+        total[...] = jnp.zeros_like(total)
+
+        def fill(part, carry):
+            base = pl.multiple_of(part * chunk, chunk)
+            lines = pl.ds(base, chunk)
+            terms[...] = back_ref[lines, :].astype(jnp.float32) + DECAY_WEIGHT * sent_ref[
+                lines, :
+            ].astype(jnp.float32)
+
+            def body(group, inner):
+                first = pl.multiple_of(group * UNROLL, UNROLL)
+                places = [targets_ref[base + first + lane] for lane in range(UNROLL)]
+                sums = [
+                    total[pl.ds(places[lane], 1), :] + terms[pl.ds(first + lane, 1), :]
+                    for lane in range(UNROLL)
+                ]
+                for lane in range(UNROLL):
+                    total[pl.ds(places[lane], 1), :] = sums[lane]
+                return inner
+
+            lax.fori_loop(0, chunk // UNROLL, body, 0)
             return carry
 
-        lax.fori_loop(0, chunk // UNROLL, body, 0)
-
-        @pl.when(step == steps - 1)
-        def _():
-            copy = pltpu.make_async_copy(total.at[pl.ds(0, rows), :], out_ref, done)
-            copy.start()
-            copy.wait()
+        lax.fori_loop(0, count // chunk, fill, 0)
+        copy = pltpu.make_async_copy(total.at[pl.ds(0, rows), :], out_ref, done)
+        copy.start()
+        copy.wait()
 
     return pl.pallas_call(
         kernel,
         out_shape=jax.ShapeDtypeStruct((rows, width), jnp.float32),
-        grid_spec=pltpu.PrefetchScalarGridSpec(
-            num_scalar_prefetch=1,
-            grid=(steps,),
-            in_specs=[
-                pl.BlockSpec((chunk, width), lambda i, ids: (i, 0)),
-                pl.BlockSpec((chunk, width), lambda i, ids: (i, 0)),
-            ],
-            out_specs=pl.BlockSpec(memory_space=pl.ANY),
-            scratch_shapes=[
-                pltpu.VMEM((rows + 8, width), jnp.float32),
-                pltpu.VMEM((chunk, width), jnp.float32),
-                pltpu.SemaphoreType.DMA,
-            ],
-        ),
+        in_specs=[whole(pltpu.SMEM), whole(), whole()],
+        out_specs=whole(pl.ANY),
+        scratch_shapes=[
+            pltpu.VMEM((rows + 8, width), jnp.float32),
+            pltpu.VMEM((chunk, width), jnp.float32),
+            pltpu.SemaphoreType.DMA,
+        ],
         compiler_params=params(),
         name="add_rows",
     )(targets, returned, outgoing)
@@ -341,14 +333,16 @@
     return None
 
 
-def up_product(normed, w_up, hidden, wait):
+def up_product(normed, w_up, hidden, turned, wait):
     tile = hidden_tile(hidden.shape[1])
 
     def body(step, carry):
         wait(step)
         columns = tile_at(step, tile)
         before = dot(normed[...], w_up[:, columns])
-        hidden[:, columns] = jnp.maximum(before, 0.0).astype(jnp.bfloat16)
+        opened = jnp.maximum(before, 0.0)
+        hidden[:, columns] = opened.astype(jnp.bfloat16)
+        turned[columns, :] = opened.T.astype(jnp.bfloat16)
         return carry
 
     lax.fori_loop(0, hidden.shape[1] // tile, body, 0)
@@ -367,29 +361,37 @@
     lax.fori_loop(0, out.shape[1] // tile, body, 0)
 
 
+def turn(rows, turned):
+    turned[...] = rows[...].astype(jnp.float32).T.astype(jnp.bfloat16)
+
+
+def opened_only(hidden, grad):
+    return jnp.where(hidden.astype(jnp.float32) > 0.0, grad, 0.0).astype(jnp.bfloat16)
+
+
 def down_back(grad, w_down, hidden, out, wait):
-    tile = hidden_tile(out.shape[1])
+    tile = hidden_tile(out.shape[0])
+
+    def body(step, carry):
+        wait(step)
+        lines = tile_at(step, tile)
+        g_hidden = dot(w_down[lines, :], grad[...])
+        if hidden is not None:
+            out[lines, :] = opened_only(hidden[lines, :], g_hidden)
+        else:
+            out[lines, :] = g_hidden.astype(jnp.bfloat16)
+        return carry
+
+    lax.fori_loop(0, out.shape[0] // tile, body, 0)
+
+
+def up_back(g_before, w_up, weighted, wait):
+    tile = model_tile(weighted.shape[1])
 
     def body(step, carry):
         wait(step)
         columns = tile_at(step, tile)
-        g_hidden = dot_nt(grad[...], w_down[columns, :])
-        if hidden is not None:
-            is_open = hidden[:, columns].astype(jnp.float32) > 0.0
-            g_hidden = jnp.where(is_open, g_hidden, 0.0)
-        out[:, columns] = g_hidden.astype(jnp.bfloat16)
-        return carry
-
-    lax.fori_loop(0, out.shape[1] // tile, body, 0)
-
-
-def up_back(g_before, w_up, weighted, wait):
-    tile = model_tile(weighted.shape[1])
-
-    def body(step, carry):
-        wait(step)
-        columns = tile_at(step, tile)
-        weighted[:, columns] = dot_nt(g_before[...], w_up[columns, :])
+        weighted[:, columns] = dot(w_up[columns, :], g_before[...]).T
         return carry
 
     lax.fori_loop(0, weighted.shape[1] // tile, body, 0)
@@ -426,7 +428,7 @@
 
 def saved_shapes(batch, model_width, hidden_width, width):
     return [
-        jax.ShapeDtypeStruct((2, batch, hidden_width), jnp.bfloat16),
+        jax.ShapeDtypeStruct((2, hidden_width, batch), jnp.bfloat16),
         jax.ShapeDtypeStruct((2, batch, model_width), jnp.float32),
         jax.ShapeDtypeStruct((2, batch, width), jnp.float32),
         jax.ShapeDtypeStruct((2, batch, model_width), jnp.bfloat16),
@@ -434,7 +436,7 @@
 
 
 def weight_specs():
-    return [whole()] + [whole(pl.ANY)] * 4
+    return [whole()] + [whole(pltpu.HBM)] * 4
 
 
 def weight_scratch(model_width, hidden_width):
@@ -484,7 +486,7 @@
     def kernel(place_ref, acts_ref, top_ref, small_ref, *refs):
         matrices, refs = refs[:4], refs[4:]
         out_ref, hid, inter, scale, kept, g_hidden = refs[:6]
-        held, normed = refs[6:9], refs[9]
+        held, (normed, hidden, top_turned) = refs[6:9], refs[9:]
         core = place_ref[0]
 
         @pl.when(place_ref[1] == 1)
@@ -498,26 +500,31 @@
                 mix_forward(
                     small_ref, layer, kept.at[layer], inter.at[layer], scale.at[layer], normed, count
                 )
-                up_product(normed, up.held, hid.at[layer], up.wait)
+                up_product(normed, up.held, hidden, hid.at[layer], up.wait)
                 to = kept.at[1] if layer == 0 else out_ref
-                down_product(hid.at[layer], down.held, kept.at[layer], to, down.wait)
+                down_product(hidden, down.held, kept.at[layer], to, down.wait)
 
         @pl.when(place_ref[2] == 1)
         def _():
             layers = streams_of(core, matrices, held, [(True, True), (True, False)])
             down = layers[1][1]
             down.start()
-            down_back(top_ref, down.held, None, g_hidden, down.wait)
+            turn(top_ref, top_turned)
+            down_back(top_turned, down.held, None, g_hidden, down.wait)
 
     out = pl.pallas_call(
         kernel,
         out_shape=[jax.ShapeDtypeStruct(acts.shape, jnp.bfloat16)]
         + saved_shapes(batch, model_width, hidden_width, width)
-        + [jax.ShapeDtypeStruct((batch, hidden_width), jnp.bfloat16)],
+        + [jax.ShapeDtypeStruct((hidden_width, batch), jnp.bfloat16)],
         in_specs=[whole(pltpu.SMEM), whole(), whole()] + weight_specs(),
         out_specs=[whole()] * 6,
         scratch_shapes=weight_scratch(model_width, hidden_width)
-        + [pltpu.VMEM((batch, model_width), jnp.bfloat16)],
+        + [
+            pltpu.VMEM((batch, model_width), jnp.bfloat16),
+            pltpu.VMEM((batch, hidden_width), jnp.bfloat16),
+            pltpu.VMEM((model_width, batch), jnp.bfloat16),
+        ],
         compiler_params=stage_params(),
         cost_estimate=stage_cost(4, batch, model_width, hidden_width),
         name="forward_stage",
@@ -533,7 +540,7 @@
     def kernel(place_ref, acts_ref, top_ref, ghid_ref, small_ref, *refs):
         matrices, refs = refs[:4], refs[4:]
         out_ref, held = refs[0], refs[1:4]
-        hid, inter, scale, upper, grad, normed, weighted, g_before = refs[4:]
+        hid, hidden, inter, scale, upper, grad, turned, normed, weighted, g_before = refs[4:]
 
         @pl.when(place_ref[1] == 1)
         def _():
@@ -542,8 +549,8 @@
             for stream in (up0, down0, up1):
                 stream.start()
             mix_forward(small_ref, 0, acts_ref, inter.at[0], scale.at[0], normed, count)
-            up_product(normed, up0.held, hid, up0.wait)
-            down_product(hid, down0.held, acts_ref, upper, down0.wait)
+            up_product(normed, up0.held, hidden, hid, up0.wait)
+            down_product(hidden, down0.held, acts_ref, upper, down0.wait)
             mix_forward(small_ref, 1, upper, inter.at[1], scale.at[1], normed, count)
             tile = hidden_tile(hidden_width)
 
@@ -551,14 +558,15 @@
                 up1.wait(step)
                 columns = tile_at(step, tile)
                 before = dot(normed[...], up1.held[:, columns])
-                g_open = jnp.where(before > 0.0, ghid_ref[:, columns].astype(jnp.float32), 0.0)
-                g_before[:, columns] = g_open.astype(jnp.bfloat16)
+                opened = jnp.maximum(before, 0.0).T
+                g_before[columns, :] = opened_only(opened, ghid_ref[columns, :].astype(jnp.float32))
                 return carry
 
             lax.fori_loop(0, hidden_width // tile, masked, 0)
             up_back(g_before, up1.held, weighted, no_wait)
             mix_backward(small_ref, 1, top_ref, upper, inter.at[1], scale.at[1], weighted, grad, count)
-            down_back(grad, down0.held, hid, g_before, no_wait)
+            turn(grad, turned)
+            down_back(turned, down0.held, hid, g_before, no_wait)
             up_back(g_before, up0.held, weighted, no_wait)
             mix_backward(small_ref, 0, grad, acts_ref, inter.at[0], scale.at[0], weighted, out_ref, count)
 
@@ -569,14 +577,16 @@
         out_specs=whole(),
         scratch_shapes=weight_scratch(model_width, hidden_width)
         + [
+            pltpu.VMEM((hidden_width, batch), jnp.bfloat16),
             pltpu.VMEM((batch, hidden_width), jnp.bfloat16),
             pltpu.VMEM((2, batch, model_width), jnp.float32),
             pltpu.VMEM((2, batch, width), jnp.float32),
             pltpu.VMEM((batch, model_width), jnp.bfloat16),
             pltpu.VMEM((batch, model_width), jnp.bfloat16),
+            pltpu.VMEM((model_width, batch), jnp.bfloat16),
             pltpu.VMEM((batch, model_width), jnp.bfloat16),
             pltpu.VMEM((batch, model_width), jnp.float32),
-            pltpu.VMEM((batch, hidden_width), jnp.bfloat16),
+            pltpu.VMEM((hidden_width, batch), jnp.bfloat16),
         ],
         compiler_params=stage_params(),
         cost_estimate=stage_cost(6, batch, model_width, hidden_width),
@@ -591,7 +601,7 @@
     def kernel(place_ref, grad_ref, hid, inter, scale, kept, small_ref, *refs):
         matrices, refs = refs[:4], refs[4:]
         out_ref, held = refs[0], refs[1:4]
-        middle, weighted, g_before = refs[4:]
+        middle, turned, weighted, g_before = refs[4:]
 
         @pl.when(place_ref[1] == 1)
         def _():
@@ -601,7 +611,8 @@
                 up.start()
             for layer, given, to in ((1, grad_ref, middle), (0, middle, out_ref)):
                 up, down = layers[layer]
-                down_back(given, down.held, hid.at[layer], g_before, down.wait)
+                turn(given, turned)
+                down_back(turned, down.held, hid.at[layer], g_before, down.wait)
                 up_back(g_before, up.held, weighted, up.wait)
                 mix_backward(
                     small_ref, layer, given, kept.at[layer], inter.at[layer], scale.at[layer],
@@ -616,8 +627,9 @@
         scratch_shapes=weight_scratch(model_width, hidden_width)
         + [
             pltpu.VMEM((batch, model_width), jnp.bfloat16),
+            pltpu.VMEM((model_width, batch), jnp.bfloat16),
             pltpu.VMEM((batch, model_width), jnp.float32),
-            pltpu.VMEM((batch, hidden_width), jnp.bfloat16),
+            pltpu.VMEM((hidden_width, batch), jnp.bfloat16),
         ],
         compiler_params=stage_params(),
         cost_estimate=stage_cost(4, batch, model_width, hidden_width),

time: 183 us -> 182 us (level)
  no operation moved by 1% of the time
where the time goes in v4:
time: 182 us
  waiting for transfers between devices  89.3 us (49%)
  Pallas kernels  62.8 us (35%)
  starting transfers between devices  18.2 us (10%)
  local copies, waits for them, and re-layouts  9.15 us (5%)
    ppermute x4, waiting for transfers between devices, moved(): return lax.ppermute(value, 'section', pairs)  44.6 us
    all_to_all x1, waiting for transfers between devices, per_device(): lax.all_to_all(slot_grad, table_axes, split_axis=0, concat_axis=0, tiled=...  27.5 us
    pallas_call x1, Pallas kernels, backward_stage(): pl.pallas_call(kernel, out_shape=jax.ShapeDtypeStruct(grad.shape, jnp.bfl...  18 us
    all_to_all x1, waiting for transfers between devices, per_device(): lax.all_to_all(outgoing.reshape(owners, cap, embed_width), table_axes, sp...  17.2 us
    pallas_call x1, Pallas kernels, forward_stage(): pl.pallas_call(kernel, out_shape=[jax.ShapeDtypeStruct(acts.shape, jnp.bf...  13.7 us
    pallas_call x1, Pallas kernels, add_rows(): pl.pallas_call(kernel, out_shape=jax.ShapeDtypeStruct((rows, width), jnp....  10.8 us
    unnamed x22, local copies, waits for them, and re-layouts  9.12 us
    all_to_all x1, starting transfers between devices, per_device(): lax.all_to_all(outgoing.reshape(owners, cap, embed_width), table_axes, sp...  7.28 us
  transfers between devices with their start and end apart: 9, of which 6 were waited for; matrix products, arithmetic and copies ran while one was open for 1% of the time, Pallas kernels for 9%

profile of v4, /device:TPU:0, one launch (start us, length us, event | category | flops | bytes accessed | tf_op | source)
XLA Modules:
  0.0 181.5 jit_solution(17007289191162683856)
XLA Ops:
  0.0 0.5 collective-permute-start.2
  0.5 1.2 copy-done.4
  1.8 0.7 copy-done.5
  2.5 5.8 %pick_rows.1.sent_ref = bf16[4096,128]{1,0:T(8,128)(2,1)} custom-call(s32[4096]{0:T(1024)S(1)} %bitcast.33, bf16[4096,128]{1,0:T(8,128)(2,1)S(1)} %copy-done.4), custom_call_target="tpu_custom_call" | custom-call | tf_op jit(solution)/shard_map/pick_rows/pallas_call | solution.py:50
  8.3 7.3 %all-to-all-start = ((bf16[32,128,128]{2,1,0:T(8,128)(2,1)}), bf16[32,128,128]{2,1,0:T(8,128)(2,1)S(1)}, u32[]{:S(2)}, u32[]{:S(2)}) async-start(bf16[32,128,128]{2,1,0:T(8,128)(2,1)} %bitcast.7), calls=%async_computation | async-start | bytes 2097152 | tf_op jit(solution)/shard_map/all_to_all | solution.py:680
  15.6 0.7 reduce
  16.3 0.7 pad_maximum_fusion.2
  17.0 0.3 collective-permute-start.1
  17.2 0.9 copy-done.7
  18.1 0.7 copy-done.8
  18.8 7.0 %spread_weights.1.spread_ref = bf16[32,512,128]{2,1,0:T(8,128)(2,1)} custom-call(s32[64,512]{1,0:T(8,128)S(1)} %bitcast.34, bf16[8,512]{1,0:T(8,128)(2,1)S(1)} %copy-done.8), custom_call_target="tpu_custom_call" | custom-call | flops 2147483648 | bytes 4194304 | tf_op jit(solution)/shard_map/spread_weights/pallas_call | solution.py:89
  25.9 0.1 pad_add_fusion.place_ref
  26.0 17.2 %all-to-all-done.rows_ref = bf16[32,128,128]{2,1,0:T(8,128)(2,1)S(1)} async-done(((bf16[32,128,128]{2,1,0:T(8,128)(2,1)}), bf16[32,128,128]{2,1,0:T(8,128)(2,1)S(1)}, u32[]{:S(2)}, u32[]{:S(2)}) %all-to-all-start) | async-done | bytes 1048608 | tf_op jit(solution)/shard_map/all_to_all | solution.py:680
  43.2 2.2 %copy-done.2 = bf16[32,512,128]{2,1,0:T(8,128)(2,1)S(1)} copy-done((bf16[32,512,128]{2,1,0:T(8,128)(2,1)S(1)}, bf16[32,512,128]{2,1,0:T(8,128)(2,1)}, u32[]{:S(2)}) %copy-start.2) | copy-done | bytes 4194328
  45.3 2.8 %compress.1 = bf16[64,1024]{1,0:T(8,128)(2,1)S(1)} custom-call(bf16[32,512,128]{2,1,0:T(8,128)(2,1)S(1)} %copy-done.2, bf16[32,128,128]{2,1,0:T(8,128)(2,1)S(1)} %all-to-all-done.rows_ref), custom_call_target="tpu_custom_call" | custom-call | tf_op jit(solution)/shard_map/compress/pallas_call | solution.py:137
  48.2 1.3 collective-permute-start
  49.5 5.6 %collective-permute-done = bf16[64,1024]{1,0:T(8,128)(2,1)S(1)} collective-permute-done((bf16[64,1024]{1,0:T(8,128)(2,1)S(1)}, bf16[64,1024]{1,0:T(8,128)(2,1)S(1)}, u32[]{:S(2)}, u32[]{:S(2)}) %collective-permute-start) | collective-permute-done | bytes 131104 | tf_op jit(solution)/shard_map/ppermute | solution.py:646
  55.2 13.7 %forward_stage.1 = (bf16[128,1024]{1,0:T(8,128)(2,1)S(1)}, bf16[2,4096,128]{2,1,0:T(8,128)(2,1)S(1)}, f32[2,128,1024]{2,1,0:T(8,128)S(1)}, f32[2,128,128]{2,1,0:...) custom-call(s32[3]{0:T(128)S(1)} %pad_add_fusion.place_ref, ...), custom_call_target="tpu_custom_call" | custom-call | flops 4294967296 | bytes 1048576 | tf_op jit(solution)/shard_map/forward_stage/pallas_call | solution.py:515
  68.9 1.3 collective-permute-start.4
  70.2 0.1 pad_add_fusion.1.place_ref
  70.3 5.0 %collective-permute-done.4.acts_ref = bf16[128,1024]{1,0:T(8,128)(2,1)S(1)} collective-permute-done((bf16[128,1024]{1,0:T(8,128)(2,1)S(1)}, bf16[128,1024]{1,0:T(8,128)(2,1)S(1)}, u32[]{:S(2)}, u32[]{:S(2)}) %collective-permute-start.4) | collective-permute-done | bytes 262176 | tf_op jit(solution)/shard_map/ppermute | solution.py:646
  75.3 3.4 %copy-done.1 = bf16[1,1024,4096]{2,1,0:T(8,128)(2,1)S(1)} copy-done((bf16[1,1024,4096]{2,1,0:T(8,128)(2,1)S(1)}, bf16[1,1024,4096]{2,1,0:T(8,128)(2,1)}, u32[]{:S(2)}) %copy-start.1) | copy-done | bytes 8388632
  78.7 1.1 turn_stage.1
  79.7 1.3 collective-permute-start.5
  81.0 31.5 %collective-permute-done.5.grad_ref = bf16[128,1024]{1,0:T(8,128)(2,1)S(1)} collective-permute-done((bf16[128,1024]{1,0:T(8,128)(2,1)S(1)}, bf16[128,1024]{1,0:T(8,128)(2,1)S(1)}, u32[]{:S(2)}, u32[]{:S(2)}) %collective-permute-start.5) | collective-permute-done | bytes 262176 | tf_op jit(solution)/shard_map/ppermute | solution.py:646
  112.5 18.0 %backward_stage.1 = bf16[128,1024]{1,0:T(8,128)(2,1)S(1)} custom-call(s32[3]{0:T(128)S(1)} %pad_add_fusion.place_ref, bf16[128,1024]{1,0:T(8,128)(2,1)S(1)} %collective-permute-done.5.grad_ref, bf16[2,4096,128]{2,1,0:T(8,128)(2,1)S(1)} %get-tuple-element.13.hid, f32[2,128,1024]{2,1,0:T(8,128)S(1)} %get-tuple-element.14.inter, ...), custom_call_target="tpu_custom_call" | custom-call | flops 4294967296 | bytes 1048576 | tf_op jit(solution)/shard_map/backward_stage/pallas_call | solution.py:622
  130.6 1.3 collective-permute-start.6
  131.9 2.5 %collective-permute-done.6 = bf16[64,1024]{1,0:T(8,128)(2,1)S(1)} collective-permute-done((bf16[64,1024]{1,0:T(8,128)(2,1)S(1)}, bf16[64,1024]{1,0:T(8,128)(2,1)S(1)}, u32[]{:S(2)}, u32[]{:S(2)}) %collective-permute-start.6) | collective-permute-done | bytes 131104 | tf_op jit(solution)/shard_map/ppermute | solution.py:646
  134.4 3.6 %expand.1 = bf16[32,128,128]{2,1,0:T(8,128)(2,1)} custom-call(bf16[32,512,128]{2,1,0:T(8,128)(2,1)S(1)} %copy-done.3, bf16[64,1024]{1,0:T(8,128)(2,1)S(1)} %slice_select_fusion.grad_ref), custom_call_target="tpu_custom_call" | custom-call | tf_op jit(solution)/shard_map/expand/pallas_call | solution.py:174
  138.0 5.0 %all-to-all-start.1 = ((bf16[32,128,128]{2,1,0:T(8,128)(2,1)}), bf16[32,128,128]{2,1,0:T(8,128)(2,1)S(1)}, u32[]{:S(2)}, u32[]{:S(2)}) async-start(bf16[32,128,128]{2,1,0:T(8,128)(2,1)} %expand.1), calls=%async_computation.1 | async-start | bytes 2097152 | tf_op jit(solution)/shard_map/all_to_all | solution.py:717
  143.1 27.5 %all-to-all-done.1 = bf16[32,128,128]{2,1,0:T(8,128)(2,1)S(1)} async-done(((bf16[32,128,128]{2,1,0:T(8,128)(2,1)}), bf16[32,128,128]{2,1,0:T(8,128)(2,1)S(1)}, u32[]{:S(2)}, u32[]{:S(2)}) %all-to-all-start.1) | async-done | bytes 1048608 | tf_op jit(solution)/shard_map/all_to_all | solution.py:717
  170.6 10.8 %add_rows.1 = f32[4096,128]{1,0:T(8,128)} custom-call(s32[4096]{0:T(1024)S(1)} %fusion.1.targets_ref, bf16[4096,128]{1,0:T(8,128)(2,1)S(1)} %bitcast.30, bf16[4096,128]{1,0:T(8,128)(2,1)} %pick_rows.1.sent_ref), custom_call_target="tpu_custom_call" | custom-call | tf_op jit(solution)/shard_map/add_rows/pallas_call | solution.py:221
  (27 shorter events, 0.3 us)
Async XLA Ops:
  0.0 17.2 %copy-start = (bf16[1,4,64,1024]{3,2,1,0:T(8,128)(2,1)S(1)}, bf16[1,4,64,1024]{3,2,1,0:T(8,128)(2,1)}, u32[]{:S(2)}) copy-start(bf16[1,4,64,1024]{3,2,1,0:T(8,128)(2,1)} %param.16) | copy-start | bytes 1572868
  0.0 55.1 %collective-permute-start.2 = (bf16[1024,4096]{1,0:T(8,128)(2,1)}, bf16[1024,4096]{1,0:T(8,128)(2,1)}, u32[]{:S(2)}, u32[]{:S(2)}) collective-permute-start(bf16[1024,4096]{1,0:T(8,128)(2,1)} %bitcast.26), channel_id=1, source_target_pairs={{0,8},{8,0},{16,24},{24,16},{1,9},{9,1},{17,25},{25,17},{2,10},{10... | collective-permute-start | bytes 25165832 | tf_op jit(solution)/shard_map/ppermute | solution.py:641
  0.5 54.7 %collective-permute-start.3 = (bf16[4096,1024]{1,0:T(8,128)(2,1)}, bf16[4096,1024]{1,0:T(8,128)(2,1)}, u32[]{:S(2)}, u32[]{:S(2)}) collective-permute-start(bf16[4096,1024]{1,0:T(8,128)(2,1)} %bitcast.35), channel_id=1, source_target_pairs={{0,8},{8,0},{16,24},{24,16},{1,9},{9,1},{17,25},{25,17},{2,10},{10... | collective-permute-start | bytes 25165832 | tf_op jit(solution)/shard_map/ppermute | solution.py:641
  0.5 1.2 copy-start.4
  1.8 0.7 copy-start.5
  8.3 41.2 %copy-start.9 = (bf16[1,8,128]{2,1,0:T(8,128)(2,1)S(1)}, bf16[1,8,128]{2,1,0:T(8,128)(2,1)}, u32[]{:S(2)}) copy-start(bf16[1,8,128]{2,1,0:T(8,128)(2,1)} %param.12) | copy-start | bytes 6148
  8.3 34.9 %all-to-all-start = ((bf16[32,128,128]{2,1,0:T(8,128)(2,1)}), bf16[32,128,128]{2,1,0:T(8,128)(2,1)S(1)}, u32[]{:S(2)}, u32[]{:S(2)}) async-start(bf16[32,128,128]{2,1,0:T(8,128)(2,1)} %bitcast.7), calls=%async_computation | async-start | bytes 2097152 | tf_op jit(solution)/shard_map/all_to_all | solution.py:680
  17.0 32.5 %collective-permute-start.1 = (bf16[16,128]{1,0:T(8,128)(2,1)S(1)}, bf16[16,128]{1,0:T(8,128)(2,1)S(1)}, u32[]{:S(2)}, u32[]{:S(2)}) collective-permute-start(bf16[16,128]{1,0:T(8,128)(2,1)S(1)} %pad_maximum_fusion.2), channel_id=1, source_target_pairs={{0,8},{8,0},{16,24},{24,16},{1,9},{9,1},{17,25},{25,17},{2,10},{10... | collective-permute-start | bytes 12296 | tf_op jit(solution)/shard_map/ppermute | solution.py:641
  17.2 0.9 copy-start.7
  18.1 0.7 copy-start.8
  43.2 2.2 %copy-start.2 = (bf16[32,512,128]{2,1,0:T(8,128)(2,1)S(1)}, bf16[32,512,128]{2,1,0:T(8,128)(2,1)}, u32[]{:S(2)}) copy-start(bf16[32,512,128]{2,1,0:T(8,128)(2,1)} %spread_weights.1.spread_ref) | copy-start | bytes 12582916
  48.2 7.0 %collective-permute-start = (bf16[64,1024]{1,0:T(8,128)(2,1)S(1)}, bf16[64,1024]{1,0:T(8,128)(2,1)S(1)}, u32[]{:S(2)}, u32[]{:S(2)}) collective-permute-start(bf16[64,1024]{1,0:T(8,128)(2,1)S(1)} %compress.1), channel_id=1, source_target_pairs={{16,0},{24,8},{17,1},{25,9},{18,2},{26,10},{19,3},{27,11},{20,4},{... | collective-permute-start | bytes 393224 | tf_op jit(solution)/shard_map/ppermute | solution.py:646
  68.9 6.4 %collective-permute-start.4 = (bf16[128,1024]{1,0:T(8,128)(2,1)S(1)}, bf16[128,1024]{1,0:T(8,128)(2,1)S(1)}, u32[]{:S(2)}, u32[]{:S(2)}) collective-permute-start(bf16[128,1024]{1,0:T(8,128)(2,1)S(1)} %get-tuple-element.11), channel_id=1, source_target_pairs={{0,16},{8,24},{1,17},{9,25},{2,18},{10,26},{3,19},{11,27},{4,20},{... | collective-permute-start | bytes 786440 | tf_op jit(solution)/shard_map/ppermute | solution.py:646
  75.3 3.4 %copy-start.1 = (bf16[1,1024,4096]{2,1,0:T(8,128)(2,1)S(1)}, bf16[1,1024,4096]{2,1,0:T(8,128)(2,1)}, u32[]{:S(2)}) copy-start(bf16[1,1024,4096]{2,1,0:T(8,128)(2,1)} %param.14) | copy-start | bytes 25165828
  79.7 32.8 %collective-permute-start.5 = (bf16[128,1024]{1,0:T(8,128)(2,1)S(1)}, bf16[128,1024]{1,0:T(8,128)(2,1)S(1)}, u32[]{:S(2)}, u32[]{:S(2)}) collective-permute-start(bf16[128,1024]{1,0:T(8,128)(2,1)S(1)} %turn_stage.1), channel_id=1, source_target_pairs={{16,0},{24,8},{17,1},{25,9},{18,2},{26,10},{19,3},{27,11},{20,4},{... | collective-permute-start | bytes 786440 | tf_op jit(solution)/shard_map/ppermute | solution.py:646
  112.5 21.9 %copy-start.3 = (bf16[32,512,128]{2,1,0:T(8,128)(2,1)S(1)}, bf16[32,512,128]{2,1,0:T(8,128)(2,1)}, u32[]{:S(2)}) copy-start(bf16[32,512,128]{2,1,0:T(8,128)(2,1)} %spread_weights.1.spread_ref) | copy-start | bytes 12582916
  112.5 30.5 %copy-start.6 = (s32[1,32,128]{2,1,0:T(8,128)S(1)}, s32[1,32,128]{2,1,0:T(8,128)}, u32[]{:S(2)}) copy-start(s32[1,32,128]{2,1,0:T(8,128)} %param.18) | copy-start | bytes 49156
  112.5 30.5 %copy-start.10 = (s32[1,32]{1,0:T(1,128)S(1)}, s32[1,32]{1,0:T(1,128)}, u32[]{:S(2)}) copy-start(s32[1,32]{1,0:T(1,128)} %param.19) | copy-start | bytes 388
  130.6 3.8 %collective-permute-start.6 = (bf16[64,1024]{1,0:T(8,128)(2,1)S(1)}, bf16[64,1024]{1,0:T(8,128)(2,1)S(1)}, u32[]{:S(2)}, u32[]{:S(2)}) collective-permute-start(bf16[64,1024]{1,0:T(8,128)(2,1)S(1)} %slice.8), channel_id=1, source_target_pairs={{0,16},{8,24},{1,17},{9,25},{2,18},{10,26},{3,19},{11,27},{4,20},{... | collective-permute-start | bytes 393224 | tf_op jit(solution)/shard_map/ppermute | solution.py:646
  138.0 32.5 %all-to-all-start.1 = ((bf16[32,128,128]{2,1,0:T(8,128)(2,1)}), bf16[32,128,128]{2,1,0:T(8,128)(2,1)S(1)}, u32[]{:S(2)}, u32[]{:S(2)}) async-start(bf16[32,128,128]{2,1,0:T(8,128)(2,1)} %expand.1), calls=%async_computation.1 | async-start | bytes 2097152 | tf_op jit(solution)/shard_map/all_to_all | solution.py:717

commit v5 on v4

--- a/solution.py
+++ b/solution.py
@@ -13,6 +13,10 @@
 
 def whole(memory_space=pltpu.VMEM):
     return pl.BlockSpec(memory_space=memory_space)
+
+
+def in_hbm(value):
+    return pltpu.with_memory_space_constraint(value, pltpu.HBM)
 
 
 def params():
@@ -61,19 +65,19 @@
     )(picked, emb_table)
 
 
-def spread_weights(lookup_slots, lcb_weight, owners, cap):
-    samples, feature_count = lookup_slots.shape
+def spread_weights(codes, lcb_weight, owners, cap):
+    views, samples, feature_count = codes.shape
     embed_count = lcb_weight.shape[0]
-    group = tiles_of(samples, 8)
-
-    def kernel(slots_ref, lcb_ref, out_ref):
+    group = tiles_of(samples, 16)
+
+    def kernel(codes_ref, lcb_ref, out_ref):
         lcb = lcb_ref[...].astype(jnp.float32)
         owner_of = lax.broadcasted_iota(jnp.int32, (owners, embed_count, feature_count), 0)
         column_of = lax.broadcasted_iota(jnp.int32, (cap, feature_count), 0)
         for pair in range(0, group, 2):
             made = []
             for sample in (pair, pair + 1):
-                slots = slots_ref[sample : sample + 1, :]
+                slots = codes_ref[0, sample : sample + 1, :]
                 owner = lax.div(slots, cap)
                 column = slots - owner * cap
                 left = jnp.where(owner_of == owner[None], lcb[None], 0.0)
@@ -84,97 +88,104 @@
                 )
                 made.append(both.reshape(owners, embed_count, cap))
             rows = pl.ds(pair * embed_count, 2 * embed_count)
-            out_ref[:, rows, :] = jnp.concatenate(made, axis=1).astype(out_ref.dtype)
+            out_ref[0, :, rows, :] = jnp.concatenate(made, axis=1).astype(out_ref.dtype)
 
     return pl.pallas_call(
         kernel,
-        out_shape=pltpu.HBM((owners, samples * embed_count, cap), jnp.bfloat16),
-        grid=(samples // group,),
+        out_shape=pltpu.HBM((views, owners, samples * embed_count, cap), jnp.bfloat16),
+        grid=(views, samples // group),
         in_specs=[
-            pl.BlockSpec((group, feature_count), lambda i: (i, 0)),
-            pl.BlockSpec((embed_count, feature_count), lambda i: (0, 0)),
+            pl.BlockSpec((1, group, feature_count), lambda v, i: (v, i, 0)),
+            pl.BlockSpec((embed_count, feature_count), lambda v, i: (0, 0)),
         ],
-        out_specs=pl.BlockSpec((owners, group * embed_count, cap), lambda i: (0, i, 0)),
+        out_specs=pl.BlockSpec((1, owners, group * embed_count, cap), lambda v, i: (v, 0, i, 0)),
         compiler_params=params(),
         cost_estimate=pl.CostEstimate(
-            flops=2 * samples * owners * embed_count * feature_count * cap,
-            bytes_accessed=2 * owners * samples * embed_count * cap,
+            flops=2 * views * samples * owners * embed_count * feature_count * cap,
+            bytes_accessed=2 * views * owners * samples * embed_count * cap,
             transcendentals=0,
         ),
         name="spread_weights",
-    )(lookup_slots, lcb_weight)
+    )(codes, lcb_weight)
 
 
 def compress(spread, fetched, embed_count):
-    owners, lines, cap = spread.shape
-    width = fetched.shape[2]
+    views, owners, lines, cap = spread.shape
+    width = fetched.shape[3]
     samples = lines // embed_count
     part = tiles_of(owners, 4)
     steps = owners // part
 
     def kernel(spread_ref, rows_ref, out_ref, held, total, sems):
-        def copy(step):
+        def copy(view, step):
             piece = tile_at(step, part)
-            return pltpu.make_async_copy(spread_ref.at[piece], held.at[piece], sems.at[step])
-
-        for step in range(steps):
-            copy(step).start()
-        total[...] = jnp.zeros_like(total)
-
-        def body(step, carry):
-            copy(step).wait()
-            first = step * part
-            left = jnp.concatenate([held[first + o] for o in range(part)], axis=1)
-            right = rows_ref[tile_at(step, part)].reshape(part * cap, width)
-            total[...] += jnp.dot(left, right, preferred_element_type=jnp.float32)
-            return carry
-
-        lax.fori_loop(0, steps, body, 0)
-        for k in range(embed_count):
-            piece = total[pl.ds(k, samples, stride=embed_count), :]
-            out_ref[:, k * width : (k + 1) * width] = piece.astype(out_ref.dtype)
+            return pltpu.make_async_copy(
+                spread_ref.at[view, piece], held.at[view, piece], sems.at[view, step]
+            )
+
+        for view in range(views):
+            for step in range(steps):
+                copy(view, step).start()
+        for view in range(views):
+            total[...] = jnp.zeros_like(total)
+
+            def body(step, carry):
+                copy(view, step).wait()
+                first = step * part
+                left = jnp.concatenate([held[view, first + o] for o in range(part)], axis=1)
+                right = jnp.concatenate([rows_ref[first + o, view] for o in range(part)], axis=0)
+                total[...] += jnp.dot(left, right, preferred_element_type=jnp.float32)
+                return carry
+
+            lax.fori_loop(0, steps, body, 0)
+            for k in range(embed_count):
+                piece = total[pl.ds(k, samples, stride=embed_count), :]
+                out_ref[view, :, k * width : (k + 1) * width] = piece.astype(out_ref.dtype)
 
     return pl.pallas_call(
         kernel,
-        out_shape=jax.ShapeDtypeStruct((samples, embed_count * width), jnp.bfloat16),
+        out_shape=jax.ShapeDtypeStruct((views, samples, embed_count * width), jnp.bfloat16),
         in_specs=[whole(pltpu.HBM), whole()],
         out_specs=whole(),
         scratch_shapes=[
             pltpu.VMEM(spread.shape, jnp.bfloat16),
             pltpu.VMEM((lines, width), jnp.float32),
-            pltpu.SemaphoreType.DMA((steps,)),
+            pltpu.SemaphoreType.DMA((views, steps)),
         ],
         compiler_params=params(),
         name="compress",
-    )(spread, fetched)
-
-
-def expand(spread, lead_share, embed_count):
-    owners, lines, cap = spread.shape
+    )(in_hbm(spread), fetched)
+
+
+def expand(spread, lead_grads, embed_count):
+    views, owners, lines, cap = spread.shape
     samples = lines // embed_count
-    width = lead_share.shape[1] // embed_count
+    width = lead_grads[0].shape[1] // embed_count
     part = tiles_of(owners, 4)
 
-    def kernel(spread_ref, grad_ref, out_ref, tall, turned):
-        for k in range(embed_count):
-            piece = grad_ref[:, k * width : (k + 1) * width].astype(jnp.float32)
-            tall[pl.ds(k, samples, stride=embed_count), :] = piece
-        turned[...] = tall[...].T.astype(jnp.bfloat16)
-
-        def body(step, carry):
-            first = step * part
-            right = jnp.concatenate([spread_ref[first + o] for o in range(part)], axis=1)
-            term = jnp.dot(turned[...], right, preferred_element_type=jnp.float32)
-            piece = term.T.astype(out_ref.dtype).reshape(part, cap, width)
-            out_ref[tile_at(step, part)] = piece
-            return carry
-
-        lax.fori_loop(0, owners // part, body, 0)
+    def kernel(spread_ref, *refs):
+        grad_refs, (out_ref, tall, turned) = refs[:views], refs[views:]
+        for view in range(views):
+            for k in range(embed_count):
+                piece = grad_refs[view][:, k * width : (k + 1) * width].astype(jnp.float32)
+                tall[pl.ds(k, samples, stride=embed_count), :] = piece
+            turned[...] = tall[...].T.astype(jnp.bfloat16)
+
+            def body(step, carry):
+                first = step * part
+                right = jnp.concatenate([spread_ref[view, first + o] for o in range(part)], axis=1)
+                term = jnp.dot(turned[...], right, preferred_element_type=jnp.float32)
+                piece = term.T.astype(out_ref.dtype).reshape(part, cap, width)
+                for o in range(part):
+                    out_ref[first + o, view] = piece[o]
+                return carry
+
+            lax.fori_loop(0, owners // part, body, 0)
 
     return pl.pallas_call(
         kernel,
-        out_shape=jax.ShapeDtypeStruct((owners, cap, width), jnp.bfloat16),
-        in_specs=[whole(), whole()],
+        out_shape=jax.ShapeDtypeStruct((owners, views, cap, width), jnp.bfloat16),
+        in_specs=[whole()] * (1 + views),
         out_specs=whole(),
         scratch_shapes=[
             pltpu.VMEM((lines, width), jnp.float32),
@@ -182,7 +193,7 @@
         ],
         compiler_params=params(),
         name="expand",
-    )(spread, lead_share)
+    )(spread, *lead_grads)
 
 
 def add_rows(targets, returned, outgoing, rows):
@@ -234,6 +245,7 @@
 
 
 GROUP = 32
+TABLE_AXES = ("section", "table")
 STAGE_LIMIT = 44 * 1024 * 1024
 NT = (((1,), (1,)), ((), ()))
 
@@ -292,11 +304,11 @@
 
 
 def hidden_tile(hidden_width):
-    return min(hidden_width, 512)
+    return min(hidden_width, 1024)
 
 
 def model_tile(model_width):
-    return min(model_width, 256)
+    return min(model_width, 512)
 
 
 def tile_at(step, size):
@@ -528,7 +540,7 @@
         compiler_params=stage_params(),
         cost_estimate=stage_cost(4, batch, model_width, hidden_width),
         name="forward_stage",
-    )(place, acts, top, *weights)
+    )(place, acts, top, weights[0], *map(in_hbm, weights[1:]))
     return out[0], out[1:5], out[5]
 
 
@@ -591,7 +603,7 @@
         compiler_params=stage_params(),
         cost_estimate=stage_cost(6, batch, model_width, hidden_width),
         name="turn_stage",
-    )(place, acts, top, g_hidden, *weights)
+    )(place, acts, top, g_hidden, weights[0], *map(in_hbm, weights[1:]))
 
 
 def backward_stage(place, grad, saved, weights, count):
@@ -634,16 +646,50 @@
         compiler_params=stage_params(),
         cost_estimate=stage_cost(4, batch, model_width, hidden_width),
         name="backward_stage",
-    )(place, grad, *saved, *weights)
+    )(place, grad, *saved, weights[0], *map(in_hbm, weights[1:]))
 
 
 def swapped(value, section_count):
     return lax.ppermute(value, "section", [(s, s ^ 1) for s in range(section_count)])
 
 
-def moved(value, from_stage, to_stage):
-    pairs = [(2 * from_stage + core, 2 * to_stage + core) for core in (0, 1)]
-    return lax.ppermute(value, "section", pairs)
+def moved(value, from_stage, to_stage, mirrored=False):
+    if not mirrored:
+        pairs = [(2 * from_stage + core, 2 * to_stage + core) for core in (0, 1)]
+        return lax.ppermute(value, "section", pairs)
+    along = lax.axis_size("table")
+    pairs = []
+    for core in (0, 1):
+        for t in range(along):
+            other = (t + along // 2) % along
+            pairs.append(((2 * from_stage + core) * along + t, (2 * to_stage + core) * along + other))
+    return lax.ppermute(value, TABLE_AXES, pairs)
+
+
+def mirror(value):
+    along = lax.axis_size("table")
+    return lax.ppermute(value, "table", [(t, (t + along // 2) % along) for t in range(along)])
+
+
+def swap_in_half(value):
+    along = lax.axis_size("table")
+    half = along // 2
+    groups = [
+        [s * along + h * half + t for s in range(lax.axis_size("section")) for t in range(half)]
+        for h in (0, 1)
+    ]
+    return lax.all_to_all(
+        value, TABLE_AXES, split_axis=0, concat_axis=0, axis_index_groups=groups, tiled=True
+    )
+
+
+def near_first(per_asker, my_half):
+    sections = lax.axis_size("section")
+    half = lax.axis_size("table") // 2
+    split = per_asker.reshape((sections, 2, half) + per_asker.shape[1:])
+    near = lax.dynamic_index_in_dim(split, my_half, 1, keepdims=False)
+    far = lax.dynamic_index_in_dim(split, 1 - my_half, 1, keepdims=False)
+    return jnp.stack([near, far], axis=2).reshape((sections * half, 2) + per_asker.shape[1:])
 
 
 def per_device(
@@ -659,35 +705,46 @@
     row_counts,
 ):
     section_count = lax.axis_size("section")
-    owners = section_count * lax.axis_size("table")
+    along = lax.axis_size("table")
+    half = along // 2
+    near_owners = section_count * half
     stages = section_count // 2
     stage = lax.axis_index("section") // 2
     core = lax.axis_index("section") % 2
+    my_half = lax.axis_index("table") // half
     cap = wanted_rows.shape[2]
     rows, embed_width = emb_table.shape
     embed_count = lcb_weight.shape[0]
     look_dev = lookup_slot.shape[1]
     model_width = top_grad.shape[3]
-    table_axes = ("section", "table")
-
+
+    slots = jnp.concatenate([lookup_slot, mirror(lookup_slot)], axis=0)
     small = jnp.concatenate([fm_proj[0], norm_gain[0].reshape(embed_count, -1)], axis=0)
     other_up = swapped(w_up[0], section_count)
     other_down = swapped(w_down[0], section_count)
     other_small = swapped(small, section_count)
 
-    picked = wanted_rows[0]
+    picked = near_first(wanted_rows[0], my_half)
     outgoing = pick_rows(emb_table, picked.reshape(-1))
-    fetched = lax.all_to_all(
-        outgoing.reshape(owners, cap, embed_width), table_axes, split_axis=0, concat_axis=0, tiled=True
-    )
-    spread = spread_weights(lookup_slot[0], lcb_weight, owners, cap)
+    fetched = swap_in_half(outgoing.reshape(near_owners, 2, cap, embed_width))
+    owner, column = slots // cap, slots % cap
+    place = owner % along
+    is_near = place // half == my_half
+    near_owner = jnp.where(is_near, owner // along * half + place % half, near_owners)
+    spread = spread_weights(near_owner * cap + column, lcb_weight, near_owners, cap)
     smalls = jnp.stack(
         [jnp.where(core == 0, small, other_small), jnp.where(core == 0, other_small, small)]
     )
     weights = [smalls, w_up[0], other_up, w_down[0], other_down]
-    lead = compress(spread, fetched, embed_count)
-
-    acts = jnp.concatenate([lead] + [moved(lead, s, 0) for s in range(1, stages)], axis=0)
+    parts = compress(spread, fetched, embed_count)
+
+    def joined(near, far):
+        return (near.astype(jnp.float32) + far.astype(jnp.float32)).astype(jnp.bfloat16)
+
+    leads = [joined(parts[0], moved(parts[1], 0, 0, mirrored=True))]
+    for s in range(1, stages):
+        leads.append(joined(moved(parts[0], s, 0), moved(parts[1], s, 0, mirrored=True)))
+    acts = jnp.concatenate(leads, axis=0)
     top = top_grad.reshape(stages, 2, look_dev, model_width)
     top = lax.dynamic_index_in_dim(top, core, 1, keepdims=False).reshape(-1, model_width)
 
@@ -708,14 +765,16 @@
         grad = moved(grad, tick + 1, tick)
         grad = backward_stage(at(tick), grad, saved, weights, embed_count)
 
-    lead_share = grad[:look_dev]
+    own_grad = grad[:look_dev]
+    mirror_grad = moved(own_grad, 0, 0, mirrored=True)
     for s in range(1, stages):
-        arrived = moved(grad[s * look_dev : (s + 1) * look_dev], 0, s)
-        lead_share = jnp.where(stage == s, arrived, lead_share)
-
-    slot_grad = expand(spread, lead_share, embed_count)
-    returned = lax.all_to_all(slot_grad, table_axes, split_axis=0, concat_axis=0, tiled=True)
-    live_slots = jnp.arange(cap)[None, :] < row_counts[0][:, None]
+        piece = grad[s * look_dev : (s + 1) * look_dev]
+        own_grad = jnp.where(stage == s, moved(piece, 0, s), own_grad)
+        mirror_grad = jnp.where(stage == s, moved(piece, 0, s, mirrored=True), mirror_grad)
+
+    slot_grad = expand(spread, [own_grad, mirror_grad], embed_count)
+    returned = swap_in_half(slot_grad)
+    live_slots = jnp.arange(cap) < near_first(row_counts[0], my_half)[..., None]
     targets = jnp.where(live_slots, picked, rows).reshape(-1)
     return add_rows(targets, returned.reshape(-1, embed_width), outgoing, rows)
 

time: 182 us -> 174 us (0.956)
  waiting for transfers between devices: 89.3 us -> 72.1 us
  starting transfers between devices: 18.2 us -> 31.9 us
  local copies, waits for them, and re-layouts: 9.15 us -> 4.55 us
  Pallas kernels: 62.8 us -> 60.8 us
    all_to_all x2, waiting for transfers between devices: 44.7 us -> 13.1 us  [swap_in_half(): lax.all_to_all(value, TABLE_AXES, split_axis=0, concat_axis=0, axis_index...]
    ppermute x0 -> x5, waiting for transfers between devices: none -> 18.2 us  [the longest x1 10.1 us: mirror(): lax.ppermute(value, 'table', [(t, (t + along // 2) % along) for t in rang...]
    ppermute x0 -> x5, starting transfers between devices: none -> 15.7 us  [the longest x4 13.2 us: moved(): return lax.ppermute(value, TABLE_AXES, pairs)]
    unnamed x22 -> x14, local copies, waits for them, and re-layouts: 9.12 us -> 3.41 us
    ppermute x4, waiting for transfers between devices: 44.6 us -> 40.8 us  [moved(): return lax.ppermute(value, 'section', pairs)]
    all_to_all x2, starting transfers between devices: 12.2 us -> 10.1 us  [swap_in_half(): lax.all_to_all(value, TABLE_AXES, split_axis=0, concat_axis=0, axis_index...]
  transfers between devices with their start and end apart: 9 -> 14, of which waited for: 6 -> 9; matrix products, arithmetic and copies ran while one was open for 1% -> 3% of each run, Pallas kernels for 9% -> 10%
where the time goes in v5:
time: 174 us; the launch traced here: 173 us
  waiting for transfers between devices  72.1 us (41%)
  Pallas kernels  60.8 us (35%)
  starting transfers between devices  31.9 us (18%)
  local copies, waits for them, and re-layouts  4.55 us (3%)
  other arithmetic  3.17 us (2%)
    ppermute x4, waiting for transfers between devices, moved(): return lax.ppermute(value, 'section', pairs)  40.8 us
    pallas_call x1, Pallas kernels, backward_stage(): pl.pallas_call(kernel, out_shape=jax.ShapeDtypeStruct(grad.shape, jnp.bfl...  16.3 us
    ppermute x4, starting transfers between devices, moved(): return lax.ppermute(value, TABLE_AXES, pairs)  13.2 us
    all_to_all x2, waiting for transfers between devices, swap_in_half(): lax.all_to_all(value, TABLE_AXES, split_axis=0, concat_axis=0, axis_index...  13.1 us
    pallas_call x1, Pallas kernels, forward_stage(): pl.pallas_call(kernel, out_shape=[jax.ShapeDtypeStruct(acts.shape, jnp.bf...  12.6 us
    pallas_call x1, Pallas kernels, add_rows(): pl.pallas_call(kernel, out_shape=jax.ShapeDtypeStruct((rows, width), jnp....  10.8 us
    ppermute x1, waiting for transfers between devices, mirror(): lax.ppermute(value, 'table', [(t, (t + along // 2) % along) for t in rang...  10.1 us
    all_to_all x2, starting transfers between devices, swap_in_half(): lax.all_to_all(value, TABLE_AXES, split_axis=0, concat_axis=0, axis_index...  10.1 us
  transfers between devices with their start and end apart: 14, of which 9 were waited for; matrix products, arithmetic and copies ran while one was open for 3% of the time, Pallas kernels for 10%

profile of v5, /device:TPU:0, one launch (start us, length us, event | category | flops | bytes accessed | tf_op | source)
XLA Modules:
  0.0 172.9 jit_solution(1135291821067238481)
XLA Ops:
  0.5 0.7 constant_dynamic-slice_fusion.2
  1.3 1.2 copy-done.2
  2.5 5.8 %pick_rows.1.sent_ref = bf16[4096,128]{1,0:T(8,128)(2,1)} custom-call(s32[4096]{0:T(1024)S(1)} %bitcast.36, bf16[4096,128]{1,0:T(8,128)(2,1)S(1)} %copy-done.2), custom_call_target="tpu_custom_call" | custom-call | tf_op jit(solution)/shard_map/pick_rows/pallas_call | solution.py:54
  8.3 6.4 %all-to-all-start = ((bf16[16,2,128,128]{3,2,1,0:T(8,128)(2,1)}), bf16[16,2,128,128]{3,2,1,0:T(8,128)(2,1)S(1)}, u32[]{:S(2)}, u32[]{:S(2)}) async-start(bf16[16,2,128,128]{3,2,1,0:T(8,128)(2,1)} %bitcast.11), calls=%async_computation | async-start | bytes 2097152 | tf_op jit(solution)/shard_map/all_to_all | solution.py:681
  16.5 2.6 %collective-permute-start = (s32[1,64,512]{2,1,0:T(8,128)}, s32[1,64,512]{2,1,0:T(8,128)S(1)}, u32[]{:S(2)}, u32[]{:S(2)}) collective-permute-start(s32[1,64,512]{2,1,0:T(8,128)} %param.17), channel_id=1, source_target_pairs={{0,4},{1,5},{2,6},{3,7},{4,0},{5,1},{6,2},{7,3},{8,12},{9,13},{10,... | collective-permute-start | bytes 393224 | tf_op jit(solution)/shard_map/ppermute | solution.py:671
  19.1 0.9 constant_dynamic-update-slice_fusion.1
  20.2 10.1 %collective-permute-done = s32[1,64,512]{2,1,0:T(8,128)S(1)} collective-permute-done((s32[1,64,512]{2,1,0:T(8,128)}, s32[1,64,512]{2,1,0:T(8,128)S(1)}, u32[]{:S(2)}, u32[]{:S(2)}) %collective-permute-start) | collective-permute-done | bytes 131104 | tf_op jit(solution)/shard_map/ppermute | solution.py:671
  30.3 0.7 fusion.5.codes_ref
  31.7 7.1 %spread_weights.1.spread_ref = bf16[2,16,512,128]{3,2,1,0:T(8,128)(2,1)} custom-call(s32[2,64,512]{2,1,0:T(8,128)S(1)} %fusion.5.codes_ref, bf16[8,512]{1,0:T(8,128)(2,1)S(1)} %copy-done.3), custom_call_target="tpu_custom_call" | custom-call | flops 2147483648 | bytes 4194304 | tf_op jit(solution)/shard_map/spread_weights/pallas_call | solution.py:93
  38.9 3.6 %compress.1 = bf16[2,64,1024]{2,1,0:T(8,128)(2,1)S(1)} custom-call(bf16[2,16,512,128]{3,2,1,0:T(8,128)(2,1)} %spread_weights.1.spread_ref, bf16[16,2,128,128]{3,2,1,0:T(8,128)(2,1)S(1)} %all-to-all-done.rows_ref), custom_call_target="tpu_custom_call" | custom-call | tf_op jit(solution)/shard_map/compress/pallas_call | solution.py:145
  42.5 5.2 %collective-permute-start.1 = (bf16[64,1024]{1,0:T(8,128)(2,1)S(1)}, bf16[64,1024]{1,0:T(8,128)(2,1)S(1)}, u32[]{:S(2)}, u32[]{:S(2)}) collective-permute-start(bf16[64,1024]{1,0:T(8,128)(2,1)S(1)} %get-tuple-element.22), channel_id=1, source_target_pairs={{0,4},{1,5},{2,6},{3,7},{4,0},{5,1},{6,2},{7,3},{8,12},{9,13},{10,... | collective-permute-start | bytes 393224 | tf_op jit(solution)/shard_map/ppermute | solution.py:666
  47.7 1.3 collective-permute-start.3
  49.0 1.3 collective-permute-start.2
  50.3 0.9 collective-permute-done.1
  51.3 5.2 %collective-permute-done.2 = bf16[64,1024]{1,0:T(8,128)(2,1)S(1)} collective-permute-done((bf16[64,1024]{1,0:T(8,128)(2,1)S(1)}, bf16[64,1024]{1,0:T(8,128)(2,1)S(1)}, u32[]{:S(2)}, u32[]{:S(2)}) %collective-permute-start.2) | collective-permute-done | bytes 131104 | tf_op jit(solution)/shard_map/ppermute | solution.py:659
  56.5 2.8 %collective-permute-done.3 = bf16[64,1024]{1,0:T(8,128)(2,1)S(1)} collective-permute-done((bf16[64,1024]{1,0:T(8,128)(2,1)S(1)}, bf16[64,1024]{1,0:T(8,128)(2,1)S(1)}, u32[]{:S(2)}, u32[]{:S(2)}) %collective-permute-start.3) | collective-permute-done | bytes 131104 | tf_op jit(solution)/shard_map/ppermute | solution.py:666
  59.4 12.6 %forward_stage.1 = (bf16[128,1024]{1,0:T(8,128)(2,1)S(1)}, bf16[2,4096,128]{2,1,0:T(8,128)(2,1)S(1)}, f32[2,128,1024]{2,1,0:T(8,128)S(1)}, f32[2,128,128]{2,1,0:...) custom-call(s32[3]{0:T(128)S(1)} %pad_add_fusion.2.place_ref, ...), custom_call_target="tpu_custom_call" | custom-call | flops 4294967296 | bytes 1048576 | tf_op jit(solution)/shard_map/forward_stage/pallas_call | solution.py:527
  72.0 1.3 collective-permute-start.7
  73.4 5.4 %collective-permute-done.7.acts_ref = bf16[128,1024]{1,0:T(8,128)(2,1)S(1)} collective-permute-done((bf16[128,1024]{1,0:T(8,128)(2,1)S(1)}, bf16[128,1024]{1,0:T(8,128)(2,1)S(1)}, u32[]{:S(2)}, u32[]{:S(2)}) %collective-permute-start.7) | collective-permute-done | bytes 262176 | tf_op jit(solution)/shard_map/ppermute | solution.py:659
  78.8 0.9 turn_stage.1
  79.7 1.3 collective-permute-start.8
  81.0 28.4 %collective-permute-done.8.grad_ref = bf16[128,1024]{1,0:T(8,128)(2,1)S(1)} collective-permute-done((bf16[128,1024]{1,0:T(8,128)(2,1)S(1)}, bf16[128,1024]{1,0:T(8,128)(2,1)S(1)}, u32[]{:S(2)}, u32[]{:S(2)}) %collective-permute-start.8) | collective-permute-done | bytes 262176 | tf_op jit(solution)/shard_map/ppermute | solution.py:659
  109.4 16.3 %backward_stage.1 = bf16[128,1024]{1,0:T(8,128)(2,1)S(1)} custom-call(s32[3]{0:T(128)S(1)} %pad_add_fusion.2.place_ref, bf16[128,1024]{1,0:T(8,128)(2,1)S(1)} %collective-permute-done.8.grad_ref, bf16[2,4096,128]{2,1,0:T(8,128)(2,1)S(1)} %get-tuple-element.13.hid, f32[2,128,1024]{2,1,0:T(8,128)S(1)} %get-tuple-element.14.inter, ...), custom_call_target="tpu_custom_call" | custom-call | flops 4294967296 | bytes 1048576 | tf_op jit(solution)/shard_map/backward_stage/pallas_call | solution.py:634
  125.7 1.3 collective-permute-start.9
  127.0 1.3 collective-permute-start.10
  128.3 1.8 %collective-permute-done.9 = bf16[64,1024]{1,0:T(8,128)(2,1)S(1)} collective-permute-done((bf16[64,1024]{1,0:T(8,128)(2,1)S(1)}, bf16[64,1024]{1,0:T(8,128)(2,1)S(1)}, u32[]{:S(2)}, u32[]{:S(2)}) %collective-permute-start.9) | collective-permute-done | bytes 131104 | tf_op jit(solution)/shard_map/ppermute | solution.py:659
  130.1 5.4 %collective-permute-start.11 = (bf16[64,1024]{1,0:T(8,128)(2,1)S(1)}, bf16[64,1024]{1,0:T(8,128)(2,1)S(1)}, u32[]{:S(2)}, u32[]{:S(2)}) collective-permute-start(bf16[64,1024]{1,0:T(8,128)(2,1)S(1)} %get-tuple-element.19), channel_id=1, source_target_pairs={{0,4},{1,5},{2,6},{3,7},{4,0},{5,1},{6,2},{7,3},{8,12},{9,13},{10,... | collective-permute-start | bytes 393224 | tf_op jit(solution)/shard_map/ppermute | solution.py:666
  135.5 4.3 %collective-permute-done.11 = bf16[64,1024]{1,0:T(8,128)(2,1)S(1)} collective-permute-done((bf16[64,1024]{1,0:T(8,128)(2,1)S(1)}, bf16[64,1024]{1,0:T(8,128)(2,1)S(1)}, u32[]{:S(2)}, u32[]{:S(2)}) %collective-permute-start.11) | collective-permute-done | bytes 131104 | tf_op jit(solution)/shard_map/ppermute | solution.py:666
  139.9 3.7 %expand.1 = bf16[16,2,128,128]{3,2,1,0:T(8,128)(2,1)} custom-call(bf16[2,16,512,128]{3,2,1,0:T(8,128)(2,1)S(1)} %copy-done.1, bf16[64,1024]{1,0:T(8,128)(2,1)S(1)} %get-tuple-element.20.refs_0_, bf16[64,1024]{1,0:T(8,128)(2,1)S(1)} %broadcast_select_fusion.refs_1_), custom_call_target="tpu_custom_call" | custom-call | tf_op jit(solution)/shard_map/expand/pallas_call | solution.py:185
  143.6 3.7 %all-to-all-start.1 = ((bf16[16,2,128,128]{3,2,1,0:T(8,128)(2,1)}), bf16[16,2,128,128]{3,2,1,0:T(8,128)(2,1)S(1)}, u32[]{:S(2)}, u32[]{:S(2)}) async-start(bf16[16,2,128,128]{3,2,1,0:T(8,128)(2,1)} %expand.1), calls=%async_computation.1 | async-start | bytes 2097152 | tf_op jit(solution)/shard_map/all_to_all | solution.py:681
  148.9 13.1 %all-to-all-done.1 = bf16[16,2,128,128]{3,2,1,0:T(8,128)(2,1)S(1)} async-done(((bf16[16,2,128,128]{3,2,1,0:T(8,128)(2,1)}), bf16[16,2,128,128]{3,2,1,0:T(8,128)(2,1)S(1)}, u32[]{:S(2)}, u32[]{:S(2)}) %all-to-all-start.1) | async-done | bytes 1048608 | tf_op jit(solution)/shard_map/all_to_all | solution.py:681
  162.0 10.8 %add_rows.1 = f32[4096,128]{1,0:T(8,128)} custom-call(s32[4096]{0:T(1024)S(1)} %bitcast.35, bf16[4096,128]{1,0:T(8,128)(2,1)S(1)} %bitcast.32, bf16[4096,128]{1,0:T(8,128)(2,1)} %pick_rows.1.sent_ref), custom_call_target="tpu_custom_call" | custom-call | tf_op jit(solution)/shard_map/add_rows/pallas_call | solution.py:232
  (44 shorter events, 5.1 us)
Async XLA Ops:
  0.0 20.1 %copy-start = (bf16[1,4,64,1024]{3,2,1,0:T(8,128)(2,1)S(1)}, bf16[1,4,64,1024]{3,2,1,0:T(8,128)(2,1)}, u32[]{:S(2)}) copy-start(bf16[1,4,64,1024]{3,2,1,0:T(8,128)(2,1)} %param.16) | copy-start | bytes 1572868
  0.0 59.4 %collective-permute-start.5 = (bf16[1024,4096]{1,0:T(8,128)(2,1)}, bf16[1024,4096]{1,0:T(8,128)(2,1)}, u32[]{:S(2)}, u32[]{:S(2)}) collective-permute-start(bf16[1024,4096]{1,0:T(8,128)(2,1)} %bitcast.37), channel_id=1, source_target_pairs={{0,8},{8,0},{16,24},{24,16},{1,9},{9,1},{17,25},{25,17},{2,10},{10... | collective-permute-start | bytes 25165832 | tf_op jit(solution)/shard_map/ppermute | solution.py:653
  0.5 58.9 %collective-permute-start.6 = (bf16[4096,1024]{1,0:T(8,128)(2,1)}, bf16[4096,1024]{1,0:T(8,128)(2,1)}, u32[]{:S(2)}, u32[]{:S(2)}) collective-permute-start(bf16[4096,1024]{1,0:T(8,128)(2,1)} %bitcast.41), channel_id=1, source_target_pairs={{0,8},{8,0},{16,24},{24,16},{1,9},{9,1},{17,25},{25,17},{2,10},{10... | collective-permute-start | bytes 25165832 | tf_op jit(solution)/shard_map/ppermute | solution.py:653
  1.3 1.2 copy-start.2
  8.3 39.4 %copy-start.4 = (bf16[1,8,128]{2,1,0:T(8,128)(2,1)S(1)}, bf16[1,8,128]{2,1,0:T(8,128)(2,1)}, u32[]{:S(2)}) copy-start(bf16[1,8,128]{2,1,0:T(8,128)(2,1)} %param.12) | copy-start | bytes 6148
  8.3 30.6 %all-to-all-start = ((bf16[16,2,128,128]{3,2,1,0:T(8,128)(2,1)}), bf16[16,2,128,128]{3,2,1,0:T(8,128)(2,1)S(1)}, u32[]{:S(2)}, u32[]{:S(2)}) async-start(bf16[16,2,128,128]{3,2,1,0:T(8,128)(2,1)} %bitcast.11), calls=%async_computation | async-start | bytes 2097152 | tf_op jit(solution)/shard_map/all_to_all | solution.py:681
  16.1 31.6 %collective-permute-start.4 = (bf16[16,128]{1,0:T(8,128)(2,1)S(1)}, bf16[16,128]{1,0:T(8,128)(2,1)S(1)}, u32[]{:S(2)}, u32[]{:S(2)}) collective-permute-start(bf16[16,128]{1,0:T(8,128)(2,1)S(1)} %pad_maximum_fusion.2), channel_id=1, source_target_pairs={{0,8},{8,0},{16,24},{24,16},{1,9},{9,1},{17,25},{25,17},{2,10},{10... | collective-permute-start | bytes 12296 | tf_op jit(solution)/shard_map/ppermute | solution.py:653
  16.5 13.8 %collective-permute-start = (s32[1,64,512]{2,1,0:T(8,128)}, s32[1,64,512]{2,1,0:T(8,128)S(1)}, u32[]{:S(2)}, u32[]{:S(2)}) collective-permute-start(s32[1,64,512]{2,1,0:T(8,128)} %param.17), channel_id=1, source_target_pairs={{0,4},{1,5},{2,6},{3,7},{4,0},{5,1},{6,2},{7,3},{8,12},{9,13},{10,... | collective-permute-start | bytes 393224 | tf_op jit(solution)/shard_map/ppermute | solution.py:671
  31.0 0.7 copy-start.3
  42.5 8.7 %collective-permute-start.1 = (bf16[64,1024]{1,0:T(8,128)(2,1)S(1)}, bf16[64,1024]{1,0:T(8,128)(2,1)S(1)}, u32[]{:S(2)}, u32[]{:S(2)}) collective-permute-start(bf16[64,1024]{1,0:T(8,128)(2,1)S(1)} %get-tuple-element.22), channel_id=1, source_target_pairs={{0,4},{1,5},{2,6},{3,7},{4,0},{5,1},{6,2},{7,3},{8,12},{9,13},{10,... | collective-permute-start | bytes 393224 | tf_op jit(solution)/shard_map/ppermute | solution.py:666
  47.7 11.6 %collective-permute-start.3 = (bf16[64,1024]{1,0:T(8,128)(2,1)S(1)}, bf16[64,1024]{1,0:T(8,128)(2,1)S(1)}, u32[]{:S(2)}, u32[]{:S(2)}) collective-permute-start(bf16[64,1024]{1,0:T(8,128)(2,1)S(1)} %get-tuple-element.22), channel_id=1, source_target_pairs={{16,4},{17,5},{18,6},{19,7},{20,0},{21,1},{22,2},{23,3},{24,12},{2... | collective-permute-start | bytes 393224 | tf_op jit(solution)/shard_map/ppermute | solution.py:666
  49.0 7.5 %collective-permute-start.2 = (bf16[64,1024]{1,0:T(8,128)(2,1)S(1)}, bf16[64,1024]{1,0:T(8,128)(2,1)S(1)}, u32[]{:S(2)}, u32[]{:S(2)}) collective-permute-start(bf16[64,1024]{1,0:T(8,128)(2,1)S(1)} %get-tuple-element.21), channel_id=1, source_target_pairs={{16,0},{24,8},{17,1},{25,9},{18,2},{26,10},{19,3},{27,11},{20,4},{... | collective-permute-start | bytes 393224 | tf_op jit(solution)/shard_map/ppermute | solution.py:659
  72.0 6.8 %collective-permute-start.7 = (bf16[128,1024]{1,0:T(8,128)(2,1)S(1)}, bf16[128,1024]{1,0:T(8,128)(2,1)S(1)}, u32[]{:S(2)}, u32[]{:S(2)}) collective-permute-start(bf16[128,1024]{1,0:T(8,128)(2,1)S(1)} %get-tuple-element.11), channel_id=1, source_target_pairs={{0,16},{8,24},{1,17},{9,25},{2,18},{10,26},{3,19},{11,27},{4,20},{... | collective-permute-start | bytes 786440 | tf_op jit(solution)/shard_map/ppermute | solution.py:659
  79.7 29.7 %collective-permute-start.8 = (bf16[128,1024]{1,0:T(8,128)(2,1)S(1)}, bf16[128,1024]{1,0:T(8,128)(2,1)S(1)}, u32[]{:S(2)}, u32[]{:S(2)}) collective-permute-start(bf16[128,1024]{1,0:T(8,128)(2,1)S(1)} %turn_stage.1), channel_id=1, source_target_pairs={{16,0},{24,8},{17,1},{25,9},{18,2},{26,10},{19,3},{27,11},{20,4},{... | collective-permute-start | bytes 786440 | tf_op jit(solution)/shard_map/ppermute | solution.py:659
  109.4 30.5 %copy-start.1 = (bf16[2,16,512,128]{3,2,1,0:T(8,128)(2,1)S(1)}, bf16[2,16,512,128]{3,2,1,0:T(8,128)(2,1)}, u32[]{:S(2)}) copy-start(bf16[2,16,512,128]{3,2,1,0:T(8,128)(2,1)} %spread_weights.1.spread_ref) | copy-start | bytes 12582916
  125.7 22.1 %copy-start.5 = (s32[1,32]{1,0:T(1,128)S(1)}, s32[1,32]{1,0:T(1,128)}, u32[]{:S(2)}) copy-start(s32[1,32]{1,0:T(1,128)} %param.19) | copy-start | bytes 388
  125.7 4.4 %collective-permute-start.9 = (bf16[64,1024]{1,0:T(8,128)(2,1)S(1)}, bf16[64,1024]{1,0:T(8,128)(2,1)S(1)}, u32[]{:S(2)}, u32[]{:S(2)}) collective-permute-start(bf16[64,1024]{1,0:T(8,128)(2,1)S(1)} %slice.20), channel_id=1, source_target_pairs={{0,16},{8,24},{1,17},{9,25},{2,18},{10,26},{3,19},{11,27},{4,20},{... | collective-permute-start | bytes 393224 | tf_op jit(solution)/shard_map/ppermute | solution.py:659
  127.0 8.5 %collective-permute-start.10 = (bf16[64,1024]{1,0:T(8,128)(2,1)S(1)}, bf16[64,1024]{1,0:T(8,128)(2,1)S(1)}, u32[]{:S(2)}, u32[]{:S(2)}) collective-permute-start(bf16[64,1024]{1,0:T(8,128)(2,1)S(1)} %slice.20), channel_id=1, source_target_pairs={{0,20},{1,21},{2,22},{3,23},{4,16},{5,17},{6,18},{7,19},{8,28},{9,... | collective-permute-start | bytes 393224 | tf_op jit(solution)/shard_map/ppermute | solution.py:666
  130.1 9.8 %collective-permute-start.11 = (bf16[64,1024]{1,0:T(8,128)(2,1)S(1)}, bf16[64,1024]{1,0:T(8,128)(2,1)S(1)}, u32[]{:S(2)}, u32[]{:S(2)}) collective-permute-start(bf16[64,1024]{1,0:T(8,128)(2,1)S(1)} %get-tuple-element.19), channel_id=1, source_target_pairs={{0,4},{1,5},{2,6},{3,7},{4,0},{5,1},{6,2},{7,3},{8,12},{9,13},{10,... | collective-permute-start | bytes 393224 | tf_op jit(solution)/shard_map/ppermute | solution.py:666
  143.6 18.4 %all-to-all-start.1 = ((bf16[16,2,128,128]{3,2,1,0:T(8,128)(2,1)}), bf16[16,2,128,128]{3,2,1,0:T(8,128)(2,1)S(1)}, u32[]{:S(2)}, u32[]{:S(2)}) async-start(bf16[16,2,128,128]{3,2,1,0:T(8,128)(2,1)} %expand.1), calls=%async_computation.1 | async-start | bytes 2097152 | tf_op jit(solution)/shard_map/all_to_all | solution.py:681

commit v6 on v4

--- a/solution.py
+++ b/solution.py
@@ -13,6 +13,10 @@
 
 def whole(memory_space=pltpu.VMEM):
     return pl.BlockSpec(memory_space=memory_space)
+
+
+def in_hbm(value):
+    return pltpu.with_memory_space_constraint(value, pltpu.HBM)
 
 
 def params():
@@ -61,19 +65,19 @@
     )(picked, emb_table)
 
 
-def spread_weights(lookup_slots, lcb_weight, owners, cap):
-    samples, feature_count = lookup_slots.shape
+def spread_weights(codes, lcb_weight, owners, cap):
+    samples, feature_count = codes.shape
     embed_count = lcb_weight.shape[0]
-    group = tiles_of(samples, 8)
-
-    def kernel(slots_ref, lcb_ref, out_ref):
+    group = tiles_of(samples, 16)
+
+    def kernel(codes_ref, lcb_ref, out_ref):
         lcb = lcb_ref[...].astype(jnp.float32)
         owner_of = lax.broadcasted_iota(jnp.int32, (owners, embed_count, feature_count), 0)
         column_of = lax.broadcasted_iota(jnp.int32, (cap, feature_count), 0)
         for pair in range(0, group, 2):
             made = []
             for sample in (pair, pair + 1):
-                slots = slots_ref[sample : sample + 1, :]
+                slots = codes_ref[sample : sample + 1, :]
                 owner = lax.div(slots, cap)
                 column = slots - owner * cap
                 left = jnp.where(owner_of == owner[None], lcb[None], 0.0)
@@ -102,17 +106,20 @@
             transcendentals=0,
         ),
         name="spread_weights",
-    )(lookup_slots, lcb_weight)
-
-
-def compress(spread, fetched, embed_count):
+    )(codes, lcb_weight)
+
+
+def compress(spread, fetched, embed_count, others=None):
     owners, lines, cap = spread.shape
     width = fetched.shape[2]
     samples = lines // embed_count
     part = tiles_of(owners, 4)
     steps = owners // part
-
-    def kernel(spread_ref, rows_ref, out_ref, held, total, sems):
+    extra = [] if others is None else [others]
+
+    def kernel(spread_ref, rows_ref, *refs):
+        other_refs, (out_ref, held, total, sems) = refs[: len(extra)], refs[len(extra) :]
+
         def copy(step):
             piece = tile_at(step, part)
             return pltpu.make_async_copy(spread_ref.at[piece], held.at[piece], sems.at[step])
@@ -131,13 +138,16 @@
 
         lax.fori_loop(0, steps, body, 0)
         for k in range(embed_count):
+            columns = slice(k * width, (k + 1) * width)
             piece = total[pl.ds(k, samples, stride=embed_count), :]
-            out_ref[:, k * width : (k + 1) * width] = piece.astype(out_ref.dtype)
+            for other in other_refs:
+                piece = piece + other[:, columns].astype(jnp.float32)
+            out_ref[:, columns] = piece.astype(out_ref.dtype)
 
     return pl.pallas_call(
         kernel,
         out_shape=jax.ShapeDtypeStruct((samples, embed_count * width), jnp.bfloat16),
-        in_specs=[whole(pltpu.HBM), whole()],
+        in_specs=[whole(pltpu.HBM), whole()] + [whole()] * len(extra),
         out_specs=whole(),
         scratch_shapes=[
             pltpu.VMEM(spread.shape, jnp.bfloat16),
@@ -146,13 +156,13 @@
         ],
         compiler_params=params(),
         name="compress",
-    )(spread, fetched)
-
-
-def expand(spread, lead_share, embed_count):
+    )(in_hbm(spread), fetched, *extra)
+
+
+def expand(spread, lead_grad, embed_count):
     owners, lines, cap = spread.shape
     samples = lines // embed_count
-    width = lead_share.shape[1] // embed_count
+    width = lead_grad.shape[1] // embed_count
     part = tiles_of(owners, 4)
 
     def kernel(spread_ref, grad_ref, out_ref, tall, turned):
@@ -182,26 +192,32 @@
         ],
         compiler_params=params(),
         name="expand",
-    )(spread, lead_share)
-
-
-def add_rows(targets, returned, outgoing, rows):
+    )(spread, lead_grad)
+
+
+def add_rows(targets, returned, outgoing, rows, base=None):
     count, width = returned.shape
     chunk = min(count, 1024)
-
-    def kernel(targets_ref, back_ref, sent_ref, out_ref, total, terms, done):
-        total[...] = jnp.zeros_like(total)
+    is_last = base is not None
+
+    def kernel(targets_ref, back_ref, sent_ref, *refs):
+        if is_last:
+            base_ref, out_ref, terms, total, done = refs
+            total[...] = base_ref[...]
+        else:
+            total, terms = refs
+            total[...] = jnp.zeros_like(total)
 
         def fill(part, carry):
-            base = pl.multiple_of(part * chunk, chunk)
-            lines = pl.ds(base, chunk)
+            first_line = pl.multiple_of(part * chunk, chunk)
+            lines = pl.ds(first_line, chunk)
             terms[...] = back_ref[lines, :].astype(jnp.float32) + DECAY_WEIGHT * sent_ref[
                 lines, :
             ].astype(jnp.float32)
 
             def body(group, inner):
                 first = pl.multiple_of(group * UNROLL, UNROLL)
-                places = [targets_ref[base + first + lane] for lane in range(UNROLL)]
+                places = [targets_ref[first_line + first + lane] for lane in range(UNROLL)]
                 sums = [
                     total[pl.ds(places[lane], 1), :] + terms[pl.ds(first + lane, 1), :]
                     for lane in range(UNROLL)
@@ -214,26 +230,28 @@
             return carry
 
         lax.fori_loop(0, count // chunk, fill, 0)
-        copy = pltpu.make_async_copy(total.at[pl.ds(0, rows), :], out_ref, done)
-        copy.start()
-        copy.wait()
-
+        if is_last:
+            copy = pltpu.make_async_copy(total.at[pl.ds(0, rows), :], out_ref, done)
+            copy.start()
+            copy.wait()
+
+    tall = (rows + 8, width)
+    scratch = [pltpu.VMEM((chunk, width), jnp.float32)]
+    if is_last:
+        scratch += [pltpu.VMEM(tall, jnp.float32), pltpu.SemaphoreType.DMA]
     return pl.pallas_call(
         kernel,
-        out_shape=jax.ShapeDtypeStruct((rows, width), jnp.float32),
-        in_specs=[whole(pltpu.SMEM), whole(), whole()],
-        out_specs=whole(pl.ANY),
-        scratch_shapes=[
-            pltpu.VMEM((rows + 8, width), jnp.float32),
-            pltpu.VMEM((chunk, width), jnp.float32),
-            pltpu.SemaphoreType.DMA,
-        ],
+        out_shape=jax.ShapeDtypeStruct((rows, width) if is_last else tall, jnp.float32),
+        in_specs=[whole(pltpu.SMEM), whole(), whole()] + [whole()] * is_last,
+        out_specs=whole(pl.ANY) if is_last else whole(),
+        scratch_shapes=scratch,
         compiler_params=params(),
         name="add_rows",
-    )(targets, returned, outgoing)
+    )(targets, returned, outgoing, *([base] if is_last else []))
 
 
 GROUP = 32
+TABLE_AXES = ("section", "table")
 STAGE_LIMIT = 44 * 1024 * 1024
 NT = (((1,), (1,)), ((), ()))
 
@@ -292,11 +310,11 @@
 
 
 def hidden_tile(hidden_width):
-    return min(hidden_width, 512)
+    return min(hidden_width, 1024)
 
 
 def model_tile(model_width):
-    return min(model_width, 256)
+    return min(model_width, 512)
 
 
 def tile_at(step, size):
@@ -333,32 +351,35 @@
     return None
 
 
-def up_product(normed, w_up, hidden, turned, wait):
-    tile = hidden_tile(hidden.shape[1])
+def over_tiles(total, tile, many, wait, work):
+    many = min(many, total // tile)
 
     def body(step, carry):
-        wait(step)
-        columns = tile_at(step, tile)
-        before = dot(normed[...], w_up[:, columns])
-        opened = jnp.maximum(before, 0.0)
+        for inner in range(many):
+            wait(step * many + inner)
+        work(tile_at(step, many * tile))
+        return carry
+
+    lax.fori_loop(0, total // (many * tile), body, 0)
+
+
+def up_product(normed, w_up, hidden, turned, wait, many=1):
+    def work(columns):
+        opened = jnp.maximum(dot(normed[...], w_up[:, columns]), 0.0)
         hidden[:, columns] = opened.astype(jnp.bfloat16)
         turned[columns, :] = opened.T.astype(jnp.bfloat16)
-        return carry
-
-    lax.fori_loop(0, hidden.shape[1] // tile, body, 0)
-
-
-def down_product(hidden, w_down, acts, out, wait):
-    tile = model_tile(out.shape[1])
-
-    def body(step, carry):
-        wait(step)
-        columns = tile_at(step, tile)
+
+    width = hidden.shape[1]
+    over_tiles(width, hidden_tile(width), many, wait, work)
+
+
+def down_product(hidden, w_down, acts, out, wait, many=1):
+    def work(columns):
         term = dot(hidden[...], w_down[:, columns])
         out[:, columns] = (acts[:, columns].astype(jnp.float32) + term).astype(jnp.bfloat16)
-        return carry
-
-    lax.fori_loop(0, out.shape[1] // tile, body, 0)
+
+    width = out.shape[1]
+    over_tiles(width, model_tile(width), many, wait, work)
 
 
 def turn(rows, turned):
@@ -369,32 +390,24 @@
     return jnp.where(hidden.astype(jnp.float32) > 0.0, grad, 0.0).astype(jnp.bfloat16)
 
 
-def down_back(grad, w_down, hidden, out, wait):
-    tile = hidden_tile(out.shape[0])
-
-    def body(step, carry):
-        wait(step)
-        lines = tile_at(step, tile)
+def down_back(grad, w_down, hidden, out, wait, many=1):
+    def work(lines):
         g_hidden = dot(w_down[lines, :], grad[...])
         if hidden is not None:
             out[lines, :] = opened_only(hidden[lines, :], g_hidden)
         else:
             out[lines, :] = g_hidden.astype(jnp.bfloat16)
-        return carry
-
-    lax.fori_loop(0, out.shape[0] // tile, body, 0)
-
-
-def up_back(g_before, w_up, weighted, wait):
-    tile = model_tile(weighted.shape[1])
-
-    def body(step, carry):
-        wait(step)
-        columns = tile_at(step, tile)
+
+    width = out.shape[0]
+    over_tiles(width, hidden_tile(width), many, wait, work)
+
+
+def up_back(g_before, w_up, weighted, wait, many=1):
+    def work(columns):
         weighted[:, columns] = dot(w_up[columns, :], g_before[...]).T
-        return carry
-
-    lax.fori_loop(0, weighted.shape[1] // tile, body, 0)
+
+    width = weighted.shape[1]
+    over_tiles(width, model_tile(width), many, wait, work)
 
 
 def mix_backward(small, layer, grad, acts, inter, scale, weighted, out, count):
@@ -478,12 +491,13 @@
     return pltpu.CompilerParams(vmem_limit_bytes=STAGE_LIMIT)
 
 
-def forward_stage(place, acts, top, weights, count):
-    batch, model_width = acts.shape
+def forward_stage(place, pieces, top, weights, count):
+    batch, model_width = top.shape
     hidden_width = weights[1].shape[1]
     width = model_width // count
 
-    def kernel(place_ref, acts_ref, top_ref, small_ref, *refs):
+    def kernel(place_ref, *refs):
+        piece_refs, (top_ref, small_ref), refs = refs[: len(pieces)], refs[len(pieces) :][:2], refs[len(pieces) + 2 :]
         matrices, refs = refs[:4], refs[4:]
         out_ref, hid, inter, scale, kept, g_hidden = refs[:6]
         held, (normed, hidden, top_turned) = refs[6:9], refs[9:]
@@ -495,7 +509,10 @@
             for up, down in layers:
                 up.start()
                 down.start()
-            kept[0] = acts_ref[...]
+            start = 0
+            for piece in piece_refs:
+                kept[0, start : start + piece.shape[0], :] = piece[...]
+                start += piece.shape[0]
             for layer, (up, down) in enumerate(layers):
                 mix_forward(
                     small_ref, layer, kept.at[layer], inter.at[layer], scale.at[layer], normed, count
@@ -514,10 +531,10 @@
 
     out = pl.pallas_call(
         kernel,
-        out_shape=[jax.ShapeDtypeStruct(acts.shape, jnp.bfloat16)]
+        out_shape=[jax.ShapeDtypeStruct(top.shape, jnp.bfloat16)]
         + saved_shapes(batch, model_width, hidden_width, width)
         + [jax.ShapeDtypeStruct((hidden_width, batch), jnp.bfloat16)],
-        in_specs=[whole(pltpu.SMEM), whole(), whole()] + weight_specs(),
+        in_specs=[whole(pltpu.SMEM)] + [whole()] * (len(pieces) + 1) + weight_specs(),
         out_specs=[whole()] * 6,
         scratch_shapes=weight_scratch(model_width, hidden_width)
         + [
@@ -528,7 +545,7 @@
         compiler_params=stage_params(),
         cost_estimate=stage_cost(4, batch, model_width, hidden_width),
         name="forward_stage",
-    )(place, acts, top, *weights)
+    )(place, *pieces, top, weights[0], *map(in_hbm, weights[1:]))
     return out[0], out[1:5], out[5]
 
 
@@ -550,24 +567,20 @@
                 stream.start()
             mix_forward(small_ref, 0, acts_ref, inter.at[0], scale.at[0], normed, count)
             up_product(normed, up0.held, hidden, hid, up0.wait)
-            down_product(hidden, down0.held, acts_ref, upper, down0.wait)
+            down_product(hidden, down0.held, acts_ref, upper, down0.wait, 2)
             mix_forward(small_ref, 1, upper, inter.at[1], scale.at[1], normed, count)
-            tile = hidden_tile(hidden_width)
-
-            def masked(step, carry):
-                up1.wait(step)
-                columns = tile_at(step, tile)
+
+            def masked(columns):
                 before = dot(normed[...], up1.held[:, columns])
                 opened = jnp.maximum(before, 0.0).T
                 g_before[columns, :] = opened_only(opened, ghid_ref[columns, :].astype(jnp.float32))
-                return carry
-
-            lax.fori_loop(0, hidden_width // tile, masked, 0)
-            up_back(g_before, up1.held, weighted, no_wait)
+
+            over_tiles(hidden_width, hidden_tile(hidden_width), 2, up1.wait, masked)
+            up_back(g_before, up1.held, weighted, no_wait, 2)
             mix_backward(small_ref, 1, top_ref, upper, inter.at[1], scale.at[1], weighted, grad, count)
             turn(grad, turned)
-            down_back(turned, down0.held, hid, g_before, no_wait)
-            up_back(g_before, up0.held, weighted, no_wait)
+            down_back(turned, down0.held, hid, g_before, no_wait, 2)
+            up_back(g_before, up0.held, weighted, no_wait, 2)
             mix_backward(small_ref, 0, grad, acts_ref, inter.at[0], scale.at[0], weighted, out_ref, count)
 
     return pl.pallas_call(
@@ -591,7 +604,7 @@
         compiler_params=stage_params(),
         cost_estimate=stage_cost(6, batch, model_width, hidden_width),
         name="turn_stage",
-    )(place, acts, top, g_hidden, *weights)
+    )(place, acts, top, g_hidden, weights[0], *map(in_hbm, weights[1:]))
 
 
 def backward_stage(place, grad, saved, weights, count):
@@ -612,8 +625,8 @@
             for layer, given, to in ((1, grad_ref, middle), (0, middle, out_ref)):
                 up, down = layers[layer]
                 turn(given, turned)
-                down_back(turned, down.held, hid.at[layer], g_before, down.wait)
-                up_back(g_before, up.held, weighted, up.wait)
+                down_back(turned, down.held, hid.at[layer], g_before, down.wait, 2 - layer)
+                up_back(g_before, up.held, weighted, up.wait, 2)
                 mix_backward(
                     small_ref, layer, given, kept.at[layer], inter.at[layer], scale.at[layer],
                     weighted, to, count,
@@ -634,7 +647,7 @@
         compiler_params=stage_params(),
         cost_estimate=stage_cost(4, batch, model_width, hidden_width),
         name="backward_stage",
-    )(place, grad, *saved, *weights)
+    )(place, grad, *saved, weights[0], *map(in_hbm, weights[1:]))
 
 
 def swapped(value, section_count):
@@ -644,6 +657,35 @@
 def moved(value, from_stage, to_stage):
     pairs = [(2 * from_stage + core, 2 * to_stage + core) for core in (0, 1)]
     return lax.ppermute(value, "section", pairs)
+
+
+def mirror(value):
+    along = lax.axis_size("table")
+    return lax.ppermute(value, "table", [(t, (t + along // 2) % along) for t in range(along)])
+
+
+def swap_in_half(value):
+    along = lax.axis_size("table")
+    half = along // 2
+    groups = [
+        [s * along + h * half + t for s in range(lax.axis_size("section")) for t in range(half)]
+        for h in (0, 1)
+    ]
+    return lax.all_to_all(
+        value, TABLE_AXES, split_axis=0, concat_axis=0, axis_index_groups=groups, tiled=True
+    )
+
+
+def by_half(per_asker, half_at):
+    sections = lax.axis_size("section")
+    half = lax.axis_size("table") // 2
+    split = per_asker.reshape((sections, 2, half) + per_asker.shape[1:])
+    chosen = lax.dynamic_index_in_dim(split, half_at, 1, keepdims=False)
+    return chosen.reshape((sections * half,) + per_asker.shape[1:])
+
+
+def after(value, earlier):
+    return lax.optimization_barrier((value, earlier))[0]
 
 
 def per_device(
@@ -659,35 +701,49 @@
     row_counts,
 ):
     section_count = lax.axis_size("section")
-    owners = section_count * lax.axis_size("table")
+    along = lax.axis_size("table")
+    half = along // 2
+    near_owners = section_count * half
     stages = section_count // 2
     stage = lax.axis_index("section") // 2
     core = lax.axis_index("section") % 2
+    my_half = lax.axis_index("table") // half
     cap = wanted_rows.shape[2]
     rows, embed_width = emb_table.shape
     embed_count = lcb_weight.shape[0]
     look_dev = lookup_slot.shape[1]
     model_width = top_grad.shape[3]
-    table_axes = ("section", "table")
-
+
+    own_slots = lookup_slot[0]
+    mirror_slots = mirror(own_slots)
     small = jnp.concatenate([fm_proj[0], norm_gain[0].reshape(embed_count, -1)], axis=0)
     other_up = swapped(w_up[0], section_count)
     other_down = swapped(w_down[0], section_count)
     other_small = swapped(small, section_count)
 
-    picked = wanted_rows[0]
-    outgoing = pick_rows(emb_table, picked.reshape(-1))
-    fetched = lax.all_to_all(
-        outgoing.reshape(owners, cap, embed_width), table_axes, split_axis=0, concat_axis=0, tiled=True
-    )
-    spread = spread_weights(lookup_slot[0], lcb_weight, owners, cap)
+    picked_far = by_half(wanted_rows[0], 1 - my_half)
+    picked_near = by_half(wanted_rows[0], my_half)
+    sent_far = pick_rows(emb_table, picked_far.reshape(-1))
+    line_shape = (near_owners, cap, embed_width)
+    fetched_far = swap_in_half(after(sent_far, mirror_slots).reshape(line_shape))
+    sent_near = pick_rows(emb_table, after(picked_near, sent_far).reshape(-1))
+    fetched_near = swap_in_half(after(sent_near, fetched_far).reshape(line_shape))
+
+    def spread_of(slots):
+        owner, column = slots // cap, slots % cap
+        place = owner % along
+        near = jnp.where(place // half == my_half, owner // along * half + place % half, near_owners)
+        return spread_weights(near * cap + column, lcb_weight, near_owners, cap)
+
+    spread_far = spread_of(mirror_slots)
+    spread_near = spread_of(after(own_slots, fetched_far))
     smalls = jnp.stack(
         [jnp.where(core == 0, small, other_small), jnp.where(core == 0, other_small, small)]
     )
     weights = [smalls, w_up[0], other_up, w_down[0], other_down]
-    lead = compress(spread, fetched, embed_count)
-
-    acts = jnp.concatenate([lead] + [moved(lead, s, 0) for s in range(1, stages)], axis=0)
+    far_part = mirror(compress(spread_far, fetched_far, embed_count))
+    lead = compress(spread_near, fetched_near, embed_count, far_part)
+    pieces = [lead] + [moved(lead, s, 0) for s in range(1, stages)]
     top = top_grad.reshape(stages, 2, look_dev, model_width)
     top = lax.dynamic_index_in_dim(top, core, 1, keepdims=False).reshape(-1, model_width)
 
@@ -697,27 +753,40 @@
 
     saved = None
     for tick in range(stages - 1):
-        out, fresh, product = forward_stage(at(tick), acts, top, weights, embed_count)
+        out, fresh, product = forward_stage(at(tick), pieces, top, weights, embed_count)
         if saved is None:
             saved, g_hidden = fresh, product
         else:
             saved = [jnp.where(stage == tick, new, old) for new, old in zip(fresh, saved)]
-        acts = moved(out, tick, tick + 1)
-    grad = turn_stage(at(stages - 1), acts, top, g_hidden, weights, embed_count)
+        pieces = [moved(out, tick, tick + 1)]
+    grad = turn_stage(at(stages - 1), pieces[0], top, g_hidden, weights, embed_count)
     for tick in reversed(range(stages - 1)):
         grad = moved(grad, tick + 1, tick)
         grad = backward_stage(at(tick), grad, saved, weights, embed_count)
 
-    lead_share = grad[:look_dev]
+    own_grad = grad[:look_dev]
     for s in range(1, stages):
-        arrived = moved(grad[s * look_dev : (s + 1) * look_dev], 0, s)
-        lead_share = jnp.where(stage == s, arrived, lead_share)
-
-    slot_grad = expand(spread, lead_share, embed_count)
-    returned = lax.all_to_all(slot_grad, table_axes, split_axis=0, concat_axis=0, tiled=True)
-    live_slots = jnp.arange(cap)[None, :] < row_counts[0][:, None]
-    targets = jnp.where(live_slots, picked, rows).reshape(-1)
-    return add_rows(targets, returned.reshape(-1, embed_width), outgoing, rows)
+        piece = grad[s * look_dev : (s + 1) * look_dev]
+        own_grad = jnp.where(stage == s, moved(piece, 0, s), own_grad)
+    mirror_grad = mirror(own_grad)
+
+    def targets_of(picked, half_at):
+        live_slots = jnp.arange(cap) < by_half(row_counts[0], half_at)[:, None]
+        return jnp.where(live_slots, picked, rows).reshape(-1)
+
+    near_grad = expand(spread_near, own_grad, embed_count)
+    returned_near = swap_in_half(near_grad)
+    far_grad = expand(spread_far, mirror_grad, embed_count)
+    returned_far = swap_in_half(after(far_grad, returned_near))
+    summed = add_rows(
+        targets_of(picked_near, my_half),
+        after(returned_near, far_grad).reshape(-1, embed_width),
+        sent_near,
+        rows,
+    )
+    return add_rows(
+        targets_of(picked_far, 1 - my_half), returned_far.reshape(-1, embed_width), sent_far, rows, summed
+    )
 
 
 def solution(mesh):

time: 182 us -> 175 us (0.962)
  waiting for transfers between devices: 89.3 us -> 56.5 us
  starting transfers between devices: 18.2 us -> 42.8 us
  Pallas kernels: 62.8 us -> 66.1 us
  local copies, waits for them, and re-layouts: 9.15 us -> 6.31 us
    all_to_all x2 -> x4, waiting for transfers between devices: 44.7 us -> 7.3 us  [swap_in_half(): lax.all_to_all(value, TABLE_AXES, split_axis=0, concat_axis=0, axis_index...]
    all_to_all x2 -> x4, starting transfers between devices: 12.2 us -> 26.2 us  [swap_in_half(): lax.all_to_all(value, TABLE_AXES, split_axis=0, concat_axis=0, axis_index...]
    ppermute x0 -> x3, starting transfers between devices: none -> 10.2 us  [mirror(): lax.ppermute(value, 'table', [(t, (t + along // 2) % along) for t in rang...]
    ppermute x0 -> x3, waiting for transfers between devices: none -> 9.48 us  [mirror(): lax.ppermute(value, 'table', [(t, (t + along // 2) % along) for t in rang...]
    ppermute x4, waiting for transfers between devices: 44.6 us -> 39.7 us  [moved(): return lax.ppermute(value, 'section', pairs)]
    unnamed x22 -> x29, local copies, waits for them, and re-layouts: 9.12 us -> 5.29 us
    pallas_call x1 -> x2, Pallas kernels: 2.8 us -> 4.66 us  [compress(): pl.pallas_call(kernel, out_shape=jax.ShapeDtypeStruct((samples, embed_cou...]
    pallas_call x1 -> x2, Pallas kernels: 5.8 us -> 7.09 us  [pick_rows(): pl.pallas_call(kernel, out_shape=jax.ShapeDtypeStruct((count, width), emb...]
  transfers between devices with their start and end apart: 9 -> 14, of which waited for: 6 -> 10; matrix products, arithmetic and copies ran while one was open for 1% -> 2% of each run, Pallas kernels for 9% -> 16%
where the time goes in v6:
time: 175 us; the launch traced here: 174 us
  Pallas kernels  66.1 us (38%)
  waiting for transfers between devices  56.5 us (32%)
  starting transfers between devices  42.8 us (24%)
  local copies, waits for them, and re-layouts  6.31 us (4%)
  other arithmetic  1.77 us (1%)
    ppermute x4, waiting for transfers between devices, moved(): return lax.ppermute(value, 'section', pairs)  39.7 us
    all_to_all x4, starting transfers between devices, swap_in_half(): lax.all_to_all(value, TABLE_AXES, split_axis=0, concat_axis=0, axis_index...  26.2 us
    pallas_call x1, Pallas kernels, backward_stage(): pl.pallas_call(kernel, out_shape=jax.ShapeDtypeStruct(grad.shape, jnp.bfl...  17.7 us
    pallas_call x1, Pallas kernels, forward_stage(): pl.pallas_call(kernel, out_shape=[jax.ShapeDtypeStruct(top.shape, jnp.bfl...  12.6 us
    pallas_call x2, Pallas kernels, add_rows(): pl.pallas_call(kernel, out_shape=jax.ShapeDtypeStruct((rows, width) if is...  12.6 us
    ppermute x3, starting transfers between devices, mirror(): lax.ppermute(value, 'table', [(t, (t + along // 2) % along) for t in rang...  10.2 us
    ppermute x3, waiting for transfers between devices, mirror(): lax.ppermute(value, 'table', [(t, (t + along // 2) % along) for t in rang...  9.48 us
    pallas_call x2, Pallas kernels, spread_weights(): pl.pallas_call(kernel, out_shape=pltpu.HBM((owners, samples * embed_count...  7.85 us
  transfers between devices with their start and end apart: 14, of which 10 were waited for; matrix products, arithmetic and copies ran while one was open for 2% of the time, Pallas kernels for 16%

profile of v6, /device:TPU:0, one launch (start us, length us, event | category | flops | bytes accessed | tf_op | source)
XLA Modules:
  0.0 173.9 jit_solution(17860155742709931447)
XLA Ops:
  0.5 4.0 %collective-permute-start = (s32[64,512]{1,0:T(8,128)}, s32[64,512]{1,0:T(8,128)S(1)}, u32[]{:S(2)}, u32[]{:S(2)}) collective-permute-start(s32[64,512]{1,0:T(8,128)} %bitcast.50), channel_id=1, source_target_pairs={{0,4},{1,5},{2,6},{3,7},{4,0},{5,1},{6,2},{7,3},{8,12},{9,13},{10,... | collective-permute-start | bytes 393224 | tf_op jit(solution)/shard_map/ppermute | solution.py:664
  5.3 1.2 copy-done.3
  6.5 3.5 %pick_rows.2.sent_ref = bf16[2048,128]{1,0:T(8,128)(2,1)} custom-call(s32[2048]{0:T(1024)S(1)} %bitcast.40, bf16[4096,128]{1,0:T(8,128)(2,1)S(1)} %copy-done.3), custom_call_target="tpu_custom_call" | custom-call | tf_op jit(solution)/shard_map/pick_rows/pallas_call | solution.py:54
  10.0 1.3 collective-permute-done
  11.3 4.2 %all-to-all-start = ((bf16[16,128,128]{2,1,0:T(8,128)(2,1)}), bf16[16,128,128]{2,1,0:T(8,128)(2,1)S(1)}, u32[]{:S(2)}, u32[]{:S(2)}) async-start(bf16[16,128,128]{2,1,0:T(8,128)(2,1)} %bitcast.7), calls=%async_computation | async-start | bytes 1048576 | tf_op jit(solution)/shard_map/all_to_all | solution.py:674
  15.5 3.5 %pick_rows.3.sent_ref = bf16[2048,128]{1,0:T(8,128)(2,1)} custom-call(s32[2048]{0:T(1024)S(1)} %bitcast.38, bf16[4096,128]{1,0:T(8,128)(2,1)S(1)} %copy-done.4), custom_call_target="tpu_custom_call" | custom-call | tf_op jit(solution)/shard_map/pick_rows/pallas_call | solution.py:54
  19.1 6.4 %all-to-all-done.rows_ref = bf16[16,128,128]{2,1,0:T(8,128)(2,1)S(1)} async-done(((bf16[16,128,128]{2,1,0:T(8,128)(2,1)}), bf16[16,128,128]{2,1,0:T(8,128)(2,1)S(1)}, u32[]{:S(2)}, u32[]{:S(2)}) %all-to-all-start) | async-done | bytes 524320 | tf_op jit(solution)/shard_map/all_to_all | solution.py:674
  25.5 6.2 %all-to-all-start.1 = ((bf16[16,128,128]{2,1,0:T(8,128)(2,1)}), bf16[16,128,128]{2,1,0:T(8,128)(2,1)S(1)}, u32[]{:S(2)}, u32[]{:S(2)}) async-start(bf16[16,128,128]{2,1,0:T(8,128)(2,1)} %bitcast.10), calls=%async_computation.1 | async-start | bytes 1048576 | tf_op jit(solution)/shard_map/all_to_all | solution.py:674
  32.7 3.9 %spread_weights.2.spread_ref = bf16[16,512,128]{2,1,0:T(8,128)(2,1)} custom-call(s32[64,512]{1,0:T(8,128)S(1)} %fusion.5.codes_ref, bf16[8,512]{1,0:T(8,128)(2,1)S(1)} %copy-done.9), custom_call_target="tpu_custom_call" | custom-call | flops 1073741824 | bytes 2097152 | tf_op jit(solution)/shard_map/spread_weights/pallas_call | solution.py:93
  36.6 2.3 %compress.2 = bf16[64,1024]{1,0:T(8,128)(2,1)S(1)} custom-call(bf16[16,512,128]{2,1,0:T(8,128)(2,1)} %spread_weights.2.spread_ref, bf16[16,128,128]{2,1,0:T(8,128)(2,1)S(1)} %all-to-all-done.rows_ref), custom_call_target="tpu_custom_call" | custom-call | tf_op jit(solution)/shard_map/compress/pallas_call | solution.py:147
  38.9 2.7 %collective-permute-start.1 = (bf16[64,1024]{1,0:T(8,128)(2,1)S(1)}, bf16[64,1024]{1,0:T(8,128)(2,1)S(1)}, u32[]{:S(2)}, u32[]{:S(2)}) collective-permute-start(bf16[64,1024]{1,0:T(8,128)(2,1)S(1)} %compress.2), channel_id=1, source_target_pairs={{0,4},{1,5},{2,6},{3,7},{4,0},{5,1},{6,2},{7,3},{8,12},{9,13},{10,... | collective-permute-start | bytes 393224 | tf_op jit(solution)/shard_map/ppermute | solution.py:664
  41.9 4.0 %spread_weights.3.spread_ref = bf16[16,512,128]{2,1,0:T(8,128)(2,1)} custom-call(s32[64,512]{1,0:T(8,128)S(1)} %fusion.11.codes_ref, bf16[8,512]{1,0:T(8,128)(2,1)S(1)} %copy-done.9), custom_call_target="tpu_custom_call" | custom-call | flops 1073741824 | bytes 2097152 | tf_op jit(solution)/shard_map/spread_weights/pallas_call | solution.py:93
  45.9 2.3 %collective-permute-done.1.refs_0_ = bf16[64,1024]{1,0:T(8,128)(2,1)S(1)} collective-permute-done((bf16[64,1024]{1,0:T(8,128)(2,1)S(1)}, bf16[64,1024]{1,0:T(8,128)(2,1)S(1)}, u32[]{:S(2)}, u32[]{:S(2)}) %collective-permute-start.1) | collective-permute-done | bytes 131104 | tf_op jit(solution)/shard_map/ppermute | solution.py:664
  48.2 2.3 %compress.3.refs_0_ = bf16[64,1024]{1,0:T(8,128)(2,1)S(1)} custom-call(bf16[16,512,128]{2,1,0:T(8,128)(2,1)} %spread_weights.3.spread_ref, bf16[16,128,128]{2,1,0:T(8,128)(2,1)S(1)} %all-to-all-done.1.rows_ref, bf16[64,1024]{1,0:T(8,128)(2,1)S(1)} %collective-permute-done.1.refs_0_), custom_call_target="tpu_custom_call" | custom-call | tf_op jit(solution)/shard_map/compress/pallas_call | solution.py:147
  50.5 1.3 collective-permute-start.2
  51.9 5.5 %collective-permute-done.2.refs_1_ = bf16[64,1024]{1,0:T(8,128)(2,1)S(1)} collective-permute-done((bf16[64,1024]{1,0:T(8,128)(2,1)S(1)}, bf16[64,1024]{1,0:T(8,128)(2,1)S(1)}, u32[]{:S(2)}, u32[]{:S(2)}) %collective-permute-start.2) | collective-permute-done | bytes 131104 | tf_op jit(solution)/shard_map/ppermute | solution.py:659
  57.4 12.6 %forward_stage.1 = (bf16[128,1024]{1,0:T(8,128)(2,1)S(1)}, bf16[2,4096,128]{2,1,0:T(8,128)(2,1)S(1)}, f32[2,128,1024]{2,1,0:T(8,128)S(1)}, f32[2,128,128]{2,1,0:...) custom-call(s32[3]{0:T(128)S(1)} %pad_add_fusion.place_ref, ...), custom_call_target="tpu_custom_call" | custom-call | flops 4294967296 | bytes 1048576 | tf_op jit(solution)/shard_map/forward_stage/pallas_call | solution.py:532
  70.0 1.3 collective-permute-start.6
  71.4 4.0 %collective-permute-done.6.acts_ref = bf16[128,1024]{1,0:T(8,128)(2,1)S(1)} collective-permute-done((bf16[128,1024]{1,0:T(8,128)(2,1)S(1)}, bf16[128,1024]{1,0:T(8,128)(2,1)S(1)}, u32[]{:S(2)}, u32[]{:S(2)}) %collective-permute-start.6) | collective-permute-done | bytes 262176 | tf_op jit(solution)/shard_map/ppermute | solution.py:659
  76.3 1.3 collective-permute-start.7
  77.6 27.6 %collective-permute-done.7.grad_ref = bf16[128,1024]{1,0:T(8,128)(2,1)S(1)} collective-permute-done((bf16[128,1024]{1,0:T(8,128)(2,1)S(1)}, bf16[128,1024]{1,0:T(8,128)(2,1)S(1)}, u32[]{:S(2)}, u32[]{:S(2)}) %collective-permute-start.7) | collective-permute-done | bytes 262176 | tf_op jit(solution)/shard_map/ppermute | solution.py:659
  105.2 17.7 %backward_stage.1 = bf16[128,1024]{1,0:T(8,128)(2,1)S(1)} custom-call(s32[3]{0:T(128)S(1)} %pad_add_fusion.place_ref, bf16[128,1024]{1,0:T(8,128)(2,1)S(1)} %collective-permute-done.7.grad_ref, bf16[2,4096,128]{2,1,0:T(8,128)(2,1)S(1)} %get-tuple-element.23.hid, f32[2,128,1024]{2,1,0:T(8,128)S(1)} %get-tuple-element.24.inter, ...), custom_call_target="tpu_custom_call" | custom-call | flops 4294967296 | bytes 1048576 | tf_op jit(solution)/shard_map/backward_stage/pallas_call | solution.py:635
  123.0 1.4 collective-permute-start.8
  124.4 2.5 %collective-permute-done.8 = bf16[64,1024]{1,0:T(8,128)(2,1)S(1)} collective-permute-done((bf16[64,1024]{1,0:T(8,128)(2,1)S(1)}, bf16[64,1024]{1,0:T(8,128)(2,1)S(1)}, u32[]{:S(2)}, u32[]{:S(2)}) %collective-permute-start.8) | collective-permute-done | bytes 131104 | tf_op jit(solution)/shard_map/ppermute | solution.py:659
  127.0 1.4 expand.3
  129.1 7.5 %all-to-all-start.2 = ((bf16[16,128,128]{2,1,0:T(8,128)(2,1)}), bf16[16,128,128]{2,1,0:T(8,128)(2,1)S(1)}, u32[]{:S(2)}, u32[]{:S(2)}) async-start(bf16[16,128,128]{2,1,0:T(8,128)(2,1)} %copy-done.8), calls=%async_computation.2 | async-start | bytes 1048576 | tf_op jit(solution)/shard_map/all_to_all | solution.py:674
  136.6 3.6 %collective-permute-start.9 = (bf16[64,1024]{1,0:T(8,128)(2,1)S(1)}, bf16[64,1024]{1,0:T(8,128)(2,1)S(1)}, u32[]{:S(2)}, u32[]{:S(2)}) collective-permute-start(bf16[64,1024]{1,0:T(8,128)(2,1)S(1)} %slice_select_fusion.grad_ref), channel_id=1, source_target_pairs={{0,4},{1,5},{2,6},{3,7},{4,0},{5,1},{6,2},{7,3},{8,12},{9,13},{10,... | collective-permute-start | bytes 393224 | tf_op jit(solution)/shard_map/ppermute | solution.py:664
  140.2 5.9 %collective-permute-done.9.grad_ref = bf16[64,1024]{1,0:T(8,128)(2,1)S(1)} collective-permute-done((bf16[64,1024]{1,0:T(8,128)(2,1)S(1)}, bf16[64,1024]{1,0:T(8,128)(2,1)S(1)}, u32[]{:S(2)}, u32[]{:S(2)}) %collective-permute-start.9) | collective-permute-done | bytes 131104 | tf_op jit(solution)/shard_map/ppermute | solution.py:664
  146.1 1.4 expand.2
  149.5 8.3 %all-to-all-start.3 = ((bf16[16,128,128]{2,1,0:T(8,128)(2,1)}), bf16[16,128,128]{2,1,0:T(8,128)(2,1)S(1)}, u32[]{:S(2)}, u32[]{:S(2)}) async-start(bf16[16,128,128]{2,1,0:T(8,128)(2,1)} %copy-done.7), calls=%async_computation.3 | async-start | bytes 1048576 | tf_op jit(solution)/shard_map/all_to_all | solution.py:674
  160.6 6.0 %add_rows.2.refs_0_ = f32[4104,128]{1,0:T(8,128)S(1)} custom-call(s32[2048]{0:T(1024)S(1)} %fusion.25.targets_ref, bf16[2048,128]{1,0:T(8,128)(2,1)S(1)} %bitcast.37, bf16[2048,128]{1,0:T(8,128)(2,1)} %pick_rows.3.sent_ref), custom_call_target="tpu_custom_call" | custom-call | tf_op jit(solution)/shard_map/add_rows/pallas_call | solution.py:242
  167.1 6.5 %add_rows.3 = f32[4096,128]{1,0:T(8,128)} custom-call(s32[2048]{0:T(1024)S(1)} %fusion.23.targets_ref, bf16[2048,128]{1,0:T(8,128)(2,1)S(1)} %bitcast.36, bf16[2048,128]{1,0:T(8,128)(2,1)} %pick_rows.2.sent_ref, f32[4104,128]{1,0:T(8,128)S(1)} %add_rows.2.refs_0_), custom_call_target="tpu_custom_call" | custom-call | tf_op jit(solution)/shard_map/add_rows/pallas_call | solution.py:242
  (57 shorter events, 9.6 us)
Async XLA Ops:
  0.0 32.3 %copy-start = (bf16[1,4,64,1024]{3,2,1,0:T(8,128)(2,1)S(1)}, bf16[1,4,64,1024]{3,2,1,0:T(8,128)(2,1)}, u32[]{:S(2)}) copy-start(bf16[1,4,64,1024]{3,2,1,0:T(8,128)(2,1)} %param.16) | copy-start | bytes 1572868
  0.0 57.4 %collective-permute-start.4 = (bf16[1024,4096]{1,0:T(8,128)(2,1)}, bf16[1024,4096]{1,0:T(8,128)(2,1)}, u32[]{:S(2)}, u32[]{:S(2)}) collective-permute-start(bf16[1024,4096]{1,0:T(8,128)(2,1)} %bitcast.42), channel_id=1, source_target_pairs={{0,8},{8,0},{16,24},{24,16},{1,9},{9,1},{17,25},{25,17},{2,10},{10... | collective-permute-start | bytes 25165832 | tf_op jit(solution)/shard_map/ppermute | solution.py:654
  0.5 56.9 %collective-permute-start.5 = (bf16[4096,1024]{1,0:T(8,128)(2,1)}, bf16[4096,1024]{1,0:T(8,128)(2,1)}, u32[]{:S(2)}, u32[]{:S(2)}) collective-permute-start(bf16[4096,1024]{1,0:T(8,128)(2,1)} %bitcast.46), channel_id=1, source_target_pairs={{0,8},{8,0},{16,24},{24,16},{1,9},{9,1},{17,25},{25,17},{2,10},{10... | collective-permute-start | bytes 25165832 | tf_op jit(solution)/shard_map/ppermute | solution.py:654
  0.5 10.8 %collective-permute-start = (s32[64,512]{1,0:T(8,128)}, s32[64,512]{1,0:T(8,128)S(1)}, u32[]{:S(2)}, u32[]{:S(2)}) collective-permute-start(s32[64,512]{1,0:T(8,128)} %bitcast.50), channel_id=1, source_target_pairs={{0,4},{1,5},{2,6},{3,7},{4,0},{5,1},{6,2},{7,3},{8,12},{9,13},{10,... | collective-permute-start | bytes 393224 | tf_op jit(solution)/shard_map/ppermute | solution.py:664
  5.3 1.2 copy-start.3
  6.5 9.0 %copy-start.4 = (bf16[4096,128]{1,0:T(8,128)(2,1)S(1)}, bf16[4096,128]{1,0:T(8,128)(2,1)}, u32[]{:S(2)}) copy-start(bf16[4096,128]{1,0:T(8,128)(2,1)} %table_ref.3) | copy-start | bytes 3145732
  6.5 12.6 %copy-start.12 = (bf16[1,1024]{1,0:T(2,128)(2,1)S(1)}, bf16[1,1024]{1,0:T(2,128)(2,1)}, u32[]{:S(2)}) copy-start(bf16[1,1024]{1,0:T(2,128)(2,1)} %param.13) | copy-start | bytes 6148
  10.0 21.7 %copy-start.11 = (bf16[1,8,128]{2,1,0:T(8,128)(2,1)S(1)}, bf16[1,8,128]{2,1,0:T(8,128)(2,1)}, u32[]{:S(2)}) copy-start(bf16[1,8,128]{2,1,0:T(8,128)(2,1)} %param.12) | copy-start | bytes 6148
  11.3 21.4 %copy-start.9 = (bf16[8,512]{1,0:T(8,128)(2,1)S(1)}, bf16[8,512]{1,0:T(8,128)(2,1)}, u32[]{:S(2)}) copy-start(bf16[8,512]{1,0:T(8,128)(2,1)} %lcb_ref.3) | copy-start | bytes 24580
  11.3 14.2 %all-to-all-start = ((bf16[16,128,128]{2,1,0:T(8,128)(2,1)}), bf16[16,128,128]{2,1,0:T(8,128)(2,1)S(1)}, u32[]{:S(2)}, u32[]{:S(2)}) async-start(bf16[16,128,128]{2,1,0:T(8,128)(2,1)} %bitcast.7), calls=%async_computation | async-start | bytes 1048576 | tf_op jit(solution)/shard_map/all_to_all | solution.py:674
  25.5 22.7 %all-to-all-start.1 = ((bf16[16,128,128]{2,1,0:T(8,128)(2,1)}), bf16[16,128,128]{2,1,0:T(8,128)(2,1)S(1)}, u32[]{:S(2)}, u32[]{:S(2)}) async-start(bf16[16,128,128]{2,1,0:T(8,128)(2,1)} %bitcast.10), calls=%async_computation.1 | async-start | bytes 1048576 | tf_op jit(solution)/shard_map/all_to_all | solution.py:674
  31.7 20.1 %collective-permute-start.3 = (bf16[16,128]{1,0:T(8,128)(2,1)S(1)}, bf16[16,128]{1,0:T(8,128)(2,1)S(1)}, u32[]{:S(2)}, u32[]{:S(2)}) collective-permute-start(bf16[16,128]{1,0:T(8,128)(2,1)S(1)} %pad_maximum_fusion.1), channel_id=1, source_target_pairs={{0,8},{8,0},{16,24},{24,16},{1,9},{9,1},{17,25},{25,17},{2,10},{10... | collective-permute-start | bytes 12296 | tf_op jit(solution)/shard_map/ppermute | solution.py:654
  36.6 5.0 %copy-start.10 = (s32[1,64,512]{2,1,0:T(8,128)S(1)}, s32[1,64,512]{2,1,0:T(8,128)}, u32[]{:S(2)}) copy-start(s32[1,64,512]{2,1,0:T(8,128)} %param.17) | copy-start | bytes 393220
  38.9 9.3 %collective-permute-start.1 = (bf16[64,1024]{1,0:T(8,128)(2,1)S(1)}, bf16[64,1024]{1,0:T(8,128)(2,1)S(1)}, u32[]{:S(2)}, u32[]{:S(2)}) collective-permute-start(bf16[64,1024]{1,0:T(8,128)(2,1)S(1)} %compress.2), channel_id=1, source_target_pairs={{0,4},{1,5},{2,6},{3,7},{4,0},{5,1},{6,2},{7,3},{8,12},{9,13},{10,... | collective-permute-start | bytes 393224 | tf_op jit(solution)/shard_map/ppermute | solution.py:664
  50.5 6.9 %collective-permute-start.2 = (bf16[64,1024]{1,0:T(8,128)(2,1)S(1)}, bf16[64,1024]{1,0:T(8,128)(2,1)S(1)}, u32[]{:S(2)}, u32[]{:S(2)}) collective-permute-start(bf16[64,1024]{1,0:T(8,128)(2,1)S(1)} %compress.3.refs_0_), channel_id=1, source_target_pairs={{16,0},{24,8},{17,1},{25,9},{18,2},{26,10},{19,3},{27,11},{20,4},{... | collective-permute-start | bytes 393224 | tf_op jit(solution)/shard_map/ppermute | solution.py:659
  70.0 5.4 %collective-permute-start.6 = (bf16[128,1024]{1,0:T(8,128)(2,1)S(1)}, bf16[128,1024]{1,0:T(8,128)(2,1)S(1)}, u32[]{:S(2)}, u32[]{:S(2)}) collective-permute-start(bf16[128,1024]{1,0:T(8,128)(2,1)S(1)} %get-tuple-element.21), channel_id=1, source_target_pairs={{0,16},{8,24},{1,17},{9,25},{2,18},{10,26},{3,19},{11,27},{4,20},{... | collective-permute-start | bytes 786440 | tf_op jit(solution)/shard_map/ppermute | solution.py:659
  76.3 28.9 %collective-permute-start.7 = (bf16[128,1024]{1,0:T(8,128)(2,1)S(1)}, bf16[128,1024]{1,0:T(8,128)(2,1)S(1)}, u32[]{:S(2)}, u32[]{:S(2)}) collective-permute-start(bf16[128,1024]{1,0:T(8,128)(2,1)S(1)} %turn_stage.1), channel_id=1, source_target_pairs={{16,0},{24,8},{17,1},{25,9},{18,2},{26,10},{19,3},{27,11},{20,4},{... | collective-permute-start | bytes 786440 | tf_op jit(solution)/shard_map/ppermute | solution.py:659
  105.2 21.7 %copy-start.2 = (bf16[16,512,128]{2,1,0:T(8,128)(2,1)S(1)}, bf16[16,512,128]{2,1,0:T(8,128)(2,1)}, u32[]{:S(2)}) copy-start(bf16[16,512,128]{2,1,0:T(8,128)(2,1)} %spread_weights.3.spread_ref) | copy-start | bytes 6291460
  123.0 23.2 %copy-start.1 = (bf16[16,512,128]{2,1,0:T(8,128)(2,1)S(1)}, bf16[16,512,128]{2,1,0:T(8,128)(2,1)}, u32[]{:S(2)}) copy-start(bf16[16,512,128]{2,1,0:T(8,128)(2,1)} %spread_weights.2.spread_ref) | copy-start | bytes 6291460
  123.0 3.9 %collective-permute-start.8 = (bf16[64,1024]{1,0:T(8,128)(2,1)S(1)}, bf16[64,1024]{1,0:T(8,128)(2,1)S(1)}, u32[]{:S(2)}, u32[]{:S(2)}) collective-permute-start(bf16[64,1024]{1,0:T(8,128)(2,1)S(1)} %slice.8), channel_id=1, source_target_pairs={{0,16},{8,24},{1,17},{9,25},{2,18},{10,26},{3,19},{11,27},{4,20},{... | collective-permute-start | bytes 393224 | tf_op jit(solution)/shard_map/ppermute | solution.py:659
  128.3 0.8 copy-start.8
  129.1 19.6 %all-to-all-start.2 = ((bf16[16,128,128]{2,1,0:T(8,128)(2,1)}), bf16[16,128,128]{2,1,0:T(8,128)(2,1)S(1)}, u32[]{:S(2)}, u32[]{:S(2)}) async-start(bf16[16,128,128]{2,1,0:T(8,128)(2,1)} %copy-done.8), calls=%async_computation.2 | async-start | bytes 1048576 | tf_op jit(solution)/shard_map/all_to_all | solution.py:674
  136.6 21.8 %copy-start.13 = (s32[1,32]{1,0:T(1,128)S(1)}, s32[1,32]{1,0:T(1,128)}, u32[]{:S(2)}) copy-start(s32[1,32]{1,0:T(1,128)} %param.19) | copy-start | bytes 388
  136.6 9.5 %collective-permute-start.9 = (bf16[64,1024]{1,0:T(8,128)(2,1)S(1)}, bf16[64,1024]{1,0:T(8,128)(2,1)S(1)}, u32[]{:S(2)}, u32[]{:S(2)}) collective-permute-start(bf16[64,1024]{1,0:T(8,128)(2,1)S(1)} %slice_select_fusion.grad_ref), channel_id=1, source_target_pairs={{0,4},{1,5},{2,6},{3,7},{4,0},{5,1},{6,2},{7,3},{8,12},{9,13},{10,... | collective-permute-start | bytes 393224 | tf_op jit(solution)/shard_map/ppermute | solution.py:664
  147.5 0.8 copy-start.7
  148.7 0.8 copy-start.5
  149.5 17.6 %all-to-all-start.3 = ((bf16[16,128,128]{2,1,0:T(8,128)(2,1)}), bf16[16,128,128]{2,1,0:T(8,128)(2,1)S(1)}, u32[]{:S(2)}, u32[]{:S(2)}) async-start(bf16[16,128,128]{2,1,0:T(8,128)(2,1)} %copy-done.7), calls=%async_computation.3 | async-start | bytes 1048576 | tf_op jit(solution)/shard_map/all_to_all | solution.py:674
  159.5 1.1 copy-start.6

commit v7 on v6

--- a/solution.py
+++ b/solution.py
@@ -109,17 +109,14 @@
     )(codes, lcb_weight)
 
 
-def compress(spread, fetched, embed_count, others=None):
+def compress(spread, fetched, view, embed_count, kind):
     owners, lines, cap = spread.shape
-    width = fetched.shape[2]
+    width = fetched.shape[3]
     samples = lines // embed_count
     part = tiles_of(owners, 4)
     steps = owners // part
-    extra = [] if others is None else [others]
-
-    def kernel(spread_ref, rows_ref, *refs):
-        other_refs, (out_ref, held, total, sems) = refs[: len(extra)], refs[len(extra) :]
-
+
+    def kernel(spread_ref, rows_ref, out_ref, held, total, sems):
         def copy(step):
             piece = tile_at(step, part)
             return pltpu.make_async_copy(spread_ref.at[piece], held.at[piece], sems.at[step])
@@ -132,7 +129,7 @@
             copy(step).wait()
             first = step * part
             left = jnp.concatenate([held[first + o] for o in range(part)], axis=1)
-            right = rows_ref[tile_at(step, part)].reshape(part * cap, width)
+            right = jnp.concatenate([rows_ref[first + o, view] for o in range(part)], axis=0)
             total[...] += jnp.dot(left, right, preferred_element_type=jnp.float32)
             return carry
 
@@ -140,14 +137,12 @@
         for k in range(embed_count):
             columns = slice(k * width, (k + 1) * width)
             piece = total[pl.ds(k, samples, stride=embed_count), :]
-            for other in other_refs:
-                piece = piece + other[:, columns].astype(jnp.float32)
             out_ref[:, columns] = piece.astype(out_ref.dtype)
 
     return pl.pallas_call(
         kernel,
-        out_shape=jax.ShapeDtypeStruct((samples, embed_count * width), jnp.bfloat16),
-        in_specs=[whole(pltpu.HBM), whole()] + [whole()] * len(extra),
+        out_shape=jax.ShapeDtypeStruct((samples, embed_count * width), kind),
+        in_specs=[whole(pltpu.HBM), whole()],
         out_specs=whole(),
         scratch_shapes=[
             pltpu.VMEM(spread.shape, jnp.bfloat16),
@@ -156,16 +151,18 @@
         ],
         compiler_params=params(),
         name="compress",
-    )(in_hbm(spread), fetched, *extra)
-
-
-def expand(spread, lead_grad, embed_count):
+    )(in_hbm(spread), fetched)
+
+
+def expand(spread, lead_grad, embed_count, near=None):
     owners, lines, cap = spread.shape
     samples = lines // embed_count
     width = lead_grad.shape[1] // embed_count
     part = tiles_of(owners, 4)
-
-    def kernel(spread_ref, grad_ref, out_ref, tall, turned):
+    extra = [] if near is None else [near]
+
+    def kernel(spread_ref, grad_ref, *refs):
+        near_refs, (out_ref, tall, turned) = refs[: len(extra)], refs[len(extra) :]
         for k in range(embed_count):
             piece = grad_ref[:, k * width : (k + 1) * width].astype(jnp.float32)
             tall[pl.ds(k, samples, stride=embed_count), :] = piece
@@ -176,15 +173,21 @@
             right = jnp.concatenate([spread_ref[first + o] for o in range(part)], axis=1)
             term = jnp.dot(turned[...], right, preferred_element_type=jnp.float32)
             piece = term.T.astype(out_ref.dtype).reshape(part, cap, width)
-            out_ref[tile_at(step, part)] = piece
+            if near_refs:
+                for o in range(part):
+                    out_ref[first + o, 0] = near_refs[0][first + o]
+                    out_ref[first + o, 1] = piece[o]
+            else:
+                out_ref[tile_at(step, part)] = piece
             return carry
 
         lax.fori_loop(0, owners // part, body, 0)
 
+    views = () if near is None else (2,)
     return pl.pallas_call(
         kernel,
-        out_shape=jax.ShapeDtypeStruct((owners, cap, width), jnp.bfloat16),
-        in_specs=[whole(), whole()],
+        out_shape=jax.ShapeDtypeStruct((owners,) + views + (cap, width), jnp.bfloat16),
+        in_specs=[whole()] * (2 + len(extra)),
         out_specs=whole(),
         scratch_shapes=[
             pltpu.VMEM((lines, width), jnp.float32),
@@ -192,32 +195,26 @@
         ],
         compiler_params=params(),
         name="expand",
-    )(spread, lead_grad)
-
-
-def add_rows(targets, returned, outgoing, rows, base=None):
+    )(spread, lead_grad, *extra)
+
+
+def add_rows(targets, returned, outgoing, rows):
     count, width = returned.shape
     chunk = min(count, 1024)
-    is_last = base is not None
-
-    def kernel(targets_ref, back_ref, sent_ref, *refs):
-        if is_last:
-            base_ref, out_ref, terms, total, done = refs
-            total[...] = base_ref[...]
-        else:
-            total, terms = refs
-            total[...] = jnp.zeros_like(total)
+
+    def kernel(targets_ref, back_ref, sent_ref, out_ref, total, terms, done):
+        total[...] = jnp.zeros_like(total)
 
         def fill(part, carry):
-            first_line = pl.multiple_of(part * chunk, chunk)
-            lines = pl.ds(first_line, chunk)
+            base = pl.multiple_of(part * chunk, chunk)
+            lines = pl.ds(base, chunk)
             terms[...] = back_ref[lines, :].astype(jnp.float32) + DECAY_WEIGHT * sent_ref[
                 lines, :
             ].astype(jnp.float32)
 
             def body(group, inner):
                 first = pl.multiple_of(group * UNROLL, UNROLL)
-                places = [targets_ref[first_line + first + lane] for lane in range(UNROLL)]
+                places = [targets_ref[base + first + lane] for lane in range(UNROLL)]
                 sums = [
                     total[pl.ds(places[lane], 1), :] + terms[pl.ds(first + lane, 1), :]
                     for lane in range(UNROLL)
@@ -230,27 +227,26 @@
             return carry
 
         lax.fori_loop(0, count // chunk, fill, 0)
-        if is_last:
-            copy = pltpu.make_async_copy(total.at[pl.ds(0, rows), :], out_ref, done)
-            copy.start()
-            copy.wait()
-
-    tall = (rows + 8, width)
-    scratch = [pltpu.VMEM((chunk, width), jnp.float32)]
-    if is_last:
-        scratch += [pltpu.VMEM(tall, jnp.float32), pltpu.SemaphoreType.DMA]
+        copy = pltpu.make_async_copy(total.at[pl.ds(0, rows), :], out_ref, done)
+        copy.start()
+        copy.wait()
+
     return pl.pallas_call(
         kernel,
-        out_shape=jax.ShapeDtypeStruct((rows, width) if is_last else tall, jnp.float32),
-        in_specs=[whole(pltpu.SMEM), whole(), whole()] + [whole()] * is_last,
-        out_specs=whole(pl.ANY) if is_last else whole(),
-        scratch_shapes=scratch,
+        out_shape=jax.ShapeDtypeStruct((rows, width), jnp.float32),
+        in_specs=[whole(pltpu.SMEM), whole(), whole()],
+        out_specs=whole(pl.ANY),
+        scratch_shapes=[
+            pltpu.VMEM((rows + 8, width), jnp.float32),
+            pltpu.VMEM((chunk, width), jnp.float32),
+            pltpu.SemaphoreType.DMA,
+        ],
         compiler_params=params(),
         name="add_rows",
-    )(targets, returned, outgoing, *([base] if is_last else []))
-
-
-GROUP = 32
+    )(targets, returned, outgoing)
+
+
+GROUP = 16
 TABLE_AXES = ("section", "table")
 STAGE_LIMIT = 44 * 1024 * 1024
 NT = (((1,), (1,)), ((), ()))
@@ -567,7 +563,7 @@
                 stream.start()
             mix_forward(small_ref, 0, acts_ref, inter.at[0], scale.at[0], normed, count)
             up_product(normed, up0.held, hidden, hid, up0.wait)
-            down_product(hidden, down0.held, acts_ref, upper, down0.wait, 2)
+            down_product(hidden, down0.held, acts_ref, upper, down0.wait)
             mix_forward(small_ref, 1, upper, inter.at[1], scale.at[1], normed, count)
 
             def masked(columns):
@@ -575,12 +571,12 @@
                 opened = jnp.maximum(before, 0.0).T
                 g_before[columns, :] = opened_only(opened, ghid_ref[columns, :].astype(jnp.float32))
 
-            over_tiles(hidden_width, hidden_tile(hidden_width), 2, up1.wait, masked)
-            up_back(g_before, up1.held, weighted, no_wait, 2)
+            over_tiles(hidden_width, hidden_tile(hidden_width), 1, up1.wait, masked)
+            up_back(g_before, up1.held, weighted, no_wait)
             mix_backward(small_ref, 1, top_ref, upper, inter.at[1], scale.at[1], weighted, grad, count)
             turn(grad, turned)
-            down_back(turned, down0.held, hid, g_before, no_wait, 2)
-            up_back(g_before, up0.held, weighted, no_wait, 2)
+            down_back(turned, down0.held, hid, g_before, no_wait)
+            up_back(g_before, up0.held, weighted, no_wait)
             mix_backward(small_ref, 0, grad, acts_ref, inter.at[0], scale.at[0], weighted, out_ref, count)
 
     return pl.pallas_call(
@@ -625,8 +621,8 @@
             for layer, given, to in ((1, grad_ref, middle), (0, middle, out_ref)):
                 up, down = layers[layer]
                 turn(given, turned)
-                down_back(turned, down.held, hid.at[layer], g_before, down.wait, 2 - layer)
-                up_back(g_before, up.held, weighted, up.wait, 2)
+                down_back(turned, down.held, hid.at[layer], g_before, down.wait)
+                up_back(g_before, up.held, weighted, up.wait)
                 mix_backward(
                     small_ref, layer, given, kept.at[layer], inter.at[layer], scale.at[layer],
                     weighted, to, count,
@@ -676,12 +672,13 @@
     )
 
 
-def by_half(per_asker, half_at):
+def near_first(per_asker, my_half):
     sections = lax.axis_size("section")
     half = lax.axis_size("table") // 2
     split = per_asker.reshape((sections, 2, half) + per_asker.shape[1:])
-    chosen = lax.dynamic_index_in_dim(split, half_at, 1, keepdims=False)
-    return chosen.reshape((sections * half,) + per_asker.shape[1:])
+    near = lax.dynamic_index_in_dim(split, my_half, 1, keepdims=False)
+    far = lax.dynamic_index_in_dim(split, 1 - my_half, 1, keepdims=False)
+    return jnp.stack([near, far], axis=2).reshape((sections * half, 2) + per_asker.shape[1:])
 
 
 def after(value, earlier):
@@ -721,13 +718,10 @@
     other_down = swapped(w_down[0], section_count)
     other_small = swapped(small, section_count)
 
-    picked_far = by_half(wanted_rows[0], 1 - my_half)
-    picked_near = by_half(wanted_rows[0], my_half)
-    sent_far = pick_rows(emb_table, picked_far.reshape(-1))
-    line_shape = (near_owners, cap, embed_width)
-    fetched_far = swap_in_half(after(sent_far, mirror_slots).reshape(line_shape))
-    sent_near = pick_rows(emb_table, after(picked_near, sent_far).reshape(-1))
-    fetched_near = swap_in_half(after(sent_near, fetched_far).reshape(line_shape))
+    picked = near_first(wanted_rows[0], my_half)
+    outgoing = pick_rows(emb_table, picked.reshape(-1))
+    sent = after(outgoing, mirror_slots).reshape(near_owners, 2, cap, embed_width)
+    fetched = swap_in_half(sent)
 
     def spread_of(slots):
         owner, column = slots // cap, slots % cap
@@ -736,13 +730,15 @@
         return spread_weights(near * cap + column, lcb_weight, near_owners, cap)
 
     spread_far = spread_of(mirror_slots)
-    spread_near = spread_of(after(own_slots, fetched_far))
+    spread_near = spread_of(own_slots)
     smalls = jnp.stack(
         [jnp.where(core == 0, small, other_small), jnp.where(core == 0, other_small, small)]
     )
     weights = [smalls, w_up[0], other_up, w_down[0], other_down]
-    far_part = mirror(compress(spread_far, fetched_far, embed_count))
-    lead = compress(spread_near, fetched_near, embed_count, far_part)
+    spread_far, spread_near = lax.optimization_barrier((spread_far, spread_near))
+    far_part = mirror(compress(spread_far, fetched, 1, embed_count, jnp.bfloat16))
+    near_part = compress(spread_near, fetched, 0, embed_count, jnp.float32)
+    lead = (near_part + far_part.astype(jnp.float32)).astype(jnp.bfloat16)
     pieces = [lead] + [moved(lead, s, 0) for s in range(1, stages)]
     top = top_grad.reshape(stages, 2, look_dev, model_width)
     top = lax.dynamic_index_in_dim(top, core, 1, keepdims=False).reshape(-1, model_width)
@@ -770,23 +766,12 @@
         own_grad = jnp.where(stage == s, moved(piece, 0, s), own_grad)
     mirror_grad = mirror(own_grad)
 
-    def targets_of(picked, half_at):
-        live_slots = jnp.arange(cap) < by_half(row_counts[0], half_at)[:, None]
-        return jnp.where(live_slots, picked, rows).reshape(-1)
-
     near_grad = expand(spread_near, own_grad, embed_count)
-    returned_near = swap_in_half(near_grad)
-    far_grad = expand(spread_far, mirror_grad, embed_count)
-    returned_far = swap_in_half(after(far_grad, returned_near))
-    summed = add_rows(
-        targets_of(picked_near, my_half),
-        after(returned_near, far_grad).reshape(-1, embed_width),
-        sent_near,
-        rows,
-    )
-    return add_rows(
-        targets_of(picked_far, 1 - my_half), returned_far.reshape(-1, embed_width), sent_far, rows, summed
-    )
+    slot_grad = expand(spread_far, mirror_grad, embed_count, near_grad)
+    returned = swap_in_half(slot_grad)
+    live_slots = jnp.arange(cap) < near_first(row_counts[0], my_half)[..., None]
+    targets = jnp.where(live_slots, picked, rows).reshape(-1)
+    return add_rows(targets, returned.reshape(-1, embed_width), outgoing, rows)
 
 
 def solution(mesh):

time: 175 us -> 157 us (0.90)
  starting transfers between devices: 42.8 us -> 23.8 us
  waiting for transfers between devices: 56.5 us -> 63.7 us
  Pallas kernels: 66.1 us -> 61.3 us
  local copies, waits for them, and re-layouts: 6.31 us -> 3.59 us
  other arithmetic: 1.77 us -> 4 us
    all_to_all x4 -> x2, starting transfers between devices: 26.2 us -> 11.9 us  [swap_in_half(): lax.all_to_all(value, TABLE_AXES, split_axis=0, concat_axis=0, axis_index...]
    all_to_all x4 -> x2, waiting for transfers between devices: 7.3 us -> 16 us  [swap_in_half(): lax.all_to_all(value, TABLE_AXES, split_axis=0, concat_axis=0, axis_index...]
    ppermute x3, starting transfers between devices: 10.2 us -> 5.68 us  [mirror(): lax.ppermute(value, 'table', [(t, (t + along // 2) % along) for t in rang...]
    unnamed x29 -> x17, local copies, waits for them, and re-layouts: 5.29 us -> 2.49 us
    pallas_call x1, Pallas kernels: 17.7 us -> 15.5 us  [backward_stage(): pl.pallas_call(kernel, out_shape=jax.ShapeDtypeStruct(grad.shape, jnp.bfl...]
    pallas_call x2 -> x1, Pallas kernels: 7.09 us -> 5.8 us  [pick_rows(): pl.pallas_call(kernel, out_shape=jax.ShapeDtypeStruct((count, width), emb...]
    pallas_call x4 -> x3, Pallas kernels: 15.3 us -> 14.5 us  [the longest x1 10.8 us: add_rows(): pl.pallas_call(kernel, out_shape=jax.ShapeDtypeStruct((rows, width), jnp....]
  transfers between devices with their start and end apart: 14 -> 12, of which waited for: 10 -> 8; matrix products, arithmetic and copies ran while one was open for 2% -> 4% of each run, Pallas kernels for 16% -> 12%
where the time goes in v7:
time: 157 us
  waiting for transfers between devices  63.7 us (41%)
  Pallas kernels  61.3 us (39%)
  starting transfers between devices  23.8 us (15%)
  other arithmetic  4 us (3%)
  local copies, waits for them, and re-layouts  3.59 us (2%)
    ppermute x4, waiting for transfers between devices, moved(): return lax.ppermute(value, 'section', pairs)  38.3 us
    all_to_all x2, waiting for transfers between devices, swap_in_half(): lax.all_to_all(value, TABLE_AXES, split_axis=0, concat_axis=0, axis_index...  16 us
    pallas_call x1, Pallas kernels, backward_stage(): pl.pallas_call(kernel, out_shape=jax.ShapeDtypeStruct(grad.shape, jnp.bfl...  15.5 us
    pallas_call x1, Pallas kernels, forward_stage(): pl.pallas_call(kernel, out_shape=[jax.ShapeDtypeStruct(top.shape, jnp.bfl...  12.2 us
    all_to_all x2, starting transfers between devices, swap_in_half(): lax.all_to_all(value, TABLE_AXES, split_axis=0, concat_axis=0, axis_index...  11.9 us
    pallas_call x1, Pallas kernels, add_rows(): pl.pallas_call(kernel, out_shape=jax.ShapeDtypeStruct((rows, width), jnp....  10.8 us
    ppermute x3, waiting for transfers between devices, mirror(): lax.ppermute(value, 'table', [(t, (t + along // 2) % along) for t in rang...  9.37 us
    pallas_call x2, Pallas kernels, spread_weights(): pl.pallas_call(kernel, out_shape=pltpu.HBM((owners, samples * embed_count...  7.77 us
  transfers between devices with their start and end apart: 12, of which 8 were waited for; matrix products, arithmetic and copies ran while one was open for 4% of the time, Pallas kernels for 12%

profile of v7, /device:TPU:0, one launch (start us, length us, event | category | flops | bytes accessed | tf_op | source)
XLA Modules:
  0.0 156.7 jit_solution(13378746452098703083)
XLA Ops:
  0.5 4.0 %collective-permute-start = (s32[64,512]{1,0:T(8,128)}, s32[64,512]{1,0:T(8,128)S(1)}, u32[]{:S(2)}, u32[]{:S(2)}) collective-permute-start(s32[64,512]{1,0:T(8,128)} %bitcast.41), channel_id=1, source_target_pairs={{0,4},{1,5},{2,6},{3,7},{4,0},{5,1},{6,2},{7,3},{8,12},{9,13},{10,... | collective-permute-start | bytes 393224 | tf_op jit(solution)/shard_map/ppermute | solution.py:660
  4.6 0.7 constant_dynamic-slice_fusion.2
  5.3 1.2 copy-done.3
  6.5 5.8 %pick_rows.1.sent_ref = bf16[4096,128]{1,0:T(8,128)(2,1)} custom-call(s32[4096]{0:T(1024)S(1)} %bitcast.32, bf16[4096,128]{1,0:T(8,128)(2,1)S(1)} %copy-done.3), custom_call_target="tpu_custom_call" | custom-call | tf_op jit(solution)/shard_map/pick_rows/pallas_call | solution.py:54
  12.3 4.8 %all-to-all-start = ((bf16[16,2,128,128]{3,2,1,0:T(8,128)(2,1)}), bf16[16,2,128,128]{3,2,1,0:T(8,128)(2,1)S(1)}, u32[]{:S(2)}, u32[]{:S(2)}) async-start(bf16[16,2,128,128]{3,2,1,0:T(8,128)(2,1)} %bitcast.12), calls=%async_computation | async-start | bytes 2097152 | tf_op jit(solution)/shard_map/all_to_all | solution.py:670
  17.2 0.7 reduce.3
  19.0 1.3 fusion.11.codes_ref
  20.3 0.7 copy-done.4
  21.0 3.9 %spread_weights.3.spread_ref = bf16[16,512,128]{2,1,0:T(8,128)(2,1)} custom-call(s32[64,512]{1,0:T(8,128)S(1)} %fusion.11.codes_ref, bf16[8,512]{1,0:T(8,128)(2,1)S(1)} %copy-done.4), custom_call_target="tpu_custom_call" | custom-call | flops 1073741824 | bytes 2097152 | tf_op jit(solution)/shard_map/spread_weights/pallas_call | solution.py:93
  25.2 3.9 %spread_weights.2.spread_ref = bf16[16,512,128]{2,1,0:T(8,128)(2,1)} custom-call(s32[64,512]{1,0:T(8,128)S(1)} %fusion.5.codes_ref, bf16[8,512]{1,0:T(8,128)(2,1)S(1)} %copy-done.5), custom_call_target="tpu_custom_call" | custom-call | flops 1073741824 | bytes 2097152 | tf_op jit(solution)/shard_map/spread_weights/pallas_call | solution.py:93
  29.1 2.9 %all-to-all-done.rows_ref = bf16[16,2,128,128]{3,2,1,0:T(8,128)(2,1)S(1)} async-done(((bf16[16,2,128,128]{3,2,1,0:T(8,128)(2,1)}), bf16[16,2,128,128]{3,2,1,0:T(8,128)(2,1)S(1)}, u32[]{:S(2)}, u32[]{:S(2)}) %all-to-all-start) | async-done | bytes 1048608 | tf_op jit(solution)/shard_map/all_to_all | solution.py:670
  32.0 2.3 %compress.3 = bf16[64,1024]{1,0:T(8,128)(2,1)S(1)} custom-call(bf16[16,512,128]{2,1,0:T(8,128)(2,1)} %spread_weights.2.spread_ref, bf16[16,2,128,128]{3,2,1,0:T(8,128)(2,1)S(1)} %all-to-all-done.rows_ref), custom_call_target="tpu_custom_call" | custom-call | tf_op jit(solution)/shard_map/compress/pallas_call | solution.py:142
  34.3 1.6 %collective-permute-start.1 = (bf16[64,1024]{1,0:T(8,128)(2,1)S(1)}, bf16[64,1024]{1,0:T(8,128)(2,1)S(1)}, u32[]{:S(2)}, u32[]{:S(2)}) collective-permute-start(bf16[64,1024]{1,0:T(8,128)(2,1)S(1)} %compress.3), channel_id=1, source_target_pairs={{0,4},{1,5},{2,6},{3,7},{4,0},{5,1},{6,2},{7,3},{8,12},{9,13},{10,... | collective-permute-start | bytes 393224 | tf_op jit(solution)/shard_map/ppermute | solution.py:660
  36.0 2.3 %compress.2 = f32[64,1024]{1,0:T(8,128)S(1)} custom-call(bf16[16,512,128]{2,1,0:T(8,128)(2,1)} %spread_weights.3.spread_ref, bf16[16,2,128,128]{3,2,1,0:T(8,128)(2,1)S(1)} %all-to-all-done.rows_ref), custom_call_target="tpu_custom_call" | custom-call | tf_op jit(solution)/shard_map/compress/pallas_call | solution.py:142
  38.3 4.9 %collective-permute-done.1 = bf16[64,1024]{1,0:T(8,128)(2,1)S(1)} collective-permute-done((bf16[64,1024]{1,0:T(8,128)(2,1)S(1)}, bf16[64,1024]{1,0:T(8,128)(2,1)S(1)}, u32[]{:S(2)}, u32[]{:S(2)}) %collective-permute-start.1) | collective-permute-done | bytes 131104 | tf_op jit(solution)/shard_map/ppermute | solution.py:660
  43.3 1.3 collective-permute-start.2
  44.6 5.5 %collective-permute-done.2.refs_1_ = bf16[64,1024]{1,0:T(8,128)(2,1)S(1)} collective-permute-done((bf16[64,1024]{1,0:T(8,128)(2,1)S(1)}, bf16[64,1024]{1,0:T(8,128)(2,1)S(1)}, u32[]{:S(2)}, u32[]{:S(2)}) %collective-permute-start.2) | collective-permute-done | bytes 131104 | tf_op jit(solution)/shard_map/ppermute | solution.py:655
  50.1 12.2 %forward_stage.1 = (bf16[128,1024]{1,0:T(8,128)(2,1)S(1)}, bf16[2,4096,128]{2,1,0:T(8,128)(2,1)S(1)}, f32[2,128,1024]{2,1,0:T(8,128)S(1)}, f32[2,128,128]{2,1,0:...) custom-call(s32[3]{0:T(128)S(1)} %pad_add_fusion.2.place_ref, ...), custom_call_target="tpu_custom_call" | custom-call | flops 4294967296 | bytes 1048576 | tf_op jit(solution)/shard_map/forward_stage/pallas_call | solution.py:528
  62.3 1.3 collective-permute-start.6
  63.7 4.1 %collective-permute-done.6.acts_ref = bf16[128,1024]{1,0:T(8,128)(2,1)S(1)} collective-permute-done((bf16[128,1024]{1,0:T(8,128)(2,1)S(1)}, bf16[128,1024]{1,0:T(8,128)(2,1)S(1)}, u32[]{:S(2)}, u32[]{:S(2)}) %collective-permute-start.6) | collective-permute-done | bytes 262176 | tf_op jit(solution)/shard_map/ppermute | solution.py:655
  67.8 0.9 turn_stage.1
  68.7 1.3 collective-permute-start.7
  70.0 26.2 %collective-permute-done.7.grad_ref = bf16[128,1024]{1,0:T(8,128)(2,1)S(1)} collective-permute-done((bf16[128,1024]{1,0:T(8,128)(2,1)S(1)}, bf16[128,1024]{1,0:T(8,128)(2,1)S(1)}, u32[]{:S(2)}, u32[]{:S(2)}) %collective-permute-start.7) | collective-permute-done | bytes 262176 | tf_op jit(solution)/shard_map/ppermute | solution.py:655
  96.2 15.5 %backward_stage.1 = bf16[128,1024]{1,0:T(8,128)(2,1)S(1)} custom-call(s32[3]{0:T(128)S(1)} %pad_add_fusion.2.place_ref, bf16[128,1024]{1,0:T(8,128)(2,1)S(1)} %collective-permute-done.7.grad_ref, bf16[2,4096,128]{2,1,0:T(8,128)(2,1)S(1)} %get-tuple-element.19.hid, f32[2,128,1024]{2,1,0:T(8,128)S(1)} %get-tuple-element.20.inter, ...), custom_call_target="tpu_custom_call" | custom-call | flops 4294967296 | bytes 1048576 | tf_op jit(solution)/shard_map/backward_stage/pallas_call | solution.py:631
  111.8 1.3 collective-permute-start.8
  113.1 2.5 %collective-permute-done.8 = bf16[64,1024]{1,0:T(8,128)(2,1)S(1)} collective-permute-done((bf16[64,1024]{1,0:T(8,128)(2,1)S(1)}, bf16[64,1024]{1,0:T(8,128)(2,1)S(1)}, u32[]{:S(2)}, u32[]{:S(2)}) %collective-permute-start.8) | collective-permute-done | bytes 131104 | tf_op jit(solution)/shard_map/ppermute | solution.py:655
  115.7 1.4 expand.2.refs_0_
  117.0 4.5 %collective-permute-done.9.grad_ref = bf16[64,1024]{1,0:T(8,128)(2,1)S(1)} collective-permute-done((bf16[64,1024]{1,0:T(8,128)(2,1)S(1)}, bf16[64,1024]{1,0:T(8,128)(2,1)S(1)}, u32[]{:S(2)}, u32[]{:S(2)}) %collective-permute-start.9) | collective-permute-done | bytes 131104 | tf_op jit(solution)/shard_map/ppermute | solution.py:660
  121.5 2.4 %expand.3 = bf16[16,2,128,128]{3,2,1,0:T(8,128)(2,1)} custom-call(bf16[16,512,128]{2,1,0:T(8,128)(2,1)S(1)} %copy-done.1, bf16[64,1024]{1,0:T(8,128)(2,1)S(1)} %collective-permute-done.9.grad_ref, bf16[16,128,128]{2,1,0:T(8,128)(2,1)S(1)} %expand.2.refs_0_), custom_call_target="tpu_custom_call" | custom-call | tf_op jit(solution)/shard_map/expand/pallas_call | solution.py:187
  123.9 7.1 %all-to-all-start.1 = ((bf16[16,2,128,128]{3,2,1,0:T(8,128)(2,1)}), bf16[16,2,128,128]{3,2,1,0:T(8,128)(2,1)S(1)}, u32[]{:S(2)}, u32[]{:S(2)}) async-start(bf16[16,2,128,128]{3,2,1,0:T(8,128)(2,1)} %expand.3), calls=%async_computation.1 | async-start | bytes 2097152 | tf_op jit(solution)/shard_map/all_to_all | solution.py:670
  132.7 13.1 %all-to-all-done.1 = bf16[16,2,128,128]{3,2,1,0:T(8,128)(2,1)S(1)} async-done(((bf16[16,2,128,128]{3,2,1,0:T(8,128)(2,1)}), bf16[16,2,128,128]{3,2,1,0:T(8,128)(2,1)S(1)}, u32[]{:S(2)}, u32[]{:S(2)}) %all-to-all-start.1) | async-done | bytes 1048608 | tf_op jit(solution)/shard_map/all_to_all | solution.py:670
  145.8 10.8 %add_rows.1 = f32[4096,128]{1,0:T(8,128)} custom-call(s32[4096]{0:T(1024)S(1)} %bitcast.31, bf16[4096,128]{1,0:T(8,128)(2,1)S(1)} %bitcast.28, bf16[4096,128]{1,0:T(8,128)(2,1)} %pick_rows.1.sent_ref), custom_call_target="tpu_custom_call" | custom-call | tf_op jit(solution)/shard_map/add_rows/pallas_call | solution.py:234
  (42 shorter events, 4.0 us)
Async XLA Ops:
  0.0 36.0 %copy-start = (bf16[1,4,64,1024]{3,2,1,0:T(8,128)(2,1)S(1)}, bf16[1,4,64,1024]{3,2,1,0:T(8,128)(2,1)}, u32[]{:S(2)}) copy-start(bf16[1,4,64,1024]{3,2,1,0:T(8,128)(2,1)} %param.16) | copy-start | bytes 1572868
  0.0 25.2 %copy-start.5 = (bf16[8,512]{1,0:T(8,128)(2,1)S(1)}, bf16[8,512]{1,0:T(8,128)(2,1)}, u32[]{:S(2)}) copy-start(bf16[8,512]{1,0:T(8,128)(2,1)} %lcb_ref.3) | copy-start | bytes 24580
  0.0 50.1 %collective-permute-start.4 = (bf16[1024,4096]{1,0:T(8,128)(2,1)}, bf16[1024,4096]{1,0:T(8,128)(2,1)}, u32[]{:S(2)}, u32[]{:S(2)}) collective-permute-start(bf16[1024,4096]{1,0:T(8,128)(2,1)} %bitcast.33), channel_id=1, source_target_pairs={{0,8},{8,0},{16,24},{24,16},{1,9},{9,1},{17,25},{25,17},{2,10},{10... | collective-permute-start | bytes 25165832 | tf_op jit(solution)/shard_map/ppermute | solution.py:650
  0.5 49.7 %collective-permute-start.5 = (bf16[4096,1024]{1,0:T(8,128)(2,1)}, bf16[4096,1024]{1,0:T(8,128)(2,1)}, u32[]{:S(2)}, u32[]{:S(2)}) collective-permute-start(bf16[4096,1024]{1,0:T(8,128)(2,1)} %bitcast.37), channel_id=1, source_target_pairs={{0,8},{8,0},{16,24},{24,16},{1,9},{9,1},{17,25},{25,17},{2,10},{10... | collective-permute-start | bytes 25165832 | tf_op jit(solution)/shard_map/ppermute | solution.py:650
  0.5 11.8 %collective-permute-start = (s32[64,512]{1,0:T(8,128)}, s32[64,512]{1,0:T(8,128)S(1)}, u32[]{:S(2)}, u32[]{:S(2)}) collective-permute-start(s32[64,512]{1,0:T(8,128)} %bitcast.41), channel_id=1, source_target_pairs={{0,4},{1,5},{2,6},{3,7},{4,0},{5,1},{6,2},{7,3},{8,12},{9,13},{10,... | collective-permute-start | bytes 393224 | tf_op jit(solution)/shard_map/ppermute | solution.py:660
  5.3 1.2 copy-start.3
  12.3 19.7 %all-to-all-start = ((bf16[16,2,128,128]{3,2,1,0:T(8,128)(2,1)}), bf16[16,2,128,128]{3,2,1,0:T(8,128)(2,1)S(1)}, u32[]{:S(2)}, u32[]{:S(2)}) async-start(bf16[16,2,128,128]{3,2,1,0:T(8,128)(2,1)} %bitcast.12), calls=%async_computation | async-start | bytes 2097152 | tf_op jit(solution)/shard_map/all_to_all | solution.py:670
  17.2 27.4 %copy-start.6 = (bf16[1,8,128]{2,1,0:T(8,128)(2,1)S(1)}, bf16[1,8,128]{2,1,0:T(8,128)(2,1)}, u32[]{:S(2)}) copy-start(bf16[1,8,128]{2,1,0:T(8,128)(2,1)} %param.12) | copy-start | bytes 6148
  18.6 26.0 %collective-permute-start.3 = (bf16[16,128]{1,0:T(8,128)(2,1)S(1)}, bf16[16,128]{1,0:T(8,128)(2,1)S(1)}, u32[]{:S(2)}, u32[]{:S(2)}) collective-permute-start(bf16[16,128]{1,0:T(8,128)(2,1)S(1)} %pad_maximum_fusion.1), channel_id=1, source_target_pairs={{0,8},{8,0},{16,24},{24,16},{1,9},{9,1},{17,25},{25,17},{2,10},{10... | collective-permute-start | bytes 12296 | tf_op jit(solution)/shard_map/ppermute | solution.py:650
  20.3 0.7 copy-start.4
  34.3 8.9 %collective-permute-start.1 = (bf16[64,1024]{1,0:T(8,128)(2,1)S(1)}, bf16[64,1024]{1,0:T(8,128)(2,1)S(1)}, u32[]{:S(2)}, u32[]{:S(2)}) collective-permute-start(bf16[64,1024]{1,0:T(8,128)(2,1)S(1)} %compress.3), channel_id=1, source_target_pairs={{0,4},{1,5},{2,6},{3,7},{4,0},{5,1},{6,2},{7,3},{8,12},{9,13},{10,... | collective-permute-start | bytes 393224 | tf_op jit(solution)/shard_map/ppermute | solution.py:660
  43.3 6.9 %collective-permute-start.2 = (bf16[64,1024]{1,0:T(8,128)(2,1)S(1)}, bf16[64,1024]{1,0:T(8,128)(2,1)S(1)}, u32[]{:S(2)}, u32[]{:S(2)}) collective-permute-start(bf16[64,1024]{1,0:T(8,128)(2,1)S(1)} %add_convert_fusion.refs_0_), channel_id=1, source_target_pairs={{16,0},{24,8},{17,1},{25,9},{18,2},{26,10},{19,3},{27,11},{20,4},{... | collective-permute-start | bytes 393224 | tf_op jit(solution)/shard_map/ppermute | solution.py:655
  62.3 5.5 %collective-permute-start.6 = (bf16[128,1024]{1,0:T(8,128)(2,1)S(1)}, bf16[128,1024]{1,0:T(8,128)(2,1)S(1)}, u32[]{:S(2)}, u32[]{:S(2)}) collective-permute-start(bf16[128,1024]{1,0:T(8,128)(2,1)S(1)} %get-tuple-element.17), channel_id=1, source_target_pairs={{0,16},{8,24},{1,17},{9,25},{2,18},{10,26},{3,19},{11,27},{4,20},{... | collective-permute-start | bytes 786440 | tf_op jit(solution)/shard_map/ppermute | solution.py:655
  68.7 27.5 %collective-permute-start.7 = (bf16[128,1024]{1,0:T(8,128)(2,1)S(1)}, bf16[128,1024]{1,0:T(8,128)(2,1)S(1)}, u32[]{:S(2)}, u32[]{:S(2)}) collective-permute-start(bf16[128,1024]{1,0:T(8,128)(2,1)S(1)} %turn_stage.1), channel_id=1, source_target_pairs={{16,0},{24,8},{17,1},{25,9},{18,2},{26,10},{19,3},{27,11},{20,4},{... | collective-permute-start | bytes 786440 | tf_op jit(solution)/shard_map/ppermute | solution.py:655
  96.2 19.4 %copy-start.2 = (bf16[16,512,128]{2,1,0:T(8,128)(2,1)S(1)}, bf16[16,512,128]{2,1,0:T(8,128)(2,1)}, u32[]{:S(2)}) copy-start(bf16[16,512,128]{2,1,0:T(8,128)(2,1)} %spread_weights.3.spread_ref) | copy-start | bytes 6291460
  96.2 25.3 %copy-start.1 = (bf16[16,512,128]{2,1,0:T(8,128)(2,1)S(1)}, bf16[16,512,128]{2,1,0:T(8,128)(2,1)}, u32[]{:S(2)}) copy-start(bf16[16,512,128]{2,1,0:T(8,128)(2,1)} %spread_weights.2.spread_ref) | copy-start | bytes 6291460
  111.7 19.8 %copy-start.7 = (s32[1,32]{1,0:T(1,128)S(1)}, s32[1,32]{1,0:T(1,128)}, u32[]{:S(2)}) copy-start(s32[1,32]{1,0:T(1,128)} %param.19) | copy-start | bytes 388
  111.8 3.8 %collective-permute-start.8 = (bf16[64,1024]{1,0:T(8,128)(2,1)S(1)}, bf16[64,1024]{1,0:T(8,128)(2,1)S(1)}, u32[]{:S(2)}, u32[]{:S(2)}) collective-permute-start(bf16[64,1024]{1,0:T(8,128)(2,1)S(1)} %slice.8), channel_id=1, source_target_pairs={{0,16},{8,24},{1,17},{9,25},{2,18},{10,26},{3,19},{11,27},{4,20},{... | collective-permute-start | bytes 393224 | tf_op jit(solution)/shard_map/ppermute | solution.py:655
  115.6 5.9 %collective-permute-start.9 = (bf16[64,1024]{1,0:T(8,128)(2,1)S(1)}, bf16[64,1024]{1,0:T(8,128)(2,1)S(1)}, u32[]{:S(2)}, u32[]{:S(2)}) collective-permute-start(bf16[64,1024]{1,0:T(8,128)(2,1)S(1)} %slice_select_fusion.grad_ref), channel_id=1, source_target_pairs={{0,4},{1,5},{2,6},{3,7},{4,0},{5,1},{6,2},{7,3},{8,12},{9,13},{10,... | collective-permute-start | bytes 393224 | tf_op jit(solution)/shard_map/ppermute | solution.py:660
  123.9 21.9 %all-to-all-start.1 = ((bf16[16,2,128,128]{3,2,1,0:T(8,128)(2,1)}), bf16[16,2,128,128]{3,2,1,0:T(8,128)(2,1)S(1)}, u32[]{:S(2)}, u32[]{:S(2)}) async-start(bf16[16,2,128,128]{3,2,1,0:T(8,128)(2,1)} %expand.3), calls=%async_computation.1 | async-start | bytes 2097152 | tf_op jit(solution)/shard_map/all_to_all | solution.py:670

commit v8 on v7

--- a/solution.py
+++ b/solution.py
@@ -31,18 +31,16 @@
     rows, width = emb_table.shape
     count = picked.shape[0]
     chunk = min(count, 1024)
-
-    def kernel(picked_ref, table_ref, out_ref, wide, lines):
-        wide[...] = table_ref[...].astype(jnp.float32)
-
+    wide = emb_table.astype(jnp.float32).reshape(rows, 1, width)
+
+    def kernel(picked_ref, wide_ref, out_ref, lines):
         def fill(part, carry):
             base = pl.multiple_of(part * chunk, chunk)
 
             def body(group, inner):
                 first = pl.multiple_of(group * UNROLL, UNROLL)
                 for lane in range(UNROLL):
-                    row = picked_ref[base + first + lane]
-                    lines[pl.ds(first + lane, 1), :] = wide[pl.ds(row, 1), :]
+                    lines[pl.ds(first + lane, 1), :] = wide_ref[picked_ref[base + first + lane]]
                 return inner
 
             lax.fori_loop(0, chunk // UNROLL, body, 0)
@@ -56,13 +54,10 @@
         out_shape=jax.ShapeDtypeStruct((count, width), emb_table.dtype),
         in_specs=[whole(pltpu.SMEM), whole()],
         out_specs=whole(),
-        scratch_shapes=[
-            pltpu.VMEM((rows, width), jnp.float32),
-            pltpu.VMEM((chunk, width), jnp.float32),
-        ],
+        scratch_shapes=[pltpu.VMEM((chunk, width), jnp.float32)],
         compiler_params=params(),
         name="pick_rows",
-    )(picked, emb_table)
+    )(picked, wide)
 
 
 def spread_weights(codes, lcb_weight, owners, cap):
@@ -92,7 +87,7 @@
 
     return pl.pallas_call(
         kernel,
-        out_shape=pltpu.HBM((owners, samples * embed_count, cap), jnp.bfloat16),
+        out_shape=pltpu.VMEM((owners, samples * embed_count, cap), jnp.bfloat16),
         grid=(samples // group,),
         in_specs=[
             pl.BlockSpec((group, feature_count), lambda i: (i, 0)),
@@ -113,22 +108,15 @@
     owners, lines, cap = spread.shape
     width = fetched.shape[3]
     samples = lines // embed_count
-    part = tiles_of(owners, 4)
+    part = tiles_of(owners, 8)
     steps = owners // part
 
-    def kernel(spread_ref, rows_ref, out_ref, held, total, sems):
-        def copy(step):
-            piece = tile_at(step, part)
-            return pltpu.make_async_copy(spread_ref.at[piece], held.at[piece], sems.at[step])
-
-        for step in range(steps):
-            copy(step).start()
+    def kernel(spread_ref, rows_ref, out_ref, total):
         total[...] = jnp.zeros_like(total)
 
         def body(step, carry):
-            copy(step).wait()
             first = step * part
-            left = jnp.concatenate([held[first + o] for o in range(part)], axis=1)
+            left = jnp.concatenate([spread_ref[first + o] for o in range(part)], axis=1)
             right = jnp.concatenate([rows_ref[first + o, view] for o in range(part)], axis=0)
             total[...] += jnp.dot(left, right, preferred_element_type=jnp.float32)
             return carry
@@ -142,16 +130,12 @@
     return pl.pallas_call(
         kernel,
         out_shape=jax.ShapeDtypeStruct((samples, embed_count * width), kind),
-        in_specs=[whole(pltpu.HBM), whole()],
+        in_specs=[whole(), whole()],
         out_specs=whole(),
-        scratch_shapes=[
-            pltpu.VMEM(spread.shape, jnp.bfloat16),
-            pltpu.VMEM((lines, width), jnp.float32),
-            pltpu.SemaphoreType.DMA((steps,)),
-        ],
+        scratch_shapes=[pltpu.VMEM((lines, width), jnp.float32)],
         compiler_params=params(),
         name="compress",
-    )(in_hbm(spread), fetched)
+    )(spread, fetched)
 
 
 def expand(spread, lead_grad, embed_count, near=None):
@@ -201,9 +185,11 @@
 def add_rows(targets, returned, outgoing, rows):
     count, width = returned.shape
     chunk = min(count, 1024)
-
-    def kernel(targets_ref, back_ref, sent_ref, out_ref, total, terms, done):
-        total[...] = jnp.zeros_like(total)
+    zeros = jnp.zeros((rows + 8, 1, width), jnp.float32)
+
+    def kernel(targets_ref, back_ref, sent_ref, zeros_ref, out_ref, total, terms, sem):
+        begin = pltpu.make_async_copy(zeros_ref, total, sem.at[0])
+        begin.start()
 
         def fill(part, carry):
             base = pl.multiple_of(part * chunk, chunk)
@@ -212,38 +198,41 @@
                 lines, :
             ].astype(jnp.float32)
 
+            @pl.when(part == 0)
+            def _():
+                begin.wait()
+
             def body(group, inner):
                 first = pl.multiple_of(group * UNROLL, UNROLL)
                 places = [targets_ref[base + first + lane] for lane in range(UNROLL)]
                 sums = [
-                    total[pl.ds(places[lane], 1), :] + terms[pl.ds(first + lane, 1), :]
-                    for lane in range(UNROLL)
+                    total[places[lane]] + terms[pl.ds(first + lane, 1), :] for lane in range(UNROLL)
                 ]
                 for lane in range(UNROLL):
-                    total[pl.ds(places[lane], 1), :] = sums[lane]
+                    total[places[lane]] = sums[lane]
                 return inner
 
             lax.fori_loop(0, chunk // UNROLL, body, 0)
             return carry
 
         lax.fori_loop(0, count // chunk, fill, 0)
-        copy = pltpu.make_async_copy(total.at[pl.ds(0, rows), :], out_ref, done)
-        copy.start()
-        copy.wait()
+        finish = pltpu.make_async_copy(total.at[pl.ds(0, rows)], out_ref, sem.at[1])
+        finish.start()
+        finish.wait()
 
     return pl.pallas_call(
         kernel,
-        out_shape=jax.ShapeDtypeStruct((rows, width), jnp.float32),
-        in_specs=[whole(pltpu.SMEM), whole(), whole()],
+        out_shape=jax.ShapeDtypeStruct((rows, 1, width), jnp.float32),
+        in_specs=[whole(pltpu.SMEM), whole(), whole(), whole(pl.ANY)],
         out_specs=whole(pl.ANY),
         scratch_shapes=[
-            pltpu.VMEM((rows + 8, width), jnp.float32),
+            pltpu.VMEM((rows + 8, 1, width), jnp.float32),
             pltpu.VMEM((chunk, width), jnp.float32),
-            pltpu.SemaphoreType.DMA,
+            pltpu.SemaphoreType.DMA((2,)),
         ],
         compiler_params=params(),
         name="add_rows",
-    )(targets, returned, outgoing)
+    )(targets, returned, outgoing, zeros).reshape(rows, width)
 
 
 GROUP = 16
@@ -260,10 +249,10 @@
     return jnp.dot(left, right, preferred_element_type=jnp.float32)
 
 
-def split_dot(left, right):
-    high = left.astype(jnp.bfloat16)
-    low = (left - high.astype(jnp.float32)).astype(jnp.bfloat16)
-    return dot(high, right) + dot(low, right)
+def halves(value):
+    high = value.astype(jnp.bfloat16)
+    low = (value - high.astype(jnp.float32)).astype(jnp.bfloat16)
+    return jnp.concatenate([high, low], axis=1)
 
 
 def same_sample(count):
@@ -282,18 +271,22 @@
     return jnp.concatenate(lines, axis=0).astype(jnp.bfloat16)
 
 
-def mix_forward(small, layer, acts, inter, scale, normed, count):
+def mix_forward(small, layer, acts, inter, scale, normed, grams, count):
     batch, model_width = acts.shape
     width = model_width // count
     both = small[layer].astype(jnp.float32)
     proj = repeated(both[:count])
     keep = same_sample(count)
-    for start in range(0, batch, GROUP):
-        rows = pl.ds(start, GROUP)
-        block = stacked(acts, rows, count, width)
+    size = GROUP * count
+    for group in range(batch // GROUP):
+        block = stacked(acts, pl.ds(group * GROUP, GROUP), count, width)
         gram = jnp.where(keep, dot_nt(block, block), 0.0)
-        mixed = split_dot(gram, proj)
-        parts = [mixed[k * GROUP : (k + 1) * GROUP] for k in range(count)]
+        grams[group * size : (group + 1) * size, :] = halves(gram)
+    mixed = dot(grams[...], jnp.concatenate([proj, proj], axis=0))
+    for group in range(batch // GROUP):
+        rows = pl.ds(group * GROUP, GROUP)
+        start = group * size
+        parts = [mixed[start + k * GROUP : start + (k + 1) * GROUP] for k in range(count)]
         squares = sum(part * part for part in parts)
         mean = jnp.sum(squares, axis=1, keepdims=True) * (1.0 / model_width)
         inv = lax.rsqrt(mean + EPSILON)
@@ -303,6 +296,10 @@
             inter[rows, columns] = parts[k]
             gain = both[count + k : count + k + 1]
             normed[rows, columns] = (parts[k] * inv * gain).astype(jnp.bfloat16)
+
+
+def gram_scratch(batch, count):
+    return pltpu.VMEM((batch * count, 2 * GROUP * count), jnp.bfloat16)
 
 
 def hidden_tile(hidden_width):
@@ -429,7 +426,7 @@
         left = jnp.concatenate([g_inter, proj], axis=1)
         right = jnp.concatenate([proj, g_inter], axis=1)
         links = jnp.where(keep, dot_nt(left, right), 0.0)
-        g_acts = split_dot(links, block)
+        g_acts = dot(halves(links), jnp.concatenate([block, block], axis=0))
         for k in range(count):
             piece = g_acts[k * GROUP : (k + 1) * GROUP] + grad[rows, columns[k]].astype(jnp.float32)
             out[rows, columns[k]] = piece.astype(jnp.bfloat16)
@@ -496,7 +493,7 @@
         piece_refs, (top_ref, small_ref), refs = refs[: len(pieces)], refs[len(pieces) :][:2], refs[len(pieces) + 2 :]
         matrices, refs = refs[:4], refs[4:]
         out_ref, hid, inter, scale, kept, g_hidden = refs[:6]
-        held, (normed, hidden, top_turned) = refs[6:9], refs[9:]
+        held, (normed, hidden, top_turned, grams) = refs[6:9], refs[9:]
         core = place_ref[0]
 
         @pl.when(place_ref[1] == 1)
@@ -511,7 +508,7 @@
                 start += piece.shape[0]
             for layer, (up, down) in enumerate(layers):
                 mix_forward(
-                    small_ref, layer, kept.at[layer], inter.at[layer], scale.at[layer], normed, count
+                    small_ref, layer, kept.at[layer], inter.at[layer], scale.at[layer], normed, grams, count
                 )
                 up_product(normed, up.held, hidden, hid.at[layer], up.wait)
                 to = kept.at[1] if layer == 0 else out_ref
@@ -537,6 +534,7 @@
             pltpu.VMEM((batch, model_width), jnp.bfloat16),
             pltpu.VMEM((batch, hidden_width), jnp.bfloat16),
             pltpu.VMEM((model_width, batch), jnp.bfloat16),
+            gram_scratch(batch, count),
         ],
         compiler_params=stage_params(),
         cost_estimate=stage_cost(4, batch, model_width, hidden_width),
@@ -553,7 +551,7 @@
     def kernel(place_ref, acts_ref, top_ref, ghid_ref, small_ref, *refs):
         matrices, refs = refs[:4], refs[4:]
         out_ref, held = refs[0], refs[1:4]
-        hid, hidden, inter, scale, upper, grad, turned, normed, weighted, g_before = refs[4:]
+        hid, hidden, inter, scale, upper, grad, turned, normed, weighted, g_before, grams = refs[4:]
 
         @pl.when(place_ref[1] == 1)
         def _():
@@ -561,10 +559,10 @@
             (up0, down0), (up1, down1) = layers
             for stream in (up0, down0, up1):
                 stream.start()
-            mix_forward(small_ref, 0, acts_ref, inter.at[0], scale.at[0], normed, count)
+            mix_forward(small_ref, 0, acts_ref, inter.at[0], scale.at[0], normed, grams, count)
             up_product(normed, up0.held, hidden, hid, up0.wait)
             down_product(hidden, down0.held, acts_ref, upper, down0.wait)
-            mix_forward(small_ref, 1, upper, inter.at[1], scale.at[1], normed, count)
+            mix_forward(small_ref, 1, upper, inter.at[1], scale.at[1], normed, grams, count)
 
             def masked(columns):
                 before = dot(normed[...], up1.held[:, columns])
@@ -596,6 +594,7 @@
             pltpu.VMEM((batch, model_width), jnp.bfloat16),
             pltpu.VMEM((batch, model_width), jnp.float32),
             pltpu.VMEM((hidden_width, batch), jnp.bfloat16),
+            gram_scratch(batch, count),
         ],
         compiler_params=stage_params(),
         cost_estimate=stage_cost(6, batch, model_width, hidden_width),

time: 157 us -> 159 us (1.013)
  local copies, waits for them, and re-layouts: 3.59 us -> 8.7 us
  Pallas kernels: 61.3 us -> 56.8 us
    unnamed x17 -> x25, local copies, waits for them, and re-layouts: 2.49 us -> 6.45 us
    pallas_call x2, Pallas kernels: 4.61 us -> 1.88 us  [compress(): pl.pallas_call(kernel, out_shape=jax.ShapeDtypeStruct((samples, embed_cou...]
    all_to_all x2, waiting for transfers between devices: 16 us -> 17.7 us  [swap_in_half(): lax.all_to_all(value, TABLE_AXES, split_axis=0, concat_axis=0, axis_index...]
  transfers between devices with their start and end apart: 12 -> 12, of which waited for: 8 -> 8; matrix products, arithmetic and copies ran while one was open for 4% -> 3% of each run, Pallas kernels for 12% -> 10%
where the time goes in v8:
time: 159 us; the launch traced here: 158 us
  waiting for transfers between devices  65.2 us (41%)
  Pallas kernels  56.8 us (36%)
  starting transfers between devices  23.6 us (15%)
  local copies, waits for them, and re-layouts  8.7 us (5%)
  other arithmetic  3.15 us (2%)
    ppermute x4, waiting for transfers between devices, moved(): return lax.ppermute(value, 'section', pairs)  38.3 us
    all_to_all x2, waiting for transfers between devices, swap_in_half(): lax.all_to_all(value, TABLE_AXES, split_axis=0, concat_axis=0, axis_index...  17.7 us
    pallas_call x1, Pallas kernels, backward_stage(): pl.pallas_call(kernel, out_shape=jax.ShapeDtypeStruct(grad.shape, jnp.bfl...  15.4 us
    pallas_call x1, Pallas kernels, forward_stage(): pl.pallas_call(kernel, out_shape=[jax.ShapeDtypeStruct(top.shape, jnp.bfl...  12.2 us
    all_to_all x2, starting transfers between devices, swap_in_half(): lax.all_to_all(value, TABLE_AXES, split_axis=0, concat_axis=0, axis_index...  11.7 us
    pallas_call x1, Pallas kernels, add_rows(): pl.pallas_call(kernel, out_shape=jax.ShapeDtypeStruct((rows, 1, width), j...  10.8 us
    ppermute x3, waiting for transfers between devices, mirror(): lax.ppermute(value, 'table', [(t, (t + along // 2) % along) for t in rang...  9.21 us
    unnamed x25, local copies, waits for them, and re-layouts  6.45 us
  transfers between devices with their start and end apart: 12, of which 8 were waited for; matrix products, arithmetic and copies ran while one was open for 3% of the time, Pallas kernels for 10%

profile of v8, /device:TPU:0, one launch (start us, length us, event | category | flops | bytes accessed | tf_op | source)
XLA Modules:
  0.0 158.0 jit_solution(15400819039642302200)
XLA Ops:
  0.5 4.0 %collective-permute-start = (s32[64,512]{1,0:T(8,128)}, s32[64,512]{1,0:T(8,128)S(1)}, u32[]{:S(2)}, u32[]{:S(2)}) collective-permute-start(s32[64,512]{1,0:T(8,128)} %bitcast.44), channel_id=1, source_target_pairs={{0,4},{1,5},{2,6},{3,7},{4,0},{5,1},{6,2},{7,3},{8,12},{9,13},{10,... | collective-permute-start | bytes 393224 | tf_op jit(solution)/shard_map/ppermute | solution.py:659
  5.3 1.4 reshape.50
  6.7 5.7 %pick_rows.1.sent_ref = bf16[4096,128]{1,0:T(8,128)(2,1)} custom-call(s32[4096]{0:T(1024)S(1)} %bitcast.35, f32[4096,1,128]{2,1,0:T(1,128)S(1)} %bitcast.30), custom_call_target="tpu_custom_call" | custom-call | tf_op jit(solution)/shard_map/pick_rows/pallas_call | solution.py:52
  12.4 4.8 %all-to-all-start = ((bf16[16,2,128,128]{3,2,1,0:T(8,128)(2,1)}), bf16[16,2,128,128]{3,2,1,0:T(8,128)(2,1)S(1)}, u32[]{:S(2)}, u32[]{:S(2)}) async-start(bf16[16,2,128,128]{3,2,1,0:T(8,128)(2,1)} %bitcast.13), calls=%async_computation | async-start | bytes 2097152 | tf_op jit(solution)/shard_map/all_to_all | solution.py:669
  18.1 3.1 %spread_weights.3.spread_ref = bf16[16,512,128]{2,1,0:T(8,128)(2,1)S(1)} custom-call(s32[64,512]{1,0:T(8,128)S(1)} %fusion.11.codes_ref, bf16[8,512]{1,0:T(8,128)(2,1)S(1)} %copy-done.7), custom_call_target="tpu_custom_call" | custom-call | flops 1073741824 | bytes 2097152 | tf_op jit(solution)/shard_map/spread_weights/pallas_call | solution.py:88
  21.2 1.3 copy-done.4
  22.9 3.1 %spread_weights.2.spread_ref = bf16[16,512,128]{2,1,0:T(8,128)(2,1)S(1)} custom-call(s32[64,512]{1,0:T(8,128)S(1)} %fusion.5.codes_ref, bf16[8,512]{1,0:T(8,128)(2,1)S(1)} %copy-done.7), custom_call_target="tpu_custom_call" | custom-call | flops 1073741824 | bytes 2097152 | tf_op jit(solution)/shard_map/spread_weights/pallas_call | solution.py:88
  26.1 1.3 copy-done.1
  27.4 4.6 %all-to-all-done.rows_ref = bf16[16,2,128,128]{3,2,1,0:T(8,128)(2,1)S(1)} async-done(((bf16[16,2,128,128]{3,2,1,0:T(8,128)(2,1)}), bf16[16,2,128,128]{3,2,1,0:T(8,128)(2,1)S(1)}, u32[]{:S(2)}, u32[]{:S(2)}) %all-to-all-start) | async-done | bytes 1048608 | tf_op jit(solution)/shard_map/all_to_all | solution.py:669
  32.0 1.6 %copy-done.2 = bf16[16,512,128]{2,1,0:T(8,128)(2,1)S(1)} copy-done((bf16[16,512,128]{2,1,0:T(8,128)(2,1)S(1)}, bf16[16,512,128]{2,1,0:T(8,128)(2,1)}, u32[]{:S(2)}) %copy-start.2) | copy-done | bytes 2097176
  33.6 0.9 compress.3
  34.6 1.5 collective-permute-start.1
  36.2 1.6 %copy-done.5 = bf16[16,512,128]{2,1,0:T(8,128)(2,1)S(1)} copy-done((bf16[16,512,128]{2,1,0:T(8,128)(2,1)S(1)}, bf16[16,512,128]{2,1,0:T(8,128)(2,1)}, u32[]{:S(2)}) %copy-start.5) | copy-done | bytes 2097176
  37.8 0.9 compress.2
  38.7 4.7 %collective-permute-done.1 = bf16[64,1024]{1,0:T(8,128)(2,1)S(1)} collective-permute-done((bf16[64,1024]{1,0:T(8,128)(2,1)S(1)}, bf16[64,1024]{1,0:T(8,128)(2,1)S(1)}, u32[]{:S(2)}, u32[]{:S(2)}) %collective-permute-start.1) | collective-permute-done | bytes 131104 | tf_op jit(solution)/shard_map/ppermute | solution.py:659
  43.5 1.3 collective-permute-start.2
  44.9 5.5 %collective-permute-done.2.refs_1_ = bf16[64,1024]{1,0:T(8,128)(2,1)S(1)} collective-permute-done((bf16[64,1024]{1,0:T(8,128)(2,1)S(1)}, bf16[64,1024]{1,0:T(8,128)(2,1)S(1)}, u32[]{:S(2)}, u32[]{:S(2)}) %collective-permute-start.2) | collective-permute-done | bytes 131104 | tf_op jit(solution)/shard_map/ppermute | solution.py:654
  50.4 12.2 %forward_stage.1 = (bf16[128,1024]{1,0:T(8,128)(2,1)S(1)}, bf16[2,4096,128]{2,1,0:T(8,128)(2,1)S(1)}, f32[2,128,1024]{2,1,0:T(8,128)S(1)}, f32[2,128,128]{2,1,0:...) custom-call(s32[3]{0:T(128)S(1)} %pad_add_fusion.2.place_ref, ...), custom_call_target="tpu_custom_call" | custom-call | flops 4294967296 | bytes 1048576 | tf_op jit(solution)/shard_map/forward_stage/pallas_call | solution.py:525
  62.6 1.3 collective-permute-start.6
  64.0 4.0 %collective-permute-done.6.acts_ref = bf16[128,1024]{1,0:T(8,128)(2,1)S(1)} collective-permute-done((bf16[128,1024]{1,0:T(8,128)(2,1)S(1)}, bf16[128,1024]{1,0:T(8,128)(2,1)S(1)}, u32[]{:S(2)}, u32[]{:S(2)}) %collective-permute-start.6) | collective-permute-done | bytes 262176 | tf_op jit(solution)/shard_map/ppermute | solution.py:654
  68.8 1.3 collective-permute-start.7
  70.1 26.3 %collective-permute-done.7.grad_ref = bf16[128,1024]{1,0:T(8,128)(2,1)S(1)} collective-permute-done((bf16[128,1024]{1,0:T(8,128)(2,1)S(1)}, bf16[128,1024]{1,0:T(8,128)(2,1)S(1)}, u32[]{:S(2)}, u32[]{:S(2)}) %collective-permute-start.7) | collective-permute-done | bytes 262176 | tf_op jit(solution)/shard_map/ppermute | solution.py:654
  96.4 15.4 %backward_stage.1 = bf16[128,1024]{1,0:T(8,128)(2,1)S(1)} custom-call(s32[3]{0:T(128)S(1)} %pad_add_fusion.2.place_ref, bf16[128,1024]{1,0:T(8,128)(2,1)S(1)} %collective-permute-done.7.grad_ref, bf16[2,4096,128]{2,1,0:T(8,128)(2,1)S(1)} %get-tuple-element.19.hid, f32[2,128,1024]{2,1,0:T(8,128)S(1)} %get-tuple-element.20.inter, ...), custom_call_target="tpu_custom_call" | custom-call | flops 4294967296 | bytes 1048576 | tf_op jit(solution)/shard_map/backward_stage/pallas_call | solution.py:630
  111.9 1.4 collective-permute-start.8
  113.4 2.5 %collective-permute-done.8 = bf16[64,1024]{1,0:T(8,128)(2,1)S(1)} collective-permute-done((bf16[64,1024]{1,0:T(8,128)(2,1)S(1)}, bf16[64,1024]{1,0:T(8,128)(2,1)S(1)}, u32[]{:S(2)}, u32[]{:S(2)}) %collective-permute-start.8) | collective-permute-done | bytes 131104 | tf_op jit(solution)/shard_map/ppermute | solution.py:654
  116.0 1.4 expand.2.refs_0_
  117.4 4.5 %collective-permute-done.9.grad_ref = bf16[64,1024]{1,0:T(8,128)(2,1)S(1)} collective-permute-done((bf16[64,1024]{1,0:T(8,128)(2,1)S(1)}, bf16[64,1024]{1,0:T(8,128)(2,1)S(1)}, u32[]{:S(2)}, u32[]{:S(2)}) %collective-permute-start.9) | collective-permute-done | bytes 131104 | tf_op jit(solution)/shard_map/ppermute | solution.py:659
  121.8 2.4 %expand.3 = bf16[16,2,128,128]{3,2,1,0:T(8,128)(2,1)} custom-call(bf16[16,512,128]{2,1,0:T(8,128)(2,1)S(1)} %copy-done.3, bf16[64,1024]{1,0:T(8,128)(2,1)S(1)} %collective-permute-done.9.grad_ref, bf16[16,128,128]{2,1,0:T(8,128)(2,1)S(1)} %expand.2.refs_0_), custom_call_target="tpu_custom_call" | custom-call | tf_op jit(solution)/shard_map/expand/pallas_call | solution.py:171
  124.2 6.9 %all-to-all-start.1 = ((bf16[16,2,128,128]{3,2,1,0:T(8,128)(2,1)}), bf16[16,2,128,128]{3,2,1,0:T(8,128)(2,1)S(1)}, u32[]{:S(2)}, u32[]{:S(2)}) async-start(bf16[16,2,128,128]{3,2,1,0:T(8,128)(2,1)} %expand.3), calls=%async_computation.1 | async-start | bytes 2097152 | tf_op jit(solution)/shard_map/all_to_all | solution.py:669
  132.8 13.0 %all-to-all-done.1 = bf16[16,2,128,128]{3,2,1,0:T(8,128)(2,1)S(1)} async-done(((bf16[16,2,128,128]{3,2,1,0:T(8,128)(2,1)}), bf16[16,2,128,128]{3,2,1,0:T(8,128)(2,1)S(1)}, u32[]{:S(2)}, u32[]{:S(2)}) %all-to-all-start.1) | async-done | bytes 1048608 | tf_op jit(solution)/shard_map/all_to_all | solution.py:669
  145.9 1.1 broadcast_in_dim.15.zeros_ref
  147.0 10.8 %add_rows.1 = f32[4096,1,128]{2,1,0:T(1,128)} custom-call(s32[4096]{0:T(1024)S(1)} %bitcast.34, bf16[4096,128]{1,0:T(8,128)(2,1)S(1)} %bitcast.31, bf16[4096,128]{1,0:T(8,128)(2,1)} %pick_rows.1.sent_ref, f32[4104,1,128]{2,1,0:T(1,128)S(1)} %broadcast_in_dim.15.zeros_ref), custom_call_target="tpu_custom_call" | custom-call | tf_op jit(solution)/shard_map/add_rows/pallas_call | solution.py:223
  (52 shorter events, 5.5 us)
Async XLA Ops:
  0.0 36.2 %copy-start = (bf16[1,4,64,1024]{3,2,1,0:T(8,128)(2,1)S(1)}, bf16[1,4,64,1024]{3,2,1,0:T(8,128)(2,1)}, u32[]{:S(2)}) copy-start(bf16[1,4,64,1024]{3,2,1,0:T(8,128)(2,1)} %param.16) | copy-start | bytes 1572868
  0.0 50.4 %collective-permute-start.4 = (bf16[1024,4096]{1,0:T(8,128)(2,1)}, bf16[1024,4096]{1,0:T(8,128)(2,1)}, u32[]{:S(2)}, u32[]{:S(2)}) collective-permute-start(bf16[1024,4096]{1,0:T(8,128)(2,1)} %bitcast.36), channel_id=1, source_target_pairs={{0,8},{8,0},{16,24},{24,16},{1,9},{9,1},{17,25},{25,17},{2,10},{10... | collective-permute-start | bytes 25165832 | tf_op jit(solution)/shard_map/ppermute | solution.py:649
  0.5 49.9 %collective-permute-start.5 = (bf16[4096,1024]{1,0:T(8,128)(2,1)}, bf16[4096,1024]{1,0:T(8,128)(2,1)}, u32[]{:S(2)}, u32[]{:S(2)}) collective-permute-start(bf16[4096,1024]{1,0:T(8,128)(2,1)} %bitcast.40), channel_id=1, source_target_pairs={{0,8},{8,0},{16,24},{24,16},{1,9},{9,1},{17,25},{25,17},{2,10},{10... | collective-permute-start | bytes 25165832 | tf_op jit(solution)/shard_map/ppermute | solution.py:649
  0.5 11.8 %collective-permute-start = (s32[64,512]{1,0:T(8,128)}, s32[64,512]{1,0:T(8,128)S(1)}, u32[]{:S(2)}, u32[]{:S(2)}) collective-permute-start(s32[64,512]{1,0:T(8,128)} %bitcast.44), channel_id=1, source_target_pairs={{0,4},{1,5},{2,6},{3,7},{4,0},{5,1},{6,2},{7,3},{8,12},{9,13},{10,... | collective-permute-start | bytes 393224 | tf_op jit(solution)/shard_map/ppermute | solution.py:659
  6.7 10.6 %copy-start.10 = (bf16[1,1024]{1,0:T(2,128)(2,1)S(1)}, bf16[1,1024]{1,0:T(2,128)(2,1)}, u32[]{:S(2)}) copy-start(bf16[1,1024]{1,0:T(2,128)(2,1)} %param.13) | copy-start | bytes 6148
  6.7 10.6 %copy-start.9 = (bf16[1,8,128]{2,1,0:T(8,128)(2,1)S(1)}, bf16[1,8,128]{2,1,0:T(8,128)(2,1)}, u32[]{:S(2)}) copy-start(bf16[1,8,128]{2,1,0:T(8,128)(2,1)} %param.12) | copy-start | bytes 6148
  6.7 11.1 %copy-start.8 = (s32[1,64,512]{2,1,0:T(8,128)S(1)}, s32[1,64,512]{2,1,0:T(8,128)}, u32[]{:S(2)}) copy-start(s32[1,64,512]{2,1,0:T(8,128)} %param.17) | copy-start | bytes 393220
  6.7 11.4 %copy-start.7 = (bf16[8,512]{1,0:T(8,128)(2,1)S(1)}, bf16[8,512]{1,0:T(8,128)(2,1)}, u32[]{:S(2)}) copy-start(bf16[8,512]{1,0:T(8,128)(2,1)} %lcb_ref.3) | copy-start | bytes 24580
  12.4 19.7 %all-to-all-start = ((bf16[16,2,128,128]{3,2,1,0:T(8,128)(2,1)}), bf16[16,2,128,128]{3,2,1,0:T(8,128)(2,1)S(1)}, u32[]{:S(2)}, u32[]{:S(2)}) async-start(bf16[16,2,128,128]{3,2,1,0:T(8,128)(2,1)} %bitcast.13), calls=%async_computation | async-start | bytes 2097152 | tf_op jit(solution)/shard_map/all_to_all | solution.py:669
  17.3 27.5 %collective-permute-start.3 = (bf16[16,128]{1,0:T(8,128)(2,1)S(1)}, bf16[16,128]{1,0:T(8,128)(2,1)S(1)}, u32[]{:S(2)}, u32[]{:S(2)}) collective-permute-start(bf16[16,128]{1,0:T(8,128)(2,1)S(1)} %pad_maximum_fusion.1), channel_id=1, source_target_pairs={{0,8},{8,0},{16,24},{24,16},{1,9},{9,1},{17,25},{25,17},{2,10},{10... | collective-permute-start | bytes 12296 | tf_op jit(solution)/shard_map/ppermute | solution.py:649
  21.2 1.3 copy-start.4
  26.1 1.3 copy-start.1
  32.0 1.6 %copy-start.2 = (bf16[16,512,128]{2,1,0:T(8,128)(2,1)S(1)}, bf16[16,512,128]{2,1,0:T(8,128)(2,1)}, u32[]{:S(2)}) copy-start(bf16[16,512,128]{2,1,0:T(8,128)(2,1)} %copy-done.1) | copy-start | bytes 6291460
  34.6 8.9 %collective-permute-start.1 = (bf16[64,1024]{1,0:T(8,128)(2,1)S(1)}, bf16[64,1024]{1,0:T(8,128)(2,1)S(1)}, u32[]{:S(2)}, u32[]{:S(2)}) collective-permute-start(bf16[64,1024]{1,0:T(8,128)(2,1)S(1)} %compress.3), channel_id=1, source_target_pairs={{0,4},{1,5},{2,6},{3,7},{4,0},{5,1},{6,2},{7,3},{8,12},{9,13},{10,... | collective-permute-start | bytes 393224 | tf_op jit(solution)/shard_map/ppermute | solution.py:659
  36.2 1.6 %copy-start.5 = (bf16[16,512,128]{2,1,0:T(8,128)(2,1)S(1)}, bf16[16,512,128]{2,1,0:T(8,128)(2,1)}, u32[]{:S(2)}) copy-start(bf16[16,512,128]{2,1,0:T(8,128)(2,1)} %copy-done.4) | copy-start | bytes 6291460
  43.5 6.9 %collective-permute-start.2 = (bf16[64,1024]{1,0:T(8,128)(2,1)S(1)}, bf16[64,1024]{1,0:T(8,128)(2,1)S(1)}, u32[]{:S(2)}, u32[]{:S(2)}) collective-permute-start(bf16[64,1024]{1,0:T(8,128)(2,1)S(1)} %add_convert_fusion.refs_0_), channel_id=1, source_target_pairs={{16,0},{24,8},{17,1},{25,9},{18,2},{26,10},{19,3},{27,11},{20,4},{... | collective-permute-start | bytes 393224 | tf_op jit(solution)/shard_map/ppermute | solution.py:654
  62.6 5.4 %collective-permute-start.6 = (bf16[128,1024]{1,0:T(8,128)(2,1)S(1)}, bf16[128,1024]{1,0:T(8,128)(2,1)S(1)}, u32[]{:S(2)}, u32[]{:S(2)}) collective-permute-start(bf16[128,1024]{1,0:T(8,128)(2,1)S(1)} %get-tuple-element.17), channel_id=1, source_target_pairs={{0,16},{8,24},{1,17},{9,25},{2,18},{10,26},{3,19},{11,27},{4,20},{... | collective-permute-start | bytes 786440 | tf_op jit(solution)/shard_map/ppermute | solution.py:654
  68.8 27.6 %collective-permute-start.7 = (bf16[128,1024]{1,0:T(8,128)(2,1)S(1)}, bf16[128,1024]{1,0:T(8,128)(2,1)S(1)}, u32[]{:S(2)}, u32[]{:S(2)}) collective-permute-start(bf16[128,1024]{1,0:T(8,128)(2,1)S(1)} %turn_stage.1), channel_id=1, source_target_pairs={{16,0},{24,8},{17,1},{25,9},{18,2},{26,10},{19,3},{27,11},{20,4},{... | collective-permute-start | bytes 786440 | tf_op jit(solution)/shard_map/ppermute | solution.py:654
  96.4 19.5 %copy-start.6 = (bf16[16,512,128]{2,1,0:T(8,128)(2,1)S(1)}, bf16[16,512,128]{2,1,0:T(8,128)(2,1)}, u32[]{:S(2)}) copy-start(bf16[16,512,128]{2,1,0:T(8,128)(2,1)} %copy-done.4) | copy-start | bytes 6291460
  111.9 9.9 %copy-start.3 = (bf16[16,512,128]{2,1,0:T(8,128)(2,1)S(1)}, bf16[16,512,128]{2,1,0:T(8,128)(2,1)}, u32[]{:S(2)}) copy-start(bf16[16,512,128]{2,1,0:T(8,128)(2,1)} %copy-done.1) | copy-start | bytes 6291460
  111.9 3.9 %collective-permute-start.8 = (bf16[64,1024]{1,0:T(8,128)(2,1)S(1)}, bf16[64,1024]{1,0:T(8,128)(2,1)S(1)}, u32[]{:S(2)}, u32[]{:S(2)}) collective-permute-start(bf16[64,1024]{1,0:T(8,128)(2,1)S(1)} %slice.8), channel_id=1, source_target_pairs={{0,16},{8,24},{1,17},{9,25},{2,18},{10,26},{3,19},{11,27},{4,20},{... | collective-permute-start | bytes 393224 | tf_op jit(solution)/shard_map/ppermute | solution.py:654
  115.9 5.9 %collective-permute-start.9 = (bf16[64,1024]{1,0:T(8,128)(2,1)S(1)}, bf16[64,1024]{1,0:T(8,128)(2,1)S(1)}, u32[]{:S(2)}, u32[]{:S(2)}) collective-permute-start(bf16[64,1024]{1,0:T(8,128)(2,1)S(1)} %slice_select_fusion.grad_ref), channel_id=1, source_target_pairs={{0,4},{1,5},{2,6},{3,7},{4,0},{5,1},{6,2},{7,3},{8,12},{9,13},{10,... | collective-permute-start | bytes 393224 | tf_op jit(solution)/shard_map/ppermute | solution.py:659
  117.4 14.3 %copy-start.11 = (s32[1,32]{1,0:T(1,128)S(1)}, s32[1,32]{1,0:T(1,128)}, u32[]{:S(2)}) copy-start(s32[1,32]{1,0:T(1,128)} %param.19) | copy-start | bytes 388
  124.2 21.7 %all-to-all-start.1 = ((bf16[16,2,128,128]{3,2,1,0:T(8,128)(2,1)}), bf16[16,2,128,128]{3,2,1,0:T(8,128)(2,1)S(1)}, u32[]{:S(2)}, u32[]{:S(2)}) async-start(bf16[16,2,128,128]{3,2,1,0:T(8,128)(2,1)} %expand.3), calls=%async_computation.1 | async-start | bytes 2097152 | tf_op jit(solution)/shard_map/all_to_all | solution.py:669

commit v9 on v8

--- a/solution.py
+++ b/solution.py
@@ -9,6 +9,7 @@
 DECAY_WEIGHT = 0.5
 VMEM_LIMIT = 28 * 1024 * 1024
 UNROLL = 32
+PICK_UNROLL = 128
 
 
 def whole(memory_space=pltpu.VMEM):
@@ -31,19 +32,21 @@
     rows, width = emb_table.shape
     count = picked.shape[0]
     chunk = min(count, 1024)
-    wide = emb_table.astype(jnp.float32).reshape(rows, 1, width)
-
-    def kernel(picked_ref, wide_ref, out_ref, lines):
+
+    def kernel(picked_ref, table_ref, out_ref, wide, lines):
+        wide[...] = table_ref[...].astype(jnp.float32)
+
         def fill(part, carry):
             base = pl.multiple_of(part * chunk, chunk)
 
             def body(group, inner):
-                first = pl.multiple_of(group * UNROLL, UNROLL)
-                for lane in range(UNROLL):
-                    lines[pl.ds(first + lane, 1), :] = wide_ref[picked_ref[base + first + lane]]
+                first = pl.multiple_of(group * PICK_UNROLL, PICK_UNROLL)
+                for lane in range(PICK_UNROLL):
+                    row = picked_ref[base + first + lane]
+                    lines[pl.ds(first + lane, 1), :] = wide[pl.ds(row, 1), :]
                 return inner
 
-            lax.fori_loop(0, chunk // UNROLL, body, 0)
+            lax.fori_loop(0, chunk // PICK_UNROLL, body, 0)
             out_ref[pl.ds(base, chunk), :] = lines[...].astype(out_ref.dtype)
             return carry
 
@@ -54,10 +57,13 @@
         out_shape=jax.ShapeDtypeStruct((count, width), emb_table.dtype),
         in_specs=[whole(pltpu.SMEM), whole()],
         out_specs=whole(),
-        scratch_shapes=[pltpu.VMEM((chunk, width), jnp.float32)],
+        scratch_shapes=[
+            pltpu.VMEM((rows, width), jnp.float32),
+            pltpu.VMEM((chunk, width), jnp.float32),
+        ],
         compiler_params=params(),
         name="pick_rows",
-    )(picked, wide)
+    )(picked, emb_table)
 
 
 def spread_weights(codes, lcb_weight, owners, cap):
@@ -65,7 +71,7 @@
     embed_count = lcb_weight.shape[0]
     group = tiles_of(samples, 16)
 
-    def kernel(codes_ref, lcb_ref, out_ref):
+    def kernel(codes_ref, lcb_ref, out_ref, kept_ref):
         lcb = lcb_ref[...].astype(jnp.float32)
         owner_of = lax.broadcasted_iota(jnp.int32, (owners, embed_count, feature_count), 0)
         column_of = lax.broadcasted_iota(jnp.int32, (cap, feature_count), 0)
@@ -83,17 +89,22 @@
                 )
                 made.append(both.reshape(owners, embed_count, cap))
             rows = pl.ds(pair * embed_count, 2 * embed_count)
-            out_ref[:, rows, :] = jnp.concatenate(made, axis=1).astype(out_ref.dtype)
+            joined = jnp.concatenate(made, axis=1).astype(out_ref.dtype)
+            out_ref[:, rows, :] = joined
+            kept_ref[:, rows, :] = joined
 
     return pl.pallas_call(
         kernel,
-        out_shape=pltpu.VMEM((owners, samples * embed_count, cap), jnp.bfloat16),
+        out_shape=[
+            pltpu.VMEM((owners, samples * embed_count, cap), jnp.bfloat16),
+            pltpu.HBM((owners, samples * embed_count, cap), jnp.bfloat16),
+        ],
         grid=(samples // group,),
         in_specs=[
             pl.BlockSpec((group, feature_count), lambda i: (i, 0)),
             pl.BlockSpec((embed_count, feature_count), lambda i: (0, 0)),
         ],
-        out_specs=pl.BlockSpec((owners, group * embed_count, cap), lambda i: (0, i, 0)),
+        out_specs=[pl.BlockSpec((owners, group * embed_count, cap), lambda i: (0, i, 0))] * 2,
         compiler_params=params(),
         cost_estimate=pl.CostEstimate(
             flops=2 * samples * owners * embed_count * feature_count * cap,
@@ -182,57 +193,63 @@
     )(spread, lead_grad, *extra)
 
 
-def add_rows(targets, returned, outgoing, rows):
+def add_rows(targets, returned, outgoing, rows, cap):
     count, width = returned.shape
-    chunk = min(count, 1024)
-    zeros = jnp.zeros((rows + 8, 1, width), jnp.float32)
-
-    def kernel(targets_ref, back_ref, sent_ref, zeros_ref, out_ref, total, terms, sem):
-        begin = pltpu.make_async_copy(zeros_ref, total, sem.at[0])
-        begin.start()
-
-        def fill(part, carry):
-            base = pl.multiple_of(part * chunk, chunk)
-            lines = pl.ds(base, chunk)
+    pair = 2 * cap
+
+    def kernel(targets_ref, back_ref, sent_ref, out_ref, total, second, terms, sem):
+        total[...] = jnp.zeros_like(total)
+        second[...] = jnp.zeros_like(second)
+
+        def body(step, carry):
+            base = pl.multiple_of(step * pair, pair)
+            lines = pl.ds(base, pair)
             terms[...] = back_ref[lines, :].astype(jnp.float32) + DECAY_WEIGHT * sent_ref[
                 lines, :
             ].astype(jnp.float32)
-
-            @pl.when(part == 0)
-            def _():
-                begin.wait()
-
-            def body(group, inner):
-                first = pl.multiple_of(group * UNROLL, UNROLL)
-                places = [targets_ref[base + first + lane] for lane in range(UNROLL)]
+            for first in range(0, cap, UNROLL):
+                lanes = range(first, first + UNROLL)
+                places = [targets_ref[base + lane] for lane in lanes]
+                others = [targets_ref[base + cap + lane] for lane in lanes]
                 sums = [
-                    total[places[lane]] + terms[pl.ds(first + lane, 1), :] for lane in range(UNROLL)
+                    total[pl.ds(place, 1), :] + terms[lane : lane + 1, :]
+                    for place, lane in zip(places, lanes)
                 ]
-                for lane in range(UNROLL):
-                    total[places[lane]] = sums[lane]
-                return inner
-
-            lax.fori_loop(0, chunk // UNROLL, body, 0)
+                other_sums = [
+                    second[pl.ds(place, 1), :] + terms[cap + lane : cap + lane + 1, :]
+                    for place, lane in zip(others, lanes)
+                ]
+                for place, value in zip(places, sums):
+                    total[pl.ds(place, 1), :] = value
+                for place, value in zip(others, other_sums):
+                    second[pl.ds(place, 1), :] = value
             return carry
 
-        lax.fori_loop(0, count // chunk, fill, 0)
-        finish = pltpu.make_async_copy(total.at[pl.ds(0, rows)], out_ref, sem.at[1])
-        finish.start()
-        finish.wait()
+        lax.fori_loop(0, count // pair, body, 0)
+        part = rows // 4
+        copies = []
+        for piece in range(4):
+            cut = pl.ds(piece * part, part)
+            total[cut, :] = total[cut, :] + second[cut, :]
+            copies.append(pltpu.make_async_copy(total.at[cut, :], out_ref.at[cut, :], sem.at[piece]))
+            copies[-1].start()
+        for copy in copies:
+            copy.wait()
 
     return pl.pallas_call(
         kernel,
-        out_shape=jax.ShapeDtypeStruct((rows, 1, width), jnp.float32),
-        in_specs=[whole(pltpu.SMEM), whole(), whole(), whole(pl.ANY)],
+        out_shape=jax.ShapeDtypeStruct((rows, width), jnp.float32),
+        in_specs=[whole(pltpu.SMEM), whole(), whole()],
         out_specs=whole(pl.ANY),
         scratch_shapes=[
-            pltpu.VMEM((rows + 8, 1, width), jnp.float32),
-            pltpu.VMEM((chunk, width), jnp.float32),
-            pltpu.SemaphoreType.DMA((2,)),
+            pltpu.VMEM((rows + 8, width), jnp.float32),
+            pltpu.VMEM((rows + 8, width), jnp.float32),
+            pltpu.VMEM((pair, width), jnp.float32),
+            pltpu.SemaphoreType.DMA((4,)),
         ],
         compiler_params=params(),
         name="add_rows",
-    )(targets, returned, outgoing, zeros).reshape(rows, width)
+    )(targets, returned, outgoing)
 
 
 GROUP = 16
@@ -358,9 +375,9 @@
 
 def up_product(normed, w_up, hidden, turned, wait, many=1):
     def work(columns):
-        opened = jnp.maximum(dot(normed[...], w_up[:, columns]), 0.0)
-        hidden[:, columns] = opened.astype(jnp.bfloat16)
-        turned[columns, :] = opened.T.astype(jnp.bfloat16)
+        opened = jnp.maximum(dot(normed[...], w_up[:, columns]), 0.0).astype(jnp.bfloat16)
+        hidden[:, columns] = opened
+        turned[columns, :] = opened.T
 
     width = hidden.shape[1]
     over_tiles(width, hidden_tile(width), many, wait, work)
@@ -376,7 +393,7 @@
 
 
 def turn(rows, turned):
-    turned[...] = rows[...].astype(jnp.float32).T.astype(jnp.bfloat16)
+    turned[...] = rows[...].T
 
 
 def opened_only(hidden, grad):
@@ -566,7 +583,7 @@
 
             def masked(columns):
                 before = dot(normed[...], up1.held[:, columns])
-                opened = jnp.maximum(before, 0.0).T
+                opened = jnp.maximum(before, 0.0).astype(jnp.bfloat16).T
                 g_before[columns, :] = opened_only(opened, ghid_ref[columns, :].astype(jnp.float32))
 
             over_tiles(hidden_width, hidden_tile(hidden_width), 1, up1.wait, masked)
@@ -728,8 +745,8 @@
         near = jnp.where(place // half == my_half, owner // along * half + place % half, near_owners)
         return spread_weights(near * cap + column, lcb_weight, near_owners, cap)
 
-    spread_far = spread_of(mirror_slots)
-    spread_near = spread_of(own_slots)
+    spread_far, kept_far = spread_of(mirror_slots)
+    spread_near, kept_near = spread_of(own_slots)
     smalls = jnp.stack(
         [jnp.where(core == 0, small, other_small), jnp.where(core == 0, other_small, small)]
     )
@@ -765,12 +782,12 @@
         own_grad = jnp.where(stage == s, moved(piece, 0, s), own_grad)
     mirror_grad = mirror(own_grad)
 
-    near_grad = expand(spread_near, own_grad, embed_count)
-    slot_grad = expand(spread_far, mirror_grad, embed_count, near_grad)
+    near_grad = expand(kept_near, own_grad, embed_count)
+    slot_grad = expand(kept_far, mirror_grad, embed_count, near_grad)
     returned = swap_in_half(slot_grad)
     live_slots = jnp.arange(cap) < near_first(row_counts[0], my_half)[..., None]
     targets = jnp.where(live_slots, picked, rows).reshape(-1)
-    return add_rows(targets, returned.reshape(-1, embed_width), outgoing, rows)
+    return add_rows(targets, returned.reshape(-1, embed_width), outgoing, rows, cap)
 
 
 def solution(mesh):

time: 159 us -> 157 us (0.987)
  waiting for transfers between devices: 65.2 us -> 63.2 us
    unnamed x25 -> x27, local copies, waits for them, and re-layouts: 6.45 us -> 7.61 us
  transfers between devices with their start and end apart: 12 -> 12, of which waited for: 8 -> 8; matrix products, arithmetic and copies ran while one was open for 3% -> 2% of each run, Pallas kernels for 10% -> 11%
where the time goes in v9:
time: 157 us; the launch traced here: 156 us
  waiting for transfers between devices  63.2 us (40%)
  Pallas kernels  57.5 us (37%)
  starting transfers between devices  24.5 us (16%)
  local copies, waits for them, and re-layouts  8.72 us (6%)
  other arithmetic  1.73 us (1%)
    ppermute x4, waiting for transfers between devices, moved(): return lax.ppermute(value, 'section', pairs)  38.2 us
    all_to_all x2, waiting for transfers between devices, swap_in_half(): lax.all_to_all(value, TABLE_AXES, split_axis=0, concat_axis=0, axis_index...  16.2 us
    pallas_call x1, Pallas kernels, backward_stage(): pl.pallas_call(kernel, out_shape=jax.ShapeDtypeStruct(grad.shape, jnp.bfl...  15.4 us
    pallas_call x1, Pallas kernels, forward_stage(): pl.pallas_call(kernel, out_shape=[jax.ShapeDtypeStruct(top.shape, jnp.bfl...  12.2 us
    all_to_all x2, starting transfers between devices, swap_in_half(): lax.all_to_all(value, TABLE_AXES, split_axis=0, concat_axis=0, axis_index...  12.1 us
    pallas_call x1, Pallas kernels, add_rows(): pl.pallas_call(kernel, out_shape=jax.ShapeDtypeStruct((rows, width), jnp....  10.2 us
    ppermute x3, waiting for transfers between devices, mirror(): lax.ppermute(value, 'table', [(t, (t + along // 2) % along) for t in rang...  8.77 us
    pallas_call x2, Pallas kernels, spread_weights(): pl.pallas_call(kernel, out_shape=[pltpu.VMEM((owners, samples * embed_cou...  7.85 us
  transfers between devices with their start and end apart: 12, of which 8 were waited for; matrix products, arithmetic and copies ran while one was open for 2% of the time, Pallas kernels for 11%

profile of v9, /device:TPU:0, one launch (start us, length us, event | category | flops | bytes accessed | tf_op | source)
XLA Modules:
  0.0 156.0 jit_solution(6540767408324812176)
XLA Ops:
  0.5 4.0 %collective-permute-start = (s32[64,512]{1,0:T(8,128)}, s32[64,512]{1,0:T(8,128)S(1)}, u32[]{:S(2)}, u32[]{:S(2)}) collective-permute-start(s32[64,512]{1,0:T(8,128)} %bitcast.41), channel_id=1, source_target_pairs={{0,4},{1,5},{2,6},{3,7},{4,0},{5,1},{6,2},{7,3},{8,12},{9,13},{10,... | collective-permute-start | bytes 393224 | tf_op jit(solution)/shard_map/ppermute | solution.py:676
  5.3 1.2 copy-done.7
  6.5 5.4 %pick_rows.1.sent_ref = bf16[4096,128]{1,0:T(8,128)(2,1)} custom-call(s32[4096]{0:T(1024)S(1)} %bitcast.32, bf16[4096,128]{1,0:T(8,128)(2,1)S(1)} %copy-done.7), custom_call_target="tpu_custom_call" | custom-call | tf_op jit(solution)/shard_map/pick_rows/pallas_call | solution.py:55
  11.9 4.8 %all-to-all-start = ((bf16[16,2,128,128]{3,2,1,0:T(8,128)(2,1)}), bf16[16,2,128,128]{3,2,1,0:T(8,128)(2,1)S(1)}, u32[]{:S(2)}, u32[]{:S(2)}) async-start(bf16[16,2,128,128]{3,2,1,0:T(8,128)(2,1)} %bitcast.12), calls=%async_computation | async-start | bytes 2097152 | tf_op jit(solution)/shard_map/all_to_all | solution.py:686
  17.7 3.9 %spread_weights.3 = (bf16[16,512,128]{2,1,0:T(8,128)(2,1)S(1)}, bf16[16,512,128]{2,1,0:T(8,128)(2,1)}) custom-call(s32[64,512]{1,0:T(8,128)S(1)} %fusion.11.codes_ref, bf16[8,512]{1,0:T(8,128)(2,1)S(1)} %copy-done.8), custom_call_target="tpu_custom_call" | custom-call | flops 1073741824 | bytes 2097152 | tf_op jit(solution)/shard_map/spread_weights/pallas_call | solution.py:96
  21.6 1.3 copy-done.5
  23.3 3.9 %spread_weights.2 = (bf16[16,512,128]{2,1,0:T(8,128)(2,1)S(1)}, bf16[16,512,128]{2,1,0:T(8,128)(2,1)}) custom-call(s32[64,512]{1,0:T(8,128)S(1)} %fusion.5.codes_ref, bf16[8,512]{1,0:T(8,128)(2,1)S(1)} %copy-done.8), custom_call_target="tpu_custom_call" | custom-call | flops 1073741824 | bytes 2097152 | tf_op jit(solution)/shard_map/spread_weights/pallas_call | solution.py:96
  27.2 1.3 copy-done.3
  28.6 3.0 %all-to-all-done.rows_ref = bf16[16,2,128,128]{3,2,1,0:T(8,128)(2,1)S(1)} async-done(((bf16[16,2,128,128]{3,2,1,0:T(8,128)(2,1)}), bf16[16,2,128,128]{3,2,1,0:T(8,128)(2,1)S(1)}, u32[]{:S(2)}, u32[]{:S(2)}) %all-to-all-start) | async-done | bytes 1048608 | tf_op jit(solution)/shard_map/all_to_all | solution.py:686
  31.6 1.6 %copy-done.4 = bf16[16,512,128]{2,1,0:T(8,128)(2,1)S(1)} copy-done((bf16[16,512,128]{2,1,0:T(8,128)(2,1)S(1)}, bf16[16,512,128]{2,1,0:T(8,128)(2,1)}, u32[]{:S(2)}) %copy-start.4) | copy-done | bytes 2097176
  33.2 0.9 compress.3
  34.1 2.0 %collective-permute-start.1 = (bf16[64,1024]{1,0:T(8,128)(2,1)S(1)}, bf16[64,1024]{1,0:T(8,128)(2,1)S(1)}, u32[]{:S(2)}, u32[]{:S(2)}) collective-permute-start(bf16[64,1024]{1,0:T(8,128)(2,1)S(1)} %compress.3), channel_id=1, source_target_pairs={{0,4},{1,5},{2,6},{3,7},{4,0},{5,1},{6,2},{7,3},{8,12},{9,13},{10,... | collective-permute-start | bytes 393224 | tf_op jit(solution)/shard_map/ppermute | solution.py:676
  36.2 1.6 %copy-done.6 = bf16[16,512,128]{2,1,0:T(8,128)(2,1)S(1)} copy-done((bf16[16,512,128]{2,1,0:T(8,128)(2,1)S(1)}, bf16[16,512,128]{2,1,0:T(8,128)(2,1)}, u32[]{:S(2)}) %copy-start.6) | copy-done | bytes 2097176
  37.8 0.9 compress.2
  38.7 4.3 %collective-permute-done.1 = bf16[64,1024]{1,0:T(8,128)(2,1)S(1)} collective-permute-done((bf16[64,1024]{1,0:T(8,128)(2,1)S(1)}, bf16[64,1024]{1,0:T(8,128)(2,1)S(1)}, u32[]{:S(2)}, u32[]{:S(2)}) %collective-permute-start.1) | collective-permute-done | bytes 131104 | tf_op jit(solution)/shard_map/ppermute | solution.py:676
  43.1 1.3 collective-permute-start.2
  44.4 5.5 %collective-permute-done.2.refs_1_ = bf16[64,1024]{1,0:T(8,128)(2,1)S(1)} collective-permute-done((bf16[64,1024]{1,0:T(8,128)(2,1)S(1)}, bf16[64,1024]{1,0:T(8,128)(2,1)S(1)}, u32[]{:S(2)}, u32[]{:S(2)}) %collective-permute-start.2) | collective-permute-done | bytes 131104 | tf_op jit(solution)/shard_map/ppermute | solution.py:671
  49.9 12.2 %forward_stage.1 = (bf16[128,1024]{1,0:T(8,128)(2,1)S(1)}, bf16[2,4096,128]{2,1,0:T(8,128)(2,1)S(1)}, f32[2,128,1024]{2,1,0:T(8,128)S(1)}, f32[2,128,128]{2,1,0:...) custom-call(s32[3]{0:T(128)S(1)} %pad_add_fusion.2.place_ref, ...), custom_call_target="tpu_custom_call" | custom-call | flops 4294967296 | bytes 1048576 | tf_op jit(solution)/shard_map/forward_stage/pallas_call | solution.py:542
  62.1 1.3 collective-permute-start.6
  63.5 4.0 %collective-permute-done.6.acts_ref = bf16[128,1024]{1,0:T(8,128)(2,1)S(1)} collective-permute-done((bf16[128,1024]{1,0:T(8,128)(2,1)S(1)}, bf16[128,1024]{1,0:T(8,128)(2,1)S(1)}, u32[]{:S(2)}, u32[]{:S(2)}) %collective-permute-start.6) | collective-permute-done | bytes 262176 | tf_op jit(solution)/shard_map/ppermute | solution.py:671
  67.5 0.9 turn_stage.1
  68.4 1.3 collective-permute-start.7
  69.7 26.2 %collective-permute-done.7.grad_ref = bf16[128,1024]{1,0:T(8,128)(2,1)S(1)} collective-permute-done((bf16[128,1024]{1,0:T(8,128)(2,1)S(1)}, bf16[128,1024]{1,0:T(8,128)(2,1)S(1)}, u32[]{:S(2)}, u32[]{:S(2)}) %collective-permute-start.7) | collective-permute-done | bytes 262176 | tf_op jit(solution)/shard_map/ppermute | solution.py:671
  95.9 15.4 %backward_stage.1 = bf16[128,1024]{1,0:T(8,128)(2,1)S(1)} custom-call(s32[3]{0:T(128)S(1)} %pad_add_fusion.2.place_ref, bf16[128,1024]{1,0:T(8,128)(2,1)S(1)} %collective-permute-done.7.grad_ref, bf16[2,4096,128]{2,1,0:T(8,128)(2,1)S(1)} %get-tuple-element.26.hid, f32[2,128,1024]{2,1,0:T(8,128)S(1)} %get-tuple-element.27.inter, ...), custom_call_target="tpu_custom_call" | custom-call | flops 4294967296 | bytes 1048576 | tf_op jit(solution)/shard_map/backward_stage/pallas_call | solution.py:647
  111.4 1.4 collective-permute-start.8
  112.8 2.5 %collective-permute-done.8 = bf16[64,1024]{1,0:T(8,128)(2,1)S(1)} collective-permute-done((bf16[64,1024]{1,0:T(8,128)(2,1)S(1)}, bf16[64,1024]{1,0:T(8,128)(2,1)S(1)}, u32[]{:S(2)}, u32[]{:S(2)}) %collective-permute-start.8) | collective-permute-done | bytes 131104 | tf_op jit(solution)/shard_map/ppermute | solution.py:671
  115.4 1.4 expand.2.refs_0_
  116.8 4.5 %collective-permute-done.9.grad_ref = bf16[64,1024]{1,0:T(8,128)(2,1)S(1)} collective-permute-done((bf16[64,1024]{1,0:T(8,128)(2,1)S(1)}, bf16[64,1024]{1,0:T(8,128)(2,1)S(1)}, u32[]{:S(2)}, u32[]{:S(2)}) %collective-permute-start.9) | collective-permute-done | bytes 131104 | tf_op jit(solution)/shard_map/ppermute | solution.py:676
  121.2 2.4 %expand.3 = bf16[16,2,128,128]{3,2,1,0:T(8,128)(2,1)} custom-call(bf16[16,512,128]{2,1,0:T(8,128)(2,1)S(1)} %copy-done.2, bf16[64,1024]{1,0:T(8,128)(2,1)S(1)} %collective-permute-done.9.grad_ref, bf16[16,128,128]{2,1,0:T(8,128)(2,1)S(1)} %expand.2.refs_0_), custom_call_target="tpu_custom_call" | custom-call | tf_op jit(solution)/shard_map/expand/pallas_call | solution.py:182
  123.6 7.3 %all-to-all-start.1 = ((bf16[16,2,128,128]{3,2,1,0:T(8,128)(2,1)}), bf16[16,2,128,128]{3,2,1,0:T(8,128)(2,1)S(1)}, u32[]{:S(2)}, u32[]{:S(2)}) async-start(bf16[16,2,128,128]{3,2,1,0:T(8,128)(2,1)} %expand.3), calls=%async_computation.1 | async-start | bytes 2097152 | tf_op jit(solution)/shard_map/all_to_all | solution.py:686
  132.6 13.2 %all-to-all-done.1 = bf16[16,2,128,128]{3,2,1,0:T(8,128)(2,1)S(1)} async-done(((bf16[16,2,128,128]{3,2,1,0:T(8,128)(2,1)}), bf16[16,2,128,128]{3,2,1,0:T(8,128)(2,1)S(1)}, u32[]{:S(2)}, u32[]{:S(2)}) %all-to-all-start.1) | async-done | bytes 1048608 | tf_op jit(solution)/shard_map/all_to_all | solution.py:686
  145.7 10.2 %add_rows.1 = f32[4096,128]{1,0:T(8,128)} custom-call(s32[4096]{0:T(1024)S(1)} %bitcast.31, bf16[4096,128]{1,0:T(8,128)(2,1)S(1)} %bitcast.28, bf16[4096,128]{1,0:T(8,128)(2,1)} %pick_rows.1.sent_ref), custom_call_target="tpu_custom_call" | custom-call | tf_op jit(solution)/shard_map/add_rows/pallas_call | solution.py:239
  (52 shorter events, 4.5 us)
Async XLA Ops:
  0.0 36.2 %copy-start = (bf16[1,4,64,1024]{3,2,1,0:T(8,128)(2,1)S(1)}, bf16[1,4,64,1024]{3,2,1,0:T(8,128)(2,1)}, u32[]{:S(2)}) copy-start(bf16[1,4,64,1024]{3,2,1,0:T(8,128)(2,1)} %param.16) | copy-start | bytes 1572868
  0.0 49.9 %collective-permute-start.4 = (bf16[1024,4096]{1,0:T(8,128)(2,1)}, bf16[1024,4096]{1,0:T(8,128)(2,1)}, u32[]{:S(2)}, u32[]{:S(2)}) collective-permute-start(bf16[1024,4096]{1,0:T(8,128)(2,1)} %bitcast.33), channel_id=1, source_target_pairs={{0,8},{8,0},{16,24},{24,16},{1,9},{9,1},{17,25},{25,17},{2,10},{10... | collective-permute-start | bytes 25165832 | tf_op jit(solution)/shard_map/ppermute | solution.py:666
  0.5 49.5 %collective-permute-start.5 = (bf16[4096,1024]{1,0:T(8,128)(2,1)}, bf16[4096,1024]{1,0:T(8,128)(2,1)}, u32[]{:S(2)}, u32[]{:S(2)}) collective-permute-start(bf16[4096,1024]{1,0:T(8,128)(2,1)} %bitcast.37), channel_id=1, source_target_pairs={{0,8},{8,0},{16,24},{24,16},{1,9},{9,1},{17,25},{25,17},{2,10},{10... | collective-permute-start | bytes 25165832 | tf_op jit(solution)/shard_map/ppermute | solution.py:666
  0.5 11.4 %collective-permute-start = (s32[64,512]{1,0:T(8,128)}, s32[64,512]{1,0:T(8,128)S(1)}, u32[]{:S(2)}, u32[]{:S(2)}) collective-permute-start(s32[64,512]{1,0:T(8,128)} %bitcast.41), channel_id=1, source_target_pairs={{0,4},{1,5},{2,6},{3,7},{4,0},{5,1},{6,2},{7,3},{8,12},{9,13},{10,... | collective-permute-start | bytes 393224 | tf_op jit(solution)/shard_map/ppermute | solution.py:676
  5.3 1.2 copy-start.7
  6.5 10.3 %copy-start.11 = (bf16[1,1024]{1,0:T(2,128)(2,1)S(1)}, bf16[1,1024]{1,0:T(2,128)(2,1)}, u32[]{:S(2)}) copy-start(bf16[1,1024]{1,0:T(2,128)(2,1)} %param.13) | copy-start | bytes 6148
  6.5 10.3 %copy-start.10 = (bf16[1,8,128]{2,1,0:T(8,128)(2,1)S(1)}, bf16[1,8,128]{2,1,0:T(8,128)(2,1)}, u32[]{:S(2)}) copy-start(bf16[1,8,128]{2,1,0:T(8,128)(2,1)} %param.12) | copy-start | bytes 6148
  6.5 10.8 %copy-start.9 = (s32[1,64,512]{2,1,0:T(8,128)S(1)}, s32[1,64,512]{2,1,0:T(8,128)}, u32[]{:S(2)}) copy-start(s32[1,64,512]{2,1,0:T(8,128)} %param.17) | copy-start | bytes 393220
  6.5 11.2 %copy-start.8 = (bf16[8,512]{1,0:T(8,128)(2,1)S(1)}, bf16[8,512]{1,0:T(8,128)(2,1)}, u32[]{:S(2)}) copy-start(bf16[8,512]{1,0:T(8,128)(2,1)} %lcb_ref.3) | copy-start | bytes 24580
  11.9 19.7 %all-to-all-start = ((bf16[16,2,128,128]{3,2,1,0:T(8,128)(2,1)}), bf16[16,2,128,128]{3,2,1,0:T(8,128)(2,1)S(1)}, u32[]{:S(2)}, u32[]{:S(2)}) async-start(bf16[16,2,128,128]{3,2,1,0:T(8,128)(2,1)} %bitcast.12), calls=%async_computation | async-start | bytes 2097152 | tf_op jit(solution)/shard_map/all_to_all | solution.py:686
  16.8 27.5 %collective-permute-start.3 = (bf16[16,128]{1,0:T(8,128)(2,1)S(1)}, bf16[16,128]{1,0:T(8,128)(2,1)S(1)}, u32[]{:S(2)}, u32[]{:S(2)}) collective-permute-start(bf16[16,128]{1,0:T(8,128)(2,1)S(1)} %pad_maximum_fusion.1), channel_id=1, source_target_pairs={{0,8},{8,0},{16,24},{24,16},{1,9},{9,1},{17,25},{25,17},{2,10},{10... | collective-permute-start | bytes 12296 | tf_op jit(solution)/shard_map/ppermute | solution.py:666
  21.6 1.3 copy-start.5
  27.2 1.3 copy-start.3
  31.6 1.6 %copy-start.4 = (bf16[16,512,128]{2,1,0:T(8,128)(2,1)S(1)}, bf16[16,512,128]{2,1,0:T(8,128)(2,1)}, u32[]{:S(2)}) copy-start(bf16[16,512,128]{2,1,0:T(8,128)(2,1)} %copy-done.3) | copy-start | bytes 6291460
  34.1 8.9 %collective-permute-start.1 = (bf16[64,1024]{1,0:T(8,128)(2,1)S(1)}, bf16[64,1024]{1,0:T(8,128)(2,1)S(1)}, u32[]{:S(2)}, u32[]{:S(2)}) collective-permute-start(bf16[64,1024]{1,0:T(8,128)(2,1)S(1)} %compress.3), channel_id=1, source_target_pairs={{0,4},{1,5},{2,6},{3,7},{4,0},{5,1},{6,2},{7,3},{8,12},{9,13},{10,... | collective-permute-start | bytes 393224 | tf_op jit(solution)/shard_map/ppermute | solution.py:676
  36.2 1.6 %copy-start.6 = (bf16[16,512,128]{2,1,0:T(8,128)(2,1)S(1)}, bf16[16,512,128]{2,1,0:T(8,128)(2,1)}, u32[]{:S(2)}) copy-start(bf16[16,512,128]{2,1,0:T(8,128)(2,1)} %copy-done.5) | copy-start | bytes 6291460
  43.1 6.9 %collective-permute-start.2 = (bf16[64,1024]{1,0:T(8,128)(2,1)S(1)}, bf16[64,1024]{1,0:T(8,128)(2,1)S(1)}, u32[]{:S(2)}, u32[]{:S(2)}) collective-permute-start(bf16[64,1024]{1,0:T(8,128)(2,1)S(1)} %add_convert_fusion.refs_0_), channel_id=1, source_target_pairs={{16,0},{24,8},{17,1},{25,9},{18,2},{26,10},{19,3},{27,11},{20,4},{... | collective-permute-start | bytes 393224 | tf_op jit(solution)/shard_map/ppermute | solution.py:671
  62.1 5.4 %collective-permute-start.6 = (bf16[128,1024]{1,0:T(8,128)(2,1)S(1)}, bf16[128,1024]{1,0:T(8,128)(2,1)S(1)}, u32[]{:S(2)}, u32[]{:S(2)}) collective-permute-start(bf16[128,1024]{1,0:T(8,128)(2,1)S(1)} %get-tuple-element.24), channel_id=1, source_target_pairs={{0,16},{8,24},{1,17},{9,25},{2,18},{10,26},{3,19},{11,27},{4,20},{... | collective-permute-start | bytes 786440 | tf_op jit(solution)/shard_map/ppermute | solution.py:671
  68.4 27.5 %collective-permute-start.7 = (bf16[128,1024]{1,0:T(8,128)(2,1)S(1)}, bf16[128,1024]{1,0:T(8,128)(2,1)S(1)}, u32[]{:S(2)}, u32[]{:S(2)}) collective-permute-start(bf16[128,1024]{1,0:T(8,128)(2,1)S(1)} %turn_stage.1), channel_id=1, source_target_pairs={{16,0},{24,8},{17,1},{25,9},{18,2},{26,10},{19,3},{27,11},{20,4},{... | collective-permute-start | bytes 786440 | tf_op jit(solution)/shard_map/ppermute | solution.py:671
  95.9 19.5 %copy-start.1 = (bf16[16,512,128]{2,1,0:T(8,128)(2,1)S(1)}, bf16[16,512,128]{2,1,0:T(8,128)(2,1)}, u32[]{:S(2)}) copy-start(bf16[16,512,128]{2,1,0:T(8,128)(2,1)} %get-tuple-element.30.spread_ref) | copy-start | bytes 6291460
  111.3 9.9 %copy-start.2 = (bf16[16,512,128]{2,1,0:T(8,128)(2,1)S(1)}, bf16[16,512,128]{2,1,0:T(8,128)(2,1)}, u32[]{:S(2)}) copy-start(bf16[16,512,128]{2,1,0:T(8,128)(2,1)} %get-tuple-element.18.spread_ref) | copy-start | bytes 6291460
  111.4 3.9 %collective-permute-start.8 = (bf16[64,1024]{1,0:T(8,128)(2,1)S(1)}, bf16[64,1024]{1,0:T(8,128)(2,1)S(1)}, u32[]{:S(2)}, u32[]{:S(2)}) collective-permute-start(bf16[64,1024]{1,0:T(8,128)(2,1)S(1)} %slice.8), channel_id=1, source_target_pairs={{0,16},{8,24},{1,17},{9,25},{2,18},{10,26},{3,19},{11,27},{4,20},{... | collective-permute-start | bytes 393224 | tf_op jit(solution)/shard_map/ppermute | solution.py:671
  115.3 5.9 %collective-permute-start.9 = (bf16[64,1024]{1,0:T(8,128)(2,1)S(1)}, bf16[64,1024]{1,0:T(8,128)(2,1)S(1)}, u32[]{:S(2)}, u32[]{:S(2)}) collective-permute-start(bf16[64,1024]{1,0:T(8,128)(2,1)S(1)} %slice_select_fusion.grad_ref), channel_id=1, source_target_pairs={{0,4},{1,5},{2,6},{3,7},{4,0},{5,1},{6,2},{7,3},{8,12},{9,13},{10,... | collective-permute-start | bytes 393224 | tf_op jit(solution)/shard_map/ppermute | solution.py:676
  121.2 10.2 %copy-start.12 = (s32[1,32]{1,0:T(1,128)S(1)}, s32[1,32]{1,0:T(1,128)}, u32[]{:S(2)}) copy-start(s32[1,32]{1,0:T(1,128)} %param.19) | copy-start | bytes 388
  123.6 22.1 %all-to-all-start.1 = ((bf16[16,2,128,128]{3,2,1,0:T(8,128)(2,1)}), bf16[16,2,128,128]{3,2,1,0:T(8,128)(2,1)S(1)}, u32[]{:S(2)}, u32[]{:S(2)}) async-start(bf16[16,2,128,128]{3,2,1,0:T(8,128)(2,1)} %expand.3), calls=%async_computation.1 | async-start | bytes 2097152 | tf_op jit(solution)/shard_map/all_to_all | solution.py:686

commit v10 on v9

--- a/solution.py
+++ b/solution.py
@@ -71,7 +71,7 @@
     embed_count = lcb_weight.shape[0]
     group = tiles_of(samples, 16)
 
-    def kernel(codes_ref, lcb_ref, out_ref, kept_ref):
+    def kernel(codes_ref, lcb_ref, out_ref):
         lcb = lcb_ref[...].astype(jnp.float32)
         owner_of = lax.broadcasted_iota(jnp.int32, (owners, embed_count, feature_count), 0)
         column_of = lax.broadcasted_iota(jnp.int32, (cap, feature_count), 0)
@@ -91,20 +91,16 @@
             rows = pl.ds(pair * embed_count, 2 * embed_count)
             joined = jnp.concatenate(made, axis=1).astype(out_ref.dtype)
             out_ref[:, rows, :] = joined
-            kept_ref[:, rows, :] = joined
 
     return pl.pallas_call(
         kernel,
-        out_shape=[
-            pltpu.VMEM((owners, samples * embed_count, cap), jnp.bfloat16),
-            pltpu.HBM((owners, samples * embed_count, cap), jnp.bfloat16),
-        ],
+        out_shape=pltpu.HBM((owners, samples * embed_count, cap), jnp.bfloat16),
         grid=(samples // group,),
         in_specs=[
             pl.BlockSpec((group, feature_count), lambda i: (i, 0)),
             pl.BlockSpec((embed_count, feature_count), lambda i: (0, 0)),
         ],
-        out_specs=[pl.BlockSpec((owners, group * embed_count, cap), lambda i: (0, i, 0))] * 2,
+        out_specs=pl.BlockSpec((owners, group * embed_count, cap), lambda i: (0, i, 0)),
         compiler_params=params(),
         cost_estimate=pl.CostEstimate(
             flops=2 * samples * owners * embed_count * feature_count * cap,
@@ -122,17 +118,19 @@
     part = tiles_of(owners, 8)
     steps = owners // part
 
-    def kernel(spread_ref, rows_ref, out_ref, total):
-        total[...] = jnp.zeros_like(total)
-
-        def body(step, carry):
-            first = step * part
-            left = jnp.concatenate([spread_ref[first + o] for o in range(part)], axis=1)
-            right = jnp.concatenate([rows_ref[first + o, view] for o in range(part)], axis=0)
-            total[...] += jnp.dot(left, right, preferred_element_type=jnp.float32)
-            return carry
-
-        lax.fori_loop(0, steps, body, 0)
+    def kernel(spread_ref, rows_ref, out_ref, held, total, sems):
+        copies = []
+        for step in range(steps):
+            piece = pl.ds(step * part, part)
+            copies.append(pltpu.make_async_copy(spread_ref.at[piece], held.at[piece], sems.at[step]))
+            copies[-1].start()
+        for step in range(steps):
+            copies[step].wait()
+            owners_here = range(step * part, (step + 1) * part)
+            left = jnp.concatenate([held[o] for o in owners_here], axis=1)
+            right = jnp.concatenate([rows_ref[o, view] for o in owners_here], axis=0)
+            term = jnp.dot(left, right, preferred_element_type=jnp.float32)
+            total[...] = term if step == 0 else total[...] + term
         for k in range(embed_count):
             columns = slice(k * width, (k + 1) * width)
             piece = total[pl.ds(k, samples, stride=embed_count), :]
@@ -141,19 +139,23 @@
     return pl.pallas_call(
         kernel,
         out_shape=jax.ShapeDtypeStruct((samples, embed_count * width), kind),
-        in_specs=[whole(), whole()],
+        in_specs=[whole(pltpu.HBM), whole()],
         out_specs=whole(),
-        scratch_shapes=[pltpu.VMEM((lines, width), jnp.float32)],
+        scratch_shapes=[
+            pltpu.VMEM(spread.shape, jnp.bfloat16),
+            pltpu.VMEM((lines, width), jnp.float32),
+            pltpu.SemaphoreType.DMA((steps,)),
+        ],
         compiler_params=params(),
         name="compress",
-    )(spread, fetched)
+    )(in_hbm(spread), fetched)
 
 
 def expand(spread, lead_grad, embed_count, near=None):
     owners, lines, cap = spread.shape
     samples = lines // embed_count
     width = lead_grad.shape[1] // embed_count
-    part = tiles_of(owners, 4)
+    part = tiles_of(owners, 8)
     extra = [] if near is None else [near]
 
     def kernel(spread_ref, grad_ref, *refs):
@@ -373,11 +375,10 @@
     lax.fori_loop(0, total // (many * tile), body, 0)
 
 
-def up_product(normed, w_up, hidden, turned, wait, many=1):
+def up_product(normed, w_up, hidden, wait, many=1):
     def work(columns):
-        opened = jnp.maximum(dot(normed[...], w_up[:, columns]), 0.0).astype(jnp.bfloat16)
-        hidden[:, columns] = opened
-        turned[columns, :] = opened.T
+        before = dot(normed[...], w_up[:, columns])
+        hidden[:, columns] = jnp.maximum(before, 0.0).astype(jnp.bfloat16)
 
     width = hidden.shape[1]
     over_tiles(width, hidden_tile(width), many, wait, work)
@@ -392,29 +393,25 @@
     over_tiles(width, model_tile(width), many, wait, work)
 
 
-def turn(rows, turned):
-    turned[...] = rows[...].T
-
-
 def opened_only(hidden, grad):
     return jnp.where(hidden.astype(jnp.float32) > 0.0, grad, 0.0).astype(jnp.bfloat16)
 
 
 def down_back(grad, w_down, hidden, out, wait, many=1):
-    def work(lines):
-        g_hidden = dot(w_down[lines, :], grad[...])
+    def work(columns):
+        g_hidden = dot_nt(grad[...], w_down[columns, :])
         if hidden is not None:
-            out[lines, :] = opened_only(hidden[lines, :], g_hidden)
+            out[:, columns] = opened_only(hidden[:, columns], g_hidden)
         else:
-            out[lines, :] = g_hidden.astype(jnp.bfloat16)
-
-    width = out.shape[0]
+            out[:, columns] = g_hidden.astype(jnp.bfloat16)
+
+    width = out.shape[1]
     over_tiles(width, hidden_tile(width), many, wait, work)
 
 
 def up_back(g_before, w_up, weighted, wait, many=1):
     def work(columns):
-        weighted[:, columns] = dot(w_up[columns, :], g_before[...]).T
+        weighted[:, columns] = dot_nt(g_before[...], w_up[columns, :])
 
     width = weighted.shape[1]
     over_tiles(width, model_tile(width), many, wait, work)
@@ -451,7 +448,7 @@
 
 def saved_shapes(batch, model_width, hidden_width, width):
     return [
-        jax.ShapeDtypeStruct((2, hidden_width, batch), jnp.bfloat16),
+        jax.ShapeDtypeStruct((2, batch, hidden_width), jnp.bfloat16),
         jax.ShapeDtypeStruct((2, batch, model_width), jnp.float32),
         jax.ShapeDtypeStruct((2, batch, width), jnp.float32),
         jax.ShapeDtypeStruct((2, batch, model_width), jnp.bfloat16),
@@ -510,7 +507,7 @@
         piece_refs, (top_ref, small_ref), refs = refs[: len(pieces)], refs[len(pieces) :][:2], refs[len(pieces) + 2 :]
         matrices, refs = refs[:4], refs[4:]
         out_ref, hid, inter, scale, kept, g_hidden = refs[:6]
-        held, (normed, hidden, top_turned, grams) = refs[6:9], refs[9:]
+        held, (normed, grams) = refs[6:9], refs[9:]
         core = place_ref[0]
 
         @pl.when(place_ref[1] == 1)
@@ -527,30 +524,27 @@
                 mix_forward(
                     small_ref, layer, kept.at[layer], inter.at[layer], scale.at[layer], normed, grams, count
                 )
-                up_product(normed, up.held, hidden, hid.at[layer], up.wait)
+                up_product(normed, up.held, hid.at[layer], up.wait)
                 to = kept.at[1] if layer == 0 else out_ref
-                down_product(hidden, down.held, kept.at[layer], to, down.wait)
+                down_product(hid.at[layer], down.held, kept.at[layer], to, down.wait)
 
         @pl.when(place_ref[2] == 1)
         def _():
             layers = streams_of(core, matrices, held, [(True, True), (True, False)])
             down = layers[1][1]
             down.start()
-            turn(top_ref, top_turned)
-            down_back(top_turned, down.held, None, g_hidden, down.wait)
+            down_back(top_ref, down.held, None, g_hidden, down.wait)
 
     out = pl.pallas_call(
         kernel,
         out_shape=[jax.ShapeDtypeStruct(top.shape, jnp.bfloat16)]
         + saved_shapes(batch, model_width, hidden_width, width)
-        + [jax.ShapeDtypeStruct((hidden_width, batch), jnp.bfloat16)],
+        + [jax.ShapeDtypeStruct((batch, hidden_width), jnp.bfloat16)],
         in_specs=[whole(pltpu.SMEM)] + [whole()] * (len(pieces) + 1) + weight_specs(),
         out_specs=[whole()] * 6,
         scratch_shapes=weight_scratch(model_width, hidden_width)
         + [
             pltpu.VMEM((batch, model_width), jnp.bfloat16),
-            pltpu.VMEM((batch, hidden_width), jnp.bfloat16),
-            pltpu.VMEM((model_width, batch), jnp.bfloat16),
             gram_scratch(batch, count),
         ],
         compiler_params=stage_params(),
@@ -568,7 +562,7 @@
     def kernel(place_ref, acts_ref, top_ref, ghid_ref, small_ref, *refs):
         matrices, refs = refs[:4], refs[4:]
         out_ref, held = refs[0], refs[1:4]
-        hid, hidden, inter, scale, upper, grad, turned, normed, weighted, g_before, grams = refs[4:]
+        hid, inter, scale, upper, grad, normed, weighted, g_before, grams = refs[4:]
 
         @pl.when(place_ref[1] == 1)
         def _():
@@ -577,20 +571,18 @@
             for stream in (up0, down0, up1):
                 stream.start()
             mix_forward(small_ref, 0, acts_ref, inter.at[0], scale.at[0], normed, grams, count)
-            up_product(normed, up0.held, hidden, hid, up0.wait)
-            down_product(hidden, down0.held, acts_ref, upper, down0.wait)
+            up_product(normed, up0.held, hid, up0.wait)
+            down_product(hid, down0.held, acts_ref, upper, down0.wait)
             mix_forward(small_ref, 1, upper, inter.at[1], scale.at[1], normed, grams, count)
 
             def masked(columns):
                 before = dot(normed[...], up1.held[:, columns])
-                opened = jnp.maximum(before, 0.0).astype(jnp.bfloat16).T
-                g_before[columns, :] = opened_only(opened, ghid_ref[columns, :].astype(jnp.float32))
+                g_before[:, columns] = opened_only(before, ghid_ref[:, columns].astype(jnp.float32))
 
             over_tiles(hidden_width, hidden_tile(hidden_width), 1, up1.wait, masked)
             up_back(g_before, up1.held, weighted, no_wait)
             mix_backward(small_ref, 1, top_ref, upper, inter.at[1], scale.at[1], weighted, grad, count)
-            turn(grad, turned)
-            down_back(turned, down0.held, hid, g_before, no_wait)
+            down_back(grad, down0.held, hid, g_before, no_wait)
             up_back(g_before, up0.held, weighted, no_wait)
             mix_backward(small_ref, 0, grad, acts_ref, inter.at[0], scale.at[0], weighted, out_ref, count)
 
@@ -601,16 +593,14 @@
         out_specs=whole(),
         scratch_shapes=weight_scratch(model_width, hidden_width)
         + [
-            pltpu.VMEM((hidden_width, batch), jnp.bfloat16),
             pltpu.VMEM((batch, hidden_width), jnp.bfloat16),
             pltpu.VMEM((2, batch, model_width), jnp.float32),
             pltpu.VMEM((2, batch, width), jnp.float32),
             pltpu.VMEM((batch, model_width), jnp.bfloat16),
             pltpu.VMEM((batch, model_width), jnp.bfloat16),
-            pltpu.VMEM((model_width, batch), jnp.bfloat16),
             pltpu.VMEM((batch, model_width), jnp.bfloat16),
             pltpu.VMEM((batch, model_width), jnp.float32),
-            pltpu.VMEM((hidden_width, batch), jnp.bfloat16),
+            pltpu.VMEM((batch, hidden_width), jnp.bfloat16),
             gram_scratch(batch, count),
         ],
         compiler_params=stage_params(),
@@ -626,7 +616,7 @@
     def kernel(place_ref, grad_ref, hid, inter, scale, kept, small_ref, *refs):
         matrices, refs = refs[:4], refs[4:]
         out_ref, held = refs[0], refs[1:4]
-        middle, turned, weighted, g_before = refs[4:]
+        middle, weighted, g_before = refs[4:]
 
         @pl.when(place_ref[1] == 1)
         def _():
@@ -636,8 +626,7 @@
                 up.start()
             for layer, given, to in ((1, grad_ref, middle), (0, middle, out_ref)):
                 up, down = layers[layer]
-                turn(given, turned)
-                down_back(turned, down.held, hid.at[layer], g_before, down.wait)
+                down_back(given, down.held, hid.at[layer], g_before, down.wait)
                 up_back(g_before, up.held, weighted, up.wait)
                 mix_backward(
                     small_ref, layer, given, kept.at[layer], inter.at[layer], scale.at[layer],
@@ -652,9 +641,8 @@
         scratch_shapes=weight_scratch(model_width, hidden_width)
         + [
             pltpu.VMEM((batch, model_width), jnp.bfloat16),
-            pltpu.VMEM((model_width, batch), jnp.bfloat16),
             pltpu.VMEM((batch, model_width), jnp.float32),
-            pltpu.VMEM((hidden_width, batch), jnp.bfloat16),
+            pltpu.VMEM((batch, hidden_width), jnp.bfloat16),
         ],
         compiler_params=stage_params(),
         cost_estimate=stage_cost(4, batch, model_width, hidden_width),
@@ -745,8 +733,8 @@
         near = jnp.where(place // half == my_half, owner // along * half + place % half, near_owners)
         return spread_weights(near * cap + column, lcb_weight, near_owners, cap)
 
-    spread_far, kept_far = spread_of(mirror_slots)
-    spread_near, kept_near = spread_of(own_slots)
+    spread_far = spread_of(mirror_slots)
+    spread_near = spread_of(own_slots)
     smalls = jnp.stack(
         [jnp.where(core == 0, small, other_small), jnp.where(core == 0, other_small, small)]
     )
@@ -782,8 +770,8 @@
         own_grad = jnp.where(stage == s, moved(piece, 0, s), own_grad)
     mirror_grad = mirror(own_grad)
 
-    near_grad = expand(kept_near, own_grad, embed_count)
-    slot_grad = expand(kept_far, mirror_grad, embed_count, near_grad)
+    near_grad = expand(spread_near, own_grad, embed_count)
+    slot_grad = expand(spread_far, mirror_grad, embed_count, near_grad)
     returned = swap_in_half(slot_grad)
     live_slots = jnp.arange(cap) < near_first(row_counts[0], my_half)[..., None]
     targets = jnp.where(live_slots, picked, rows).reshape(-1)

time: 157 us -> 159 us (1.013)
  local copies, waits for them, and re-layouts: 8.72 us -> 3.59 us
  Pallas kernels: 57.5 us -> 61.6 us
  other arithmetic: 1.73 us -> 4 us
    unnamed x27 -> x17, local copies, waits for them, and re-layouts: 7.61 us -> 2.49 us
    pallas_call x2, Pallas kernels: 1.88 us -> 5.3 us  [compress(): pl.pallas_call(kernel, out_shape=jax.ShapeDtypeStruct((samples, embed_cou...]
    pallas_call x1, Pallas kernels: 15.4 us -> 17 us  [backward_stage(): pl.pallas_call(kernel, out_shape=jax.ShapeDtypeStruct(grad.shape, jnp.bfl...]
  transfers between devices with their start and end apart: 12 -> 12, of which waited for: 8 -> 8; matrix products, arithmetic and copies ran while one was open for 2% -> 4% of each run, Pallas kernels for 11% -> 12%
where the time goes in v10:
time: 159 us; the launch traced here: 158 us
  waiting for transfers between devices  64.1 us (40%)
  Pallas kernels  61.6 us (39%)
  starting transfers between devices  24.4 us (15%)
  other arithmetic  4 us (3%)
  local copies, waits for them, and re-layouts  3.59 us (2%)
    ppermute x4, waiting for transfers between devices, moved(): return lax.ppermute(value, 'section', pairs)  38.9 us
    pallas_call x1, Pallas kernels, backward_stage(): pl.pallas_call(kernel, out_shape=jax.ShapeDtypeStruct(grad.shape, jnp.bfl...  17 us
    all_to_all x2, waiting for transfers between devices, swap_in_half(): lax.all_to_all(value, TABLE_AXES, split_axis=0, concat_axis=0, axis_index...  16 us
    all_to_all x2, starting transfers between devices, swap_in_half(): lax.all_to_all(value, TABLE_AXES, split_axis=0, concat_axis=0, axis_index...  12.2 us
    pallas_call x1, Pallas kernels, forward_stage(): pl.pallas_call(kernel, out_shape=[jax.ShapeDtypeStruct(top.shape, jnp.bfl...  12.2 us
    pallas_call x1, Pallas kernels, add_rows(): pl.pallas_call(kernel, out_shape=jax.ShapeDtypeStruct((rows, width), jnp....  10.2 us
    ppermute x3, waiting for transfers between devices, mirror(): lax.ppermute(value, 'table', [(t, (t + along // 2) % along) for t in rang...  9.09 us
    pallas_call x2, Pallas kernels, spread_weights(): pl.pallas_call(kernel, out_shape=pltpu.HBM((owners, samples * embed_count...  7.77 us
  transfers between devices with their start and end apart: 12, of which 8 were waited for; matrix products, arithmetic and copies ran while one was open for 4% of the time, Pallas kernels for 12%

profile of v10, /device:TPU:0, one launch (start us, length us, event | category | flops | bytes accessed | tf_op | source)
XLA Modules:
  0.0 158.0 jit_solution(9373762981962451070)
XLA Ops:
  0.5 4.0 %collective-permute-start = (s32[64,512]{1,0:T(8,128)}, s32[64,512]{1,0:T(8,128)S(1)}, u32[]{:S(2)}, u32[]{:S(2)}) collective-permute-start(s32[64,512]{1,0:T(8,128)} %bitcast.41), channel_id=1, source_target_pairs={{0,4},{1,5},{2,6},{3,7},{4,0},{5,1},{6,2},{7,3},{8,12},{9,13},{10,... | collective-permute-start | bytes 393224 | tf_op jit(solution)/shard_map/ppermute | solution.py:664
  4.6 0.7 constant_dynamic-slice_fusion.2
  5.3 1.2 copy-done.3
  6.5 5.4 %pick_rows.1.sent_ref = bf16[4096,128]{1,0:T(8,128)(2,1)} custom-call(s32[4096]{0:T(1024)S(1)} %bitcast.32, bf16[4096,128]{1,0:T(8,128)(2,1)S(1)} %copy-done.3), custom_call_target="tpu_custom_call" | custom-call | tf_op jit(solution)/shard_map/pick_rows/pallas_call | solution.py:55
  11.9 4.8 %all-to-all-start = ((bf16[16,2,128,128]{3,2,1,0:T(8,128)(2,1)}), bf16[16,2,128,128]{3,2,1,0:T(8,128)(2,1)S(1)}, u32[]{:S(2)}, u32[]{:S(2)}) async-start(bf16[16,2,128,128]{3,2,1,0:T(8,128)(2,1)} %bitcast.12), calls=%async_computation | async-start | bytes 2097152 | tf_op jit(solution)/shard_map/all_to_all | solution.py:674
  16.8 0.7 reduce.3
  18.6 1.3 fusion.11.codes_ref
  19.9 0.7 copy-done.4
  20.6 3.9 %spread_weights.3.spread_ref = bf16[16,512,128]{2,1,0:T(8,128)(2,1)} custom-call(s32[64,512]{1,0:T(8,128)S(1)} %fusion.11.codes_ref, bf16[8,512]{1,0:T(8,128)(2,1)S(1)} %copy-done.4), custom_call_target="tpu_custom_call" | custom-call | flops 1073741824 | bytes 2097152 | tf_op jit(solution)/shard_map/spread_weights/pallas_call | solution.py:95
  24.8 3.9 %spread_weights.2.spread_ref = bf16[16,512,128]{2,1,0:T(8,128)(2,1)} custom-call(s32[64,512]{1,0:T(8,128)S(1)} %fusion.5.codes_ref, bf16[8,512]{1,0:T(8,128)(2,1)S(1)} %copy-done.5), custom_call_target="tpu_custom_call" | custom-call | flops 1073741824 | bytes 2097152 | tf_op jit(solution)/shard_map/spread_weights/pallas_call | solution.py:95
  28.7 2.9 %all-to-all-done.rows_ref = bf16[16,2,128,128]{3,2,1,0:T(8,128)(2,1)S(1)} async-done(((bf16[16,2,128,128]{3,2,1,0:T(8,128)(2,1)}), bf16[16,2,128,128]{3,2,1,0:T(8,128)(2,1)S(1)}, u32[]{:S(2)}, u32[]{:S(2)}) %all-to-all-start) | async-done | bytes 1048608 | tf_op jit(solution)/shard_map/all_to_all | solution.py:674
  31.6 2.7 %compress.3 = bf16[64,1024]{1,0:T(8,128)(2,1)S(1)} custom-call(bf16[16,512,128]{2,1,0:T(8,128)(2,1)} %spread_weights.2.spread_ref, bf16[16,2,128,128]{3,2,1,0:T(8,128)(2,1)S(1)} %all-to-all-done.rows_ref), custom_call_target="tpu_custom_call" | custom-call | tf_op jit(solution)/shard_map/compress/pallas_call | solution.py:139
  34.2 2.0 %collective-permute-start.1 = (bf16[64,1024]{1,0:T(8,128)(2,1)S(1)}, bf16[64,1024]{1,0:T(8,128)(2,1)S(1)}, u32[]{:S(2)}, u32[]{:S(2)}) collective-permute-start(bf16[64,1024]{1,0:T(8,128)(2,1)S(1)} %compress.3), channel_id=1, source_target_pairs={{0,4},{1,5},{2,6},{3,7},{4,0},{5,1},{6,2},{7,3},{8,12},{9,13},{10,... | collective-permute-start | bytes 393224 | tf_op jit(solution)/shard_map/ppermute | solution.py:664
  36.3 2.7 %compress.2 = f32[64,1024]{1,0:T(8,128)S(1)} custom-call(bf16[16,512,128]{2,1,0:T(8,128)(2,1)} %spread_weights.3.spread_ref, bf16[16,2,128,128]{3,2,1,0:T(8,128)(2,1)S(1)} %all-to-all-done.rows_ref), custom_call_target="tpu_custom_call" | custom-call | tf_op jit(solution)/shard_map/compress/pallas_call | solution.py:139
  39.0 4.2 %collective-permute-done.1 = bf16[64,1024]{1,0:T(8,128)(2,1)S(1)} collective-permute-done((bf16[64,1024]{1,0:T(8,128)(2,1)S(1)}, bf16[64,1024]{1,0:T(8,128)(2,1)S(1)}, u32[]{:S(2)}, u32[]{:S(2)}) %collective-permute-start.1) | collective-permute-done | bytes 131104 | tf_op jit(solution)/shard_map/ppermute | solution.py:664
  43.2 1.3 collective-permute-start.2
  44.5 5.5 %collective-permute-done.2.refs_1_ = bf16[64,1024]{1,0:T(8,128)(2,1)S(1)} collective-permute-done((bf16[64,1024]{1,0:T(8,128)(2,1)S(1)}, bf16[64,1024]{1,0:T(8,128)(2,1)S(1)}, u32[]{:S(2)}, u32[]{:S(2)}) %collective-permute-start.2) | collective-permute-done | bytes 131104 | tf_op jit(solution)/shard_map/ppermute | solution.py:659
  50.1 12.2 %forward_stage.1 = (bf16[128,1024]{1,0:T(8,128)(2,1)S(1)}, bf16[2,128,4096]{2,1,0:T(8,128)(2,1)S(1)}, f32[2,128,1024]{2,1,0:T(8,128)S(1)}, f32[2,128,128]{2,1,0:...) custom-call(s32[3]{0:T(128)S(1)} %pad_add_fusion.2.place_ref, ...), custom_call_target="tpu_custom_call" | custom-call | flops 4294967296 | bytes 1048576 | tf_op jit(solution)/shard_map/forward_stage/pallas_call | solution.py:538
  62.2 1.3 collective-permute-start.6
  63.6 4.0 %collective-permute-done.6.acts_ref = bf16[128,1024]{1,0:T(8,128)(2,1)S(1)} collective-permute-done((bf16[128,1024]{1,0:T(8,128)(2,1)S(1)}, bf16[128,1024]{1,0:T(8,128)(2,1)S(1)}, u32[]{:S(2)}, u32[]{:S(2)}) %collective-permute-start.6) | collective-permute-done | bytes 262176 | tf_op jit(solution)/shard_map/ppermute | solution.py:659
  67.6 0.9 turn_stage.1
  68.5 1.3 collective-permute-start.7
  69.8 27.0 %collective-permute-done.7.grad_ref = bf16[128,1024]{1,0:T(8,128)(2,1)S(1)} collective-permute-done((bf16[128,1024]{1,0:T(8,128)(2,1)S(1)}, bf16[128,1024]{1,0:T(8,128)(2,1)S(1)}, u32[]{:S(2)}, u32[]{:S(2)}) %collective-permute-start.7) | collective-permute-done | bytes 262176 | tf_op jit(solution)/shard_map/ppermute | solution.py:659
  96.8 17.0 %backward_stage.1 = bf16[128,1024]{1,0:T(8,128)(2,1)S(1)} custom-call(s32[3]{0:T(128)S(1)} %pad_add_fusion.2.place_ref, bf16[128,1024]{1,0:T(8,128)(2,1)S(1)} %collective-permute-done.7.grad_ref, bf16[2,128,4096]{2,1,0:T(8,128)(2,1)S(1)} %get-tuple-element.19.hid, f32[2,128,1024]{2,1,0:T(8,128)S(1)} %get-tuple-element.20.inter, ...), custom_call_target="tpu_custom_call" | custom-call | flops 4294967296 | bytes 1048576 | tf_op jit(solution)/shard_map/backward_stage/pallas_call | solution.py:636
  113.8 1.3 collective-permute-start.8
  115.1 2.5 %collective-permute-done.8 = bf16[64,1024]{1,0:T(8,128)(2,1)S(1)} collective-permute-done((bf16[64,1024]{1,0:T(8,128)(2,1)S(1)}, bf16[64,1024]{1,0:T(8,128)(2,1)S(1)}, u32[]{:S(2)}, u32[]{:S(2)}) %collective-permute-start.8) | collective-permute-done | bytes 131104 | tf_op jit(solution)/shard_map/ppermute | solution.py:659
  117.8 0.9 expand.2.refs_0_
  118.7 4.9 %collective-permute-done.9.grad_ref = bf16[64,1024]{1,0:T(8,128)(2,1)S(1)} collective-permute-done((bf16[64,1024]{1,0:T(8,128)(2,1)S(1)}, bf16[64,1024]{1,0:T(8,128)(2,1)S(1)}, u32[]{:S(2)}, u32[]{:S(2)}) %collective-permute-start.9) | collective-permute-done | bytes 131104 | tf_op jit(solution)/shard_map/ppermute | solution.py:664
  123.6 1.9 %expand.3 = bf16[16,2,128,128]{3,2,1,0:T(8,128)(2,1)} custom-call(bf16[16,512,128]{2,1,0:T(8,128)(2,1)S(1)} %copy-done.1, bf16[64,1024]{1,0:T(8,128)(2,1)S(1)} %collective-permute-done.9.grad_ref, bf16[16,128,128]{2,1,0:T(8,128)(2,1)S(1)} %expand.2.refs_0_), custom_call_target="tpu_custom_call" | custom-call | tf_op jit(solution)/shard_map/expand/pallas_call | solution.py:184
  125.5 7.4 %all-to-all-start.1 = ((bf16[16,2,128,128]{3,2,1,0:T(8,128)(2,1)}), bf16[16,2,128,128]{3,2,1,0:T(8,128)(2,1)S(1)}, u32[]{:S(2)}, u32[]{:S(2)}) async-start(bf16[16,2,128,128]{3,2,1,0:T(8,128)(2,1)} %expand.3), calls=%async_computation.1 | async-start | bytes 2097152 | tf_op jit(solution)/shard_map/all_to_all | solution.py:674
  134.5 13.1 %all-to-all-done.1 = bf16[16,2,128,128]{3,2,1,0:T(8,128)(2,1)S(1)} async-done(((bf16[16,2,128,128]{3,2,1,0:T(8,128)(2,1)}), bf16[16,2,128,128]{3,2,1,0:T(8,128)(2,1)S(1)}, u32[]{:S(2)}, u32[]{:S(2)}) %all-to-all-start.1) | async-done | bytes 1048608 | tf_op jit(solution)/shard_map/all_to_all | solution.py:674
  147.7 10.2 %add_rows.1 = f32[4096,128]{1,0:T(8,128)} custom-call(s32[4096]{0:T(1024)S(1)} %bitcast.31, bf16[4096,128]{1,0:T(8,128)(2,1)S(1)} %bitcast.28, bf16[4096,128]{1,0:T(8,128)(2,1)} %pick_rows.1.sent_ref), custom_call_target="tpu_custom_call" | custom-call | tf_op jit(solution)/shard_map/add_rows/pallas_call | solution.py:241
  (42 shorter events, 4.0 us)
Async XLA Ops:
  0.0 36.3 %copy-start = (bf16[1,4,64,1024]{3,2,1,0:T(8,128)(2,1)S(1)}, bf16[1,4,64,1024]{3,2,1,0:T(8,128)(2,1)}, u32[]{:S(2)}) copy-start(bf16[1,4,64,1024]{3,2,1,0:T(8,128)(2,1)} %param.16) | copy-start | bytes 1572868
  0.0 24.8 %copy-start.5 = (bf16[8,512]{1,0:T(8,128)(2,1)S(1)}, bf16[8,512]{1,0:T(8,128)(2,1)}, u32[]{:S(2)}) copy-start(bf16[8,512]{1,0:T(8,128)(2,1)} %lcb_ref.3) | copy-start | bytes 24580
  0.0 50.0 %collective-permute-start.4 = (bf16[1024,4096]{1,0:T(8,128)(2,1)}, bf16[1024,4096]{1,0:T(8,128)(2,1)}, u32[]{:S(2)}, u32[]{:S(2)}) collective-permute-start(bf16[1024,4096]{1,0:T(8,128)(2,1)} %bitcast.33), channel_id=1, source_target_pairs={{0,8},{8,0},{16,24},{24,16},{1,9},{9,1},{17,25},{25,17},{2,10},{10... | collective-permute-start | bytes 25165832 | tf_op jit(solution)/shard_map/ppermute | solution.py:654
  0.5 49.6 %collective-permute-start.5 = (bf16[4096,1024]{1,0:T(8,128)(2,1)}, bf16[4096,1024]{1,0:T(8,128)(2,1)}, u32[]{:S(2)}, u32[]{:S(2)}) collective-permute-start(bf16[4096,1024]{1,0:T(8,128)(2,1)} %bitcast.37), channel_id=1, source_target_pairs={{0,8},{8,0},{16,24},{24,16},{1,9},{9,1},{17,25},{25,17},{2,10},{10... | collective-permute-start | bytes 25165832 | tf_op jit(solution)/shard_map/ppermute | solution.py:654
  0.5 11.4 %collective-permute-start = (s32[64,512]{1,0:T(8,128)}, s32[64,512]{1,0:T(8,128)S(1)}, u32[]{:S(2)}, u32[]{:S(2)}) collective-permute-start(s32[64,512]{1,0:T(8,128)} %bitcast.41), channel_id=1, source_target_pairs={{0,4},{1,5},{2,6},{3,7},{4,0},{5,1},{6,2},{7,3},{8,12},{9,13},{10,... | collective-permute-start | bytes 393224 | tf_op jit(solution)/shard_map/ppermute | solution.py:664
  5.3 1.2 copy-start.3
  11.9 19.7 %all-to-all-start = ((bf16[16,2,128,128]{3,2,1,0:T(8,128)(2,1)}), bf16[16,2,128,128]{3,2,1,0:T(8,128)(2,1)S(1)}, u32[]{:S(2)}, u32[]{:S(2)}) async-start(bf16[16,2,128,128]{3,2,1,0:T(8,128)(2,1)} %bitcast.12), calls=%async_computation | async-start | bytes 2097152 | tf_op jit(solution)/shard_map/all_to_all | solution.py:674
  16.8 27.7 %copy-start.6 = (bf16[1,8,128]{2,1,0:T(8,128)(2,1)S(1)}, bf16[1,8,128]{2,1,0:T(8,128)(2,1)}, u32[]{:S(2)}) copy-start(bf16[1,8,128]{2,1,0:T(8,128)(2,1)} %param.12) | copy-start | bytes 6148
  18.2 26.3 %collective-permute-start.3 = (bf16[16,128]{1,0:T(8,128)(2,1)S(1)}, bf16[16,128]{1,0:T(8,128)(2,1)S(1)}, u32[]{:S(2)}, u32[]{:S(2)}) collective-permute-start(bf16[16,128]{1,0:T(8,128)(2,1)S(1)} %pad_maximum_fusion.1), channel_id=1, source_target_pairs={{0,8},{8,0},{16,24},{24,16},{1,9},{9,1},{17,25},{25,17},{2,10},{10... | collective-permute-start | bytes 12296 | tf_op jit(solution)/shard_map/ppermute | solution.py:654
  19.9 0.7 copy-start.4
  34.2 8.9 %collective-permute-start.1 = (bf16[64,1024]{1,0:T(8,128)(2,1)S(1)}, bf16[64,1024]{1,0:T(8,128)(2,1)S(1)}, u32[]{:S(2)}, u32[]{:S(2)}) collective-permute-start(bf16[64,1024]{1,0:T(8,128)(2,1)S(1)} %compress.3), channel_id=1, source_target_pairs={{0,4},{1,5},{2,6},{3,7},{4,0},{5,1},{6,2},{7,3},{8,12},{9,13},{10,... | collective-permute-start | bytes 393224 | tf_op jit(solution)/shard_map/ppermute | solution.py:664
  43.2 6.9 %collective-permute-start.2 = (bf16[64,1024]{1,0:T(8,128)(2,1)S(1)}, bf16[64,1024]{1,0:T(8,128)(2,1)S(1)}, u32[]{:S(2)}, u32[]{:S(2)}) collective-permute-start(bf16[64,1024]{1,0:T(8,128)(2,1)S(1)} %add_convert_fusion.refs_0_), channel_id=1, source_target_pairs={{16,0},{24,8},{17,1},{25,9},{18,2},{26,10},{19,3},{27,11},{20,4},{... | collective-permute-start | bytes 393224 | tf_op jit(solution)/shard_map/ppermute | solution.py:659
  62.2 5.4 %collective-permute-start.6 = (bf16[128,1024]{1,0:T(8,128)(2,1)S(1)}, bf16[128,1024]{1,0:T(8,128)(2,1)S(1)}, u32[]{:S(2)}, u32[]{:S(2)}) collective-permute-start(bf16[128,1024]{1,0:T(8,128)(2,1)S(1)} %get-tuple-element.17), channel_id=1, source_target_pairs={{0,16},{8,24},{1,17},{9,25},{2,18},{10,26},{3,19},{11,27},{4,20},{... | collective-permute-start | bytes 786440 | tf_op jit(solution)/shard_map/ppermute | solution.py:659
  68.5 28.3 %collective-permute-start.7 = (bf16[128,1024]{1,0:T(8,128)(2,1)S(1)}, bf16[128,1024]{1,0:T(8,128)(2,1)S(1)}, u32[]{:S(2)}, u32[]{:S(2)}) collective-permute-start(bf16[128,1024]{1,0:T(8,128)(2,1)S(1)} %turn_stage.1), channel_id=1, source_target_pairs={{16,0},{24,8},{17,1},{25,9},{18,2},{26,10},{19,3},{27,11},{20,4},{... | collective-permute-start | bytes 786440 | tf_op jit(solution)/shard_map/ppermute | solution.py:659
  96.8 21.0 %copy-start.2 = (bf16[16,512,128]{2,1,0:T(8,128)(2,1)S(1)}, bf16[16,512,128]{2,1,0:T(8,128)(2,1)}, u32[]{:S(2)}) copy-start(bf16[16,512,128]{2,1,0:T(8,128)(2,1)} %spread_weights.3.spread_ref) | copy-start | bytes 6291460
  96.8 26.8 %copy-start.1 = (bf16[16,512,128]{2,1,0:T(8,128)(2,1)S(1)}, bf16[16,512,128]{2,1,0:T(8,128)(2,1)}, u32[]{:S(2)}) copy-start(bf16[16,512,128]{2,1,0:T(8,128)(2,1)} %spread_weights.2.spread_ref) | copy-start | bytes 6291460
  113.8 19.6 %copy-start.7 = (s32[1,32]{1,0:T(1,128)S(1)}, s32[1,32]{1,0:T(1,128)}, u32[]{:S(2)}) copy-start(s32[1,32]{1,0:T(1,128)} %param.19) | copy-start | bytes 388
  113.8 3.8 %collective-permute-start.8 = (bf16[64,1024]{1,0:T(8,128)(2,1)S(1)}, bf16[64,1024]{1,0:T(8,128)(2,1)S(1)}, u32[]{:S(2)}, u32[]{:S(2)}) collective-permute-start(bf16[64,1024]{1,0:T(8,128)(2,1)S(1)} %slice.8), channel_id=1, source_target_pairs={{0,16},{8,24},{1,17},{9,25},{2,18},{10,26},{3,19},{11,27},{4,20},{... | collective-permute-start | bytes 393224 | tf_op jit(solution)/shard_map/ppermute | solution.py:659
  117.7 5.9 %collective-permute-start.9 = (bf16[64,1024]{1,0:T(8,128)(2,1)S(1)}, bf16[64,1024]{1,0:T(8,128)(2,1)S(1)}, u32[]{:S(2)}, u32[]{:S(2)}) collective-permute-start(bf16[64,1024]{1,0:T(8,128)(2,1)S(1)} %slice_select_fusion.grad_ref), channel_id=1, source_target_pairs={{0,4},{1,5},{2,6},{3,7},{4,0},{5,1},{6,2},{7,3},{8,12},{9,13},{10,... | collective-permute-start | bytes 393224 | tf_op jit(solution)/shard_map/ppermute | solution.py:664
  125.5 22.2 %all-to-all-start.1 = ((bf16[16,2,128,128]{3,2,1,0:T(8,128)(2,1)}), bf16[16,2,128,128]{3,2,1,0:T(8,128)(2,1)S(1)}, u32[]{:S(2)}, u32[]{:S(2)}) async-start(bf16[16,2,128,128]{3,2,1,0:T(8,128)(2,1)} %expand.3), calls=%async_computation.1 | async-start | bytes 2097152 | tf_op jit(solution)/shard_map/all_to_all | solution.py:674

commit v11 on v9

--- a/solution.py
+++ b/solution.py
@@ -9,7 +9,6 @@
 DECAY_WEIGHT = 0.5
 VMEM_LIMIT = 28 * 1024 * 1024
 UNROLL = 32
-PICK_UNROLL = 128
 
 
 def whole(memory_space=pltpu.VMEM):
@@ -28,42 +27,57 @@
     return max(step for step in range(1, most + 1) if count % step == 0)
 
 
-def pick_rows(emb_table, picked):
+def pick_rows(emb_table, wanted, my_half):
     rows, width = emb_table.shape
-    count = picked.shape[0]
-    chunk = min(count, 1024)
-
-    def kernel(picked_ref, table_ref, out_ref, wide, lines):
-        wide[...] = table_ref[...].astype(jnp.float32)
+    askers, cap = wanted.shape
+    half = lax.axis_size("table") // 2
+    together = tiles_of(askers, 8)
+    pieces = 4
+
+    def kernel(half_ref, wanted_ref, table_ref, out_ref, narrow, wide, lines, sems):
+        copies = []
+        for piece in range(pieces):
+            cut = pl.ds(piece * (rows // pieces), rows // pieces)
+            copies.append(pltpu.make_async_copy(table_ref.at[cut], narrow.at[cut], sems.at[piece]))
+            copies[-1].start()
+        for piece in range(pieces):
+            cut = pl.ds(piece * (rows // pieces), rows // pieces)
+            copies[piece].wait()
+            wide[cut, :] = narrow[cut, :].astype(jnp.float32)
 
         def fill(part, carry):
-            base = pl.multiple_of(part * chunk, chunk)
-
-            def body(group, inner):
-                first = pl.multiple_of(group * PICK_UNROLL, PICK_UNROLL)
-                for lane in range(PICK_UNROLL):
-                    row = picked_ref[base + first + lane]
+            def one(line, inner):
+                at = part * together + line
+                device, is_mirror = at // 2, at % 2
+                side = jnp.where(is_mirror == 0, half_ref[0], 1 - half_ref[0])
+                asker = (device // half * 2 + side) * half + device % half
+                first = pl.multiple_of(line * cap, cap)
+                for lane in range(cap):
+                    row = wanted_ref[asker * cap + lane]
                     lines[pl.ds(first + lane, 1), :] = wide[pl.ds(row, 1), :]
                 return inner
 
-            lax.fori_loop(0, chunk // PICK_UNROLL, body, 0)
-            out_ref[pl.ds(base, chunk), :] = lines[...].astype(out_ref.dtype)
+            lax.fori_loop(0, together, one, 0)
+            base = pl.multiple_of(part * (together * cap), together * cap)
+            out_ref[pl.ds(base, together * cap), :] = lines[...].astype(out_ref.dtype)
             return carry
 
-        lax.fori_loop(0, count // chunk, fill, 0)
+        lax.fori_loop(0, askers // together, fill, 0)
 
     return pl.pallas_call(
         kernel,
-        out_shape=jax.ShapeDtypeStruct((count, width), emb_table.dtype),
-        in_specs=[whole(pltpu.SMEM), whole()],
+        out_shape=jax.ShapeDtypeStruct((askers * cap, width), emb_table.dtype),
+        in_specs=[whole(pltpu.SMEM), whole(pltpu.SMEM), whole(pltpu.HBM)],
         out_specs=whole(),
         scratch_shapes=[
+            pltpu.VMEM((rows, width), emb_table.dtype),
             pltpu.VMEM((rows, width), jnp.float32),
-            pltpu.VMEM((chunk, width), jnp.float32),
+            pltpu.VMEM((together * cap, width), jnp.float32),
+            pltpu.SemaphoreType.DMA((pieces,)),
         ],
         compiler_params=params(),
         name="pick_rows",
-    )(picked, emb_table)
+    )(my_half.astype(jnp.int32).reshape(1), wanted.reshape(-1), in_hbm(emb_table))
 
 
 def spread_weights(codes, lcb_weight, owners, cap):
@@ -153,7 +167,7 @@
     owners, lines, cap = spread.shape
     samples = lines // embed_count
     width = lead_grad.shape[1] // embed_count
-    part = tiles_of(owners, 4)
+    part = tiles_of(owners, 8)
     extra = [] if near is None else [near]
 
     def kernel(spread_ref, grad_ref, *refs):
@@ -735,7 +749,7 @@
     other_small = swapped(small, section_count)
 
     picked = near_first(wanted_rows[0], my_half)
-    outgoing = pick_rows(emb_table, picked.reshape(-1))
+    outgoing = pick_rows(emb_table, wanted_rows[0], my_half)
     sent = after(outgoing, mirror_slots).reshape(near_owners, 2, cap, embed_width)
     fetched = swap_in_half(sent)
 

time: 157 us -> 156 us (level)
    pallas_call x1, Pallas kernels: 5.4 us -> 7 us  [pick_rows(): pl.pallas_call(kernel, out_shape=jax.ShapeDtypeStruct((askers * cap, widt...]
    unnamed x27 -> x29, local copies, waits for them, and re-layouts: 7.61 us -> 7.12 us
where the time goes in v11:
time: 156 us
  waiting for transfers between devices  64 us (41%)
  Pallas kernels  58.2 us (37%)
  starting transfers between devices  23.7 us (15%)
  local copies, waits for them, and re-layouts  7.52 us (5%)
  other arithmetic  1.71 us (1%)
    ppermute x4, waiting for transfers between devices, moved(): return lax.ppermute(value, 'section', pairs)  38.2 us
    all_to_all x2, waiting for transfers between devices, swap_in_half(): lax.all_to_all(value, TABLE_AXES, split_axis=0, concat_axis=0, axis_index...  16.1 us
    pallas_call x1, Pallas kernels, backward_stage(): pl.pallas_call(kernel, out_shape=jax.ShapeDtypeStruct(grad.shape, jnp.bfl...  15.4 us
    pallas_call x1, Pallas kernels, forward_stage(): pl.pallas_call(kernel, out_shape=[jax.ShapeDtypeStruct(top.shape, jnp.bfl...  12.2 us
    all_to_all x2, starting transfers between devices, swap_in_half(): lax.all_to_all(value, TABLE_AXES, split_axis=0, concat_axis=0, axis_index...  11.8 us
    pallas_call x1, Pallas kernels, add_rows(): pl.pallas_call(kernel, out_shape=jax.ShapeDtypeStruct((rows, width), jnp....  10.2 us
    ppermute x3, waiting for transfers between devices, mirror(): lax.ppermute(value, 'table', [(t, (t + along // 2) % along) for t in rang...  9.63 us
    pallas_call x2, Pallas kernels, spread_weights(): pl.pallas_call(kernel, out_shape=[pltpu.VMEM((owners, samples * embed_cou...  7.9 us
  transfers between devices with their start and end apart: 12, of which 8 were waited for; matrix products, arithmetic and copies ran while one was open for 2% of the time, Pallas kernels for 11%

profile of v11, /device:TPU:0, one launch (start us, length us, event | category | flops | bytes accessed | tf_op | source)
XLA Modules:
  0.0 155.6 jit_solution(109724752874758874)
XLA Ops:
  0.5 4.0 %collective-permute-start = (s32[64,512]{1,0:T(8,128)}, s32[64,512]{1,0:T(8,128)S(1)}, u32[]{:S(2)}, u32[]{:S(2)}) collective-permute-start(s32[64,512]{1,0:T(8,128)} %bitcast.41), channel_id=1, source_target_pairs={{0,4},{1,5},{2,6},{3,7},{4,0},{5,1},{6,2},{7,3},{8,12},{9,13},{10,... | collective-permute-start | bytes 393224 | tf_op jit(solution)/shard_map/ppermute | solution.py:690
  4.6 0.7 copy-done.7
  5.3 7.0 %pick_rows.1.sent_ref = bf16[4096,128]{1,0:T(8,128)(2,1)} custom-call(s32[1]{0:T(128)} %bitcast.9.half_ref, s32[4096]{0:T(1024)S(1)} %bitcast.30, bf16[4096,128]{1,0:T(8,128)(2,1)} %table_ref.1), custom_call_target="tpu_custom_call" | custom-call | tf_op jit(solution)/shard_map/pick_rows/pallas_call | solution.py:67
  12.3 4.9 %all-to-all-start = ((bf16[16,2,128,128]{3,2,1,0:T(8,128)(2,1)}), bf16[16,2,128,128]{3,2,1,0:T(8,128)(2,1)S(1)}, u32[]{:S(2)}, u32[]{:S(2)}) async-start(bf16[16,2,128,128]{3,2,1,0:T(8,128)(2,1)} %bitcast.11), calls=%async_computation | async-start | bytes 2097152 | tf_op jit(solution)/shard_map/all_to_all | solution.py:700
  18.1 4.0 %spread_weights.3 = (bf16[16,512,128]{2,1,0:T(8,128)(2,1)S(1)}, bf16[16,512,128]{2,1,0:T(8,128)(2,1)}) custom-call(s32[64,512]{1,0:T(8,128)S(1)} %fusion.11.codes_ref, bf16[8,512]{1,0:T(8,128)(2,1)S(1)} %copy-done.9), custom_call_target="tpu_custom_call" | custom-call | flops 1073741824 | bytes 2097152 | tf_op jit(solution)/shard_map/spread_weights/pallas_call | solution.py:110
  22.1 1.3 copy-done.5
  23.7 3.9 %spread_weights.2 = (bf16[16,512,128]{2,1,0:T(8,128)(2,1)S(1)}, bf16[16,512,128]{2,1,0:T(8,128)(2,1)}) custom-call(s32[64,512]{1,0:T(8,128)S(1)} %fusion.5.codes_ref, bf16[8,512]{1,0:T(8,128)(2,1)S(1)} %copy-done.9), custom_call_target="tpu_custom_call" | custom-call | flops 1073741824 | bytes 2097152 | tf_op jit(solution)/shard_map/spread_weights/pallas_call | solution.py:110
  27.6 1.3 copy-done.3
  29.0 3.0 %all-to-all-done.rows_ref = bf16[16,2,128,128]{3,2,1,0:T(8,128)(2,1)S(1)} async-done(((bf16[16,2,128,128]{3,2,1,0:T(8,128)(2,1)}), bf16[16,2,128,128]{3,2,1,0:T(8,128)(2,1)S(1)}, u32[]{:S(2)}, u32[]{:S(2)}) %all-to-all-start) | async-done | bytes 1048608 | tf_op jit(solution)/shard_map/all_to_all | solution.py:700
  32.0 1.6 %copy-done.4 = bf16[16,512,128]{2,1,0:T(8,128)(2,1)S(1)} copy-done((bf16[16,512,128]{2,1,0:T(8,128)(2,1)S(1)}, bf16[16,512,128]{2,1,0:T(8,128)(2,1)}, u32[]{:S(2)}) %copy-start.4) | copy-done | bytes 2097176
  33.6 0.9 compress.3
  34.5 1.6 %collective-permute-start.1 = (bf16[64,1024]{1,0:T(8,128)(2,1)S(1)}, bf16[64,1024]{1,0:T(8,128)(2,1)S(1)}, u32[]{:S(2)}, u32[]{:S(2)}) collective-permute-start(bf16[64,1024]{1,0:T(8,128)(2,1)S(1)} %compress.3), channel_id=1, source_target_pairs={{0,4},{1,5},{2,6},{3,7},{4,0},{5,1},{6,2},{7,3},{8,12},{9,13},{10,... | collective-permute-start | bytes 393224 | tf_op jit(solution)/shard_map/ppermute | solution.py:690
  36.2 1.6 %copy-done.6 = bf16[16,512,128]{2,1,0:T(8,128)(2,1)S(1)} copy-done((bf16[16,512,128]{2,1,0:T(8,128)(2,1)S(1)}, bf16[16,512,128]{2,1,0:T(8,128)(2,1)}, u32[]{:S(2)}) %copy-start.6) | copy-done | bytes 2097176
  37.8 0.9 compress.2
  38.7 4.7 %collective-permute-done.1 = bf16[64,1024]{1,0:T(8,128)(2,1)S(1)} collective-permute-done((bf16[64,1024]{1,0:T(8,128)(2,1)S(1)}, bf16[64,1024]{1,0:T(8,128)(2,1)S(1)}, u32[]{:S(2)}, u32[]{:S(2)}) %collective-permute-start.1) | collective-permute-done | bytes 131104 | tf_op jit(solution)/shard_map/ppermute | solution.py:690
  43.5 1.3 collective-permute-start.2
  44.8 5.5 %collective-permute-done.2.refs_1_ = bf16[64,1024]{1,0:T(8,128)(2,1)S(1)} collective-permute-done((bf16[64,1024]{1,0:T(8,128)(2,1)S(1)}, bf16[64,1024]{1,0:T(8,128)(2,1)S(1)}, u32[]{:S(2)}, u32[]{:S(2)}) %collective-permute-start.2) | collective-permute-done | bytes 131104 | tf_op jit(solution)/shard_map/ppermute | solution.py:685
  50.3 12.2 %forward_stage.1 = (bf16[128,1024]{1,0:T(8,128)(2,1)S(1)}, bf16[2,4096,128]{2,1,0:T(8,128)(2,1)S(1)}, f32[2,128,1024]{2,1,0:T(8,128)S(1)}, f32[2,128,128]{2,1,0:...) custom-call(s32[3]{0:T(128)S(1)} %pad_add_fusion.1.place_ref, ...), custom_call_target="tpu_custom_call" | custom-call | flops 4294967296 | bytes 1048576 | tf_op jit(solution)/shard_map/forward_stage/pallas_call | solution.py:556
  62.5 1.3 collective-permute-start.6
  63.9 4.0 %collective-permute-done.6.acts_ref = bf16[128,1024]{1,0:T(8,128)(2,1)S(1)} collective-permute-done((bf16[128,1024]{1,0:T(8,128)(2,1)S(1)}, bf16[128,1024]{1,0:T(8,128)(2,1)S(1)}, u32[]{:S(2)}, u32[]{:S(2)}) %collective-permute-start.6) | collective-permute-done | bytes 262176 | tf_op jit(solution)/shard_map/ppermute | solution.py:685
  67.9 0.9 turn_stage.1
  68.8 1.3 collective-permute-start.7
  70.1 26.2 %collective-permute-done.7.grad_ref = bf16[128,1024]{1,0:T(8,128)(2,1)S(1)} collective-permute-done((bf16[128,1024]{1,0:T(8,128)(2,1)S(1)}, bf16[128,1024]{1,0:T(8,128)(2,1)S(1)}, u32[]{:S(2)}, u32[]{:S(2)}) %collective-permute-start.7) | collective-permute-done | bytes 262176 | tf_op jit(solution)/shard_map/ppermute | solution.py:685
  96.3 15.4 %backward_stage.1 = bf16[128,1024]{1,0:T(8,128)(2,1)S(1)} custom-call(s32[3]{0:T(128)S(1)} %pad_add_fusion.1.place_ref, bf16[128,1024]{1,0:T(8,128)(2,1)S(1)} %collective-permute-done.7.grad_ref, bf16[2,4096,128]{2,1,0:T(8,128)(2,1)S(1)} %get-tuple-element.26.hid, f32[2,128,1024]{2,1,0:T(8,128)S(1)} %get-tuple-element.27.inter, ...), custom_call_target="tpu_custom_call" | custom-call | flops 4294967296 | bytes 1048576 | tf_op jit(solution)/shard_map/backward_stage/pallas_call | solution.py:661
  111.7 1.4 collective-permute-start.8
  113.2 2.5 %collective-permute-done.8 = bf16[64,1024]{1,0:T(8,128)(2,1)S(1)} collective-permute-done((bf16[64,1024]{1,0:T(8,128)(2,1)S(1)}, bf16[64,1024]{1,0:T(8,128)(2,1)S(1)}, u32[]{:S(2)}, u32[]{:S(2)}) %collective-permute-start.8) | collective-permute-done | bytes 131104 | tf_op jit(solution)/shard_map/ppermute | solution.py:685
  115.8 0.9 expand.2.refs_0_
  116.7 4.9 %collective-permute-done.9.grad_ref = bf16[64,1024]{1,0:T(8,128)(2,1)S(1)} collective-permute-done((bf16[64,1024]{1,0:T(8,128)(2,1)S(1)}, bf16[64,1024]{1,0:T(8,128)(2,1)S(1)}, u32[]{:S(2)}, u32[]{:S(2)}) %collective-permute-start.9) | collective-permute-done | bytes 131104 | tf_op jit(solution)/shard_map/ppermute | solution.py:690
  121.6 1.9 %expand.3 = bf16[16,2,128,128]{3,2,1,0:T(8,128)(2,1)} custom-call(bf16[16,512,128]{2,1,0:T(8,128)(2,1)S(1)} %copy-done.1, bf16[64,1024]{1,0:T(8,128)(2,1)S(1)} %collective-permute-done.9.grad_ref, bf16[16,128,128]{2,1,0:T(8,128)(2,1)S(1)} %expand.2.refs_0_), custom_call_target="tpu_custom_call" | custom-call | tf_op jit(solution)/shard_map/expand/pallas_call | solution.py:196
  123.5 6.9 %all-to-all-start.1 = ((bf16[16,2,128,128]{3,2,1,0:T(8,128)(2,1)}), bf16[16,2,128,128]{3,2,1,0:T(8,128)(2,1)S(1)}, u32[]{:S(2)}, u32[]{:S(2)}) async-start(bf16[16,2,128,128]{3,2,1,0:T(8,128)(2,1)} %expand.3), calls=%async_computation.1 | async-start | bytes 2097152 | tf_op jit(solution)/shard_map/all_to_all | solution.py:700
  132.1 13.1 %all-to-all-done.1 = bf16[16,2,128,128]{3,2,1,0:T(8,128)(2,1)S(1)} async-done(((bf16[16,2,128,128]{3,2,1,0:T(8,128)(2,1)}), bf16[16,2,128,128]{3,2,1,0:T(8,128)(2,1)S(1)}, u32[]{:S(2)}, u32[]{:S(2)}) %all-to-all-start.1) | async-done | bytes 1048608 | tf_op jit(solution)/shard_map/all_to_all | solution.py:700
  145.3 10.2 %add_rows.1 = f32[4096,128]{1,0:T(8,128)} custom-call(s32[4096]{0:T(1024)S(1)} %bitcast.32, bf16[4096,128]{1,0:T(8,128)(2,1)S(1)} %bitcast.27, bf16[4096,128]{1,0:T(8,128)(2,1)} %pick_rows.1.sent_ref), custom_call_target="tpu_custom_call" | custom-call | tf_op jit(solution)/shard_map/add_rows/pallas_call | solution.py:253
  (53 shorter events, 3.8 us)
Async XLA Ops:
  0.0 36.2 %copy-start = (bf16[1,4,64,1024]{3,2,1,0:T(8,128)(2,1)S(1)}, bf16[1,4,64,1024]{3,2,1,0:T(8,128)(2,1)}, u32[]{:S(2)}) copy-start(bf16[1,4,64,1024]{3,2,1,0:T(8,128)(2,1)} %param.16) | copy-start | bytes 1572868
  0.0 50.3 %collective-permute-start.4 = (bf16[1024,4096]{1,0:T(8,128)(2,1)}, bf16[1024,4096]{1,0:T(8,128)(2,1)}, u32[]{:S(2)}, u32[]{:S(2)}) collective-permute-start(bf16[1024,4096]{1,0:T(8,128)(2,1)} %bitcast.33), channel_id=1, source_target_pairs={{0,8},{8,0},{16,24},{24,16},{1,9},{9,1},{17,25},{25,17},{2,10},{10... | collective-permute-start | bytes 25165832 | tf_op jit(solution)/shard_map/ppermute | solution.py:680
  0.5 49.9 %collective-permute-start.5 = (bf16[4096,1024]{1,0:T(8,128)(2,1)}, bf16[4096,1024]{1,0:T(8,128)(2,1)}, u32[]{:S(2)}, u32[]{:S(2)}) collective-permute-start(bf16[4096,1024]{1,0:T(8,128)(2,1)} %bitcast.37), channel_id=1, source_target_pairs={{0,8},{8,0},{16,24},{24,16},{1,9},{9,1},{17,25},{25,17},{2,10},{10... | collective-permute-start | bytes 25165832 | tf_op jit(solution)/shard_map/ppermute | solution.py:680
  0.5 11.8 %collective-permute-start = (s32[64,512]{1,0:T(8,128)}, s32[64,512]{1,0:T(8,128)S(1)}, u32[]{:S(2)}, u32[]{:S(2)}) collective-permute-start(s32[64,512]{1,0:T(8,128)} %bitcast.41), channel_id=1, source_target_pairs={{0,4},{1,5},{2,6},{3,7},{4,0},{5,1},{6,2},{7,3},{8,12},{9,13},{10,... | collective-permute-start | bytes 393224 | tf_op jit(solution)/shard_map/ppermute | solution.py:690
  4.6 0.7 copy-start.7
  5.3 11.9 %copy-start.12 = (bf16[1,1024]{1,0:T(2,128)(2,1)S(1)}, bf16[1,1024]{1,0:T(2,128)(2,1)}, u32[]{:S(2)}) copy-start(bf16[1,1024]{1,0:T(2,128)(2,1)} %param.13) | copy-start | bytes 6148
  5.3 11.9 %copy-start.11 = (bf16[1,8,128]{2,1,0:T(8,128)(2,1)S(1)}, bf16[1,8,128]{2,1,0:T(8,128)(2,1)}, u32[]{:S(2)}) copy-start(bf16[1,8,128]{2,1,0:T(8,128)(2,1)} %param.12) | copy-start | bytes 6148
  5.3 12.4 %copy-start.10 = (s32[1,64,512]{2,1,0:T(8,128)S(1)}, s32[1,64,512]{2,1,0:T(8,128)}, u32[]{:S(2)}) copy-start(s32[1,64,512]{2,1,0:T(8,128)} %param.17) | copy-start | bytes 393220
  5.3 12.8 %copy-start.9 = (bf16[8,512]{1,0:T(8,128)(2,1)S(1)}, bf16[8,512]{1,0:T(8,128)(2,1)}, u32[]{:S(2)}) copy-start(bf16[8,512]{1,0:T(8,128)(2,1)} %lcb_ref.3) | copy-start | bytes 24580
  12.3 19.7 %all-to-all-start = ((bf16[16,2,128,128]{3,2,1,0:T(8,128)(2,1)}), bf16[16,2,128,128]{3,2,1,0:T(8,128)(2,1)S(1)}, u32[]{:S(2)}, u32[]{:S(2)}) async-start(bf16[16,2,128,128]{3,2,1,0:T(8,128)(2,1)} %bitcast.11), calls=%async_computation | async-start | bytes 2097152 | tf_op jit(solution)/shard_map/all_to_all | solution.py:700
  17.2 27.5 %collective-permute-start.3 = (bf16[16,128]{1,0:T(8,128)(2,1)S(1)}, bf16[16,128]{1,0:T(8,128)(2,1)S(1)}, u32[]{:S(2)}, u32[]{:S(2)}) collective-permute-start(bf16[16,128]{1,0:T(8,128)(2,1)S(1)} %pad_maximum_fusion.1), channel_id=1, source_target_pairs={{0,8},{8,0},{16,24},{24,16},{1,9},{9,1},{17,25},{25,17},{2,10},{10... | collective-permute-start | bytes 12296 | tf_op jit(solution)/shard_map/ppermute | solution.py:680
  22.1 1.3 copy-start.5
  27.6 1.3 copy-start.3
  32.0 1.6 %copy-start.4 = (bf16[16,512,128]{2,1,0:T(8,128)(2,1)S(1)}, bf16[16,512,128]{2,1,0:T(8,128)(2,1)}, u32[]{:S(2)}) copy-start(bf16[16,512,128]{2,1,0:T(8,128)(2,1)} %copy-done.3) | copy-start | bytes 6291460
  34.5 8.9 %collective-permute-start.1 = (bf16[64,1024]{1,0:T(8,128)(2,1)S(1)}, bf16[64,1024]{1,0:T(8,128)(2,1)S(1)}, u32[]{:S(2)}, u32[]{:S(2)}) collective-permute-start(bf16[64,1024]{1,0:T(8,128)(2,1)S(1)} %compress.3), channel_id=1, source_target_pairs={{0,4},{1,5},{2,6},{3,7},{4,0},{5,1},{6,2},{7,3},{8,12},{9,13},{10,... | collective-permute-start | bytes 393224 | tf_op jit(solution)/shard_map/ppermute | solution.py:690
  36.2 1.6 %copy-start.6 = (bf16[16,512,128]{2,1,0:T(8,128)(2,1)S(1)}, bf16[16,512,128]{2,1,0:T(8,128)(2,1)}, u32[]{:S(2)}) copy-start(bf16[16,512,128]{2,1,0:T(8,128)(2,1)} %copy-done.5) | copy-start | bytes 6291460
  43.5 6.9 %collective-permute-start.2 = (bf16[64,1024]{1,0:T(8,128)(2,1)S(1)}, bf16[64,1024]{1,0:T(8,128)(2,1)S(1)}, u32[]{:S(2)}, u32[]{:S(2)}) collective-permute-start(bf16[64,1024]{1,0:T(8,128)(2,1)S(1)} %add_convert_fusion.refs_0_), channel_id=1, source_target_pairs={{16,0},{24,8},{17,1},{25,9},{18,2},{26,10},{19,3},{27,11},{20,4},{... | collective-permute-start | bytes 393224 | tf_op jit(solution)/shard_map/ppermute | solution.py:685
  62.5 5.4 %collective-permute-start.6 = (bf16[128,1024]{1,0:T(8,128)(2,1)S(1)}, bf16[128,1024]{1,0:T(8,128)(2,1)S(1)}, u32[]{:S(2)}, u32[]{:S(2)}) collective-permute-start(bf16[128,1024]{1,0:T(8,128)(2,1)S(1)} %get-tuple-element.24), channel_id=1, source_target_pairs={{0,16},{8,24},{1,17},{9,25},{2,18},{10,26},{3,19},{11,27},{4,20},{... | collective-permute-start | bytes 786440 | tf_op jit(solution)/shard_map/ppermute | solution.py:685
  68.8 27.5 %collective-permute-start.7 = (bf16[128,1024]{1,0:T(8,128)(2,1)S(1)}, bf16[128,1024]{1,0:T(8,128)(2,1)S(1)}, u32[]{:S(2)}, u32[]{:S(2)}) collective-permute-start(bf16[128,1024]{1,0:T(8,128)(2,1)S(1)} %turn_stage.1), channel_id=1, source_target_pairs={{16,0},{24,8},{17,1},{25,9},{18,2},{26,10},{19,3},{27,11},{20,4},{... | collective-permute-start | bytes 786440 | tf_op jit(solution)/shard_map/ppermute | solution.py:685
  96.3 19.5 %copy-start.2 = (bf16[16,512,128]{2,1,0:T(8,128)(2,1)S(1)}, bf16[16,512,128]{2,1,0:T(8,128)(2,1)}, u32[]{:S(2)}) copy-start(bf16[16,512,128]{2,1,0:T(8,128)(2,1)} %get-tuple-element.30.spread_ref) | copy-start | bytes 6291460
  111.7 9.9 %copy-start.1 = (bf16[16,512,128]{2,1,0:T(8,128)(2,1)S(1)}, bf16[16,512,128]{2,1,0:T(8,128)(2,1)}, u32[]{:S(2)}) copy-start(bf16[16,512,128]{2,1,0:T(8,128)(2,1)} %get-tuple-element.18.spread_ref) | copy-start | bytes 6291460
  111.7 3.9 %collective-permute-start.8 = (bf16[64,1024]{1,0:T(8,128)(2,1)S(1)}, bf16[64,1024]{1,0:T(8,128)(2,1)S(1)}, u32[]{:S(2)}, u32[]{:S(2)}) collective-permute-start(bf16[64,1024]{1,0:T(8,128)(2,1)S(1)} %slice.8), channel_id=1, source_target_pairs={{0,16},{8,24},{1,17},{9,25},{2,18},{10,26},{3,19},{11,27},{4,20},{... | collective-permute-start | bytes 393224 | tf_op jit(solution)/shard_map/ppermute | solution.py:685
  115.7 5.9 %collective-permute-start.9 = (bf16[64,1024]{1,0:T(8,128)(2,1)S(1)}, bf16[64,1024]{1,0:T(8,128)(2,1)S(1)}, u32[]{:S(2)}, u32[]{:S(2)}) collective-permute-start(bf16[64,1024]{1,0:T(8,128)(2,1)S(1)} %slice_select_fusion.grad_ref), channel_id=1, source_target_pairs={{0,4},{1,5},{2,6},{3,7},{4,0},{5,1},{6,2},{7,3},{8,12},{9,13},{10,... | collective-permute-start | bytes 393224 | tf_op jit(solution)/shard_map/ppermute | solution.py:690
  121.6 9.4 %copy-start.13 = (s32[1,32]{1,0:T(1,128)S(1)}, s32[1,32]{1,0:T(1,128)}, u32[]{:S(2)}) copy-start(s32[1,32]{1,0:T(1,128)} %param.19) | copy-start | bytes 388
  121.6 10.4 %copy-start.8 = (s32[1,32,128]{2,1,0:T(8,128)S(1)}, s32[1,32,128]{2,1,0:T(8,128)}, u32[]{:S(2)}) copy-start(s32[1,32,128]{2,1,0:T(8,128)} %param.18) | copy-start | bytes 49156
  123.5 21.7 %all-to-all-start.1 = ((bf16[16,2,128,128]{3,2,1,0:T(8,128)(2,1)}), bf16[16,2,128,128]{3,2,1,0:T(8,128)(2,1)S(1)}, u32[]{:S(2)}, u32[]{:S(2)}) async-start(bf16[16,2,128,128]{3,2,1,0:T(8,128)(2,1)} %expand.3), calls=%async_computation.1 | async-start | bytes 2097152 | tf_op jit(solution)/shard_map/all_to_all | solution.py:700

commit v12 on v11

--- a/solution.py
+++ b/solution.py
@@ -268,7 +268,7 @@
 
 GROUP = 16
 TABLE_AXES = ("section", "table")
-STAGE_LIMIT = 44 * 1024 * 1024
+STAGE_LIMIT = 28 * 1024 * 1024
 NT = (((1,), (1,)), ((), ()))
 
 
@@ -373,6 +373,15 @@
 
 def no_wait(step):
     return None
+
+
+class Held:
+    def __init__(self, held):
+        self.held = held
+        self.wait = no_wait
+
+    def start(self):
+        return None
 
 
 def over_tiles(total, tile, many, wait, work):
@@ -473,36 +482,70 @@
 
 
 def weight_specs():
-    return [whole()] + [whole(pltpu.HBM)] * 4
+    return [whole()] + [whole(pltpu.HBM)] * 4 + [whole()] * 2
 
 
 def weight_scratch(model_width, hidden_width):
     tiles = max(hidden_width // hidden_tile(hidden_width), model_width // model_tile(model_width))
     return [
-        pltpu.VMEM((2, model_width, hidden_width), jnp.bfloat16),
-        pltpu.VMEM((2, hidden_width, model_width), jnp.bfloat16),
-        pltpu.SemaphoreType.DMA((4, tiles)),
+        pltpu.VMEM((model_width, hidden_width), jnp.bfloat16),
+        pltpu.VMEM((hidden_width, model_width), jnp.bfloat16),
+        pltpu.SemaphoreType.DMA((2, tiles)),
     ]
 
 
-def streams_of(core, weights, held, forward):
-    own_up, other_up, own_down, other_down = weights
+def streams_of(core, weights, held, forward, ready):
+    own_up, other_up, own_down, other_down, ready_up, ready_down = weights
     held_up, held_down, sems = held
     model_width, hidden_width = own_up.shape
     wide, narrow = hidden_tile(hidden_width), model_tile(model_width)
     made = []
     for layer in (0, 1):
+        if layer == ready:
+            made.append((Held(ready_up), Held(ready_down)))
+            continue
         mine = core == layer
         up_forward, down_forward = forward[layer]
         up_cut = (1, wide) if up_forward else (0, narrow)
         down_cut = (1, narrow) if down_forward else (0, wide)
         made.append(
             (
-                Stream(mine, own_up, other_up, held_up.at[layer], sems.at[2 * layer], *up_cut),
-                Stream(mine, own_down, other_down, held_down.at[layer], sems.at[2 * layer + 1], *down_cut),
+                Stream(mine, own_up, other_up, held_up, sems.at[0], *up_cut),
+                Stream(mine, own_down, other_down, held_down, sems.at[1], *down_cut),
             )
         )
     return made
+
+
+def hold_layer(place, layer, weights):
+    small, own_up, other_up, own_down, other_down = weights
+
+    def kernel(place_ref, own_up_ref, other_up_ref, own_down_ref, other_down_ref, up_out, down_out, sems):
+        def load(up_ref, down_ref):
+            up = pltpu.make_async_copy(up_ref, up_out, sems.at[0])
+            down = pltpu.make_async_copy(down_ref, down_out, sems.at[1])
+            up.start()
+            down.start()
+            up.wait()
+            down.wait()
+
+        @pl.when((place_ref[1] == 1) & (place_ref[0] == layer))
+        def _():
+            load(own_up_ref, own_down_ref)
+
+        @pl.when((place_ref[1] == 1) & (place_ref[0] != layer))
+        def _():
+            load(other_up_ref, other_down_ref)
+
+    return pl.pallas_call(
+        kernel,
+        out_shape=[pltpu.VMEM(own_up.shape, own_up.dtype), pltpu.VMEM(own_down.shape, own_down.dtype)],
+        in_specs=[whole(pltpu.SMEM)] + [whole(pltpu.HBM)] * 4,
+        out_specs=[whole(), whole()],
+        scratch_shapes=[pltpu.SemaphoreType.DMA((2,))],
+        compiler_params=pltpu.CompilerParams(vmem_limit_bytes=4 * 1024 * 1024),
+        name="hold_layer",
+    )(place, *map(in_hbm, weights[1:]))
 
 
 def stage_cost(products, batch, model_width, hidden_width):
@@ -515,21 +558,21 @@
     return pltpu.CompilerParams(vmem_limit_bytes=STAGE_LIMIT)
 
 
-def forward_stage(place, pieces, top, weights, count):
+def forward_stage(place, pieces, top, weights, ready, count):
     batch, model_width = top.shape
     hidden_width = weights[1].shape[1]
     width = model_width // count
 
     def kernel(place_ref, *refs):
         piece_refs, (top_ref, small_ref), refs = refs[: len(pieces)], refs[len(pieces) :][:2], refs[len(pieces) + 2 :]
-        matrices, refs = refs[:4], refs[4:]
+        matrices, refs = refs[:6], refs[6:]
         out_ref, hid, inter, scale, kept, g_hidden = refs[:6]
         held, (normed, hidden, top_turned, grams) = refs[6:9], refs[9:]
         core = place_ref[0]
 
         @pl.when(place_ref[1] == 1)
         def _():
-            layers = streams_of(core, matrices, held, [(True, True), (True, True)])
+            layers = streams_of(core, matrices, held, [(True, True), (True, True)], 0)
             for up, down in layers:
                 up.start()
                 down.start()
@@ -547,7 +590,7 @@
 
         @pl.when(place_ref[2] == 1)
         def _():
-            layers = streams_of(core, matrices, held, [(True, True), (True, False)])
+            layers = streams_of(core, matrices, held, [(True, True), (True, False)], 0)
             down = layers[1][1]
             down.start()
             turn(top_ref, top_turned)
@@ -570,23 +613,23 @@
         compiler_params=stage_params(),
         cost_estimate=stage_cost(4, batch, model_width, hidden_width),
         name="forward_stage",
-    )(place, *pieces, top, weights[0], *map(in_hbm, weights[1:]))
+    )(place, *pieces, top, weights[0], *map(in_hbm, weights[1:]), *ready)
     return out[0], out[1:5], out[5]
 
 
-def turn_stage(place, acts, top, g_hidden, weights, count):
+def turn_stage(place, acts, top, g_hidden, weights, ready, count):
     batch, model_width = acts.shape
     hidden_width = weights[1].shape[1]
     width = model_width // count
 
     def kernel(place_ref, acts_ref, top_ref, ghid_ref, small_ref, *refs):
-        matrices, refs = refs[:4], refs[4:]
+        matrices, refs = refs[:6], refs[6:]
         out_ref, held = refs[0], refs[1:4]
         hid, hidden, inter, scale, upper, grad, turned, normed, weighted, g_before, grams = refs[4:]
 
         @pl.when(place_ref[1] == 1)
         def _():
-            layers = streams_of(place_ref[0], matrices, held, [(True, True), (True, True)])
+            layers = streams_of(place_ref[0], matrices, held, [(True, True), (True, True)], 0)
             (up0, down0), (up1, down1) = layers
             for stream in (up0, down0, up1):
                 stream.start()
@@ -630,21 +673,21 @@
         compiler_params=stage_params(),
         cost_estimate=stage_cost(6, batch, model_width, hidden_width),
         name="turn_stage",
-    )(place, acts, top, g_hidden, weights[0], *map(in_hbm, weights[1:]))
-
-
-def backward_stage(place, grad, saved, weights, count):
+    )(place, acts, top, g_hidden, weights[0], *map(in_hbm, weights[1:]), *ready)
+
+
+def backward_stage(place, grad, saved, weights, ready, count):
     batch, model_width = grad.shape
     hidden_width = weights[1].shape[1]
 
     def kernel(place_ref, grad_ref, hid, inter, scale, kept, small_ref, *refs):
-        matrices, refs = refs[:4], refs[4:]
+        matrices, refs = refs[:6], refs[6:]
         out_ref, held = refs[0], refs[1:4]
         middle, turned, weighted, g_before = refs[4:]
 
         @pl.when(place_ref[1] == 1)
         def _():
-            layers = streams_of(place_ref[0], matrices, held, [(False, False), (False, False)])
+            layers = streams_of(place_ref[0], matrices, held, [(False, False), (False, False)], 1)
             for up, down in reversed(layers):
                 down.start()
                 up.start()
@@ -673,7 +716,7 @@
         compiler_params=stage_params(),
         cost_estimate=stage_cost(4, batch, model_width, hidden_width),
         name="backward_stage",
-    )(place, grad, *saved, weights[0], *map(in_hbm, weights[1:]))
+    )(place, grad, *saved, weights[0], *map(in_hbm, weights[1:]), *ready)
 
 
 def swapped(value, section_count):
@@ -779,16 +822,22 @@
 
     saved = None
     for tick in range(stages - 1):
-        out, fresh, product = forward_stage(at(tick), pieces, top, weights, embed_count)
+        place = at(tick)
+        ready = hold_layer(after(place, lead if tick == 0 else out), 0, weights)
+        out, fresh, product = forward_stage(place, pieces, top, weights, ready, embed_count)
         if saved is None:
             saved, g_hidden = fresh, product
         else:
             saved = [jnp.where(stage == tick, new, old) for new, old in zip(fresh, saved)]
         pieces = [moved(out, tick, tick + 1)]
-    grad = turn_stage(at(stages - 1), pieces[0], top, g_hidden, weights, embed_count)
+    place = at(stages - 1)
+    ready = hold_layer(after(place, out), 0, weights)
+    grad = turn_stage(place, pieces[0], top, g_hidden, weights, ready, embed_count)
     for tick in reversed(range(stages - 1)):
+        place = at(tick)
+        ready = hold_layer(after(place, grad), 1, weights)
         grad = moved(grad, tick + 1, tick)
-        grad = backward_stage(at(tick), grad, saved, weights, embed_count)
+        grad = backward_stage(place, grad, saved, weights, ready, embed_count)
 
     own_grad = grad[:look_dev]
     for s in range(1, stages):

time: 156 us -> 152 us (0.974)
  waiting for transfers between devices: 64 us -> 50 us
  Pallas kernels: 58.2 us -> 66.4 us
  other arithmetic: 1.71 us -> 4.05 us
  starting transfers between devices: 23.7 us -> 22.1 us
    ppermute x4, waiting for transfers between devices: 38.2 us -> 24.9 us  [moved(): return lax.ppermute(value, 'section', pairs)]
    pallas_call x0 -> x3, Pallas kernels: none -> 13.2 us  [hold_layer(): pl.pallas_call(kernel, out_shape=[pltpu.VMEM(own_up.shape, own_up.dtype),...]
    pallas_call x1, Pallas kernels: 12.2 us -> 9.09 us  [forward_stage(): pl.pallas_call(kernel, out_shape=[jax.ShapeDtypeStruct(top.shape, jnp.bfl...]
    all_to_all x2, waiting for transfers between devices: 16.1 us -> 13.2 us  [swap_in_half(): lax.all_to_all(value, TABLE_AXES, split_axis=0, concat_axis=0, axis_index...]
    ppermute x3, waiting for transfers between devices: 9.63 us -> 11.9 us  [mirror(): lax.ppermute(value, 'table', [(t, (t + along // 2) % along) for t in rang...]
    pallas_call x1, Pallas kernels: 15.4 us -> 13.6 us  [backward_stage(): pl.pallas_call(kernel, out_shape=jax.ShapeDtypeStruct(grad.shape, jnp.bfl...]
  transfers between devices with their start and end apart: 12 -> 12, of which waited for: 8 -> 7; matrix products, arithmetic and copies ran while one was open for 2% -> 3% of each run, Pallas kernels for 11% -> 20%
where the time goes in v12:
time: 152 us; the launch traced here: 151 us
  Pallas kernels  66.4 us (44%)
  waiting for transfers between devices  50 us (33%)
  starting transfers between devices  22.1 us (15%)
  local copies, waits for them, and re-layouts  8.26 us (5%)
  other arithmetic  4.05 us (3%)
    ppermute x4, waiting for transfers between devices, moved(): return lax.ppermute(value, 'section', pairs)  24.9 us
    pallas_call x1, Pallas kernels, backward_stage(): pl.pallas_call(kernel, out_shape=jax.ShapeDtypeStruct(grad.shape, jnp.bfl...  13.6 us
    pallas_call x3, Pallas kernels, hold_layer(): pl.pallas_call(kernel, out_shape=[pltpu.VMEM(own_up.shape, own_up.dtype),...  13.2 us
    all_to_all x2, waiting for transfers between devices, swap_in_half(): lax.all_to_all(value, TABLE_AXES, split_axis=0, concat_axis=0, axis_index...  13.2 us
    ppermute x3, waiting for transfers between devices, mirror(): lax.ppermute(value, 'table', [(t, (t + along // 2) % along) for t in rang...  11.9 us
    all_to_all x2, starting transfers between devices, swap_in_half(): lax.all_to_all(value, TABLE_AXES, split_axis=0, concat_axis=0, axis_index...  10.3 us
    pallas_call x1, Pallas kernels, add_rows(): pl.pallas_call(kernel, out_shape=jax.ShapeDtypeStruct((rows, width), jnp....  10.2 us
    pallas_call x1, Pallas kernels, forward_stage(): pl.pallas_call(kernel, out_shape=[jax.ShapeDtypeStruct(top.shape, jnp.bfl...  9.09 us
  transfers between devices with their start and end apart: 12, of which 7 were waited for; matrix products, arithmetic and copies ran while one was open for 3% of the time, Pallas kernels for 20%

profile of v12, /device:TPU:0, one launch (start us, length us, event | category | flops | bytes accessed | tf_op | source)
XLA Modules:
  0.0 151.2 jit_solution(11005474332339225582)
XLA Ops:
  0.5 4.0 %collective-permute-start = (s32[64,512]{1,0:T(8,128)}, s32[64,512]{1,0:T(8,128)S(1)}, u32[]{:S(2)}, u32[]{:S(2)}) collective-permute-start(s32[64,512]{1,0:T(8,128)} %bitcast.47), channel_id=1, source_target_pairs={{0,4},{1,5},{2,6},{3,7},{4,0},{5,1},{6,2},{7,3},{8,12},{9,13},{10,... | collective-permute-start | bytes 393224 | tf_op jit(solution)/shard_map/ppermute | solution.py:733
  5.3 7.0 %pick_rows.1.sent_ref = bf16[4096,128]{1,0:T(8,128)(2,1)} custom-call(s32[1]{0:T(128)} %bitcast.9.half_ref, s32[4096]{0:T(1024)S(1)} %bitcast.30, bf16[4096,128]{1,0:T(8,128)(2,1)} %table_ref.1), custom_call_target="tpu_custom_call" | custom-call | tf_op jit(solution)/shard_map/pick_rows/pallas_call | solution.py:67
  12.3 4.9 %all-to-all-start = ((bf16[16,2,128,128]{3,2,1,0:T(8,128)(2,1)}), bf16[16,2,128,128]{3,2,1,0:T(8,128)(2,1)S(1)}, u32[]{:S(2)}, u32[]{:S(2)}) async-start(bf16[16,2,128,128]{3,2,1,0:T(8,128)(2,1)} %bitcast.11), calls=%async_computation | async-start | bytes 2097152 | tf_op jit(solution)/shard_map/all_to_all | solution.py:743
  19.0 1.3 fusion.11.codes_ref
  20.9 3.9 %spread_weights.3 = (bf16[16,512,128]{2,1,0:T(8,128)(2,1)S(1)}, bf16[16,512,128]{2,1,0:T(8,128)(2,1)}) custom-call(s32[64,512]{1,0:T(8,128)S(1)} %fusion.11.codes_ref, bf16[8,512]{1,0:T(8,128)(2,1)S(1)} %copy-done.10), custom_call_target="tpu_custom_call" | custom-call | flops 1073741824 | bytes 2097152 | tf_op jit(solution)/shard_map/spread_weights/pallas_call | solution.py:110
  24.8 1.3 copy-done.6
  26.5 3.9 %spread_weights.2 = (bf16[16,512,128]{2,1,0:T(8,128)(2,1)S(1)}, bf16[16,512,128]{2,1,0:T(8,128)(2,1)}) custom-call(s32[64,512]{1,0:T(8,128)S(1)} %fusion.5.codes_ref, bf16[8,512]{1,0:T(8,128)(2,1)S(1)} %copy-done.11), custom_call_target="tpu_custom_call" | custom-call | flops 1073741824 | bytes 2097152 | tf_op jit(solution)/shard_map/spread_weights/pallas_call | solution.py:110
  30.4 1.3 copy-done.4
  31.9 1.6 %copy-done.5 = bf16[16,512,128]{2,1,0:T(8,128)(2,1)S(1)} copy-done((bf16[16,512,128]{2,1,0:T(8,128)(2,1)S(1)}, bf16[16,512,128]{2,1,0:T(8,128)(2,1)}, u32[]{:S(2)}) %copy-start.5) | copy-done | bytes 2097176
  33.5 0.9 compress.3
  34.5 1.6 %collective-permute-start.1 = (bf16[64,1024]{1,0:T(8,128)(2,1)S(1)}, bf16[64,1024]{1,0:T(8,128)(2,1)S(1)}, u32[]{:S(2)}, u32[]{:S(2)}) collective-permute-start(bf16[64,1024]{1,0:T(8,128)(2,1)S(1)} %compress.3), channel_id=1, source_target_pairs={{0,4},{1,5},{2,6},{3,7},{4,0},{5,1},{6,2},{7,3},{8,12},{9,13},{10,... | collective-permute-start | bytes 393224 | tf_op jit(solution)/shard_map/ppermute | solution.py:733
  36.2 1.6 %copy-done.7 = bf16[16,512,128]{2,1,0:T(8,128)(2,1)S(1)} copy-done((bf16[16,512,128]{2,1,0:T(8,128)(2,1)S(1)}, bf16[16,512,128]{2,1,0:T(8,128)(2,1)}, u32[]{:S(2)}) %copy-start.7) | copy-done | bytes 2097176
  37.8 0.9 compress.2
  38.7 4.8 %collective-permute-done.1 = bf16[64,1024]{1,0:T(8,128)(2,1)S(1)} collective-permute-done((bf16[64,1024]{1,0:T(8,128)(2,1)S(1)}, bf16[64,1024]{1,0:T(8,128)(2,1)S(1)}, u32[]{:S(2)}, u32[]{:S(2)}) %collective-permute-start.1) | collective-permute-done | bytes 131104 | tf_op jit(solution)/shard_map/ppermute | solution.py:733
  43.6 1.3 collective-permute-start.2
  45.0 6.3 %hold_layer.3 = (bf16[1024,4096]{1,0:T(8,128)(2,1)S(1)}, bf16[4096,1024]{1,0:T(8,128)(2,1)S(1)}) custom-call(s32[3]{0:T(128)S(1)} %pad_add_fusion.1.place_ref, bf16[1024,4096]{1,0:T(8,128)(2,1)} %bitcast.34, bf16[1024,4096]{1,0:T(8,128)(2,1)} %collective-permute-done.4.other_up_ref.refs_5_.refs_1_, bf16[4096,1024]{1,0:T(8,128)(2,1)} %bitcast.41, ...), custom_call_target="tpu_custom_call" | custom-call | tf_op jit(solution)/shard_map/hold_layer/pallas_call | solution.py:540
  51.3 9.1 %forward_stage.1 = (bf16[128,1024]{1,0:T(8,128)(2,1)S(1)}, bf16[2,4096,128]{2,1,0:T(8,128)(2,1)S(1)}, f32[2,128,1024]{2,1,0:T(8,128)S(1)}, f32[2,128,128]{2,1,0:...) custom-call(s32[3]{0:T(128)S(1)} %pad_add_fusion.1.place_ref, ...), custom_call_target="tpu_custom_call" | custom-call | flops 4294967296 | bytes 1048576 | tf_op jit(solution)/shard_map/forward_stage/pallas_call | solution.py:599
  60.4 1.3 collective-permute-start.6
  62.4 4.4 %collective-permute-done.6.acts_ref = bf16[128,1024]{1,0:T(8,128)(2,1)S(1)} collective-permute-done((bf16[128,1024]{1,0:T(8,128)(2,1)S(1)}, bf16[128,1024]{1,0:T(8,128)(2,1)S(1)}, u32[]{:S(2)}, u32[]{:S(2)}) %collective-permute-start.6) | collective-permute-done | bytes 262176 | tf_op jit(solution)/shard_map/ppermute | solution.py:728
  66.8 0.8 turn_stage.1
  67.6 1.3 collective-permute-start.7
  68.9 6.3 %hold_layer.5 = (bf16[1024,4096]{1,0:T(8,128)(2,1)S(1)}, bf16[4096,1024]{1,0:T(8,128)(2,1)S(1)}) custom-call(s32[3]{0:T(128)S(1)} %pad_add_fusion.1.place_ref, bf16[1024,4096]{1,0:T(8,128)(2,1)} %bitcast.38, bf16[1024,4096]{1,0:T(8,128)(2,1)} %collective-permute-done.4.other_up_ref.refs_5_.refs_1_, bf16[4096,1024]{1,0:T(8,128)(2,1)} %bitcast.45, ...), custom_call_target="tpu_custom_call" | custom-call | tf_op jit(solution)/shard_map/hold_layer/pallas_call | solution.py:540
  75.2 18.0 %collective-permute-done.7.grad_ref = bf16[128,1024]{1,0:T(8,128)(2,1)S(1)} collective-permute-done((bf16[128,1024]{1,0:T(8,128)(2,1)S(1)}, bf16[128,1024]{1,0:T(8,128)(2,1)S(1)}, u32[]{:S(2)}, u32[]{:S(2)}) %collective-permute-start.7) | collective-permute-done | bytes 262176 | tf_op jit(solution)/shard_map/ppermute | solution.py:728
  93.2 13.6 %backward_stage.1 = bf16[128,1024]{1,0:T(8,128)(2,1)S(1)} custom-call(s32[3]{0:T(128)S(1)} %pad_add_fusion.1.place_ref, bf16[128,1024]{1,0:T(8,128)(2,1)S(1)} %collective-permute-done.7.grad_ref, bf16[2,4096,128]{2,1,0:T(8,128)(2,1)S(1)} %get-tuple-element.41.hid, f32[2,128,1024]{2,1,0:T(8,128)S(1)} %get-tuple-element.42.inter, ...), custom_call_target="tpu_custom_call" | custom-call | flops 4294967296 | bytes 1048576 | tf_op jit(solution)/shard_map/backward_stage/pallas_call | solution.py:704
  106.9 1.3 collective-permute-start.8
  108.2 2.5 %collective-permute-done.8 = bf16[64,1024]{1,0:T(8,128)(2,1)S(1)} collective-permute-done((bf16[64,1024]{1,0:T(8,128)(2,1)S(1)}, bf16[64,1024]{1,0:T(8,128)(2,1)S(1)}, u32[]{:S(2)}, u32[]{:S(2)}) %collective-permute-start.8) | collective-permute-done | bytes 131104 | tf_op jit(solution)/shard_map/ppermute | solution.py:728
  110.8 0.9 expand.2.refs_0_
  111.7 7.1 %collective-permute-done.9.grad_ref = bf16[64,1024]{1,0:T(8,128)(2,1)S(1)} collective-permute-done((bf16[64,1024]{1,0:T(8,128)(2,1)S(1)}, bf16[64,1024]{1,0:T(8,128)(2,1)S(1)}, u32[]{:S(2)}, u32[]{:S(2)}) %collective-permute-start.9) | collective-permute-done | bytes 131104 | tf_op jit(solution)/shard_map/ppermute | solution.py:733
  118.8 1.9 %expand.3 = bf16[16,2,128,128]{3,2,1,0:T(8,128)(2,1)} custom-call(bf16[16,512,128]{2,1,0:T(8,128)(2,1)S(1)} %copy-done.2, bf16[64,1024]{1,0:T(8,128)(2,1)S(1)} %collective-permute-done.9.grad_ref, bf16[16,128,128]{2,1,0:T(8,128)(2,1)S(1)} %expand.2.refs_0_), custom_call_target="tpu_custom_call" | custom-call | tf_op jit(solution)/shard_map/expand/pallas_call | solution.py:196
  120.7 5.4 %all-to-all-start.1 = ((bf16[16,2,128,128]{3,2,1,0:T(8,128)(2,1)}), bf16[16,2,128,128]{3,2,1,0:T(8,128)(2,1)S(1)}, u32[]{:S(2)}, u32[]{:S(2)}) async-start(bf16[16,2,128,128]{3,2,1,0:T(8,128)(2,1)} %expand.3), calls=%async_computation.1 | async-start | bytes 2097152 | tf_op jit(solution)/shard_map/all_to_all | solution.py:743
  127.9 13.0 %all-to-all-done.1 = bf16[16,2,128,128]{3,2,1,0:T(8,128)(2,1)S(1)} async-done(((bf16[16,2,128,128]{3,2,1,0:T(8,128)(2,1)}), bf16[16,2,128,128]{3,2,1,0:T(8,128)(2,1)S(1)}, u32[]{:S(2)}, u32[]{:S(2)}) %all-to-all-start.1) | async-done | bytes 1048608 | tf_op jit(solution)/shard_map/all_to_all | solution.py:743
  140.9 10.2 %add_rows.1 = f32[4096,128]{1,0:T(8,128)} custom-call(s32[4096]{0:T(1024)S(1)} %bitcast.32, bf16[4096,128]{1,0:T(8,128)(2,1)S(1)} %bitcast.27, bf16[4096,128]{1,0:T(8,128)(2,1)} %pick_rows.1.sent_ref), custom_call_target="tpu_custom_call" | custom-call | tf_op jit(solution)/shard_map/add_rows/pallas_call | solution.py:253
  (56 shorter events, 7.0 us)
Async XLA Ops:
  0.0 36.2 %copy-start = (bf16[1,4,64,1024]{3,2,1,0:T(8,128)(2,1)S(1)}, bf16[1,4,64,1024]{3,2,1,0:T(8,128)(2,1)}, u32[]{:S(2)}) copy-start(bf16[1,4,64,1024]{3,2,1,0:T(8,128)(2,1)} %param.16) | copy-start | bytes 1572868
  0.0 26.5 %copy-start.11 = (bf16[8,512]{1,0:T(8,128)(2,1)S(1)}, bf16[8,512]{1,0:T(8,128)(2,1)}, u32[]{:S(2)}) copy-start(bf16[8,512]{1,0:T(8,128)(2,1)} %lcb_ref.3) | copy-start | bytes 24580
  0.0 44.9 %collective-permute-start.4 = (bf16[1024,4096]{1,0:T(8,128)(2,1)}, bf16[1024,4096]{1,0:T(8,128)(2,1)}, u32[]{:S(2)}, u32[]{:S(2)}) collective-permute-start(bf16[1024,4096]{1,0:T(8,128)(2,1)} %bitcast.33), channel_id=1, source_target_pairs={{0,8},{8,0},{16,24},{24,16},{1,9},{9,1},{17,25},{25,17},{2,10},{10... | collective-permute-start | bytes 25165832 | tf_op jit(solution)/shard_map/ppermute | solution.py:723
  0.5 44.5 %collective-permute-start.5 = (bf16[4096,1024]{1,0:T(8,128)(2,1)}, bf16[4096,1024]{1,0:T(8,128)(2,1)}, u32[]{:S(2)}, u32[]{:S(2)}) collective-permute-start(bf16[4096,1024]{1,0:T(8,128)(2,1)} %bitcast.40), channel_id=1, source_target_pairs={{0,8},{8,0},{16,24},{24,16},{1,9},{9,1},{17,25},{25,17},{2,10},{10... | collective-permute-start | bytes 25165832 | tf_op jit(solution)/shard_map/ppermute | solution.py:723
  0.5 11.7 %collective-permute-start = (s32[64,512]{1,0:T(8,128)}, s32[64,512]{1,0:T(8,128)S(1)}, u32[]{:S(2)}, u32[]{:S(2)}) collective-permute-start(s32[64,512]{1,0:T(8,128)} %bitcast.47), channel_id=1, source_target_pairs={{0,4},{1,5},{2,6},{3,7},{4,0},{5,1},{6,2},{7,3},{8,12},{9,13},{10,... | collective-permute-start | bytes 393224 | tf_op jit(solution)/shard_map/ppermute | solution.py:733
  4.6 0.7 copy-start.8
  12.3 19.7 %all-to-all-start = ((bf16[16,2,128,128]{3,2,1,0:T(8,128)(2,1)}), bf16[16,2,128,128]{3,2,1,0:T(8,128)(2,1)S(1)}, u32[]{:S(2)}, u32[]{:S(2)}) async-start(bf16[16,2,128,128]{3,2,1,0:T(8,128)(2,1)} %bitcast.11), calls=%async_computation | async-start | bytes 2097152 | tf_op jit(solution)/shard_map/all_to_all | solution.py:743
  17.1 27.8 %copy-start.12 = (bf16[1,8,128]{2,1,0:T(8,128)(2,1)S(1)}, bf16[1,8,128]{2,1,0:T(8,128)(2,1)}, u32[]{:S(2)}) copy-start(bf16[1,8,128]{2,1,0:T(8,128)(2,1)} %param.12) | copy-start | bytes 6148
  18.5 26.4 %collective-permute-start.3 = (bf16[16,128]{1,0:T(8,128)(2,1)S(1)}, bf16[16,128]{1,0:T(8,128)(2,1)S(1)}, u32[]{:S(2)}, u32[]{:S(2)}) collective-permute-start(bf16[16,128]{1,0:T(8,128)(2,1)S(1)} %pad_maximum_fusion.1), channel_id=1, source_target_pairs={{0,8},{8,0},{16,24},{24,16},{1,9},{9,1},{17,25},{25,17},{2,10},{10... | collective-permute-start | bytes 12296 | tf_op jit(solution)/shard_map/ppermute | solution.py:723
  20.2 0.7 copy-start.10
  24.8 1.3 copy-start.6
  30.4 1.3 copy-start.4
  31.9 1.6 %copy-start.5 = (bf16[16,512,128]{2,1,0:T(8,128)(2,1)S(1)}, bf16[16,512,128]{2,1,0:T(8,128)(2,1)}, u32[]{:S(2)}) copy-start(bf16[16,512,128]{2,1,0:T(8,128)(2,1)} %copy-done.4) | copy-start | bytes 6291460
  34.5 9.1 %collective-permute-start.1 = (bf16[64,1024]{1,0:T(8,128)(2,1)S(1)}, bf16[64,1024]{1,0:T(8,128)(2,1)S(1)}, u32[]{:S(2)}, u32[]{:S(2)}) collective-permute-start(bf16[64,1024]{1,0:T(8,128)(2,1)S(1)} %compress.3), channel_id=1, source_target_pairs={{0,4},{1,5},{2,6},{3,7},{4,0},{5,1},{6,2},{7,3},{8,12},{9,13},{10,... | collective-permute-start | bytes 393224 | tf_op jit(solution)/shard_map/ppermute | solution.py:733
  36.2 1.6 %copy-start.7 = (bf16[16,512,128]{2,1,0:T(8,128)(2,1)S(1)}, bf16[16,512,128]{2,1,0:T(8,128)(2,1)}, u32[]{:S(2)}) copy-start(bf16[16,512,128]{2,1,0:T(8,128)(2,1)} %copy-done.6) | copy-start | bytes 6291460
  43.6 7.7 %collective-permute-start.2 = (bf16[64,1024]{1,0:T(8,128)(2,1)S(1)}, bf16[64,1024]{1,0:T(8,128)(2,1)S(1)}, u32[]{:S(2)}, u32[]{:S(2)}) collective-permute-start(bf16[64,1024]{1,0:T(8,128)(2,1)S(1)} %add_convert_fusion.refs_0_), channel_id=1, source_target_pairs={{16,0},{24,8},{17,1},{25,9},{18,2},{26,10},{19,3},{27,11},{20,4},{... | collective-permute-start | bytes 393224 | tf_op jit(solution)/shard_map/ppermute | solution.py:728
  60.4 6.4 %collective-permute-start.6 = (bf16[128,1024]{1,0:T(8,128)(2,1)S(1)}, bf16[128,1024]{1,0:T(8,128)(2,1)S(1)}, u32[]{:S(2)}, u32[]{:S(2)}) collective-permute-start(bf16[128,1024]{1,0:T(8,128)(2,1)S(1)} %get-tuple-element.36), channel_id=1, source_target_pairs={{0,16},{8,24},{1,17},{9,25},{2,18},{10,26},{3,19},{11,27},{4,20},{... | collective-permute-start | bytes 786440 | tf_op jit(solution)/shard_map/ppermute | solution.py:728
  67.6 25.7 %collective-permute-start.7 = (bf16[128,1024]{1,0:T(8,128)(2,1)S(1)}, bf16[128,1024]{1,0:T(8,128)(2,1)S(1)}, u32[]{:S(2)}, u32[]{:S(2)}) collective-permute-start(bf16[128,1024]{1,0:T(8,128)(2,1)S(1)} %turn_stage.1), channel_id=1, source_target_pairs={{16,0},{24,8},{17,1},{25,9},{18,2},{26,10},{19,3},{27,11},{20,4},{... | collective-permute-start | bytes 786440 | tf_op jit(solution)/shard_map/ppermute | solution.py:728
  93.2 17.5 %copy-start.3 = (bf16[16,512,128]{2,1,0:T(8,128)(2,1)S(1)}, bf16[16,512,128]{2,1,0:T(8,128)(2,1)}, u32[]{:S(2)}) copy-start(bf16[16,512,128]{2,1,0:T(8,128)(2,1)} %get-tuple-element.48.spread_ref) | copy-start | bytes 6291460
  93.2 25.5 %copy-start.2 = (bf16[16,512,128]{2,1,0:T(8,128)(2,1)S(1)}, bf16[16,512,128]{2,1,0:T(8,128)(2,1)}, u32[]{:S(2)}) copy-start(bf16[16,512,128]{2,1,0:T(8,128)(2,1)} %get-tuple-element.27.spread_ref) | copy-start | bytes 6291460
  93.2 57.8 %copy-start.1 = (bf16[1,4,64,1024]{3,2,1,0:T(8,128)(2,1)S(1)}, bf16[1,4,64,1024]{3,2,1,0:T(8,128)(2,1)}, u32[]{:S(2)}) copy-start(bf16[1,4,64,1024]{3,2,1,0:T(8,128)(2,1)} %param.16) | copy-start | bytes 1572868
  106.8 19.9 %copy-start.13 = (s32[1,32]{1,0:T(1,128)S(1)}, s32[1,32]{1,0:T(1,128)}, u32[]{:S(2)}) copy-start(s32[1,32]{1,0:T(1,128)} %param.19) | copy-start | bytes 388
  106.8 21.0 %copy-start.9 = (s32[1,32,128]{2,1,0:T(8,128)S(1)}, s32[1,32,128]{2,1,0:T(8,128)}, u32[]{:S(2)}) copy-start(s32[1,32,128]{2,1,0:T(8,128)} %param.18) | copy-start | bytes 49156
  106.9 3.8 %collective-permute-start.8 = (bf16[64,1024]{1,0:T(8,128)(2,1)S(1)}, bf16[64,1024]{1,0:T(8,128)(2,1)S(1)}, u32[]{:S(2)}, u32[]{:S(2)}) collective-permute-start(bf16[64,1024]{1,0:T(8,128)(2,1)S(1)} %slice.8), channel_id=1, source_target_pairs={{0,16},{8,24},{1,17},{9,25},{2,18},{10,26},{3,19},{11,27},{4,20},{... | collective-permute-start | bytes 393224 | tf_op jit(solution)/shard_map/ppermute | solution.py:728
  110.7 8.1 %collective-permute-start.9 = (bf16[64,1024]{1,0:T(8,128)(2,1)S(1)}, bf16[64,1024]{1,0:T(8,128)(2,1)S(1)}, u32[]{:S(2)}, u32[]{:S(2)}) collective-permute-start(bf16[64,1024]{1,0:T(8,128)(2,1)S(1)} %slice_select_fusion.grad_ref), channel_id=1, source_target_pairs={{0,4},{1,5},{2,6},{3,7},{4,0},{5,1},{6,2},{7,3},{8,12},{9,13},{10,... | collective-permute-start | bytes 393224 | tf_op jit(solution)/shard_map/ppermute | solution.py:733
  120.7 20.2 %all-to-all-start.1 = ((bf16[16,2,128,128]{3,2,1,0:T(8,128)(2,1)}), bf16[16,2,128,128]{3,2,1,0:T(8,128)(2,1)S(1)}, u32[]{:S(2)}, u32[]{:S(2)}) async-start(bf16[16,2,128,128]{3,2,1,0:T(8,128)(2,1)} %expand.3), calls=%async_computation.1 | async-start | bytes 2097152 | tf_op jit(solution)/shard_map/all_to_all | solution.py:743

commit v13 on v12

--- a/solution.py
+++ b/solution.py
@@ -517,35 +517,46 @@
     return made
 
 
-def hold_layer(place, layer, weights):
-    small, own_up, other_up, own_down, other_down = weights
-
-    def kernel(place_ref, own_up_ref, other_up_ref, own_down_ref, other_down_ref, up_out, down_out, sems):
-        def load(up_ref, down_ref):
-            up = pltpu.make_async_copy(up_ref, up_out, sems.at[0])
-            down = pltpu.make_async_copy(down_ref, down_out, sems.at[1])
-            up.start()
-            down.start()
-            up.wait()
-            down.wait()
+def hold_matrix(place, layer, own, other):
+    pieces = 8
+    part = own.shape[0] // pieces
+
+    def kernel(place_ref, own_ref, other_ref, out_ref, sems):
+        def load(source):
+            copies = []
+            for piece in range(pieces):
+                cut = pl.ds(piece * part, part)
+                copies.append(pltpu.make_async_copy(source.at[cut], out_ref.at[cut], sems.at[piece]))
+                copies[-1].start()
+            for copy in copies:
+                copy.wait()
 
         @pl.when((place_ref[1] == 1) & (place_ref[0] == layer))
         def _():
-            load(own_up_ref, own_down_ref)
+            load(own_ref)
 
         @pl.when((place_ref[1] == 1) & (place_ref[0] != layer))
         def _():
-            load(other_up_ref, other_down_ref)
+            load(other_ref)
 
     return pl.pallas_call(
         kernel,
-        out_shape=[pltpu.VMEM(own_up.shape, own_up.dtype), pltpu.VMEM(own_down.shape, own_down.dtype)],
-        in_specs=[whole(pltpu.SMEM)] + [whole(pltpu.HBM)] * 4,
-        out_specs=[whole(), whole()],
-        scratch_shapes=[pltpu.SemaphoreType.DMA((2,))],
+        out_shape=pltpu.VMEM(own.shape, own.dtype),
+        in_specs=[whole(pltpu.SMEM)] + [whole(pltpu.HBM)] * 2,
+        out_specs=whole(),
+        scratch_shapes=[pltpu.SemaphoreType.DMA((pieces,))],
         compiler_params=pltpu.CompilerParams(vmem_limit_bytes=4 * 1024 * 1024),
-        name="hold_layer",
-    )(place, *map(in_hbm, weights[1:]))
+        name="hold_matrix",
+    )(place, in_hbm(own), in_hbm(other))
+
+
+def hold_layer(place, layer, weights, earlier):
+    small, own_up, other_up, own_down, other_down = weights
+    place = after(place, earlier)
+    return [
+        hold_matrix(place, layer, own_up, other_up),
+        hold_matrix(place, layer, own_down, other_down),
+    ]
 
 
 def stage_cost(products, batch, model_width, hidden_width):
@@ -811,19 +822,23 @@
     spread_far, spread_near = lax.optimization_barrier((spread_far, spread_near))
     far_part = mirror(compress(spread_far, fetched, 1, embed_count, jnp.bfloat16))
     near_part = compress(spread_near, fetched, 0, embed_count, jnp.float32)
+
+    def at(tick):
+        is_last = (stage == stages - 1) & (tick == 0)
+        return jnp.stack([core, stage == tick, is_last]).astype(jnp.int32)
+
+    first_up = hold_matrix(after(at(0), near_part), 0, weights[1], weights[2])
+    far_part = after(far_part, first_up)
     lead = (near_part + far_part.astype(jnp.float32)).astype(jnp.bfloat16)
+    first_down = hold_matrix(after(at(0), lead), 0, weights[3], weights[4])
     pieces = [lead] + [moved(lead, s, 0) for s in range(1, stages)]
     top = top_grad.reshape(stages, 2, look_dev, model_width)
     top = lax.dynamic_index_in_dim(top, core, 1, keepdims=False).reshape(-1, model_width)
 
-    def at(tick):
-        is_last = (stage == stages - 1) & (tick == 0)
-        return jnp.stack([core, stage == tick, is_last]).astype(jnp.int32)
-
     saved = None
     for tick in range(stages - 1):
         place = at(tick)
-        ready = hold_layer(after(place, lead if tick == 0 else out), 0, weights)
+        ready = [first_up, first_down] if tick == 0 else hold_layer(place, 0, weights, out)
         out, fresh, product = forward_stage(place, pieces, top, weights, ready, embed_count)
         if saved is None:
             saved, g_hidden = fresh, product
@@ -831,11 +846,11 @@
             saved = [jnp.where(stage == tick, new, old) for new, old in zip(fresh, saved)]
         pieces = [moved(out, tick, tick + 1)]
     place = at(stages - 1)
-    ready = hold_layer(after(place, out), 0, weights)
+    ready = hold_layer(place, 0, weights, out)
     grad = turn_stage(place, pieces[0], top, g_hidden, weights, ready, embed_count)
     for tick in reversed(range(stages - 1)):
         place = at(tick)
-        ready = hold_layer(after(place, grad), 1, weights)
+        ready = hold_layer(place, 1, weights, grad)
         grad = moved(grad, tick + 1, tick)
         grad = backward_stage(place, grad, saved, weights, ready, embed_count)
 

time: 152 us -> 149 us (0.980)
  waiting for transfers between devices: 50 us -> 40 us
  Pallas kernels: 66.4 us -> 70.6 us
  starting transfers between devices: 22.1 us -> 25.4 us
    ppermute x3, waiting for transfers between devices: 11.9 us -> 4.48 us  [mirror(): lax.ppermute(value, 'table', [(t, (t + along // 2) % along) for t in rang...]
    pallas_call x3 -> x6, Pallas kernels: 13.2 us -> 17.4 us  [hold_matrix(): pl.pallas_call(kernel, out_shape=pltpu.VMEM(own.shape, own.dtype), in_spe...]
    ppermute x4, waiting for transfers between devices: 24.9 us -> 22.2 us  [moved(): return lax.ppermute(value, 'section', pairs)]
    ppermute x3, starting transfers between devices: 5.7 us -> 7.49 us  [mirror(): lax.ppermute(value, 'table', [(t, (t + along // 2) % along) for t in rang...]
  transfers between devices with their start and end apart: 12 -> 12, of which waited for: 7 -> 8; matrix products, arithmetic and copies ran while one was open for 3% -> 3% of each run, Pallas kernels for 20% -> 24%
where the time goes in v13:
time: 149 us
  Pallas kernels  70.6 us (47%)
  waiting for transfers between devices  40 us (27%)
  starting transfers between devices  25.4 us (17%)
  local copies, waits for them, and re-layouts  8.21 us (6%)
  other arithmetic  3.99 us (3%)
    ppermute x4, waiting for transfers between devices, moved(): return lax.ppermute(value, 'section', pairs)  22.2 us
    pallas_call x6, Pallas kernels, hold_matrix(): pl.pallas_call(kernel, out_shape=pltpu.VMEM(own.shape, own.dtype), in_spe...  17.4 us
    pallas_call x1, Pallas kernels, backward_stage(): pl.pallas_call(kernel, out_shape=jax.ShapeDtypeStruct(grad.shape, jnp.bfl...  13.6 us
    all_to_all x2, waiting for transfers between devices, swap_in_half(): lax.all_to_all(value, TABLE_AXES, split_axis=0, concat_axis=0, axis_index...  13.3 us
    all_to_all x2, starting transfers between devices, swap_in_half(): lax.all_to_all(value, TABLE_AXES, split_axis=0, concat_axis=0, axis_index...  11.8 us
    pallas_call x1, Pallas kernels, add_rows(): pl.pallas_call(kernel, out_shape=jax.ShapeDtypeStruct((rows, width), jnp....  10.2 us
    pallas_call x1, Pallas kernels, forward_stage(): pl.pallas_call(kernel, out_shape=[jax.ShapeDtypeStruct(top.shape, jnp.bfl...  9.12 us
    pallas_call x2, Pallas kernels, spread_weights(): pl.pallas_call(kernel, out_shape=[pltpu.VMEM((owners, samples * embed_cou...  7.88 us
  transfers between devices with their start and end apart: 12, of which 8 were waited for; matrix products, arithmetic and copies ran while one was open for 3% of the time, Pallas kernels for 24%

profile of v13, /device:TPU:0, one launch (start us, length us, event | category | flops | bytes accessed | tf_op | source)
XLA Modules:
  0.0 148.7 jit_solution(7569228227363975585)
XLA Ops:
  0.5 4.0 %collective-permute-start = (s32[64,512]{1,0:T(8,128)}, s32[64,512]{1,0:T(8,128)S(1)}, u32[]{:S(2)}, u32[]{:S(2)}) collective-permute-start(s32[64,512]{1,0:T(8,128)} %bitcast.47), channel_id=1, source_target_pairs={{0,4},{1,5},{2,6},{3,7},{4,0},{5,1},{6,2},{7,3},{8,12},{9,13},{10,... | collective-permute-start | bytes 393224 | tf_op jit(solution)/shard_map/ppermute | solution.py:744
  5.3 7.0 %pick_rows.1.sent_ref = bf16[4096,128]{1,0:T(8,128)(2,1)} custom-call(s32[1]{0:T(128)} %bitcast.9.half_ref, s32[4096]{0:T(1024)S(1)} %bitcast.30, bf16[4096,128]{1,0:T(8,128)(2,1)} %table_ref.1), custom_call_target="tpu_custom_call" | custom-call | tf_op jit(solution)/shard_map/pick_rows/pallas_call | solution.py:67
  12.3 4.9 %all-to-all-start = ((bf16[16,2,128,128]{3,2,1,0:T(8,128)(2,1)}), bf16[16,2,128,128]{3,2,1,0:T(8,128)(2,1)S(1)}, u32[]{:S(2)}, u32[]{:S(2)}) async-start(bf16[16,2,128,128]{3,2,1,0:T(8,128)(2,1)} %bitcast.11), calls=%async_computation | async-start | bytes 2097152 | tf_op jit(solution)/shard_map/all_to_all | solution.py:754
  19.0 1.3 fusion.11.codes_ref
  20.9 4.0 %spread_weights.3 = (bf16[16,512,128]{2,1,0:T(8,128)(2,1)S(1)}, bf16[16,512,128]{2,1,0:T(8,128)(2,1)}) custom-call(s32[64,512]{1,0:T(8,128)S(1)} %fusion.11.codes_ref, bf16[8,512]{1,0:T(8,128)(2,1)S(1)} %copy-done.10), custom_call_target="tpu_custom_call" | custom-call | flops 1073741824 | bytes 2097152 | tf_op jit(solution)/shard_map/spread_weights/pallas_call | solution.py:110
  24.9 1.3 copy-done.6
  26.6 3.9 %spread_weights.2 = (bf16[16,512,128]{2,1,0:T(8,128)(2,1)S(1)}, bf16[16,512,128]{2,1,0:T(8,128)(2,1)}) custom-call(s32[64,512]{1,0:T(8,128)S(1)} %fusion.5.codes_ref, bf16[8,512]{1,0:T(8,128)(2,1)S(1)} %copy-done.11), custom_call_target="tpu_custom_call" | custom-call | flops 1073741824 | bytes 2097152 | tf_op jit(solution)/shard_map/spread_weights/pallas_call | solution.py:110
  30.5 1.3 copy-done.4
  32.0 1.6 %copy-done.5 = bf16[16,512,128]{2,1,0:T(8,128)(2,1)S(1)} copy-done((bf16[16,512,128]{2,1,0:T(8,128)(2,1)S(1)}, bf16[16,512,128]{2,1,0:T(8,128)(2,1)}, u32[]{:S(2)}) %copy-start.5) | copy-done | bytes 2097176
  33.5 0.9 compress.3
  34.5 1.6 %collective-permute-start.1 = (bf16[64,1024]{1,0:T(8,128)(2,1)S(1)}, bf16[64,1024]{1,0:T(8,128)(2,1)S(1)}, u32[]{:S(2)}, u32[]{:S(2)}) collective-permute-start(bf16[64,1024]{1,0:T(8,128)(2,1)S(1)} %compress.3), channel_id=1, source_target_pairs={{0,4},{1,5},{2,6},{3,7},{4,0},{5,1},{6,2},{7,3},{8,12},{9,13},{10,... | collective-permute-start | bytes 393224 | tf_op jit(solution)/shard_map/ppermute | solution.py:744
  36.2 1.6 %copy-done.7 = bf16[16,512,128]{2,1,0:T(8,128)(2,1)S(1)} copy-done((bf16[16,512,128]{2,1,0:T(8,128)(2,1)S(1)}, bf16[16,512,128]{2,1,0:T(8,128)(2,1)}, u32[]{:S(2)}) %copy-start.7) | copy-done | bytes 2097176
  38.8 4.0 %hold_matrix.6.refs_8_ = bf16[1024,4096]{1,0:T(8,128)(2,1)S(1)} custom-call(s32[3]{0:T(128)S(1)} %pad_add_fusion.1.place_ref, bf16[1024,4096]{1,0:T(8,128)(2,1)} %bitcast.34, bf16[1024,4096]{1,0:T(8,128)(2,1)} %collective-permute-done.2.other_ref.refs_5_.refs_1_), custom_call_target="tpu_custom_call" | custom-call | tf_op jit(solution)/shard_map/hold_matrix/pallas_call | solution.py:542
  43.7 1.3 collective-permute-start.3
  45.0 4.0 %hold_matrix.7.refs_9_ = bf16[4096,1024]{1,0:T(8,128)(2,1)S(1)} custom-call(s32[3]{0:T(128)S(1)} %pad_add_fusion.1.place_ref, bf16[4096,1024]{1,0:T(8,128)(2,1)} %bitcast.41, bf16[4096,1024]{1,0:T(8,128)(2,1)} %collective-permute-done.5.other_ref.refs_7_.refs_3_), custom_call_target="tpu_custom_call" | custom-call | tf_op jit(solution)/shard_map/hold_matrix/pallas_call | solution.py:542
  49.1 1.5 collective-permute-done.3.refs_1_
  50.5 9.1 %forward_stage.1 = (bf16[128,1024]{1,0:T(8,128)(2,1)S(1)}, bf16[2,4096,128]{2,1,0:T(8,128)(2,1)S(1)}, f32[2,128,1024]{2,1,0:T(8,128)S(1)}, f32[2,128,128]{2,1,0:...) custom-call(s32[3]{0:T(128)S(1)} %pad_add_fusion.1.place_ref, ...), custom_call_target="tpu_custom_call" | custom-call | flops 4294967296 | bytes 1048576 | tf_op jit(solution)/shard_map/forward_stage/pallas_call | solution.py:610
  59.7 1.3 collective-permute-start.6
  62.4 2.5 %collective-permute-done.6.acts_ref = bf16[128,1024]{1,0:T(8,128)(2,1)S(1)} collective-permute-done((bf16[128,1024]{1,0:T(8,128)(2,1)S(1)}, bf16[128,1024]{1,0:T(8,128)(2,1)S(1)}, u32[]{:S(2)}, u32[]{:S(2)}) %collective-permute-start.6) | collective-permute-done | bytes 262176 | tf_op jit(solution)/shard_map/ppermute | solution.py:739
  65.7 1.3 collective-permute-start.7
  67.0 4.0 %hold_matrix.11.refs_5_ = bf16[4096,1024]{1,0:T(8,128)(2,1)S(1)} custom-call(s32[3]{0:T(128)S(1)} %pad_add_fusion.1.place_ref, bf16[4096,1024]{1,0:T(8,128)(2,1)} %bitcast.45, bf16[4096,1024]{1,0:T(8,128)(2,1)} %collective-permute-done.5.other_ref.refs_7_.refs_3_), custom_call_target="tpu_custom_call" | custom-call | tf_op jit(solution)/shard_map/hold_matrix/pallas_call | solution.py:542
  71.1 4.0 %hold_matrix.10.refs_4_ = bf16[1024,4096]{1,0:T(8,128)(2,1)S(1)} custom-call(s32[3]{0:T(128)S(1)} %pad_add_fusion.1.place_ref, bf16[1024,4096]{1,0:T(8,128)(2,1)} %bitcast.38, bf16[1024,4096]{1,0:T(8,128)(2,1)} %collective-permute-done.2.other_ref.refs_5_.refs_1_), custom_call_target="tpu_custom_call" | custom-call | tf_op jit(solution)/shard_map/hold_matrix/pallas_call | solution.py:542
  75.1 15.7 %collective-permute-done.7.grad_ref = bf16[128,1024]{1,0:T(8,128)(2,1)S(1)} collective-permute-done((bf16[128,1024]{1,0:T(8,128)(2,1)S(1)}, bf16[128,1024]{1,0:T(8,128)(2,1)S(1)}, u32[]{:S(2)}, u32[]{:S(2)}) %collective-permute-start.7) | collective-permute-done | bytes 262176 | tf_op jit(solution)/shard_map/ppermute | solution.py:739
  90.8 13.6 %backward_stage.1 = bf16[128,1024]{1,0:T(8,128)(2,1)S(1)} custom-call(s32[3]{0:T(128)S(1)} %pad_add_fusion.1.place_ref, bf16[128,1024]{1,0:T(8,128)(2,1)S(1)} %collective-permute-done.7.grad_ref, bf16[2,4096,128]{2,1,0:T(8,128)(2,1)S(1)} %get-tuple-element.35.hid, f32[2,128,1024]{2,1,0:T(8,128)S(1)} %get-tuple-element.36.inter, ...), custom_call_target="tpu_custom_call" | custom-call | flops 4294967296 | bytes 1048576 | tf_op jit(solution)/shard_map/backward_stage/pallas_call | solution.py:715
  104.5 1.3 collective-permute-start.8
  105.8 2.5 %collective-permute-done.8 = bf16[64,1024]{1,0:T(8,128)(2,1)S(1)} collective-permute-done((bf16[64,1024]{1,0:T(8,128)(2,1)S(1)}, bf16[64,1024]{1,0:T(8,128)(2,1)S(1)}, u32[]{:S(2)}, u32[]{:S(2)}) %collective-permute-start.8) | collective-permute-done | bytes 131104 | tf_op jit(solution)/shard_map/ppermute | solution.py:739
  108.3 1.9 %collective-permute-start.9 = (bf16[64,1024]{1,0:T(8,128)(2,1)S(1)}, bf16[64,1024]{1,0:T(8,128)(2,1)S(1)}, u32[]{:S(2)}, u32[]{:S(2)}) collective-permute-start(bf16[64,1024]{1,0:T(8,128)(2,1)S(1)} %slice_select_fusion.grad_ref), channel_id=1, source_target_pairs={{0,4},{1,5},{2,6},{3,7},{4,0},{5,1},{6,2},{7,3},{8,12},{9,13},{10,... | collective-permute-start | bytes 393224 | tf_op jit(solution)/shard_map/ppermute | solution.py:744
  111.1 3.6 %collective-permute-done.9.grad_ref = bf16[64,1024]{1,0:T(8,128)(2,1)S(1)} collective-permute-done((bf16[64,1024]{1,0:T(8,128)(2,1)S(1)}, bf16[64,1024]{1,0:T(8,128)(2,1)S(1)}, u32[]{:S(2)}, u32[]{:S(2)}) %collective-permute-start.9) | collective-permute-done | bytes 131104 | tf_op jit(solution)/shard_map/ppermute | solution.py:744
  114.7 1.9 %expand.3 = bf16[16,2,128,128]{3,2,1,0:T(8,128)(2,1)} custom-call(bf16[16,512,128]{2,1,0:T(8,128)(2,1)S(1)} %copy-done.2, bf16[64,1024]{1,0:T(8,128)(2,1)S(1)} %collective-permute-done.9.grad_ref, bf16[16,128,128]{2,1,0:T(8,128)(2,1)S(1)} %expand.2.refs_0_), custom_call_target="tpu_custom_call" | custom-call | tf_op jit(solution)/shard_map/expand/pallas_call | solution.py:196
  116.6 6.9 %all-to-all-start.1 = ((bf16[16,2,128,128]{3,2,1,0:T(8,128)(2,1)}), bf16[16,2,128,128]{3,2,1,0:T(8,128)(2,1)S(1)}, u32[]{:S(2)}, u32[]{:S(2)}) async-start(bf16[16,2,128,128]{3,2,1,0:T(8,128)(2,1)} %expand.3), calls=%async_computation.1 | async-start | bytes 2097152 | tf_op jit(solution)/shard_map/all_to_all | solution.py:754
  125.2 13.1 %all-to-all-done.1 = bf16[16,2,128,128]{3,2,1,0:T(8,128)(2,1)S(1)} async-done(((bf16[16,2,128,128]{3,2,1,0:T(8,128)(2,1)}), bf16[16,2,128,128]{3,2,1,0:T(8,128)(2,1)S(1)}, u32[]{:S(2)}, u32[]{:S(2)}) %all-to-all-start.1) | async-done | bytes 1048608 | tf_op jit(solution)/shard_map/all_to_all | solution.py:754
  138.3 10.2 %add_rows.1 = f32[4096,128]{1,0:T(8,128)} custom-call(s32[4096]{0:T(1024)S(1)} %bitcast.32, bf16[4096,128]{1,0:T(8,128)(2,1)S(1)} %bitcast.27, bf16[4096,128]{1,0:T(8,128)(2,1)} %pick_rows.1.sent_ref), custom_call_target="tpu_custom_call" | custom-call | tf_op jit(solution)/shard_map/add_rows/pallas_call | solution.py:253
  (59 shorter events, 11.0 us)
Async XLA Ops:
  0.0 36.2 %copy-start = (bf16[1,4,64,1024]{3,2,1,0:T(8,128)(2,1)S(1)}, bf16[1,4,64,1024]{3,2,1,0:T(8,128)(2,1)}, u32[]{:S(2)}) copy-start(bf16[1,4,64,1024]{3,2,1,0:T(8,128)(2,1)} %param.16) | copy-start | bytes 1572868
  0.0 26.6 %copy-start.11 = (bf16[8,512]{1,0:T(8,128)(2,1)S(1)}, bf16[8,512]{1,0:T(8,128)(2,1)}, u32[]{:S(2)}) copy-start(bf16[8,512]{1,0:T(8,128)(2,1)} %lcb_ref.3) | copy-start | bytes 24580
  0.0 38.7 %collective-permute-start.2 = (bf16[1024,4096]{1,0:T(8,128)(2,1)}, bf16[1024,4096]{1,0:T(8,128)(2,1)}, u32[]{:S(2)}, u32[]{:S(2)}) collective-permute-start(bf16[1024,4096]{1,0:T(8,128)(2,1)} %bitcast.33), channel_id=1, source_target_pairs={{0,8},{8,0},{16,24},{24,16},{1,9},{9,1},{17,25},{25,17},{2,10},{10... | collective-permute-start | bytes 25165832 | tf_op jit(solution)/shard_map/ppermute | solution.py:734
  0.5 44.6 %collective-permute-start.5 = (bf16[4096,1024]{1,0:T(8,128)(2,1)}, bf16[4096,1024]{1,0:T(8,128)(2,1)}, u32[]{:S(2)}, u32[]{:S(2)}) collective-permute-start(bf16[4096,1024]{1,0:T(8,128)(2,1)} %bitcast.40), channel_id=1, source_target_pairs={{0,8},{8,0},{16,24},{24,16},{1,9},{9,1},{17,25},{25,17},{2,10},{10... | collective-permute-start | bytes 25165832 | tf_op jit(solution)/shard_map/ppermute | solution.py:734
  0.5 11.7 %collective-permute-start = (s32[64,512]{1,0:T(8,128)}, s32[64,512]{1,0:T(8,128)S(1)}, u32[]{:S(2)}, u32[]{:S(2)}) collective-permute-start(s32[64,512]{1,0:T(8,128)} %bitcast.47), channel_id=1, source_target_pairs={{0,4},{1,5},{2,6},{3,7},{4,0},{5,1},{6,2},{7,3},{8,12},{9,13},{10,... | collective-permute-start | bytes 393224 | tf_op jit(solution)/shard_map/ppermute | solution.py:744
  4.6 0.7 copy-start.8
  12.3 19.7 %all-to-all-start = ((bf16[16,2,128,128]{3,2,1,0:T(8,128)(2,1)}), bf16[16,2,128,128]{3,2,1,0:T(8,128)(2,1)S(1)}, u32[]{:S(2)}, u32[]{:S(2)}) async-start(bf16[16,2,128,128]{3,2,1,0:T(8,128)(2,1)} %bitcast.11), calls=%async_computation | async-start | bytes 2097152 | tf_op jit(solution)/shard_map/all_to_all | solution.py:754
  18.5 26.4 %collective-permute-start.4 = (bf16[16,128]{1,0:T(8,128)(2,1)S(1)}, bf16[16,128]{1,0:T(8,128)(2,1)S(1)}, u32[]{:S(2)}, u32[]{:S(2)}) collective-permute-start(bf16[16,128]{1,0:T(8,128)(2,1)S(1)} %pad_maximum_fusion.1), channel_id=1, source_target_pairs={{0,8},{8,0},{16,24},{24,16},{1,9},{9,1},{17,25},{25,17},{2,10},{10... | collective-permute-start | bytes 12296 | tf_op jit(solution)/shard_map/ppermute | solution.py:734
  20.2 0.7 copy-start.10
  24.9 1.3 copy-start.6
  30.5 1.3 copy-start.4
  32.0 1.6 %copy-start.5 = (bf16[16,512,128]{2,1,0:T(8,128)(2,1)S(1)}, bf16[16,512,128]{2,1,0:T(8,128)(2,1)}, u32[]{:S(2)}) copy-start(bf16[16,512,128]{2,1,0:T(8,128)(2,1)} %copy-done.4) | copy-start | bytes 6291460
  34.5 9.1 %collective-permute-start.1 = (bf16[64,1024]{1,0:T(8,128)(2,1)S(1)}, bf16[64,1024]{1,0:T(8,128)(2,1)S(1)}, u32[]{:S(2)}, u32[]{:S(2)}) collective-permute-start(bf16[64,1024]{1,0:T(8,128)(2,1)S(1)} %compress.3), channel_id=1, source_target_pairs={{0,4},{1,5},{2,6},{3,7},{4,0},{5,1},{6,2},{7,3},{8,12},{9,13},{10,... | collective-permute-start | bytes 393224 | tf_op jit(solution)/shard_map/ppermute | solution.py:744
  36.2 1.6 %copy-start.7 = (bf16[16,512,128]{2,1,0:T(8,128)(2,1)S(1)}, bf16[16,512,128]{2,1,0:T(8,128)(2,1)}, u32[]{:S(2)}) copy-start(bf16[16,512,128]{2,1,0:T(8,128)(2,1)} %copy-done.6) | copy-start | bytes 6291460
  38.7 6.2 %copy-start.12 = (bf16[1,8,128]{2,1,0:T(8,128)(2,1)S(1)}, bf16[1,8,128]{2,1,0:T(8,128)(2,1)}, u32[]{:S(2)}) copy-start(bf16[1,8,128]{2,1,0:T(8,128)(2,1)} %param.12) | copy-start | bytes 6148
  43.7 6.9 %collective-permute-start.3 = (bf16[64,1024]{1,0:T(8,128)(2,1)S(1)}, bf16[64,1024]{1,0:T(8,128)(2,1)S(1)}, u32[]{:S(2)}, u32[]{:S(2)}) collective-permute-start(bf16[64,1024]{1,0:T(8,128)(2,1)S(1)} %add_convert_fusion.refs_0_), channel_id=1, source_target_pairs={{16,0},{24,8},{17,1},{25,9},{18,2},{26,10},{19,3},{27,11},{20,4},{... | collective-permute-start | bytes 393224 | tf_op jit(solution)/shard_map/ppermute | solution.py:739
  59.7 5.2 %collective-permute-start.6 = (bf16[128,1024]{1,0:T(8,128)(2,1)S(1)}, bf16[128,1024]{1,0:T(8,128)(2,1)S(1)}, u32[]{:S(2)}, u32[]{:S(2)}) collective-permute-start(bf16[128,1024]{1,0:T(8,128)(2,1)S(1)} %get-tuple-element.32), channel_id=1, source_target_pairs={{0,16},{8,24},{1,17},{9,25},{2,18},{10,26},{3,19},{11,27},{4,20},{... | collective-permute-start | bytes 786440 | tf_op jit(solution)/shard_map/ppermute | solution.py:739
  65.7 25.1 %collective-permute-start.7 = (bf16[128,1024]{1,0:T(8,128)(2,1)S(1)}, bf16[128,1024]{1,0:T(8,128)(2,1)S(1)}, u32[]{:S(2)}, u32[]{:S(2)}) collective-permute-start(bf16[128,1024]{1,0:T(8,128)(2,1)S(1)} %turn_stage.1), channel_id=1, source_target_pairs={{16,0},{24,8},{17,1},{25,9},{18,2},{26,10},{19,3},{27,11},{20,4},{... | collective-permute-start | bytes 786440 | tf_op jit(solution)/shard_map/ppermute | solution.py:739
  90.8 19.3 %copy-start.3 = (bf16[16,512,128]{2,1,0:T(8,128)(2,1)S(1)}, bf16[16,512,128]{2,1,0:T(8,128)(2,1)}, u32[]{:S(2)}) copy-start(bf16[16,512,128]{2,1,0:T(8,128)(2,1)} %get-tuple-element.40.spread_ref) | copy-start | bytes 6291460
  90.8 23.9 %copy-start.2 = (bf16[16,512,128]{2,1,0:T(8,128)(2,1)S(1)}, bf16[16,512,128]{2,1,0:T(8,128)(2,1)}, u32[]{:S(2)}) copy-start(bf16[16,512,128]{2,1,0:T(8,128)(2,1)} %get-tuple-element.23.spread_ref) | copy-start | bytes 6291460
  90.8 57.7 %copy-start.1 = (bf16[1,4,64,1024]{3,2,1,0:T(8,128)(2,1)S(1)}, bf16[1,4,64,1024]{3,2,1,0:T(8,128)(2,1)}, u32[]{:S(2)}) copy-start(bf16[1,4,64,1024]{3,2,1,0:T(8,128)(2,1)} %param.16) | copy-start | bytes 1572868
  104.4 19.7 %copy-start.13 = (s32[1,32]{1,0:T(1,128)S(1)}, s32[1,32]{1,0:T(1,128)}, u32[]{:S(2)}) copy-start(s32[1,32]{1,0:T(1,128)} %param.19) | copy-start | bytes 388
  104.4 20.7 %copy-start.9 = (s32[1,32,128]{2,1,0:T(8,128)S(1)}, s32[1,32,128]{2,1,0:T(8,128)}, u32[]{:S(2)}) copy-start(s32[1,32,128]{2,1,0:T(8,128)} %param.18) | copy-start | bytes 49156
  104.5 3.8 %collective-permute-start.8 = (bf16[64,1024]{1,0:T(8,128)(2,1)S(1)}, bf16[64,1024]{1,0:T(8,128)(2,1)S(1)}, u32[]{:S(2)}, u32[]{:S(2)}) collective-permute-start(bf16[64,1024]{1,0:T(8,128)(2,1)S(1)} %slice.8), channel_id=1, source_target_pairs={{0,16},{8,24},{1,17},{9,25},{2,18},{10,26},{3,19},{11,27},{4,20},{... | collective-permute-start | bytes 393224 | tf_op jit(solution)/shard_map/ppermute | solution.py:739
  108.3 6.4 %collective-permute-start.9 = (bf16[64,1024]{1,0:T(8,128)(2,1)S(1)}, bf16[64,1024]{1,0:T(8,128)(2,1)S(1)}, u32[]{:S(2)}, u32[]{:S(2)}) collective-permute-start(bf16[64,1024]{1,0:T(8,128)(2,1)S(1)} %slice_select_fusion.grad_ref), channel_id=1, source_target_pairs={{0,4},{1,5},{2,6},{3,7},{4,0},{5,1},{6,2},{7,3},{8,12},{9,13},{10,... | collective-permute-start | bytes 393224 | tf_op jit(solution)/shard_map/ppermute | solution.py:744
  116.6 21.7 %all-to-all-start.1 = ((bf16[16,2,128,128]{3,2,1,0:T(8,128)(2,1)}), bf16[16,2,128,128]{3,2,1,0:T(8,128)(2,1)S(1)}, u32[]{:S(2)}, u32[]{:S(2)}) async-start(bf16[16,2,128,128]{3,2,1,0:T(8,128)(2,1)} %expand.3), calls=%async_computation.1 | async-start | bytes 2097152 | tf_op jit(solution)/shard_map/all_to_all | solution.py:754

commit v14 on v13

--- a/solution.py
+++ b/solution.py
@@ -400,7 +400,8 @@
     def work(columns):
         opened = jnp.maximum(dot(normed[...], w_up[:, columns]), 0.0).astype(jnp.bfloat16)
         hidden[:, columns] = opened
-        turned[columns, :] = opened.T
+        if turned is not None:
+            turned[columns, :] = opened.T
 
     width = hidden.shape[1]
     over_tiles(width, hidden_tile(width), many, wait, work)
@@ -474,7 +475,7 @@
 
 def saved_shapes(batch, model_width, hidden_width, width):
     return [
-        jax.ShapeDtypeStruct((2, hidden_width, batch), jnp.bfloat16),
+        jax.ShapeDtypeStruct((2, batch, hidden_width), jnp.bfloat16),
         jax.ShapeDtypeStruct((2, batch, model_width), jnp.float32),
         jax.ShapeDtypeStruct((2, batch, width), jnp.float32),
         jax.ShapeDtypeStruct((2, batch, model_width), jnp.bfloat16),
@@ -578,7 +579,7 @@
         piece_refs, (top_ref, small_ref), refs = refs[: len(pieces)], refs[len(pieces) :][:2], refs[len(pieces) + 2 :]
         matrices, refs = refs[:6], refs[6:]
         out_ref, hid, inter, scale, kept, g_hidden = refs[:6]
-        held, (normed, hidden, top_turned, grams) = refs[6:9], refs[9:]
+        held, (normed, top_turned, grams) = refs[6:9], refs[9:]
         core = place_ref[0]
 
         @pl.when(place_ref[1] == 1)
@@ -595,9 +596,9 @@
                 mix_forward(
                     small_ref, layer, kept.at[layer], inter.at[layer], scale.at[layer], normed, grams, count
                 )
-                up_product(normed, up.held, hidden, hid.at[layer], up.wait)
+                up_product(normed, up.held, hid.at[layer], None, up.wait)
                 to = kept.at[1] if layer == 0 else out_ref
-                down_product(hidden, down.held, kept.at[layer], to, down.wait)
+                down_product(hid.at[layer], down.held, kept.at[layer], to, down.wait)
 
         @pl.when(place_ref[2] == 1)
         def _():
@@ -617,7 +618,6 @@
         scratch_shapes=weight_scratch(model_width, hidden_width)
         + [
             pltpu.VMEM((batch, model_width), jnp.bfloat16),
-            pltpu.VMEM((batch, hidden_width), jnp.bfloat16),
             pltpu.VMEM((model_width, batch), jnp.bfloat16),
             gram_scratch(batch, count),
         ],
@@ -626,6 +626,31 @@
         name="forward_stage",
     )(place, *pieces, top, weights[0], *map(in_hbm, weights[1:]), *ready)
     return out[0], out[1:5], out[5]
+
+
+def turn_hidden(active, hidden):
+    layers, batch, hidden_width = hidden.shape
+
+    def kernel(active_ref, hidden_ref, out_ref):
+        @pl.when(active_ref[0] == 1)
+        def _():
+            tile = hidden_tile(hidden_width)
+
+            def body(step, carry):
+                for layer in range(layers):
+                    out_ref[layer, tile_at(step, tile), :] = hidden_ref[layer, :, tile_at(step, tile)].T
+                return carry
+
+            lax.fori_loop(0, hidden_width // tile, body, 0)
+
+    return pl.pallas_call(
+        kernel,
+        out_shape=jax.ShapeDtypeStruct((layers, hidden_width, batch), hidden.dtype),
+        in_specs=[whole(pltpu.SMEM), whole()],
+        out_specs=whole(),
+        compiler_params=pltpu.CompilerParams(vmem_limit_bytes=8 * 1024 * 1024),
+        name="turn_hidden",
+    )(active, hidden)
 
 
 def turn_stage(place, acts, top, g_hidden, weights, ready, count):
@@ -848,6 +873,8 @@
     place = at(stages - 1)
     ready = hold_layer(place, 0, weights, out)
     grad = turn_stage(place, pieces[0], top, g_hidden, weights, ready, embed_count)
+    was_forward = (stage < stages - 1).astype(jnp.int32).reshape(1)
+    saved = [turn_hidden(after(was_forward, grad), saved[0])] + list(saved[1:])
     for tick in reversed(range(stages - 1)):
         place = at(tick)
         ready = hold_layer(place, 1, weights, grad)

time: 149 us -> 150 us (level)
    unnamed x29 -> x33, local copies, waits for them, and re-layouts: 7.81 us -> 7.8 us
where the time goes in v14:
time: 150 us; the launch traced here: 149 us
  Pallas kernels  71.5 us (48%)
  waiting for transfers between devices  39.5 us (26%)
  starting transfers between devices  25.3 us (17%)
  local copies, waits for them, and re-layouts  8.19 us (5%)
  other arithmetic  3.98 us (3%)
    ppermute x4, waiting for transfers between devices, moved(): return lax.ppermute(value, 'section', pairs)  21.7 us
    pallas_call x6, Pallas kernels, hold_matrix(): pl.pallas_call(kernel, out_shape=pltpu.VMEM(own.shape, own.dtype), in_spe...  17.4 us
    pallas_call x1, Pallas kernels, backward_stage(): pl.pallas_call(kernel, out_shape=jax.ShapeDtypeStruct(grad.shape, jnp.bfl...  13.6 us
    all_to_all x2, waiting for transfers between devices, swap_in_half(): lax.all_to_all(value, TABLE_AXES, split_axis=0, concat_axis=0, axis_index...  13.3 us
    all_to_all x2, starting transfers between devices, swap_in_half(): lax.all_to_all(value, TABLE_AXES, split_axis=0, concat_axis=0, axis_index...  11.7 us
    pallas_call x1, Pallas kernels, add_rows(): pl.pallas_call(kernel, out_shape=jax.ShapeDtypeStruct((rows, width), jnp....  10.2 us
    pallas_call x1, Pallas kernels, forward_stage(): pl.pallas_call(kernel, out_shape=[jax.ShapeDtypeStruct(top.shape, jnp.bfl...  8.51 us
    pallas_call x2, Pallas kernels, spread_weights(): pl.pallas_call(kernel, out_shape=[pltpu.VMEM((owners, samples * embed_cou...  7.9 us
  transfers between devices with their start and end apart: 12, of which 8 were waited for; matrix products, arithmetic and copies ran while one was open for 3% of the time, Pallas kernels for 24%

profile of v14, /device:TPU:0, one launch (start us, length us, event | category | flops | bytes accessed | tf_op | source)
XLA Modules:
  0.0 149.0 jit_solution(14570714126319998304)
XLA Ops:
  0.5 4.0 %collective-permute-start = (s32[64,512]{1,0:T(8,128)}, s32[64,512]{1,0:T(8,128)S(1)}, u32[]{:S(2)}, u32[]{:S(2)}) collective-permute-start(s32[64,512]{1,0:T(8,128)} %bitcast.48), channel_id=1, source_target_pairs={{0,4},{1,5},{2,6},{3,7},{4,0},{5,1},{6,2},{7,3},{8,12},{9,13},{10,... | collective-permute-start | bytes 393224 | tf_op jit(solution)/shard_map/ppermute | solution.py:769
  5.3 7.0 %pick_rows.1.sent_ref = bf16[4096,128]{1,0:T(8,128)(2,1)} custom-call(s32[1]{0:T(128)} %bitcast.9.half_ref, s32[4096]{0:T(1024)S(1)} %bitcast.31, bf16[4096,128]{1,0:T(8,128)(2,1)} %table_ref.1), custom_call_target="tpu_custom_call" | custom-call | tf_op jit(solution)/shard_map/pick_rows/pallas_call | solution.py:67
  12.3 4.9 %all-to-all-start = ((bf16[16,2,128,128]{3,2,1,0:T(8,128)(2,1)}), bf16[16,2,128,128]{3,2,1,0:T(8,128)(2,1)S(1)}, u32[]{:S(2)}, u32[]{:S(2)}) async-start(bf16[16,2,128,128]{3,2,1,0:T(8,128)(2,1)} %bitcast.11), calls=%async_computation | async-start | bytes 2097152 | tf_op jit(solution)/shard_map/all_to_all | solution.py:779
  18.9 1.3 fusion.11.codes_ref
  20.9 4.0 %spread_weights.3 = (bf16[16,512,128]{2,1,0:T(8,128)(2,1)S(1)}, bf16[16,512,128]{2,1,0:T(8,128)(2,1)}) custom-call(s32[64,512]{1,0:T(8,128)S(1)} %fusion.11.codes_ref, bf16[8,512]{1,0:T(8,128)(2,1)S(1)} %copy-done.12), custom_call_target="tpu_custom_call" | custom-call | flops 1073741824 | bytes 2097152 | tf_op jit(solution)/shard_map/spread_weights/pallas_call | solution.py:110
  24.9 1.3 copy-done.6
  26.6 3.9 %spread_weights.2 = (bf16[16,512,128]{2,1,0:T(8,128)(2,1)S(1)}, bf16[16,512,128]{2,1,0:T(8,128)(2,1)}) custom-call(s32[64,512]{1,0:T(8,128)S(1)} %fusion.5.codes_ref, bf16[8,512]{1,0:T(8,128)(2,1)S(1)} %copy-done.13), custom_call_target="tpu_custom_call" | custom-call | flops 1073741824 | bytes 2097152 | tf_op jit(solution)/shard_map/spread_weights/pallas_call | solution.py:110
  30.5 1.3 copy-done.4
  32.0 1.6 %copy-done.5 = bf16[16,512,128]{2,1,0:T(8,128)(2,1)S(1)} copy-done((bf16[16,512,128]{2,1,0:T(8,128)(2,1)S(1)}, bf16[16,512,128]{2,1,0:T(8,128)(2,1)}, u32[]{:S(2)}) %copy-start.5) | copy-done | bytes 2097176
  34.5 1.6 %collective-permute-start.1 = (bf16[64,1024]{1,0:T(8,128)(2,1)S(1)}, bf16[64,1024]{1,0:T(8,128)(2,1)S(1)}, u32[]{:S(2)}, u32[]{:S(2)}) collective-permute-start(bf16[64,1024]{1,0:T(8,128)(2,1)S(1)} %compress.3), channel_id=1, source_target_pairs={{0,4},{1,5},{2,6},{3,7},{4,0},{5,1},{6,2},{7,3},{8,12},{9,13},{10,... | collective-permute-start | bytes 393224 | tf_op jit(solution)/shard_map/ppermute | solution.py:769
  36.2 1.6 %copy-done.7 = bf16[16,512,128]{2,1,0:T(8,128)(2,1)S(1)} copy-done((bf16[16,512,128]{2,1,0:T(8,128)(2,1)S(1)}, bf16[16,512,128]{2,1,0:T(8,128)(2,1)}, u32[]{:S(2)}) %copy-start.7) | copy-done | bytes 2097176
  38.8 4.0 %hold_matrix.6.refs_8_ = bf16[1024,4096]{1,0:T(8,128)(2,1)S(1)} custom-call(s32[3]{0:T(128)S(1)} %pad_add_fusion.1.place_ref, bf16[1024,4096]{1,0:T(8,128)(2,1)} %bitcast.35, bf16[1024,4096]{1,0:T(8,128)(2,1)} %collective-permute-done.2.other_ref.refs_5_.refs_1_), custom_call_target="tpu_custom_call" | custom-call | tf_op jit(solution)/shard_map/hold_matrix/pallas_call | solution.py:543
  43.7 1.3 collective-permute-start.3
  45.0 4.0 %hold_matrix.7.refs_9_ = bf16[4096,1024]{1,0:T(8,128)(2,1)S(1)} custom-call(s32[3]{0:T(128)S(1)} %pad_add_fusion.1.place_ref, bf16[4096,1024]{1,0:T(8,128)(2,1)} %bitcast.42, bf16[4096,1024]{1,0:T(8,128)(2,1)} %collective-permute-done.5.other_ref.refs_7_.refs_3_), custom_call_target="tpu_custom_call" | custom-call | tf_op jit(solution)/shard_map/hold_matrix/pallas_call | solution.py:543
  49.1 1.5 collective-permute-done.3.refs_1_
  50.6 8.5 %forward_stage.1 = (bf16[128,1024]{1,0:T(8,128)(2,1)S(1)}, bf16[2,128,4096]{2,1,0:T(8,128)(2,1)S(1)}, f32[2,128,1024]{2,1,0:T(8,128)S(1)}, f32[2,128,128]{2,1,0:...) custom-call(s32[3]{0:T(128)S(1)} %pad_add_fusion.1.place_ref, ...), custom_call_target="tpu_custom_call" | custom-call | flops 4294967296 | bytes 1048576 | tf_op jit(solution)/shard_map/forward_stage/pallas_call | solution.py:611
  59.1 1.3 collective-permute-start.6
  61.8 2.6 %collective-permute-done.6.acts_ref = bf16[128,1024]{1,0:T(8,128)(2,1)S(1)} collective-permute-done((bf16[128,1024]{1,0:T(8,128)(2,1)S(1)}, bf16[128,1024]{1,0:T(8,128)(2,1)S(1)}, u32[]{:S(2)}, u32[]{:S(2)}) %collective-permute-start.6) | collective-permute-done | bytes 262176 | tf_op jit(solution)/shard_map/ppermute | solution.py:764
  64.4 1.5 %turn_stage.1 = bf16[128,1024]{1,0:T(8,128)(2,1)} custom-call(s32[3]{0:T(128)S(1)} %pad_add_fusion.2.place_ref, bf16[128,1024]{1,0:T(8,128)(2,1)S(1)} %collective-permute-done.6.acts_ref, bf16[128,1024]{1,0:T(8,128)(2,1)S(1)} %bitcast.30, bf16[4096,128]{1,0:T(8,128)(2,1)S(1)} %get-tuple-element.34.ghid_ref, ...), custom_call_target="tpu_custom_call" | custom-call | flops 6442450944 | bytes 1048576 | tf_op jit(solution)/shard_map/turn_stage/pallas_call | solution.py:690
  65.9 1.3 collective-permute-start.7
  68.0 4.0 %hold_matrix.11.refs_5_ = bf16[4096,1024]{1,0:T(8,128)(2,1)S(1)} custom-call(s32[3]{0:T(128)S(1)} %pad_add_fusion.1.place_ref, bf16[4096,1024]{1,0:T(8,128)(2,1)} %bitcast.46, bf16[4096,1024]{1,0:T(8,128)(2,1)} %collective-permute-done.5.other_ref.refs_7_.refs_3_), custom_call_target="tpu_custom_call" | custom-call | tf_op jit(solution)/shard_map/hold_matrix/pallas_call | solution.py:543
  72.0 4.0 %hold_matrix.10.refs_4_ = bf16[1024,4096]{1,0:T(8,128)(2,1)S(1)} custom-call(s32[3]{0:T(128)S(1)} %pad_add_fusion.1.place_ref, bf16[1024,4096]{1,0:T(8,128)(2,1)} %bitcast.39, bf16[1024,4096]{1,0:T(8,128)(2,1)} %collective-permute-done.2.other_ref.refs_5_.refs_1_), custom_call_target="tpu_custom_call" | custom-call | tf_op jit(solution)/shard_map/hold_matrix/pallas_call | solution.py:543
  76.1 15.1 %collective-permute-done.7.grad_ref = bf16[128,1024]{1,0:T(8,128)(2,1)S(1)} collective-permute-done((bf16[128,1024]{1,0:T(8,128)(2,1)}, bf16[128,1024]{1,0:T(8,128)(2,1)S(1)}, u32[]{:S(2)}, u32[]{:S(2)}) %collective-permute-start.7) | collective-permute-done | bytes 262176 | tf_op jit(solution)/shard_map/ppermute | solution.py:764
  91.2 13.6 %backward_stage.1 = bf16[128,1024]{1,0:T(8,128)(2,1)S(1)} custom-call(s32[3]{0:T(128)S(1)} %pad_add_fusion.1.place_ref, bf16[128,1024]{1,0:T(8,128)(2,1)S(1)} %collective-permute-done.7.grad_ref, bf16[2,4096,128]{2,1,0:T(8,128)(2,1)S(1)} %turn_hidden.1.hid, f32[2,128,1024]{2,1,0:T(8,128)S(1)} %get-tuple-element.38.inter, ...), custom_call_target="tpu_custom_call" | custom-call | flops 4294967296 | bytes 1048576 | tf_op jit(solution)/shard_map/backward_stage/pallas_call | solution.py:740
  104.8 1.3 collective-permute-start.8
  106.1 2.5 %collective-permute-done.8 = bf16[64,1024]{1,0:T(8,128)(2,1)S(1)} collective-permute-done((bf16[64,1024]{1,0:T(8,128)(2,1)S(1)}, bf16[64,1024]{1,0:T(8,128)(2,1)S(1)}, u32[]{:S(2)}, u32[]{:S(2)}) %collective-permute-start.8) | collective-permute-done | bytes 131104 | tf_op jit(solution)/shard_map/ppermute | solution.py:764
  108.7 1.9 %collective-permute-start.9 = (bf16[64,1024]{1,0:T(8,128)(2,1)S(1)}, bf16[64,1024]{1,0:T(8,128)(2,1)S(1)}, u32[]{:S(2)}, u32[]{:S(2)}) collective-permute-start(bf16[64,1024]{1,0:T(8,128)(2,1)S(1)} %slice_select_fusion.grad_ref), channel_id=1, source_target_pairs={{0,4},{1,5},{2,6},{3,7},{4,0},{5,1},{6,2},{7,3},{8,12},{9,13},{10,... | collective-permute-start | bytes 393224 | tf_op jit(solution)/shard_map/ppermute | solution.py:769
  111.5 3.6 %collective-permute-done.9.grad_ref = bf16[64,1024]{1,0:T(8,128)(2,1)S(1)} collective-permute-done((bf16[64,1024]{1,0:T(8,128)(2,1)S(1)}, bf16[64,1024]{1,0:T(8,128)(2,1)S(1)}, u32[]{:S(2)}, u32[]{:S(2)}) %collective-permute-start.9) | collective-permute-done | bytes 131104 | tf_op jit(solution)/shard_map/ppermute | solution.py:769
  115.1 1.9 %expand.3 = bf16[16,2,128,128]{3,2,1,0:T(8,128)(2,1)} custom-call(bf16[16,512,128]{2,1,0:T(8,128)(2,1)S(1)} %copy-done.2, bf16[64,1024]{1,0:T(8,128)(2,1)S(1)} %collective-permute-done.9.grad_ref, bf16[16,128,128]{2,1,0:T(8,128)(2,1)S(1)} %expand.2.refs_0_), custom_call_target="tpu_custom_call" | custom-call | tf_op jit(solution)/shard_map/expand/pallas_call | solution.py:196
  117.0 6.8 %all-to-all-start.1 = ((bf16[16,2,128,128]{3,2,1,0:T(8,128)(2,1)}), bf16[16,2,128,128]{3,2,1,0:T(8,128)(2,1)S(1)}, u32[]{:S(2)}, u32[]{:S(2)}) async-start(bf16[16,2,128,128]{3,2,1,0:T(8,128)(2,1)} %expand.3), calls=%async_computation.1 | async-start | bytes 2097152 | tf_op jit(solution)/shard_map/all_to_all | solution.py:779
  125.5 13.1 %all-to-all-done.1 = bf16[16,2,128,128]{3,2,1,0:T(8,128)(2,1)S(1)} async-done(((bf16[16,2,128,128]{3,2,1,0:T(8,128)(2,1)}), bf16[16,2,128,128]{3,2,1,0:T(8,128)(2,1)S(1)}, u32[]{:S(2)}, u32[]{:S(2)}) %all-to-all-start.1) | async-done | bytes 1048608 | tf_op jit(solution)/shard_map/all_to_all | solution.py:779
  138.7 10.2 %add_rows.1 = f32[4096,128]{1,0:T(8,128)} custom-call(s32[4096]{0:T(1024)S(1)} %bitcast.33, bf16[4096,128]{1,0:T(8,128)(2,1)S(1)} %bitcast.28, bf16[4096,128]{1,0:T(8,128)(2,1)} %pick_rows.1.sent_ref), custom_call_target="tpu_custom_call" | custom-call | tf_op jit(solution)/shard_map/add_rows/pallas_call | solution.py:253
  (64 shorter events, 11.9 us)
Async XLA Ops:
  0.0 36.2 %copy-start = (bf16[1,4,64,1024]{3,2,1,0:T(8,128)(2,1)S(1)}, bf16[1,4,64,1024]{3,2,1,0:T(8,128)(2,1)}, u32[]{:S(2)}) copy-start(bf16[1,4,64,1024]{3,2,1,0:T(8,128)(2,1)} %param.16) | copy-start | bytes 1572868
  0.0 26.6 %copy-start.13 = (bf16[8,512]{1,0:T(8,128)(2,1)S(1)}, bf16[8,512]{1,0:T(8,128)(2,1)}, u32[]{:S(2)}) copy-start(bf16[8,512]{1,0:T(8,128)(2,1)} %lcb_ref.3) | copy-start | bytes 24580
  0.0 38.7 %collective-permute-start.2 = (bf16[1024,4096]{1,0:T(8,128)(2,1)}, bf16[1024,4096]{1,0:T(8,128)(2,1)}, u32[]{:S(2)}, u32[]{:S(2)}) collective-permute-start(bf16[1024,4096]{1,0:T(8,128)(2,1)} %bitcast.34), channel_id=1, source_target_pairs={{0,8},{8,0},{16,24},{24,16},{1,9},{9,1},{17,25},{25,17},{2,10},{10... | collective-permute-start | bytes 25165832 | tf_op jit(solution)/shard_map/ppermute | solution.py:759
  0.5 44.6 %collective-permute-start.5 = (bf16[4096,1024]{1,0:T(8,128)(2,1)}, bf16[4096,1024]{1,0:T(8,128)(2,1)}, u32[]{:S(2)}, u32[]{:S(2)}) collective-permute-start(bf16[4096,1024]{1,0:T(8,128)(2,1)} %bitcast.41), channel_id=1, source_target_pairs={{0,8},{8,0},{16,24},{24,16},{1,9},{9,1},{17,25},{25,17},{2,10},{10... | collective-permute-start | bytes 25165832 | tf_op jit(solution)/shard_map/ppermute | solution.py:759
  0.5 11.7 %collective-permute-start = (s32[64,512]{1,0:T(8,128)}, s32[64,512]{1,0:T(8,128)S(1)}, u32[]{:S(2)}, u32[]{:S(2)}) collective-permute-start(s32[64,512]{1,0:T(8,128)} %bitcast.48), channel_id=1, source_target_pairs={{0,4},{1,5},{2,6},{3,7},{4,0},{5,1},{6,2},{7,3},{8,12},{9,13},{10,... | collective-permute-start | bytes 393224 | tf_op jit(solution)/shard_map/ppermute | solution.py:769
  4.6 0.7 copy-start.10
  12.3 19.7 %all-to-all-start = ((bf16[16,2,128,128]{3,2,1,0:T(8,128)(2,1)}), bf16[16,2,128,128]{3,2,1,0:T(8,128)(2,1)S(1)}, u32[]{:S(2)}, u32[]{:S(2)}) async-start(bf16[16,2,128,128]{3,2,1,0:T(8,128)(2,1)} %bitcast.11), calls=%async_computation | async-start | bytes 2097152 | tf_op jit(solution)/shard_map/all_to_all | solution.py:779
  18.5 26.5 %collective-permute-start.4 = (bf16[16,128]{1,0:T(8,128)(2,1)S(1)}, bf16[16,128]{1,0:T(8,128)(2,1)S(1)}, u32[]{:S(2)}, u32[]{:S(2)}) collective-permute-start(bf16[16,128]{1,0:T(8,128)(2,1)S(1)} %pad_maximum_fusion.1), channel_id=1, source_target_pairs={{0,8},{8,0},{16,24},{24,16},{1,9},{9,1},{17,25},{25,17},{2,10},{10... | collective-permute-start | bytes 12296 | tf_op jit(solution)/shard_map/ppermute | solution.py:759
  20.2 0.7 copy-start.12
  24.9 1.3 copy-start.6
  30.5 1.3 copy-start.4
  31.9 1.6 %copy-start.5 = (bf16[16,512,128]{2,1,0:T(8,128)(2,1)S(1)}, bf16[16,512,128]{2,1,0:T(8,128)(2,1)}, u32[]{:S(2)}) copy-start(bf16[16,512,128]{2,1,0:T(8,128)(2,1)} %copy-done.4) | copy-start | bytes 6291460
  34.5 9.2 %collective-permute-start.1 = (bf16[64,1024]{1,0:T(8,128)(2,1)S(1)}, bf16[64,1024]{1,0:T(8,128)(2,1)S(1)}, u32[]{:S(2)}, u32[]{:S(2)}) collective-permute-start(bf16[64,1024]{1,0:T(8,128)(2,1)S(1)} %compress.3), channel_id=1, source_target_pairs={{0,4},{1,5},{2,6},{3,7},{4,0},{5,1},{6,2},{7,3},{8,12},{9,13},{10,... | collective-permute-start | bytes 393224 | tf_op jit(solution)/shard_map/ppermute | solution.py:769
  36.2 1.6 %copy-start.7 = (bf16[16,512,128]{2,1,0:T(8,128)(2,1)S(1)}, bf16[16,512,128]{2,1,0:T(8,128)(2,1)}, u32[]{:S(2)}) copy-start(bf16[16,512,128]{2,1,0:T(8,128)(2,1)} %copy-done.6) | copy-start | bytes 6291460
  38.7 6.3 %copy-start.14 = (bf16[1,8,128]{2,1,0:T(8,128)(2,1)S(1)}, bf16[1,8,128]{2,1,0:T(8,128)(2,1)}, u32[]{:S(2)}) copy-start(bf16[1,8,128]{2,1,0:T(8,128)(2,1)} %param.12) | copy-start | bytes 6148
  43.7 6.9 %collective-permute-start.3 = (bf16[64,1024]{1,0:T(8,128)(2,1)S(1)}, bf16[64,1024]{1,0:T(8,128)(2,1)S(1)}, u32[]{:S(2)}, u32[]{:S(2)}) collective-permute-start(bf16[64,1024]{1,0:T(8,128)(2,1)S(1)} %add_convert_fusion.refs_0_), channel_id=1, source_target_pairs={{16,0},{24,8},{17,1},{25,9},{18,2},{26,10},{19,3},{27,11},{20,4},{... | collective-permute-start | bytes 393224 | tf_op jit(solution)/shard_map/ppermute | solution.py:764
  59.1 2.1 %copy-start.8 = (bf16[2,128,1024]{2,1,0:T(8,128)(2,1)}, bf16[2,128,1024]{2,1,0:T(8,128)(2,1)S(1)}, u32[]{:S(2)}) copy-start(bf16[2,128,1024]{2,1,0:T(8,128)(2,1)S(1)} %get-tuple-element.40.kept) | copy-start | bytes 1572868
  59.1 5.3 %collective-permute-start.6 = (bf16[128,1024]{1,0:T(8,128)(2,1)S(1)}, bf16[128,1024]{1,0:T(8,128)(2,1)S(1)}, u32[]{:S(2)}, u32[]{:S(2)}) collective-permute-start(bf16[128,1024]{1,0:T(8,128)(2,1)S(1)} %get-tuple-element.33), channel_id=1, source_target_pairs={{0,16},{8,24},{1,17},{9,25},{2,18},{10,26},{3,19},{11,27},{4,20},{... | collective-permute-start | bytes 786440 | tf_op jit(solution)/shard_map/ppermute | solution.py:764
  65.9 25.3 %collective-permute-start.7 = (bf16[128,1024]{1,0:T(8,128)(2,1)}, bf16[128,1024]{1,0:T(8,128)(2,1)S(1)}, u32[]{:S(2)}, u32[]{:S(2)}) collective-permute-start(bf16[128,1024]{1,0:T(8,128)(2,1)} %turn_stage.1), channel_id=1, source_target_pairs={{16,0},{24,8},{17,1},{25,9},{18,2},{26,10},{19,3},{27,11},{20,4},{... | collective-permute-start | bytes 786440 | tf_op jit(solution)/shard_map/ppermute | solution.py:764
  72.0 19.2 %copy-start.9 = (bf16[2,128,1024]{2,1,0:T(8,128)(2,1)S(1)}, bf16[2,128,1024]{2,1,0:T(8,128)(2,1)}, u32[]{:S(2)}) copy-start(bf16[2,128,1024]{2,1,0:T(8,128)(2,1)} %copy-done.8) | copy-start | bytes 1572868
  91.2 19.3 %copy-start.3 = (bf16[16,512,128]{2,1,0:T(8,128)(2,1)S(1)}, bf16[16,512,128]{2,1,0:T(8,128)(2,1)}, u32[]{:S(2)}) copy-start(bf16[16,512,128]{2,1,0:T(8,128)(2,1)} %get-tuple-element.42.spread_ref) | copy-start | bytes 6291460
  91.2 23.9 %copy-start.2 = (bf16[16,512,128]{2,1,0:T(8,128)(2,1)S(1)}, bf16[16,512,128]{2,1,0:T(8,128)(2,1)}, u32[]{:S(2)}) copy-start(bf16[16,512,128]{2,1,0:T(8,128)(2,1)} %get-tuple-element.24.spread_ref) | copy-start | bytes 6291460
  91.2 57.6 %copy-start.1 = (bf16[1,4,64,1024]{3,2,1,0:T(8,128)(2,1)S(1)}, bf16[1,4,64,1024]{3,2,1,0:T(8,128)(2,1)}, u32[]{:S(2)}) copy-start(bf16[1,4,64,1024]{3,2,1,0:T(8,128)(2,1)} %param.16) | copy-start | bytes 1572868
  104.8 19.6 %copy-start.15 = (s32[1,32]{1,0:T(1,128)S(1)}, s32[1,32]{1,0:T(1,128)}, u32[]{:S(2)}) copy-start(s32[1,32]{1,0:T(1,128)} %param.19) | copy-start | bytes 388
  104.8 20.6 %copy-start.11 = (s32[1,32,128]{2,1,0:T(8,128)S(1)}, s32[1,32,128]{2,1,0:T(8,128)}, u32[]{:S(2)}) copy-start(s32[1,32,128]{2,1,0:T(8,128)} %param.18) | copy-start | bytes 49156
  104.8 3.8 %collective-permute-start.8 = (bf16[64,1024]{1,0:T(8,128)(2,1)S(1)}, bf16[64,1024]{1,0:T(8,128)(2,1)S(1)}, u32[]{:S(2)}, u32[]{:S(2)}) collective-permute-start(bf16[64,1024]{1,0:T(8,128)(2,1)S(1)} %slice.8), channel_id=1, source_target_pairs={{0,16},{8,24},{1,17},{9,25},{2,18},{10,26},{3,19},{11,27},{4,20},{... | collective-permute-start | bytes 393224 | tf_op jit(solution)/shard_map/ppermute | solution.py:764
  108.7 6.4 %collective-permute-start.9 = (bf16[64,1024]{1,0:T(8,128)(2,1)S(1)}, bf16[64,1024]{1,0:T(8,128)(2,1)S(1)}, u32[]{:S(2)}, u32[]{:S(2)}) collective-permute-start(bf16[64,1024]{1,0:T(8,128)(2,1)S(1)} %slice_select_fusion.grad_ref), channel_id=1, source_target_pairs={{0,4},{1,5},{2,6},{3,7},{4,0},{5,1},{6,2},{7,3},{8,12},{9,13},{10,... | collective-permute-start | bytes 393224 | tf_op jit(solution)/shard_map/ppermute | solution.py:769
  117.0 21.6 %all-to-all-start.1 = ((bf16[16,2,128,128]{3,2,1,0:T(8,128)(2,1)}), bf16[16,2,128,128]{3,2,1,0:T(8,128)(2,1)S(1)}, u32[]{:S(2)}, u32[]{:S(2)}) async-start(bf16[16,2,128,128]{3,2,1,0:T(8,128)(2,1)} %expand.3), calls=%async_computation.1 | async-start | bytes 2097152 | tf_op jit(solution)/shard_map/all_to_all | solution.py:779
